TPU v7x, 32 devices: a whole 2x2x4 slice. The times are simulated.
32 devices in a mesh: row: 8 (over z, y), col: 4 (over x, core).
Axes of the slice: x: 2, y: 2, z: 4, core: 2. Of those that a mesh axis runs over, the one named last changes fastest.
Arguments:
- latents: float32 [16384, 16], P('row'), may hold values from -6 to 6
- noise: float32 [16384, 16], P('row'), may hold values from -6 to 6
- timesteps: int32 [64], P('row'), may hold values from 0 to 999
- labels: int32 [64], P('row'), may hold values from 0 to 999
- loss_mask: int32 [16384], P('row'), may hold values from 0 to 1
- weights_in: float32 [2, 768, 13, 768], P(None, 'row', None, 'col'), may hold values from -0.21875 to 0.21875
- weights_out: float32 [2, 5, 768, 768], P(None, None, 'col', 'row'), may hold values from -0.4375 to 0.4375
- time_mlp: float32 [1024, 768], P('row', 'col'), may hold values from -0.375 to 0.375
- embed_table: float32 [1016, 768], P(None, 'col'), may hold values from -1.5 to 1.5
- final_layer: float32 [768, 1552], replicated, may hold values from -0.21875 to 0.21875
- bias_table: float32 [31, 768], P(None, 'col'), may hold values from -1.3 to 1.8
- final_bias: float32 [1552], replicated, may hold values from -1.75 to 1.75
- momentum_in: float32 [2, 768, 13, 768], P(None, 'row', None, 'col'), may hold values from -0.00012207031 to 0.00012207031
- momentum_out: float32 [2, 5, 768, 768], P(None, None, 'col', 'row'), may hold values from -0.00012207031 to 0.00012207031
- momentum_time: float32 [1024, 768], P('row', 'col'), may hold values from -0.00012207031 to 0.00012207031
- momentum_embed: float32 [1016, 768], P(None, 'col'), may hold values from -0.00012207031 to 0.00012207031
- momentum_final: float32 [768, 1552], replicated, may hold values from -0.00012207031 to 0.00012207031
- momentum_bias: float32 [31, 768], P(None, 'col'), may hold values from -0.00012207031 to 0.00012207031
- momentum_final_bias: float32 [1552], replicated, may hold values from -0.00012207031 to 0.00012207031
- variance_in: float32 [2, 768, 13, 768], P(None, 'row', None, 'col'), may hold values from 4.1635993e-11 to 1.6654397e-10
- variance_out: float32 [2, 5, 768, 768], P(None, None, 'col', 'row'), may hold values from 4.1635993e-11 to 1.6654397e-10
- variance_time: float32 [1024, 768], P('row', 'col'), may hold values from 4.1635993e-11 to 1.6654397e-10
- variance_embed: float32 [1016, 768], P(None, 'col'), may hold values from 4.1635996e-12 to 1.6654398e-11
- variance_final: float32 [768, 1552], replicated, may hold values from 4.1635993e-11 to 1.6654397e-10
- variance_bias: float32 [31, 768], P(None, 'col'), may hold values from 4.1635993e-11 to 1.6654397e-10
- variance_final_bias: float32 [1552], replicated, may hold values from 4.1635993e-11 to 1.6654397e-10
Outputs:
- loss_sum: float32 [], replicated
- token_count: float32 [], replicated
- grad_norm: float32 [], replicated
- new_weights_in: float32 [2, 768, 13, 768], P(None, 'row', None, 'col')
- new_momentum_in: float32 [2, 768, 13, 768], P(None, 'row', None, 'col')
- new_variance_in: float32 [2, 768, 13, 768], P(None, 'row', None, 'col')
- new_weights_out: float32 [2, 5, 768, 768], P(None, None, 'col', 'row')
- new_momentum_out: float32 [2, 5, 768, 768], P(None, None, 'col', 'row')
- new_variance_out: float32 [2, 5, 768, 768], P(None, None, 'col', 'row')
- new_time_mlp: float32 [1024, 768], P('row', 'col')
- new_momentum_time: float32 [1024, 768], P('row', 'col')
- new_variance_time: float32 [1024, 768], P('row', 'col')
- new_embed_table: float32 [1016, 768], P(None, 'col')
- new_momentum_embed: float32 [1016, 768], P(None, 'col')
- new_variance_embed: float32 [1016, 768], P(None, 'col')
- new_final_layer: float32 [768, 1552], replicated
- new_momentum_final: float32 [768, 1552], replicated
- new_variance_final: float32 [768, 1552], replicated
- new_bias_table: float32 [31, 768], P(None, 'col')
- new_momentum_bias: float32 [31, 768], P(None, 'col')
- new_variance_bias: float32 [31, 768], P(None, 'col')
- new_final_bias: float32 [1552], replicated
- new_momentum_final_bias: float32 [1552], replicated
- new_variance_final_bias: float32 [1552], replicated
All inputs are finite; a program needn't handle non-finite values.
Results may differ from a plain program's by a relative error of at most 0.012.
Values may be sent and summed in bfloat16 or wider, within the bound.
No kernel may reach another device: no remote copies, remote signals or barrier semaphores. Data moves between devices by JAX's collectives and lax.ppermute only.
A program may use at most 256 MiB of HBM per device.

v0:
```python
import math

import jax
import jax.numpy as jnp
from jax import lax
from jax.sharding import PartitionSpec as P

HEAD_DIM = 64
CLASSES = 1000
FREQ = 256
PATCH = 16
LEN = 256
STEPS_T = 1000
STEP = 10


HIGHEST = lax.Precision.HIGHEST
EPS_NORM = 1e-06
CLIP_NORM = 1.0
RATE = 0.05
RATE_BIAS = 0.25
BETA_ONE = 0.9
BETA_TWO = 0.999
DECAY = 0.01
ADAM_EPS = 1e-08


def positions(token_place, feature_index, model_width):
    half_width = model_width // 2
    freq_index = (feature_index % half_width).astype(jnp.float32)
    freq_rate = jnp.exp(-math.log(10000.0) * freq_index / half_width)
    angle_grid = token_place.astype(jnp.float32)[:, None] * freq_rate[None, :]
    return jnp.where(feature_index[None, :] < half_width, jnp.sin(angle_grid), jnp.cos(angle_grid))


def silu_slope(values):
    sigmoid_part = jax.nn.sigmoid(values)
    return sigmoid_part * (1.0 + values * (1.0 - sigmoid_part))


def per_token(values, vector, length):
    shaped = values.reshape(vector.shape[0], length, values.shape[-1])
    return (shaped * vector[:, None, :]).reshape(values.shape)


def sample_sums(values, sample_count, length):
    return jnp.sum(values.reshape(sample_count, length, values.shape[-1]), axis=1)


def modulate(normed, shift_part, scale_part, length):
    shaped = normed.reshape(shift_part.shape[0], length, normed.shape[-1])
    return (shaped * (1.0 + scale_part[:, None, :]) + shift_part[:, None, :]).reshape(normed.shape)


def gather_features(values):
    return lax.all_gather(values, "col", axis=1, tiled=True)


def branch_sum(partial_sum):
    return lax.psum_scatter(
        partial_sum.astype(jnp.bfloat16), "col", scatter_dimension=1, tiled=True
    ).astype(jnp.float32)


def gather_grads(values):
    return lax.all_gather(values, "col", axis=1, tiled=True)


def input_grads(partial_sum):
    return lax.psum_scatter(
        partial_sum.astype(jnp.bfloat16), "col", scatter_dimension=1, tiled=True
    ).astype(jnp.float32)


def normalize(residual, model_width):
    totals = lax.psum((jnp.sum(residual, axis=-1), jnp.sum(residual * residual, axis=-1)), "col")
    center = totals[0] / model_width
    spread = totals[1] / model_width - center * center
    inverse = lax.rsqrt(spread + EPS_NORM)
    return ((residual - center[:, None]) * inverse[:, None], inverse)


def normalize_back(grad_normed, normed, inverse, model_width):
    totals = lax.psum(
        (jnp.sum(grad_normed, axis=-1), jnp.sum(grad_normed * normed, axis=-1)), "col"
    )
    return inverse[:, None] * (
        grad_normed - totals[0][:, None] / model_width - normed * (totals[1][:, None] / model_width)
    )


def attention_forward(triple, sample_count, length, head_count):
    shaped = triple.reshape(sample_count, length, 3, head_count, HEAD_DIM)
    scores = jnp.einsum(
        "sqhd,skhd->shqk", shaped[:, :, 0], shaped[:, :, 1], preferred_element_type=jnp.float32
    ) * HEAD_DIM ** (-0.5)
    row_max = jnp.max(scores, axis=-1, keepdims=True)
    exp_scores = jnp.exp(scores - row_max)
    exp_total = jnp.sum(exp_scores, axis=-1, keepdims=True)
    attention_probs = exp_scores / exp_total
    log_total = row_max + jnp.log(exp_total)
    output = jnp.einsum(
        "shqk,skhd->sqhd",
        attention_probs.astype(jnp.bfloat16),
        shaped[:, :, 2],
        preferred_element_type=jnp.float32,
    )
    return (
        output.reshape(sample_count * length, head_count * HEAD_DIM).astype(jnp.bfloat16),
        log_total,
    )


def attention_backward(triple, log_total, grad_output, sample_count, length, head_count):
    shaped = triple.reshape(sample_count, length, 3, head_count, HEAD_DIM)
    query = shaped[:, :, 0]
    keys_part = shaped[:, :, 1]
    values_part = shaped[:, :, 2]
    factor = HEAD_DIM ** (-0.5)
    scores = (
        jnp.einsum("sqhd,skhd->shqk", query, keys_part, preferred_element_type=jnp.float32) * factor
    )
    attention_probs = jnp.exp(scores - log_total)
    grad_heads = grad_output.reshape(sample_count, length, head_count, HEAD_DIM)
    grad_probs = jnp.einsum(
        "sqhd,skhd->shqk", grad_heads, values_part, preferred_element_type=jnp.float32
    )
    grad_scores = attention_probs * (
        grad_probs - jnp.sum(grad_probs * attention_probs, axis=-1, keepdims=True)
    )
    grad_scores = grad_scores.astype(jnp.bfloat16)
    grad_query = (
        jnp.einsum("shqk,skhd->sqhd", grad_scores, keys_part, preferred_element_type=jnp.float32)
        * factor
    )
    grad_keys = (
        jnp.einsum("shqk,sqhd->skhd", grad_scores, query, preferred_element_type=jnp.float32)
        * factor
    )
    grad_values = jnp.einsum(
        "shqk,sqhd->skhd",
        attention_probs.astype(jnp.bfloat16),
        grad_heads,
        preferred_element_type=jnp.float32,
    )
    stacked = jnp.stack([grad_query, grad_keys, grad_values], axis=2)
    return stacked.reshape(sample_count * length, 3, head_count * HEAD_DIM)


def layer_forward(
    residual, cond_act, wide_in, wide_out, layer_rows, sample_count, length, head_count, model_width
):
    f_type = jnp.float32
    modes = (
        jnp.einsum("sd,dke->ske", cond_act, wide_in[:, :6], preferred_element_type=f_type)
        + layer_rows[None, :6]
    )
    normed_a, inverse_a = normalize(residual, model_width)
    input_a = gather_features(
        modulate(normed_a, modes[:, 0], modes[:, 1], length).astype(jnp.bfloat16)
    )
    triple = jnp.einsum("td,dke->tke", input_a, wide_in[:, 6:9], preferred_element_type=f_type)
    triple = (
        triple + jnp.stack([layer_rows[6], jnp.zeros_like(layer_rows[6]), layer_rows[7]])
    ).astype(jnp.bfloat16)
    attended, log_total = attention_forward(triple, sample_count, length, head_count)
    branch_a = (
        branch_sum(jnp.dot(attended, wide_out[0], preferred_element_type=f_type)) + layer_rows[12]
    )
    middle = residual + per_token(branch_a, modes[:, 2], length)
    normed_b, inverse_b = normalize(middle, model_width)
    input_b = gather_features(
        modulate(normed_b, modes[:, 3], modes[:, 4], length).astype(jnp.bfloat16)
    )
    hidden = (
        jnp.einsum("td,dke->tke", input_b, wide_in[:, 9:], preferred_element_type=f_type)
        + layer_rows[8:12]
    )
    activated = jax.nn.gelu(hidden, approximate=True).astype(jnp.bfloat16)
    branch_b = (
        branch_sum(
            jnp.einsum("tke,kef->tf", activated, wide_out[1:], preferred_element_type=f_type)
        )
        + layer_rows[13]
    )
    output = middle + per_token(branch_b, modes[:, 5], length)
    layer_cache = (
        modes,
        normed_a,
        inverse_a,
        input_a,
        triple,
        attended,
        log_total,
        branch_a,
        normed_b,
        inverse_b,
        input_b,
        hidden,
        activated,
        branch_b,
    )
    return (output, layer_cache)


def layer_backward(
    grad_resid,
    layer_cache,
    cond_act,
    wide_in,
    wide_out,
    sample_count,
    length,
    head_count,
    model_width,
):
    f_type = jnp.float32
    (
        modes,
        normed_a,
        inverse_a,
        input_a,
        triple,
        attended,
        log_total,
        branch_a,
        normed_b,
        inverse_b,
        input_b,
        hidden,
        activated,
        branch_b,
    ) = layer_cache
    grad_gate_b = sample_sums(grad_resid * branch_b, sample_count, length)
    grad_branch_b = per_token(grad_resid, modes[:, 5], length)
    full_grad_b = gather_grads(grad_branch_b.astype(jnp.bfloat16))
    grad_out_mlp = jnp.einsum("tke,tf->kef", activated, full_grad_b, preferred_element_type=f_type)
    grad_act = jnp.einsum("tf,kef->tke", full_grad_b, wide_out[1:], preferred_element_type=f_type)
    grad_hidden = jax.vjp(lambda hidden_in: jax.nn.gelu(hidden_in, approximate=True), hidden)[1](
        grad_act
    )[0]
    hidden_low = grad_hidden.astype(jnp.bfloat16)
    grad_in_mlp = jnp.einsum("td,tke->dke", input_b, hidden_low, preferred_element_type=f_type)
    grad_input_b = input_grads(
        jnp.einsum("tke,dke->td", hidden_low, wide_in[:, 9:], preferred_element_type=f_type)
    )
    grad_shift_b = sample_sums(grad_input_b, sample_count, length)
    grad_scale_b = sample_sums(grad_input_b * normed_b, sample_count, length)
    grad_middle = grad_resid + normalize_back(
        per_token(grad_input_b, 1.0 + modes[:, 4], length), normed_b, inverse_b, model_width
    )
    grad_gate_a = sample_sums(grad_middle * branch_a, sample_count, length)
    grad_branch_a = per_token(grad_middle, modes[:, 2], length)
    full_grad_a = gather_grads(grad_branch_a.astype(jnp.bfloat16))
    grad_out_attn = jnp.einsum("te,tf->ef", attended, full_grad_a, preferred_element_type=f_type)
    grad_attended = jnp.einsum(
        "tf,ef->te", full_grad_a, wide_out[0], preferred_element_type=f_type
    ).astype(jnp.bfloat16)
    grad_triple = attention_backward(
        triple, log_total, grad_attended, sample_count, length, head_count
    )
    triple_low = grad_triple.astype(jnp.bfloat16)
    grad_in_attn = jnp.einsum("td,tke->dke", input_a, triple_low, preferred_element_type=f_type)
    grad_input_a = input_grads(
        jnp.einsum("tke,dke->td", triple_low, wide_in[:, 6:9], preferred_element_type=f_type)
    )
    grad_shift_a = sample_sums(grad_input_a, sample_count, length)
    grad_scale_a = sample_sums(grad_input_a * normed_a, sample_count, length)
    grad_before = grad_middle + normalize_back(
        per_token(grad_input_a, 1.0 + modes[:, 1], length), normed_a, inverse_a, model_width
    )
    grad_modes = jnp.stack(
        [grad_shift_a, grad_scale_a, grad_gate_a, grad_shift_b, grad_scale_b, grad_gate_b], axis=1
    )
    modes_low = grad_modes.astype(jnp.bfloat16)
    grad_in_mod = jnp.einsum("sd,ske->dke", cond_act, modes_low, preferred_element_type=f_type)
    grad_cond = jnp.einsum("ske,dke->sd", modes_low, wide_in[:, :6], preferred_element_type=f_type)
    grad_rows = jnp.concatenate(
        [
            jnp.sum(grad_modes, axis=0),
            jnp.sum(grad_triple[:, 0], axis=0)[None],
            jnp.sum(grad_triple[:, 2], axis=0)[None],
            jnp.sum(grad_hidden, axis=0),
            jnp.sum(grad_branch_a, axis=0)[None],
            jnp.sum(grad_branch_b, axis=0)[None],
        ],
        axis=0,
    )
    grad_in = jnp.concatenate([grad_in_mod, grad_in_attn, grad_in_mlp], axis=1)
    grad_out = jnp.concatenate([grad_out_attn[None], grad_out_mlp], axis=0)
    return (grad_before, grad_cond, grad_in, grad_out, grad_rows)


def adam_update(weight, gradient, moment, second, clip_factor, step_rate):
    gradient = gradient * clip_factor
    moment = BETA_ONE * moment + (1.0 - BETA_ONE) * gradient
    second = BETA_TWO * second + (1.0 - BETA_TWO) * gradient * gradient
    update = (
        moment / (1.0 - BETA_ONE**STEP) / (jnp.sqrt(second / (1.0 - BETA_TWO**STEP)) + ADAM_EPS)
    )
    return (weight - step_rate * (update + DECAY * weight), moment, second)


def squared(values):
    return jnp.sum(values * values)


def on_device(
    latents,
    noise,
    timesteps,
    labels,
    loss_mask,
    weights_in,
    weights_out,
    time_mlp,
    embed_table,
    final_layer,
    bias_table,
    final_bias,
    momentum_in,
    momentum_out,
    momentum_time,
    momentum_embed,
    momentum_final,
    momentum_bias,
    momentum_final_bias,
    variance_in,
    variance_out,
    variance_time,
    variance_embed,
    variance_final,
    variance_bias,
    variance_final_bias,
):
    f_type = jnp.float32
    col_index = lax.axis_index("col")
    row_index = lax.axis_index("row")
    row_total = lax.axis_size("row")
    sample_count = timesteps.shape[0]
    token_count = latents.shape[0]
    length = LEN
    model_width = final_layer.shape[0]
    col_width = weights_in.shape[3]
    head_count = col_width // HEAD_DIM
    layer_count = weights_in.shape[0]
    bias_base = layer_count * 14
    col_offset = col_index * col_width
    first_col = (col_index == 0).astype(f_type)
    last_row = (row_index == row_total - 1).astype(f_type)
    time_full, in_full, out_full = (
        lax.all_gather(time_mlp.astype(jnp.bfloat16), "row", axis=0, tiled=True),
        lax.all_gather(weights_in.astype(jnp.bfloat16), "row", axis=1, tiled=True),
        lax.all_gather(weights_out.astype(jnp.bfloat16), "row", axis=3, tiled=True),
    )
    embed_low = embed_table.astype(jnp.bfloat16)
    final_low = final_layer.astype(jnp.bfloat16)
    steps_value = timesteps.astype(f_type)
    alpha_bar = jnp.cos((steps_value / STEPS_T + 0.008) / 1.008 * (math.pi / 2)) ** 2
    keep_part = jnp.repeat(jnp.sqrt(alpha_bar), length)[:, None]
    noise_part = jnp.repeat(jnp.sqrt(1.0 - alpha_bar), length)[:, None]
    noisy_input = (keep_part * latents + noise_part * noise).astype(jnp.bfloat16)
    half_freq = FREQ // 2
    freq_rate = jnp.exp(-math.log(10000.0) * jnp.arange(half_freq, dtype=f_type) / half_freq)
    angle_grid = steps_value[:, None] * freq_rate[None, :]
    freq_low = jnp.concatenate([jnp.cos(angle_grid), jnp.sin(angle_grid)], axis=1).astype(
        jnp.bfloat16
    )
    first_time = (
        jnp.dot(freq_low, time_full[:FREQ], preferred_element_type=f_type) + bias_table[bias_base]
    )
    first_act = gather_features(jax.nn.silu(first_time).astype(jnp.bfloat16))
    second_time = (
        jnp.dot(first_act, time_full[FREQ:], preferred_element_type=f_type)
        + bias_table[bias_base + 1]
    )
    one_hot = labels[:, None] == jnp.arange(CLASSES, dtype=jnp.int32)[None, :]
    condition = second_time + jnp.dot(
        one_hot.astype(jnp.bfloat16), embed_low[:CLASSES], preferred_element_type=f_type
    )
    cond_act = gather_features(jax.nn.silu(condition).astype(jnp.bfloat16))
    token_place = jnp.arange(token_count, dtype=jnp.int32) % length
    feature_index = col_offset + jnp.arange(col_width, dtype=jnp.int32)
    residual = (
        jnp.dot(noisy_input, embed_low[CLASSES:], preferred_element_type=f_type)
        + bias_table[bias_base + 2]
        + positions(token_place, feature_index, model_width)
    )
    caches = []
    for layer_index in range(layer_count):
        residual, layer_cache = layer_forward(
            residual,
            cond_act,
            in_full[layer_index],
            out_full[layer_index],
            bias_table[layer_index * 14 : (layer_index + 1) * 14],
            sample_count,
            length,
            head_count,
            model_width,
        )
        caches.append(layer_cache)
    final_mod = (
        jnp.dot(cond_act, final_low[:, : 2 * model_width], preferred_element_type=f_type)
        + final_bias[: 2 * model_width]
    )
    shift_final = lax.dynamic_slice_in_dim(final_mod, col_offset, col_width, 1)
    scale_final = lax.dynamic_slice_in_dim(final_mod, model_width + col_offset, col_width, 1)
    normed_final, inverse_final = normalize(residual, model_width)
    input_final = gather_features(
        modulate(normed_final, shift_final, scale_final, length).astype(jnp.bfloat16)
    )
    head_weight = final_low[:, 2 * model_width :]
    predicted = (
        jnp.dot(input_final, head_weight, preferred_element_type=f_type)
        + final_bias[2 * model_width :]
    )
    mask_value = loss_mask.astype(f_type)[:, None]
    error = predicted - noise
    loss_local = jnp.sum(mask_value * error * error)
    count_local = jnp.sum(loss_mask.astype(f_type))
    grad_pred = 2.0 * mask_value * error
    pred_low = grad_pred.astype(jnp.bfloat16)
    grad_head = jnp.einsum("td,tp->dp", input_final, pred_low, preferred_element_type=f_type)
    grad_head_bias = jnp.sum(grad_pred, axis=0)
    head_rows = lax.dynamic_slice_in_dim(head_weight, col_offset, col_width, 0)
    grad_input_final = jnp.einsum("tp,dp->td", pred_low, head_rows, preferred_element_type=f_type)
    grad_shift_final = sample_sums(grad_input_final, sample_count, length)
    grad_scale_final = sample_sums(grad_input_final * normed_final, sample_count, length)
    grad_resid = normalize_back(
        per_token(grad_input_final, 1.0 + scale_final, length),
        normed_final,
        inverse_final,
        model_width,
    )
    final_mod_low = jnp.concatenate([grad_shift_final, grad_scale_final], axis=1).astype(
        jnp.bfloat16
    )
    grad_final_mod = jnp.einsum("sd,se->de", cond_act, final_mod_low, preferred_element_type=f_type)
    final_cols = jnp.concatenate(
        [
            lax.dynamic_slice_in_dim(final_low, col_offset, col_width, 1),
            lax.dynamic_slice_in_dim(final_low, model_width + col_offset, col_width, 1),
        ],
        axis=1,
    )
    grad_cond_total = jnp.einsum(
        "se,de->sd", final_mod_low, final_cols, preferred_element_type=f_type
    )
    back_time, back_in, back_out = (time_full, in_full, out_full)
    grads_in = [None] * layer_count
    grads_out = [None] * layer_count
    grads_rows = [None] * layer_count
    for layer_index in reversed(range(layer_count)):
        (
            grad_resid,
            grad_cond,
            grads_in[layer_index],
            grads_out[layer_index],
            grads_rows[layer_index],
        ) = layer_backward(
            grad_resid,
            caches[layer_index],
            cond_act,
            back_in[layer_index],
            back_out[layer_index],
            sample_count,
            length,
            head_count,
            model_width,
        )
        grad_cond_total = grad_cond_total + grad_cond
    grad_cond_act = input_grads(grad_cond_total)
    grad_condition = grad_cond_act * silu_slope(condition)
    grad_classes = jnp.dot(one_hot.astype(f_type).T, grad_condition, precision=HIGHEST)
    condition_low = grad_condition.astype(jnp.bfloat16)
    grad_time_second = jnp.einsum(
        "sd,se->de", first_act, condition_low, preferred_element_type=f_type
    )
    grad_first_act = input_grads(
        jnp.einsum("se,de->sd", condition_low, back_time[FREQ:], preferred_element_type=f_type)
    )
    grad_first = grad_first_act * silu_slope(first_time)
    grad_time_first = jnp.einsum(
        "sf,se->fe", freq_low, grad_first.astype(jnp.bfloat16), preferred_element_type=f_type
    )
    grad_patch = jnp.einsum(
        "tp,td->pd", noisy_input, grad_resid.astype(jnp.bfloat16), preferred_element_type=f_type
    )
    grad_bias_rows = jnp.concatenate(
        grads_rows
        + [
            jnp.sum(grad_first, axis=0)[None],
            jnp.sum(grad_condition, axis=0)[None],
            jnp.sum(grad_resid, axis=0)[None],
        ],
        axis=0,
    )
    grad_embed_cols = jnp.concatenate([grad_classes, grad_patch], axis=0)
    shift_sum = jnp.sum(grad_shift_final, axis=0)
    scale_sum = jnp.sum(grad_scale_final, axis=0)
    grad_time = jnp.concatenate([grad_time_first, grad_time_second], axis=0)
    summed_time, summed_in, summed_out = (
        lax.psum_scatter(grad_time, "row", scatter_dimension=0, tiled=True),
        lax.psum_scatter(jnp.stack(grads_in), "row", scatter_dimension=1, tiled=True),
        lax.psum_scatter(jnp.stack(grads_out), "row", scatter_dimension=3, tiled=True),
    )

    def widen_cols(piece):
        return lax.dynamic_update_slice(
            jnp.zeros((piece.shape[0], model_width), f_type), piece, (0, col_offset)
        )

    wide_final = jnp.zeros((model_width, 2 * model_width + PATCH), f_type)
    wide_final = lax.dynamic_update_slice(
        wide_final, grad_final_mod[:, :col_width], (0, col_offset)
    )
    wide_final = lax.dynamic_update_slice(
        wide_final, grad_final_mod[:, col_width:], (0, model_width + col_offset)
    )
    wide_final = wide_final.at[:, 2 * model_width :].set(grad_head * first_col)
    wide_bias = jnp.zeros((2 * model_width + PATCH,), f_type)
    wide_bias = lax.dynamic_update_slice(wide_bias, shift_sum, (col_offset,))
    wide_bias = lax.dynamic_update_slice(wide_bias, scale_sum, (model_width + col_offset,))
    wide_bias = wide_bias.at[2 * model_width :].set(grad_head_bias * first_col)
    shared = lax.psum(
        (
            widen_cols(grad_bias_rows),
            widen_cols(grad_embed_cols),
            wide_final,
            wide_bias,
            loss_local * first_col,
            count_local * first_col,
        ),
        ("row", "col"),
    )
    bias_grad = lax.dynamic_slice_in_dim(shared[0], col_offset, col_width, 1)
    embed_grad = lax.dynamic_slice_in_dim(shared[1], col_offset, col_width, 1)
    final_grad = shared[2]
    final_bias_grad = shared[3]
    loss_total = shared[4]
    count_total = shared[5]
    shared_squares = (
        last_row
        * first_col
        * (squared(shared[0]) + squared(shared[1]) + squared(shared[2]) + squared(shared[3]))
    )
    own_squares = squared(summed_time) + squared(summed_in) + squared(summed_out)
    norm_squares = lax.psum(own_squares + shared_squares, ("row", "col"))
    grad_norm = jnp.sqrt(norm_squares)
    clip_factor = jnp.minimum(1.0, CLIP_NORM / (grad_norm + 1e-06))
    results = [loss_total, count_total, grad_norm]
    groups = (
        (weights_in, summed_in, momentum_in, variance_in, RATE),
        (weights_out, summed_out, momentum_out, variance_out, RATE),
        (time_mlp, summed_time, momentum_time, variance_time, RATE),
        (embed_table, embed_grad, momentum_embed, variance_embed, RATE),
        (final_layer, final_grad, momentum_final, variance_final, RATE),
        (bias_table, bias_grad, momentum_bias, variance_bias, RATE_BIAS),
        (final_bias, final_bias_grad, momentum_final_bias, variance_final_bias, RATE_BIAS),
    )
    for weight, gradient, moment, second, step_rate in groups:
        results.extend(adam_update(weight, gradient, moment, second, clip_factor, step_rate))
    return tuple(results)


def solution(mesh):
    placed = (
        P("row", None),
        P("row", None),
        P("row"),
        P("row"),
        P("row"),
        P(None, "row", None, "col"),
        P(None, None, "col", "row"),
        P("row", "col"),
        P(None, "col"),
        P(),
        P(None, "col"),
        P(),
        P(None, "row", None, "col"),
        P(None, None, "col", "row"),
        P("row", "col"),
        P(None, "col"),
        P(),
        P(None, "col"),
        P(),
        P(None, "row", None, "col"),
        P(None, None, "col", "row"),
        P("row", "col"),
        P(None, "col"),
        P(),
        P(None, "col"),
        P(),
    )
    return jax.shard_map(
        on_device,
        mesh=mesh,
        in_specs=placed,
        out_specs=(
            P(),
            P(),
            P(),
            P(None, "row", None, "col"),
            P(None, "row", None, "col"),
            P(None, "row", None, "col"),
            P(None, None, "col", "row"),
            P(None, None, "col", "row"),
            P(None, None, "col", "row"),
            P("row", "col"),
            P("row", "col"),
            P("row", "col"),
            P(None, "col"),
            P(None, "col"),
            P(None, "col"),
            P(),
            P(),
            P(),
            P(None, "col"),
            P(None, "col"),
            P(None, "col"),
            P(),
            P(),
            P(),
        ),
        check_vma=False,
    )
```

profile of v0, /device:TPU:0, one launch (start us, length us, event | category | flops | bytes accessed | tf_op | source)
XLA Modules:
  0.0 1909.6 jit_solution(6895514704288675696)
XLA Ops:
  14.6 30.5 %all_gather.42 = bf16[1024,192]{0,1:T(8,128)(2,1)S(1)} all-gather(bf16[128,192]{0,1:T(8,128)(2,1)S(1)} %convert_element_type.232), channel_id=1, replica_groups=mesh['row'=8,'col'=4] {'row'}, dimensions={0}, use_global_device_ids=true | all-gather | bytes 442368 | tf_op jit(solution)/shard_map/all_gather | solution.py:352
  74.6 92.7 %all-gather.14.cloned.1.call-done = bf16[2,768,13,192]{3,0,2,1:T(2,128)(2,1)} async-done(((bf16[2,96,13,192]{3,0,2,1:T(2,128)(2,1)}), bf16[2,768,13,192]{3,0,2,1:T(2,128)(2,1)}) %all-gather.14.cloned.1.call-update) | async-done | bytes 7667728 | tf_op jit(solution)/shard_map/all_gather | solution.py:353
  167.3 20.9 %fusion.190 = (bf16[1,768,13,192]{3,0,2,1:T(2,128)(2,1)}, bf16[1,768,13,192]{3,0,2,1:T(2,128)(2,1)}) fusion(bf16[2,768,13,192]{3,0,2,1:T(2,128)(2,1)} %all-gather.14.cloned.1.call-done), kind=kLoop, calls=%fused_computation.396 | loop fusion | bytes 15335424 | tf_op jit(solution)/shard_map/slice | solution.py:394
  188.2 23.2 %copy.441 = bf16[1,768,13,192]{1,3,2,0:T(8,128)(2,1)} copy(bf16[1,768,13,192]{3,0,2,1:T(2,128)(2,1)} %get-tuple-element.281) | data formatting | bytes 7667712
  217.1 21.2 %all-gather.18.cloned.1.call-done = bf16[2,5,192,768]{2,0,1,3:T(2,128)(2,1)} async-done(((bf16[2,5,192,96]{2,0,1,3:T(2,128)(2,1)}), bf16[2,5,192,768]{2,0,1,3:T(2,128)(2,1)}) %all-gather.18.cloned.1.call-update) | async-done | bytes 2949136 | tf_op jit(solution)/shard_map/all_gather | solution.py:354
  243.9 23.6 %all-gather.16.cloned.1.call-done = bf16[2048,768]{0,1:T(8,128)(2,1)} async-done(((bf16[2048,192]{0,1:T(8,128)(2,1)}), bf16[2048,768]{0,1:T(8,128)(2,1)}) %all-gather.16.cloned.1.call-update) | async-done | bytes 3145744 | tf_op jit(solution)/shard_map/all_gather | solution.py:56
  297.2 23.1 %reduce-scatter.22.cloned.1.call-done = bf16[2048,192]{0,1:T(8,128)(2,1)} async-done(((bf16[2048,768]{0,1:T(8,128)(2,1)}), bf16[2048,192]{0,1:T(8,128)(2,1)}) %reduce-scatter.22.cloned.1.call-update) | async-done | bytes 786448 | tf_op jit(solution)/shard_map/reduce_scatter | solution.py:60
  380.3 23.4 %copy.447 = bf16[1,768,13,192]{1,3,2,0:T(8,128)(2,1)} copy(bf16[1,768,13,192]{3,0,2,1:T(2,128)(2,1)} %get-tuple-element.280) | data formatting | bytes 7667712
  435.6 25.9 %all-gather.22.cloned.1.call-done = bf16[2048,768]{0,1:T(8,128)(2,1)} async-done(((bf16[2048,192]{0,1:T(8,128)(2,1)}), bf16[2048,768]{0,1:T(8,128)(2,1)}) %all-gather.22.cloned.1.call-update) | async-done | bytes 3145744 | tf_op jit(solution)/shard_map/all_gather | solution.py:56
  482.5 31.7 %reduce-scatter.26.cloned.1.call-done = bf16[2048,192]{0,1:T(8,128)(2,1)} async-done(((bf16[2048,768]{0,1:T(8,128)(2,1)}), bf16[2048,192]{0,1:T(8,128)(2,1)}) %reduce-scatter.26.cloned.1.call-update) | async-done | bytes 786448 | tf_op jit(solution)/shard_map/reduce_scatter | solution.py:60
  541.0 19.1 %all-gather.24.cloned.1.call-done = bf16[2048,768]{0,1:T(8,128)(2,1)} async-done(((bf16[2048,192]{0,1:T(8,128)(2,1)}), bf16[2048,768]{0,1:T(8,128)(2,1)}) %all-gather.24.cloned.1.call-update) | async-done | bytes 3145744 | tf_op jit(solution)/shard_map/all_gather | solution.py:56
  591.0 20.1 %reduce-scatter.28.cloned.1.call-done = bf16[2048,192]{0,1:T(8,128)(2,1)} async-done(((bf16[2048,768]{0,1:T(8,128)(2,1)}), bf16[2048,192]{0,1:T(8,128)(2,1)}) %reduce-scatter.28.cloned.1.call-update) | async-done | bytes 786448 | tf_op jit(solution)/shard_map/reduce_scatter | solution.py:60
  630.1 27.9 %all-gather.26.cloned.1.call-done = bf16[2048,768]{0,1:T(8,128)(2,1)} async-done(((bf16[2048,192]{0,1:T(8,128)(2,1)}), bf16[2048,768]{0,1:T(8,128)(2,1)}) %all-gather.26.cloned.1.call-update) | async-done | bytes 3145744 | tf_op jit(solution)/shard_map/all_gather | solution.py:56
  681.8 28.8 %all-gather.28.cloned.1.call-done = bf16[2048,768]{0,1:T(8,128)(2,1)} async-done(((bf16[2048,192]{0,1:T(8,128)(2,1)}), bf16[2048,768]{0,1:T(8,128)(2,1)}) %all-gather.28.cloned.1.call-update) | async-done | bytes 3145744 | tf_op jit(solution)/shard_map/all_gather | solution.py:66
  728.3 38.1 %reduce-scatter.30.cloned.1.call-done = bf16[2048,192]{0,1:T(8,128)(2,1)} async-done(((bf16[2048,768]{0,1:T(8,128)(2,1)}), bf16[2048,192]{0,1:T(8,128)(2,1)}) %reduce-scatter.30.cloned.1.call-update) | async-done | bytes 786448 | tf_op jit(solution)/shard_map/reduce_scatter | solution.py:70
  788.0 29.2 %all-gather.30.cloned.1.call-done = bf16[2048,768]{0,1:T(8,128)(2,1)} async-done(((bf16[2048,192]{0,1:T(8,128)(2,1)}), bf16[2048,768]{0,1:T(8,128)(2,1)}) %all-gather.30.cloned.1.call-update) | async-done | bytes 3145744 | tf_op jit(solution)/shard_map/all_gather | solution.py:66
  856.3 38.1 %reduce-scatter.32.cloned.1.call-done = bf16[2048,192]{0,1:T(8,128)(2,1)} async-done(((bf16[2048,768]{0,1:T(8,128)(2,1)}), bf16[2048,192]{0,1:T(8,128)(2,1)}) %reduce-scatter.32.cloned.1.call-update) | async-done | bytes 786448 | tf_op jit(solution)/shard_map/reduce_scatter | solution.py:70
  915.5 29.7 %all-gather.32.cloned.1.call-done = bf16[2048,768]{0,1:T(8,128)(2,1)} async-done(((bf16[2048,192]{0,1:T(8,128)(2,1)}), bf16[2048,768]{0,1:T(8,128)(2,1)}) %all-gather.32.cloned.1.call-update) | async-done | bytes 3145744 | tf_op jit(solution)/shard_map/all_gather | solution.py:66
  962.8 38.0 %reduce-scatter.34.cloned.1.call-done = bf16[2048,192]{0,1:T(8,128)(2,1)} async-done(((bf16[2048,768]{0,1:T(8,128)(2,1)}), bf16[2048,192]{0,1:T(8,128)(2,1)}) %reduce-scatter.34.cloned.1.call-update) | async-done | bytes 786448 | tf_op jit(solution)/shard_map/reduce_scatter | solution.py:70
  1021.8 29.4 %all-gather.34.cloned.1.call-done = bf16[2048,768]{0,1:T(8,128)(2,1)} async-done(((bf16[2048,192]{0,1:T(8,128)(2,1)}), bf16[2048,768]{0,1:T(8,128)(2,1)}) %all-gather.34.cloned.1.call-update) | async-done | bytes 3145744 | tf_op jit(solution)/shard_map/all_gather | solution.py:66
  1149.4 18.9 reduce-scatter.40.cloned.1.call-done
  1175.3 18.0 reduce-scatter.42.cloned.1.call-done
  1225.9 12.6 copy.439
  1274.0 12.7 pad_maximum_fusion
  1286.7 23.0 %copy.437 = f32[2,768,13,192]{3,2,0,1:T(8,128)} copy(f32[2,768,13,192]{1,3,2,0:T(8,128)} %pad_maximum_fusion) | data formatting | bytes 30670848
  1309.8 22.8 %reshape.406 = f32[768,4992]{1,0:T(8,128)} reshape(f32[768,2,13,192]{3,2,1,0:T(8,128)} %bitcast.459) | data formatting | bytes 30670848
  1341.6 41.2 %psum.214 = f32[1552]{0:T(1024)S(1)} all-reduce(f32[1552]{0:T(1024)S(1)} %multiply_dynamic-update-slice_fusion), channel_id=1, replica_groups=mesh['row'=8,'col'=4] {'row','col'}, use_global_device_ids=true, to_apply=%region_104.105 | all-reduce | flops 1552 | bytes 12416 | tf_op jit(solution)/shard_map/psum | solution.py:526
  1385.0 59.6 %all-reduce.14.cloned.1.call-done = (f32[31,768]{1,0:T(8,128)}, f32[1016,768]{0,1:T(8,128)}, f32[768,1552]{0,1:T(8,128)}) async-done(((f32[31,768]{1,0:T(8,128)}, f32[1016,768]{0,1:T(8,128)}, f32[768,1552]{0,1:T(8,128)}), (f32[31,768]{1,0:T(8,128)}, f32[1016,768]{0,1:T(8,128)}, f32[768,1552]{0,1:T(8,128)})) %all-reduce.14.cloned.1.call-update) | async-done | bytes 7984144 | tf_op jit(solution)/shard_map/psum | solution.py:526
  1456.2 103.5 %reduce-scatter.46.cloned.1.call-done = f32[96,1920]{1,0:T(8,128)} async-done(((f32[768,1920]{1,0:T(8,128)}), f32[96,1920]{1,0:T(8,128)}) %reduce-scatter.46.cloned.1.call-update) | async-done | bytes 737296
  1563.0 245.8 %reduce-scatter.44.cloned.1.call-done = f32[96,4992]{1,0:T(8,128)} async-done(((f32[768,4992]{1,0:T(8,128)}), f32[96,4992]{1,0:T(8,128)}) %reduce-scatter.44.cloned.1.call-update) | async-done | bytes 1916944
  1822.3 39.5 %all-reduce = (f32[]{:T(128)}, f32[]{:T(128)}, f32[]{:T(128)}) all-reduce(f32[]{:T(128)S(6)} %mul.1046, f32[]{:T(128)S(6)} %mul.1047, f32[]{:T(128)S(6)} %add.706), channel_id=1, replica_groups=mesh['row'=8,'col'=4] {'row','col'}, use_global_device_ids=true, to_apply=%region_29.30 | all-reduce | flops 3 | bytes 24 | tf_op jit(solution)/shard_map/psum | solution.py:526
  1882.3 13.2 multiply_subtract_fusion
  (745 shorter events, 659.4 us)
Async XLA Ops:
  7.2 160.1 %all-gather.14.cloned.1.call-start = ((), (), s32[]{:S(2)}) async-start(), calls=%async_computation.13 | async-start | bytes 11501568 | tf_op jit(solution)/shard_map/all_gather | solution.py:353
  12.2 226.2 %all-gather.18.cloned.1.call-start = ((), (), s32[]{:S(2)}) async-start(), calls=%async_computation.15 | async-start | bytes 4423680 | tf_op jit(solution)/shard_map/all_gather | solution.py:354
  13.6 253.8 %all-gather.16.cloned.1.call-start = ((), (), s32[]{:S(2)}) async-start(), calls=%async_computation.14 | async-start | bytes 3932160 | tf_op jit(solution)/shard_map/all_gather | solution.py:56
  14.4 305.9 %copy-start.128 = (f32[1,192]{1,0:T(1,128)}, f32[1,192]{1,0:T(1,128)S(1)}, u32[]{:S(2)}) copy-start(f32[1,192]{1,0:T(1,128)S(1)} %get-tuple-element.331) | copy-start | bytes 2308
  14.4 401.8 %copy-start.130 = (f32[1,192]{1,0:T(1,128)}, f32[1,192]{1,0:T(1,128)S(1)}, u32[]{:S(2)}) copy-start(f32[1,192]{1,0:T(1,128)S(1)} %get-tuple-element.330) | copy-start | bytes 2308
  45.1 143.0 %copy-start.61 = (bf16[1024,192]{0,1:T(8,128)(2,1)}, bf16[1024,192]{0,1:T(8,128)(2,1)S(1)}, u32[]{:S(2)}) copy-start(bf16[1024,192]{0,1:T(8,128)(2,1)S(1)} %all_gather.42) | copy-start | bytes 1179652
  45.2 142.9 %copy-start.122 = (bf16[8,128]{1,0:T(8,128)(2,1)}, bf16[8,128]{1,0:T(8,128)(2,1)S(1)}, u32[]{:S(2)}) copy-start(bf16[8,128]{1,0:T(8,128)(2,1)S(1)} %get-tuple-element.351) | copy-start | bytes 6148
  45.2 142.9 %copy-start.123 = (bf16[8,128]{1,0:T(8,128)(2,1)}, bf16[8,128]{1,0:T(8,128)(2,1)S(1)}, u32[]{:S(2)}) copy-start(bf16[8,128]{1,0:T(8,128)(2,1)S(1)} %get-tuple-element.352) | copy-start | bytes 6148
  56.5 347.1 %copy-start.82 = (bf16[768,8,1]{0,1,2:T(8,128)(2,1)}, bf16[768,8,1]{0,1,2:T(8,128)(2,1)S(1)}, u32[]{:S(2)}) copy-start(bf16[768,8,1]{0,1,2:T(8,128)(2,1)S(1)} %reshape.374) | copy-start | bytes 36868
  62.5 153.0 %copy-start.12 = (f32[2048,192]{0,1:T(8,128)}, f32[2048,192]{0,1:T(8,128)S(1)}, u32[]{:S(2)}) copy-start(f32[2048,192]{0,1:T(8,128)S(1)} %get-tuple-element.357) | copy-start | bytes 4718596
  216.9 103.4 %reduce-scatter.22.cloned.1.call-start = ((), (), s32[]{:S(2)}) async-start(), calls=%async_computation.16 | async-start | bytes 3932160 | tf_op jit(solution)/shard_map/reduce_scatter | solution.py:60
  282.2 83.3 %all-gather.20.cloned.1.call-start = ((), (), s32[]{:S(2)}) async-start(), calls=%async_computation.17 | async-start | bytes 3932160 | tf_op jit(solution)/shard_map/all_gather | solution.py:56
  335.9 80.4 %reduce-scatter.24.cloned.1.call-start = ((), (), s32[]{:S(2)}) async-start(), calls=%async_computation.18 | async-start | bytes 3932160 | tf_op jit(solution)/shard_map/reduce_scatter | solution.py:60
  378.1 83.4 %all-gather.22.cloned.1.call-start = ((), (), s32[]{:S(2)}) async-start(), calls=%async_computation.19 | async-start | bytes 3932160 | tf_op jit(solution)/shard_map/all_gather | solution.py:56
  431.7 82.5 %reduce-scatter.26.cloned.1.call-start = ((), (), s32[]{:S(2)}) async-start(), calls=%async_computation.20 | async-start | bytes 3932160 | tf_op jit(solution)/shard_map/reduce_scatter | solution.py:60
  476.1 84.1 %all-gather.24.cloned.1.call-start = ((), (), s32[]{:S(2)}) async-start(), calls=%async_computation.21 | async-start | bytes 3932160 | tf_op jit(solution)/shard_map/all_gather | solution.py:56
  530.4 80.8 %reduce-scatter.28.cloned.1.call-start = ((), (), s32[]{:S(2)}) async-start(), calls=%async_computation.22 | async-start | bytes 3932160 | tf_op jit(solution)/shard_map/reduce_scatter | solution.py:60
  573.0 84.9 %all-gather.26.cloned.1.call-start = ((), (), s32[]{:S(2)}) async-start(), calls=%async_computation.23 | async-start | bytes 3932160 | tf_op jit(solution)/shard_map/all_gather | solution.py:56
  628.2 82.4 %all-gather.28.cloned.1.call-start = ((), (), s32[]{:S(2)}) async-start(), calls=%async_computation.24 | async-start | bytes 3932160 | tf_op jit(solution)/shard_map/all_gather | solution.py:66
  681.5 84.9 %reduce-scatter.30.cloned.1.call-start = ((), (), s32[]{:S(2)}) async-start(), calls=%async_computation.25 | async-start | bytes 3932160 | tf_op jit(solution)/shard_map/reduce_scatter | solution.py:70
  728.3 89.0 %all-gather.30.cloned.1.call-start = ((), (), s32[]{:S(2)}) async-start(), calls=%async_computation.26 | async-start | bytes 3932160 | tf_op jit(solution)/shard_map/all_gather | solution.py:66
  787.5 106.8 %reduce-scatter.32.cloned.1.call-start = ((), (), s32[]{:S(2)}) async-start(), calls=%async_computation.27 | async-start | bytes 3932160 | tf_op jit(solution)/shard_map/reduce_scatter | solution.py:70
  856.3 88.9 %all-gather.32.cloned.1.call-start = ((), (), s32[]{:S(2)}) async-start(), calls=%async_computation.28 | async-start | bytes 3932160 | tf_op jit(solution)/shard_map/all_gather | solution.py:66
  915.4 85.5 %reduce-scatter.34.cloned.1.call-start = ((), (), s32[]{:S(2)}) async-start(), calls=%async_computation.29 | async-start | bytes 3932160 | tf_op jit(solution)/shard_map/reduce_scatter | solution.py:70
  962.8 88.5 %all-gather.34.cloned.1.call-start = ((), (), s32[]{:S(2)}) async-start(), calls=%async_computation.30 | async-start | bytes 3932160 | tf_op jit(solution)/shard_map/all_gather | solution.py:66
  1021.5 95.1 %reduce-scatter.36.cloned.1.call-start = ((), (), s32[]{:S(2)}) async-start(), calls=%async_computation.31 | async-start | bytes 3932160 | tf_op jit(solution)/shard_map/reduce_scatter | solution.py:70
  1078.5 89.8 %reduce-scatter.40.cloned.1.call-start = ((), (), s32[]{:S(2)}) async-start(), calls=%async_computation.33 | async-start | bytes 245760
  1147.4 45.9 %reduce-scatter.42.cloned.1.call-start = ((), (), s32[]{:S(2)}) async-start(), calls=%async_computation.34 | async-start | bytes 245760
  1173.4 210.0 %reduce-scatter.38.cloned.1.call-start = ((), (), s32[]{:S(2)}) async-start(), calls=%async_computation.32 | async-start | bytes 884736 | tf_op jit(solution)/shard_map/reduce_scatter | solution.py:504
  1197.2 247.4 %all-reduce.14.cloned.1.call-start = ((), (), s32[]{:S(2)}) async-start(), calls=%async_computation.37 | async-start | bytes 16023552 | tf_op jit(solution)/shard_map/psum | solution.py:526
  1205.9 353.8 %reduce-scatter.46.cloned.1.call-start = ((), (), s32[]{:S(2)}) async-start(), calls=%async_computation.36 | async-start | bytes 6635520
  1250.0 558.8 %reduce-scatter.44.cloned.1.call-start = ((), (), s32[]{:S(2)}) async-start(), calls=%async_computation.35 | async-start | bytes 17252352
  (165 other events, 2274.3 us)
Sparse Core Ops, SparseCore 0:
  12.3 154.9 all-gather.13
  170.1 68.2 all-gather.17
  240.5 26.8 all-gather.15
  282.3 37.9 reduce-scatter.21
  336.0 29.5 all-gather.19
  378.2 37.9 reduce-scatter.23
  431.8 29.5 all-gather.21
  476.2 37.9 reduce-scatter.25
  530.5 29.6 all-gather.23
  573.2 37.9 reduce-scatter.27
  628.4 29.5 all-gather.25
  681.7 28.8 all-gather.27
  728.4 37.9 reduce-scatter.29
  787.7 29.5 all-gather.29
  856.4 37.9 reduce-scatter.31
  915.5 29.6 all-gather.31
  962.9 37.9 reduce-scatter.33
  1021.6 29.5 all-gather.33
  1078.6 37.9 reduce-scatter.35
  1147.5 20.7 reduce-scatter.39
  1173.5 19.7 reduce-scatter.41
  1197.3 63.1 reduce-scatter.37
  1269.1 175.4 all-reduce.13
  1448.1 111.5 reduce-scatter.45
  1563.3 245.4 reduce-scatter.43
where the time goes:
time: 1920 us; the launch traced here: 1910 us
  waiting for transfers between devices  983 us (51%)
  local copies, waits for them, and re-layouts  333 us (17%)
  blocking collectives  226 us (12%)
  matrix products  169 us (9%)
  other arithmetic  160 us (8%)
  between operations  24.6 us (1%)
    unnamed x29, waiting for transfers between devices  387 us
    unnamed x422, local copies, waits for them, and re-layouts  253 us
    reduce_scatter x4, waiting for transfers between devices, input_grads(): lax.psum_scatter(partial_sum.astype(jnp.bfloat16), 'col', scatter_dimensi...  118 us
    all_gather x4, waiting for transfers between devices, gather_grads(): return lax.all_gather(values, 'col', axis=1, tiled=True)  117 us
    all_gather x5, waiting for transfers between devices, gather_features(): return lax.all_gather(values, 'col', axis=1, tiled=True)  107 us
    all_gather x1, waiting for transfers between devices, on_device(): lax.all_gather(weights_in.astype(jnp.bfloat16), 'row', axis=1, tiled=True)  92.7 us
    reduce_scatter x4, waiting for transfers between devices, branch_sum(): lax.psum_scatter(partial_sum.astype(jnp.bfloat16), 'col', scatter_dimensi...  81.1 us
    psum x2, blocking collectives, on_device(): lax.psum((widen_cols(grad_bias_rows), widen_cols(grad_embed_cols), wide_f...  80.8 us
  transfers between devices with their start and end apart: 25, of which 24 were waited for; matrix products, arithmetic and copies ran while one was open for 18% of the time, Pallas kernels for 0%

commit v1 on v0

v1 whole, which is shorter than its diff:
```python
import functools
import math

import jax
import jax.numpy as jnp
import numpy as np
from jax import lax
from jax.experimental import pallas as pl
from jax.experimental.pallas import tpu as pltpu
from jax.sharding import PartitionSpec as P

HEAD_DIM = 64
CLASSES = 1000
FREQ = 256
PATCH = 16
LEN = 256
STEPS_T = 1000
STEP = 10

HIGHEST = lax.Precision.HIGHEST
EPS_NORM = 1e-06
CLIP_NORM = 1.0
RATE = 0.05
RATE_BIAS = 0.25
BETA_ONE = 0.9
BETA_TWO = 0.999
DECAY = 0.01
ADAM_EPS = 1e-08

F32 = jnp.float32
BF16 = jnp.bfloat16
MIB = 1024 * 1024
ANY = pl.BlockSpec(memory_space=pl.ANY)
SMEM = pl.BlockSpec(memory_space=pltpu.SMEM)
NT = (((1,), (1,)), ((), ()))
TN = (((0,), (0,)), ((), ()))


def dot_nt(a, b):
    return lax.dot_general(a, b, NT, preferred_element_type=F32)


def dot_tn(a, b):
    return lax.dot_general(a, b, TN, preferred_element_type=F32)


def dot_nn(a, b):
    return jnp.dot(a, b, preferred_element_type=F32)


class Place:
    def __init__(self, row_block):
        self.rows = lax.axis_size("row")
        self.cols = lax.axis_size("col")
        self.row = lax.axis_index("row")
        self.col = lax.axis_index("col")
        self.direct = self.rows == 8 and self.cols == 4 and row_block % 32 == 0
        self.z = self.row // 2
        self.y = self.row % 2
        self.x = self.col // 2
        self.core = self.col % 2
        if self.direct:
            self.col_order = [
                (self.x ^ kx) * 2 + (self.core ^ kc) for kx in (0, 1) for kc in (0, 1)
            ]
            self.row_offsets = jnp.stack(
                [
                    (((self.z + 4 - kz) % 4) * 2 + (self.y ^ ky)) * row_block
                    for ky in (0, 1)
                    for kz in range(4)
                ]
            ).astype(jnp.int32)
        else:
            self.col_order = [jnp.int32(c) for c in range(self.cols)]
            self.row_offsets = jnp.zeros((8,), jnp.int32)
        self.offsets = jnp.concatenate(
            [self.row_offsets, jnp.stack(self.col_order).astype(jnp.int32)]
        )

    def found_at(self):
        device = jnp.arange(self.rows * self.cols, dtype=jnp.int32)
        if not self.direct:
            return device
        row, col = device // 4, device % 4
        kz = (self.z + 4 - row // 2) % 4
        ky = (row % 2) ^ self.y
        kx = (col // 2) ^ self.x
        kc = (col % 2) ^ self.core
        return ((kc * 2 + kx) * 2 + ky) * 4 + kz


def swap_x(v):
    return lax.ppermute(v, "col", [(c, c ^ 2) for c in range(4)])


def swap_core(v):
    return lax.ppermute(v, "col", [(c, c ^ 1) for c in range(4)])


def swap_y(v):
    return lax.ppermute(v, "row", [(r, r ^ 1) for r in range(8)])


def turn_z(v, k):
    return lax.ppermute(v, "row", [(r, (r // 2 + k) % 4 * 2 + r % 2) for r in range(8)])


def pair(index, own, other):
    first = index == 0
    return jnp.stack([jnp.where(first, own, other), jnp.where(first, other, own)])


def gather_z(place, own):
    got = [own] + [turn_z(own, k) for k in (1, 2, 3)]
    ring = jnp.stack([got[3], got[2], got[1], got[0], got[3], got[2], got[1]])
    return lax.dynamic_slice_in_dim(ring, 3 - place.z, 4, 0)


def gather_cols(place, own):
    if not place.direct:
        return lax.all_gather(own, "col")
    both = pair(place.core, own, swap_core(own))
    return pair(place.x, both, swap_x(both)).reshape((4,) + own.shape)


def gather_all(place, own):
    if not place.direct:
        return lax.all_gather(lax.all_gather(own, "col"), "row")
    by_z = gather_z(place, own)
    by_x = pair(place.x, by_z, swap_x(by_z))
    by_y = pair(place.y, by_x, swap_y(by_x))
    every = pair(place.core, by_y, swap_core(by_y))
    rank = own.ndim
    every = jnp.transpose(every, (3, 1, 2, 0) + tuple(range(4, 4 + rank)))
    return every.reshape((8, 4) + own.shape)


def gather_near(place, own):
    if not place.direct:
        return lax.all_gather(own, ("row", "col"))
    every = jnp.stack([own] + [turn_z(own, k) for k in (1, 2, 3)])
    every = jnp.concatenate([every, swap_y(every)])
    every = jnp.concatenate([every, swap_x(every)])
    return jnp.concatenate([every, swap_core(every)])


def sum_all(place, own):
    if not place.direct:
        return lax.psum(own, ("row", "col"))
    parts = own.reshape((4, own.shape[0] // 4) + own.shape[1:])
    total = lax.dynamic_index_in_dim(parts, place.z, 0, False)
    for k in (1, 2, 3):
        total = total + turn_z(
            lax.dynamic_index_in_dim(parts, (place.z + k) % 4, 0, False), k
        )
    total = total + swap_core(total)
    total = total + swap_x(total)
    total = total + swap_y(total)
    return gather_z(place, total).reshape(own.shape)


def sum_scalar(place, value):
    if not place.direct:
        return lax.psum(value, ("row", "col"))
    total = jnp.broadcast_to(value, (8, 128))
    total = total + swap_core(total)
    total = total + swap_x(total)
    total = total + swap_y(total)
    total = total + lax.ppermute(total, "row", [(r, r ^ 2) for r in range(8)])
    total = total + lax.ppermute(total, "row", [(r, r ^ 4) for r in range(8)])
    return total[0, 0]


def scatter_modes(place, partial):
    rows, cols = place.rows, place.cols
    samples, count, width = partial.shape
    mine = samples // (rows * cols)
    if not place.direct:
        summed = lax.psum_scatter(partial, "row", scatter_dimension=0, tiled=True)
        spread = lax.all_gather(summed, "col")
        spread = lax.dynamic_slice_in_dim(spread, place.col * mine, mine, 1)
        return jnp.transpose(spread, (1, 2, 0, 3)).reshape(mine, count, cols * width)
    by_y = partial.reshape(4, 2, samples // 8, count, width)
    own = lax.dynamic_index_in_dim(by_y, place.y, 1, False)
    own = own + swap_y(lax.dynamic_index_in_dim(by_y, 1 - place.y, 1, False))
    total = lax.dynamic_index_in_dim(own, place.z, 0, False)
    for k in (1, 2, 3):
        total = total + turn_z(lax.dynamic_index_in_dim(own, (place.z + k) % 4, 0, False), k)
    by_x = total.reshape(2, 2, mine, count, width)
    own = lax.dynamic_index_in_dim(by_x, place.x, 0, False)
    got = swap_x(lax.dynamic_index_in_dim(by_x, 1 - place.x, 0, False))
    both = pair(place.x, own, got)
    own = lax.dynamic_index_in_dim(both, place.core, 1, False)
    got = swap_core(lax.dynamic_index_in_dim(both, 1 - place.core, 1, False))
    every = pair(place.core, own, got)
    return jnp.transpose(every, (2, 3, 1, 0, 4)).reshape(mine, count, cols * width)


def weight_tables(place, kind, block):
    cols = place.cols
    if not place.direct:
        return [
            [[(m * cols + c, 0, 0, 0, block * place.rows)] for c in range(cols)]
            for m in range(2 if kind == "mlp" else 1)
        ]
    part = block if kind == "mlp" else block // 2
    first, second = [], []
    for kx in (0, 1):
        for kc in (0, 1):
            one, two = [], []
            for ky in (0, 1):
                for kz in range(4):
                    one.append((kc * 4 + ky, kx * 4 + kz, ky * 4 + kz, 0, part))
                    two.append(
                        (
                            kc * 4 + 2 + kx,
                            ky * 4 + kz,
                            ky * 4 + kz,
                            0 if kind == "mlp" else part,
                            part,
                        )
                    )
            first.append(one)
            second.append(two)
    if kind == "mlp":
        return [first, second]
    return [[one + two for one, two in zip(first, second)]]


class Stages:
    def __init__(self):
        self.last = None

    def run(self, moves, works=()):
        operands = ([v for _, v in moves], [w[1:] for w in works])
        if self.last is not None:
            operands, _ = lax.optimization_barrier((operands, self.last))
        moved = [move(v) for (move, _), v in zip(moves, operands[0])]
        done = [w[0](*v) for w, v in zip(works, operands[1])]
        self.last = (moved, done)
        return moved, done


def turn(k):
    return lambda v: turn_z(v, k)


def add_low(a, b):
    return (a.astype(F32) + b.astype(F32)).astype(BF16)


class Spread:
    def __init__(self, own):
        self.own = own

    def turns(self, ks):
        return [(turn(k), self.own) for k in ks]

    def turned(self, one, two, three):
        got = [self.own, one, two, three]
        self.z_a = jnp.stack([t[0] for t in got])
        self.z_b = jnp.stack([t[1] for t in got])

    def first(self):
        return [(swap_x, self.z_a), (swap_y, self.z_b)]

    def second(self, x_a, y_b):
        self.p_a = jnp.concatenate([self.z_a, x_a])
        self.p_b = jnp.concatenate([self.z_b, y_b])
        return [(swap_y, self.p_a), (swap_x, self.p_b)]

    def cores(self):
        return [(swap_core, self.p_a), (swap_core, self.p_b)]

    def late_cores(self, q_a, q_b):
        self.q_a, self.q_b = q_a, q_b
        return [(swap_core, q_a), (swap_core, q_b)]

    def buffers(self, cores, late_cores):
        return [self.p_a, self.q_a, self.p_b, self.q_b] + [
            cores[0],
            late_cores[0],
            cores[1],
            late_cores[1],
        ]


class Gathered:
    def __init__(self, buffers):
        self.own, other = buffers[:4], buffers[4:]
        self.cores = [(swap_core, v) for v in other]

    def first(self, got):
        p_a, q_a, p_b, q_b = [add_low(a, b) for a, b in zip(self.own, got)]
        self.p_a, self.p_b = p_a, p_b
        return [(swap_y, q_a), (swap_x, q_b)]

    def second(self, got):
        self.p_a = add_low(self.p_a, got[0])
        self.p_b = add_low(self.p_b, got[1])
        return [(swap_x, self.p_a[4:]), (swap_y, self.p_b[4:])]

    def third(self, got):
        z_a = add_low(self.p_a[:4], got[0])
        z_b = add_low(self.p_b[:4], got[1])
        self.z = [jnp.stack([z_a[k], z_b[k]]) for k in range(4)]

    def turns(self, ks):
        return [(turn(4 - k), self.z[k]) for k in ks]

    def total(self, got):
        total = self.z[0].astype(F32)
        for v in got:
            total = total + v.astype(F32)
        return total


def plain_gather(place, kind, own):
    parts = own if kind == "mlp" else own.reshape(1, -1, own.shape[2])
    every = lax.all_gather(lax.all_gather(parts, "row", axis=1, tiled=True), "col")
    return [every[c, m][None] for m in range(parts.shape[0]) for c in range(place.cols)]


def plain_scatter(place, buffers):
    count = len(buffers) // place.cols
    stacked = jnp.stack(
        [
            jnp.stack([buffers[m * place.cols + c][0] for m in range(count)])
            for c in range(place.cols)
        ]
    )
    summed = lax.psum_scatter(stacked.astype(F32), "row", scatter_dimension=2, tiled=True)
    return lax.psum_scatter(summed, "col", scatter_dimension=0, tiled=False)


def normal(v):
    center = jnp.mean(v, axis=-1, keepdims=True)
    moved = v - center
    inverse = lax.rsqrt(jnp.mean(moved * moved, axis=-1, keepdims=True) + EPS_NORM)
    return moved * inverse, inverse


def start_loads(table, offsets, buffers, target, sems):
    for c, entries in enumerate(table):
        for buf, block, at, add, rows in entries:
            begin = pl.multiple_of(offsets[at] + add, 16) if rows < target.shape[1] else 0
            pltpu.make_async_copy(
                buffers[buf].at[block], target.at[c, pl.ds(begin, rows), :], sems.at[c]
            ).start()


def start_stores(entries, offsets, source, buffers, sem):
    for buf, block, at, add, rows in entries:
        begin = pl.multiple_of(offsets[at] + add, 16) if rows < source.shape[0] else 0
        pltpu.make_async_copy(
            source.at[pl.ds(begin, rows), :], buffers[buf].at[block], sem
        ).start()


def wait_all(ref, sem):
    pltpu.make_async_copy(ref, ref, sem).wait()


def row_of(shared_ref, at):
    return jnp.concatenate(
        [shared_ref[c, at : at + 1, :] for c in range(shared_ref.shape[0])], axis=1
    )


def attention_forward_body(table, n_buf, base, offsets, x_ref, mod_ref, shared_ref, *refs):
    buffers = refs[:n_buf]
    out_ref, h_ref, qkv_ref, p_ref, o_ref, a_ref, w_ref, sems = refs[n_buf:]
    c = pl.program_id(0)
    samples = mod_ref.shape[0]

    @pl.when(c == 0)
    def _():
        start_loads(table, offsets, buffers, w_ref, sems)
        for s in range(samples):
            rows = pl.ds(s * LEN, LEN)
            n, _ = normal(x_ref[rows, :])
            h_ref[rows, :] = (n * (1.0 + mod_ref[s, 1:2]) + mod_ref[s, 0:1]).astype(BF16)
        a_ref[...] = jnp.zeros_like(a_ref)

    wait_all(w_ref.at[c], sems.at[c])
    width = shared_ref.shape[-1]
    col = offsets[8 + c]
    query_bias = shared_ref[col, base + 6 : base + 7, :]
    value_bias = shared_ref[col, base + 7 : base + 8, :]
    bias = jnp.concatenate([query_bias, jnp.zeros_like(query_bias), value_bias], axis=1)
    triple = dot_nn(h_ref[...], w_ref[c, :, : 3 * width]) + bias
    qkv_ref[0] = triple.astype(BF16)
    for s in range(samples):
        rows = pl.ds(s * LEN, LEN)
        pieces = []
        for j in range(width // HEAD_DIM):
            q = qkv_ref[0, rows, j * HEAD_DIM : (j + 1) * HEAD_DIM]
            k = qkv_ref[0, rows, width + j * HEAD_DIM : width + (j + 1) * HEAD_DIM]
            v = qkv_ref[0, rows, 2 * width + j * HEAD_DIM : 2 * width + (j + 1) * HEAD_DIM]
            scores = dot_nt(q, k) * HEAD_DIM ** (-0.5)
            powers = jnp.exp(scores - jnp.max(scores, axis=-1, keepdims=True))
            probs = (powers / jnp.sum(powers, axis=-1, keepdims=True)).astype(BF16)
            p_ref[0, j, s] = probs
            pieces.append(dot_nn(probs, v).astype(BF16))
        o_ref[0, rows, :] = jnp.concatenate(pieces, axis=1)
    a_ref[...] += dot_nt(o_ref[0], w_ref[c, :, 3 * width :])

    @pl.when(c == pl.num_programs(0) - 1)
    def _():
        a_ref[...] += row_of(shared_ref, base + 12)
        for s in range(samples):
            rows = pl.ds(s * LEN, LEN)
            out_ref[rows, :] = x_ref[rows, :] + mod_ref[s, 2:3] * a_ref[rows, :]


def mlp_forward_body(tables, n_buf, base, offsets, x_ref, mod_ref, shared_ref, *refs):
    buffers = refs[:n_buf]
    out_ref, h_ref, u_ref, m_ref, wi_ref, wo_ref, sems_i, sems_o = refs[n_buf:]
    c = pl.program_id(0)
    samples = mod_ref.shape[0]

    @pl.when(c == 0)
    def _():
        start_loads(tables[0], offsets, buffers, wi_ref, sems_i)
        start_loads(tables[1], offsets, buffers, wo_ref, sems_o)
        for s in range(samples):
            rows = pl.ds(s * LEN, LEN)
            n, _ = normal(x_ref[rows, :])
            h_ref[rows, :] = (n * (1.0 + mod_ref[s, 1:2]) + mod_ref[s, 0:1]).astype(BF16)
        m_ref[...] = jnp.zeros_like(m_ref)

    wait_all(wi_ref.at[c], sems_i.at[c])
    col = offsets[8 + c]
    blocks = wi_ref.shape[-1] // shared_ref.shape[-1]
    bias = jnp.concatenate(
        [shared_ref[col, base + 8 + k : base + 9 + k, :] for k in range(blocks)], axis=1
    )
    hidden = dot_nn(h_ref[...], wi_ref[c]) + bias
    u_ref[0] = hidden
    active = jax.nn.gelu(hidden, approximate=True).astype(BF16)
    wait_all(wo_ref.at[c], sems_o.at[c])
    m_ref[...] += dot_nt(active, wo_ref[c])

    @pl.when(c == pl.num_programs(0) - 1)
    def _():
        m_ref[...] += row_of(shared_ref, base + 13)
        for s in range(samples):
            rows = pl.ds(s * LEN, LEN)
            out_ref[rows, :] = x_ref[rows, :] + mod_ref[s, 2:3] * m_ref[rows, :]


def norm_backward(s, x_ref, mod_ref, dx_ref, dh_ref, out_ref, dmod_ref):
    rows = pl.ds(s * LEN, LEN)
    n, inverse = normal(x_ref[rows, :])
    dh = dh_ref[rows, :]
    dmod_ref[s, 0:1] = jnp.sum(dh, axis=0, keepdims=True)
    dmod_ref[s, 1:2] = jnp.sum(dh * n, axis=0, keepdims=True)
    dn = dh * (1.0 + mod_ref[s, 1:2])
    back = inverse * (
        dn
        - jnp.mean(dn, axis=-1, keepdims=True)
        - n * jnp.mean(dn * n, axis=-1, keepdims=True)
    )
    if dx_ref is None:
        out_ref[rows, :] = back
    else:
        out_ref[rows, :] = dx_ref[rows, :] + back


def branch_gradient(dx_ref, mod_ref, branch_ref, dmod_ref, sum_ref, low_ref):
    total = None
    for s in range(mod_ref.shape[0]):
        rows = pl.ds(s * LEN, LEN)
        dx = dx_ref[rows, :]
        dmod_ref[s, 2:3] = jnp.sum(dx * branch_ref[rows, :], axis=0, keepdims=True)
        db = mod_ref[s, 2:3] * dx
        low_ref[rows, :] = db.astype(BF16)
        part = jnp.sum(db, axis=0, keepdims=True)
        total = part if total is None else total + part
    sum_ref[...] = total


def gelu_slope(u):
    k = math.sqrt(2.0 / math.pi)
    square = u * u
    t = jnp.tanh(k * (u + 0.044715 * square * u))
    half = 0.5 * (1.0 + t)
    slope = half + 0.5 * u * (1.0 - t * t) * (k * (1.0 + 3 * 0.044715 * square))
    return u * half, slope


def mlp_backward_body(
    tables, n_buf, offsets, dx_ref, x_ref, mod_ref, m_ref, h_ref, u_ref, *refs
):
    buffers = refs[:n_buf]
    out_ref, dmod_ref, dbias_ref, dtail_ref = refs[n_buf : n_buf + 4]
    grads = refs[n_buf + 4 : 2 * n_buf + 4]
    wi_ref, wo_ref, low_ref, dh_ref, gi_ref, go_ref, sems_i, sems_o, sems_gi, sems_go = refs[
        2 * n_buf + 4 :
    ]
    c = pl.program_id(0)
    count = len(tables[0])
    samples = mod_ref.shape[0]

    @pl.when(c == 0)
    def _():
        start_loads(tables[1], offsets, buffers, wo_ref, sems_o)
        start_loads(tables[0], offsets, buffers, wi_ref, sems_i)
        branch_gradient(dx_ref, mod_ref, m_ref, dmod_ref, dtail_ref, low_ref)
        dh_ref[...] = jnp.zeros_like(dh_ref)

    slot = lax.rem(c, 2)

    @pl.when(c >= 2)
    def _():
        wait_all(gi_ref.at[slot], sems_gi.at[slot])
        wait_all(go_ref.at[slot], sems_go.at[slot])

    wait_all(wo_ref.at[c], sems_o.at[c])
    active, slope = gelu_slope(u_ref[0])
    low = low_ref[...]
    go_ref[slot] = dot_tn(low, active.astype(BF16)).astype(BF16)
    for cc in range(count):

        @pl.when(c == cc)
        def _(cc=cc):
            start_stores(tables[1][cc], offsets, go_ref.at[slot], grads, sems_go.at[slot])

    du = dot_nn(low, wo_ref[c]) * slope
    dbias_ref[offsets[8 + c]] = jnp.sum(du, axis=0, keepdims=True)
    du = du.astype(BF16)
    gi_ref[slot] = dot_tn(h_ref[...], du).astype(BF16)
    for cc in range(count):

        @pl.when(c == cc)
        def _(cc=cc):
            start_stores(tables[0][cc], offsets, gi_ref.at[slot], grads, sems_gi.at[slot])

    wait_all(wi_ref.at[c], sems_i.at[c])
    dh_ref[...] += dot_nt(du, wi_ref[c])

    @pl.when(c == count - 1)
    def _():
        for s in range(samples):
            norm_backward(s, x_ref, mod_ref, dx_ref, dh_ref, out_ref, dmod_ref)
        for k in range(2):
            wait_all(gi_ref.at[k], sems_gi.at[k])
            wait_all(go_ref.at[k], sems_go.at[k])


def attention_backward_body(
    table, n_buf, offsets, dx_ref, x_ref, mod_ref, a_ref, h_ref, qkv_ref, p_ref, o_ref, *refs
):
    buffers = refs[:n_buf]
    out_ref, dmod_ref, dbias_ref, dtail_ref = refs[n_buf : n_buf + 4]
    grads = refs[n_buf + 4 : 2 * n_buf + 4]
    w_ref, low_ref, dh_ref, d_ref, g_ref, sems, sems_g = refs[2 * n_buf + 4 :]
    c = pl.program_id(0)
    count = len(table)
    samples = mod_ref.shape[0]
    width = qkv_ref.shape[-1] // 3
    factor = HEAD_DIM ** (-0.5)

    @pl.when(c == 0)
    def _():
        start_loads(table, offsets, buffers, w_ref, sems)
        branch_gradient(dx_ref, mod_ref, a_ref, dmod_ref, dtail_ref, low_ref)
        dh_ref[...] = jnp.zeros_like(dh_ref)

    slot = lax.rem(c, 2)

    @pl.when(c >= 2)
    def _():
        wait_all(g_ref.at[slot], sems_g.at[slot])

    wait_all(w_ref.at[c], sems.at[c])
    do_all = dot_nn(low_ref[...], w_ref[c, :, 3 * width :]).astype(BF16)
    sums = [None] * (width // HEAD_DIM)
    for s in range(samples):
        rows = pl.ds(s * LEN, LEN)
        dqs, dks, dvs = [], [], []
        for j in range(width // HEAD_DIM):
            q = qkv_ref[0, rows, j * HEAD_DIM : (j + 1) * HEAD_DIM]
            k = qkv_ref[0, rows, width + j * HEAD_DIM : width + (j + 1) * HEAD_DIM]
            v = qkv_ref[0, rows, 2 * width + j * HEAD_DIM : 2 * width + (j + 1) * HEAD_DIM]
            o = o_ref[0, rows, j * HEAD_DIM : (j + 1) * HEAD_DIM]
            do = do_all[s * LEN : (s + 1) * LEN, j * HEAD_DIM : (j + 1) * HEAD_DIM]
            probs = p_ref[0, j, s]
            dp = dot_nt(do, v)
            delta = jnp.sum(do.astype(F32) * o.astype(F32), axis=-1, keepdims=True)
            ds = (probs.astype(F32) * (dp - delta)).astype(BF16)
            dqs.append(dot_nn(ds, k) * factor)
            dks.append(dot_tn(ds, q) * factor)
            dvs.append(dot_tn(probs, do))
        joined = jnp.concatenate(dqs + dks + dvs, axis=1)
        part = jnp.sum(joined, axis=0, keepdims=True)
        sums = part if s == 0 else sums + part
        d_ref[rows, :] = joined.astype(BF16)
    dbias_ref[offsets[8 + c]] = sums
    grad_in = dot_tn(h_ref[...], d_ref[...])
    grad_out = dot_tn(low_ref[...], o_ref[0])
    g_ref[slot] = jnp.concatenate([grad_in, grad_out], axis=1).astype(BF16)
    for cc in range(count):

        @pl.when(c == cc)
        def _(cc=cc):
            start_stores(table[cc], offsets, g_ref.at[slot], grads, sems_g.at[slot])

    dh_ref[...] += dot_nt(d_ref[...], w_ref[c, :, : 3 * width])

    @pl.when(c == count - 1)
    def _():
        for s in range(samples):
            norm_backward(s, x_ref, mod_ref, dx_ref, dh_ref, out_ref, dmod_ref)
        for k in range(2):
            wait_all(g_ref.at[k], sems_g.at[k])


def final_body(
    x_ref, mod_ref, head_ref, bias_ref, noise_ref, mask_ref,
    dx_ref, loss_ref, dhead_ref, dbias_ref, dmod_ref, h_ref, dh_ref,
):
    samples = mod_ref.shape[0]
    for s in range(samples):
        rows = pl.ds(s * LEN, LEN)
        n, _ = normal(x_ref[rows, :])
        h_ref[rows, :] = (n * (1.0 + mod_ref[s, 1:2]) + mod_ref[s, 0:1]).astype(BF16)
    predicted = dot_nt(h_ref[...], head_ref[...]) + bias_ref[...]
    error = predicted - noise_ref[...]
    masked = mask_ref[...] * error
    loss_ref[...] = jnp.sum(masked * error, axis=0, keepdims=True)
    dpred = 2.0 * masked
    dbias_ref[...] = jnp.sum(dpred, axis=0, keepdims=True)
    low = dpred.astype(BF16)
    dhead_ref[...] = dot_tn(low, h_ref[...])
    dh_ref[...] = dot_nn(low, head_ref[...])
    for s in range(samples):
        norm_backward(s, x_ref, mod_ref, None, dh_ref, dx_ref, dmod_ref)


def whole_block(shape):
    rank = len(shape)
    return pl.BlockSpec(shape, lambda c: (0,) * rank, pipeline_mode=pl.Buffered(1))


def whole_out(shape):
    rank = len(shape)
    return pl.BlockSpec(shape, lambda c: (0,) * rank)


def block_of(shape):
    rank = len(shape)
    return pl.BlockSpec((1,) + tuple(shape[1:]), lambda c: (c,) + (0,) * (rank - 1))


def params(mib):
    return pltpu.CompilerParams(
        dimension_semantics=("arbitrary",), vmem_limit_bytes=mib * MIB
    )


def cost(flops, nbytes, exps=0):
    return pl.CostEstimate(flops=int(flops), bytes_accessed=int(nbytes), transcendentals=int(exps))


def shaped(shape, dtype):
    return jax.ShapeDtypeStruct(tuple(shape), dtype)


def attention_forward(place, block, base, buffers, x, mods, shared):
    table = weight_tables(place, "attn", block)[0]
    count = len(table)
    tokens, width = x.shape
    samples = mods.shape[0]
    narrow = shared.shape[-1]
    heads = narrow // HEAD_DIM
    outs = [
        shaped((tokens, width), F32),
        shaped((tokens, width), BF16),
        shaped((count, tokens, 3 * narrow), BF16),
        shaped((count, heads, samples, LEN, LEN), BF16),
        shaped((count, tokens, narrow), BF16),
        shaped((tokens, width), F32),
    ]
    return pl.pallas_call(
        functools.partial(attention_forward_body, table, len(buffers), base),
        grid=(count,),
        in_specs=[SMEM, whole_block(x.shape), whole_block(mods.shape), whole_block(shared.shape)]
        + [ANY] * len(buffers),
        out_specs=[whole_out(outs[0].shape), whole_out(outs[1].shape)]
        + [block_of(o.shape) for o in outs[2:5]]
        + [whole_out(outs[5].shape)],
        out_shape=outs,
        scratch_shapes=[
            pltpu.VMEM((count, width, 4 * narrow), BF16),
            pltpu.SemaphoreType.DMA((count,)),
        ],
        compiler_params=params(58),
        cost_estimate=cost(
            2 * tokens * width * width * 4 + 4 * tokens * LEN * width,
            8 * width * width + 30 * tokens * width,
            tokens * LEN * width // HEAD_DIM,
        ),
        name="attention_forward",
    )(place.offsets, x, mods, shared, *buffers)


def mlp_forward(place, block, base, buffers, x, mods, shared):
    tables = weight_tables(place, "mlp", block)
    count = len(tables[0])
    tokens, width = x.shape
    wide = buffers[0].shape[-1]
    outs = [
        shaped((tokens, width), F32),
        shaped((tokens, width), BF16),
        shaped((count, tokens, wide), F32),
        shaped((tokens, width), F32),
    ]
    return pl.pallas_call(
        functools.partial(mlp_forward_body, tables, len(buffers), base),
        grid=(count,),
        in_specs=[SMEM, whole_block(x.shape), whole_block(mods.shape), whole_block(shared.shape)]
        + [ANY] * len(buffers),
        out_specs=[whole_out(outs[0].shape), whole_out(outs[1].shape), block_of(outs[2].shape)]
        + [whole_out(outs[3].shape)],
        out_shape=outs,
        scratch_shapes=[
            pltpu.VMEM((count, width, wide), BF16),
            pltpu.VMEM((count, width, wide), BF16),
            pltpu.SemaphoreType.DMA((count,)),
            pltpu.SemaphoreType.DMA((count,)),
        ],
        compiler_params=params(58),
        cost_estimate=cost(
            2 * tokens * width * wide * count * 2,
            4 * width * wide * count + 30 * tokens * width,
            tokens * wide * count,
        ),
        name="mlp_forward",
    )(place.offsets, x, mods, shared, *buffers)


def mlp_backward(place, block, buffers, dx, x, mods, m, h, u):
    tables = weight_tables(place, "mlp", block)
    count = len(tables[0])
    tokens, width = x.shape
    wide = u.shape[-1]
    outs = [
        shaped((tokens, width), F32),
        shaped(mods.shape, F32),
        shaped((count, 1, wide), F32),
        shaped((1, width), F32),
    ] + [shaped(b.shape, BF16) for b in buffers]
    out = pl.pallas_call(
        functools.partial(mlp_backward_body, tables, len(buffers)),
        grid=(count,),
        in_specs=[SMEM, whole_block(x.shape), whole_block(x.shape), whole_block(mods.shape)]
        + [whole_block(m.shape), whole_block(h.shape), block_of(u.shape)]
        + [ANY] * len(buffers),
        out_specs=[whole_out(x.shape), whole_out(mods.shape), whole_out(outs[2].shape)]
        + [whole_out((1, width))]
        + [ANY] * len(buffers),
        out_shape=outs,
        scratch_shapes=[
            pltpu.VMEM((count, width, wide), BF16),
            pltpu.VMEM((count, width, wide), BF16),
            pltpu.VMEM((tokens, width), BF16),
            pltpu.VMEM((tokens, width), F32),
            pltpu.VMEM((2, width, wide), BF16),
            pltpu.VMEM((2, width, wide), BF16),
            pltpu.SemaphoreType.DMA((count,)),
            pltpu.SemaphoreType.DMA((count,)),
            pltpu.SemaphoreType.DMA((2,)),
            pltpu.SemaphoreType.DMA((2,)),
        ],
        compiler_params=params(58),
        cost_estimate=cost(
            4 * 2 * tokens * width * wide * count,
            8 * width * wide * count + 40 * tokens * width,
            tokens * wide * count,
        ),
        name="mlp_backward",
    )(place.offsets, dx, x, mods, m, h, u, *buffers)
    return out[:4], out[4:]


def attention_backward(place, block, buffers, dx, x, mods, a, h, qkv, p, o):
    table = weight_tables(place, "attn", block)[0]
    count = len(table)
    tokens, width = x.shape
    narrow = o.shape[-1]
    outs = [
        shaped((tokens, width), F32),
        shaped(mods.shape, F32),
        shaped((count, 1, 3 * narrow), F32),
        shaped((1, width), F32),
    ] + [shaped(b.shape, BF16) for b in buffers]
    out = pl.pallas_call(
        functools.partial(attention_backward_body, table, len(buffers)),
        grid=(count,),
        in_specs=[SMEM, whole_block(x.shape), whole_block(x.shape), whole_block(mods.shape)]
        + [whole_block(a.shape), whole_block(h.shape)]
        + [block_of(qkv.shape), block_of(p.shape), block_of(o.shape)]
        + [ANY] * len(buffers),
        out_specs=[whole_out(x.shape), whole_out(mods.shape), whole_out(outs[2].shape)]
        + [whole_out((1, width))]
        + [ANY] * len(buffers),
        out_shape=outs,
        scratch_shapes=[
            pltpu.VMEM((count, width, 4 * narrow), BF16),
            pltpu.VMEM((tokens, width), BF16),
            pltpu.VMEM((tokens, width), F32),
            pltpu.VMEM((tokens, 3 * narrow), BF16),
            pltpu.VMEM((2, width, 4 * narrow), BF16),
            pltpu.SemaphoreType.DMA((count,)),
            pltpu.SemaphoreType.DMA((2,)),
        ],
        compiler_params=params(58),
        cost_estimate=cost(
            4 * tokens * width * width * 4 + 10 * tokens * LEN * width,
            16 * width * width + 40 * tokens * width,
        ),
        name="attention_backward",
    )(place.offsets, dx, x, mods, a, h, qkv, p, o, *buffers)
    return out[:4], out[4:]


def final_step(x, mods, head, bias, noise, mask):
    tokens, width = x.shape
    vmem = pl.BlockSpec(memory_space=pltpu.VMEM)
    return pl.pallas_call(
        final_body,
        in_specs=[vmem] * 6,
        out_specs=[vmem] * 5,
        out_shape=[
            shaped((tokens, width), F32),
            shaped((1, PATCH), F32),
            shaped((PATCH, width), F32),
            shaped((1, PATCH), F32),
            shaped(mods.shape, F32),
        ],
        scratch_shapes=[pltpu.VMEM((tokens, width), BF16), pltpu.VMEM((tokens, width), F32)],
        compiler_params=pltpu.CompilerParams(vmem_limit_bytes=32 * MIB),
        cost_estimate=cost(6 * tokens * width * PATCH, 12 * tokens * width),
        name="final_step",
    )(x, mods, head, bias, noise, mask)


def pack_body(in_ref, out_ref, attn_ref, mlp_ref, mode_ref):
    blocks = out_ref.shape[1] - 1
    for k in range(6):
        mode_ref[0, k] = in_ref[0, k].astype(BF16)
    attn = [in_ref[0, 6 + k] for k in range(3)] + [out_ref[0, 0].T]
    attn_ref[0] = jnp.concatenate(attn, axis=1).astype(BF16)
    first = [in_ref[0, 9 + k] for k in range(blocks)]
    mlp_ref[0, 0] = jnp.concatenate(first, axis=1).astype(BF16)
    second = [out_ref[0, 1 + k].T for k in range(blocks)]
    mlp_ref[0, 1] = jnp.concatenate(second, axis=1).astype(BF16)


def pack_weights(weights_in, weights_out):
    layers, kinds, block, narrow = weights_in.shape
    blocks = weights_out.shape[1] - 1
    outs = [
        shaped((layers, block, 4 * narrow), BF16),
        shaped((layers, 2, block, blocks * narrow), BF16),
        shaped((layers, 6, block, narrow), BF16),
    ]
    return pl.pallas_call(
        pack_body,
        grid=(layers,),
        in_specs=[block_of(weights_in.shape), block_of(weights_out.shape)],
        out_specs=[block_of(o.shape) for o in outs],
        out_shape=outs,
        compiler_params=params(32),
        name="pack_weights",
    )(weights_in, weights_out)


def embed_body(base, noisy_ref, shared_ref, table_ref, out_ref):
    patch = jnp.concatenate(
        [
            shared_ref[c, base + 3 : base + 3 + PATCH, :]
            for c in range(shared_ref.shape[0])
        ],
        axis=1,
    ).astype(BF16)
    constant = row_of(shared_ref, base + 2) + table_ref[...]
    for s in range(noisy_ref.shape[0] // LEN):
        rows = pl.ds(s * LEN, LEN)
        out_ref[rows, :] = dot_nn(noisy_ref[rows, :], patch) + constant


def embed_tokens(base, noisy, shared, table):
    vmem = pl.BlockSpec(memory_space=pltpu.VMEM)
    return pl.pallas_call(
        functools.partial(embed_body, base),
        in_specs=[vmem] * 3,
        out_specs=vmem,
        out_shape=shaped((noisy.shape[0], table.shape[1]), F32),
        compiler_params=pltpu.CompilerParams(vmem_limit_bytes=32 * MIB),
        name="embed_tokens",
    )(noisy, shared, table)


def modes_backward_body(with_final, *refs):
    if with_final:
        near_ref, at_ref, rows_ref, pick_ref, mode_ref, act_ref, final_ref = refs[:7]
        block_ref, partial_ref, square_ref, grad_ref, cond_ref, shared_ref = refs[7:]
    else:
        near_ref, at_ref, rows_ref, pick_ref, mode_ref = refs[:5]
        block_ref, partial_ref, square_ref = refs[5:]
    near = near_ref[...]
    at = at_ref[...]
    where = lax.broadcasted_iota(jnp.int32, (at.shape[0], near.shape[0]), 1)

    def rows_at(step, offset):
        spread = (where == at[:, 0:1] + at[:, 1:2] * step + offset).astype(BF16)
        return dot_nn(spread, near).astype(BF16)

    total = None
    squares = jnp.zeros((1, 1), F32)
    for k in range(6):
        low = rows_at(3, 6 * (k // 3) + k % 3)
        low = dot_nn(low, pick_ref[...]).astype(BF16)
        grad = dot_tn(rows_ref[...], low)
        block_ref[k] = grad
        squares = squares + jnp.sum(grad * grad, keepdims=True)
        part = dot_nt(low, mode_ref[k])
        total = part if total is None else total + part
    partial_ref[...] = total
    if with_final:
        width = act_ref.shape[1]
        shift, scale = rows_at(2, 12), rows_at(2, 13)
        shared_squares = jnp.zeros((1, 1), F32)
        for k, low in enumerate((shift, scale)):
            grad = dot_tn(low, act_ref[...])
            grad_ref[k * width : (k + 1) * width, :] = grad
            shared_squares = shared_squares + jnp.sum(grad * grad, keepdims=True)
        cond_ref[...] = dot_nn(shift, final_ref[:width, :]) + dot_nn(
            scale, final_ref[width : 2 * width, :]
        )
        shared_ref[...] = shared_squares
    square_ref[...] = squares


def modes_backward(near, at, cond_rows, pick, mode_low, act=None, final=None):
    vmem = pl.BlockSpec(memory_space=pltpu.VMEM)
    samples, block = cond_rows.shape
    width = near.shape[2]
    narrow = mode_low.shape[2]
    outs = [shaped((6, block, narrow), F32), shaped((samples, block), F32), shaped((1, 1), F32)]
    operands = [near.reshape(-1, width), at, cond_rows, pick, mode_low]
    if act is not None:
        outs += [shaped((2 * width, width), F32), shaped((samples, width), F32)]
        outs += [shaped((1, 1), F32)]
        operands += [act, final]
    return pl.pallas_call(
        functools.partial(modes_backward_body, act is not None),
        in_specs=[vmem] * len(operands),
        out_specs=[vmem] * len(outs),
        out_shape=outs,
        compiler_params=pltpu.CompilerParams(vmem_limit_bytes=48 * MIB),
        name="modes_backward",
    )(*operands)


def collect_body(layers, *refs):
    out_ref = refs[-1]
    at = 0
    out_ref[...] = jnp.zeros_like(out_ref)
    take = list(refs[:-1])
    for _ in range(layers):
        dmod_a, dmod_b, dbias_a, dbias_b, dtail_a, dtail_b = [take.pop(0) for _ in range(6)]
        for k, source in enumerate((dmod_a, dmod_b)):
            total = source[0]
            for s in range(1, source.shape[0]):
                total = total + source[s]
            out_ref[at + 3 * k : at + 3 * k + 3, :] = total
        for c in range(dbias_b.shape[0]):
            out_ref[at + 6 + c : at + 7 + c, : dbias_b.shape[2]] = dbias_b[c]
            out_ref[at + 10 + c : at + 11 + c, : dbias_a.shape[2]] = dbias_a[c]
        out_ref[at + 14 : at + 15, :] = dtail_a[...]
        out_ref[at + 15 : at + 16, :] = dtail_b[...]
        at += 16
    head, head_bias, loss, mask, dfinal, dx, noisy, first, second, row = take
    out_ref[at : at + PATCH, :] = head[...]
    out_ref[at + PATCH : at + 2 * PATCH, :] = dot_tn(noisy[...], dx[...].astype(BF16))
    at += 2 * PATCH
    out_ref[at : at + 1, :] = jnp.sum(dx[...], axis=0, keepdims=True)
    total = dfinal[0]
    for s in range(1, dfinal.shape[0]):
        total = total + dfinal[s]
    out_ref[at + 1 : at + 3, :] = total
    out_ref[at + 3 : at + 4, 0:PATCH] = head_bias[...]
    out_ref[at + 4 : at + 5, 0:PATCH] = loss[...]
    out_ref[at + 5 : at + 6, 0:1] = jnp.sum(mask[...], keepdims=True)
    at += 16
    cond = first[...] + second[...]
    block, width = cond.shape[1], out_ref.shape[1]
    lane = lax.broadcasted_iota(jnp.int32, (block, width), 1)
    sub = lax.broadcasted_iota(jnp.int32, (block, width), 0)
    spread = (lane == sub + row[0] * block).astype(F32)
    out_ref[at : at + cond.shape[0], :] = jnp.dot(
        cond, spread, precision=HIGHEST, preferred_element_type=F32
    )


def collect(layers, parts, row, height, width):
    vmem = pl.BlockSpec(memory_space=pltpu.VMEM)
    return pl.pallas_call(
        functools.partial(collect_body, layers),
        in_specs=[vmem] * len(parts) + [SMEM],
        out_specs=vmem,
        out_shape=shaped((height, width), F32),
        compiler_params=pltpu.CompilerParams(vmem_limit_bytes=48 * MIB),
        name="collect_small",
    )(*parts, row)


def adam(weight, gradient, moment, second, clip, rate):
    gradient = gradient * clip
    moment = BETA_ONE * moment + (1.0 - BETA_ONE) * gradient
    second = BETA_TWO * second + (1.0 - BETA_TWO) * gradient * gradient
    update = (
        moment / (1.0 - BETA_ONE**STEP) / (jnp.sqrt(second / (1.0 - BETA_TWO**STEP)) + ADAM_EPS)
    )
    return weight - rate * (update + DECAY * weight), moment, second


def adam_blocks_body(clip_ref, mode_ref, attn_ref, mlp_ref, *refs):
    wi, mi, vi, wo, mo, vo = refs[:6]
    out_i, out_o = refs[6:9], refs[9:12]
    clip = clip_ref[0]
    narrow = wi.shape[3]
    for k in range(wi.shape[1]):
        if k < 6:
            grad = mode_ref[0, k]
        elif k < 9:
            grad = attn_ref[0, :, (k - 6) * narrow : (k - 5) * narrow]
        else:
            grad = mlp_ref[0, 0, :, (k - 9) * narrow : (k - 8) * narrow]
        new = adam(wi[0, k], grad, mi[0, k], vi[0, k], clip, RATE)
        for ref, value in zip(out_i, new):
            ref[0, k] = value
    for k in range(wo.shape[1]):
        if k == 0:
            grad = attn_ref[0, :, 3 * narrow :]
        else:
            grad = mlp_ref[0, 1, :, (k - 1) * narrow : k * narrow]
        new = adam(wo[0, k], grad.T, mo[0, k], vo[0, k], clip, RATE)
        for ref, value in zip(out_o, new):
            ref[0, k] = value


def adam_blocks(clip, modes, attn, mlp, ins, outs):
    arrays = [modes, attn, mlp] + list(ins) + list(outs)
    results = [shaped(v.shape, F32) for v in list(ins) + list(outs)]
    return pl.pallas_call(
        adam_blocks_body,
        grid=(ins[0].shape[0],),
        in_specs=[SMEM] + [block_of(v.shape) for v in arrays],
        out_specs=[block_of(v.shape) for v in results],
        out_shape=results,
        compiler_params=params(58),
        name="adam_blocks",
    )(clip, *arrays)


def adam_final_body(clip_ref, grad_ref, head_ref, w, m, v, *outs):
    clip = clip_ref[0]
    step = pl.program_id(0)
    last = pl.num_programs(0) - 1

    def update(rows, gradient):
        new = adam(w[rows, :], gradient, m[rows, :], v[rows, :], clip, RATE)
        for ref, value in zip(outs, new):
            ref[rows, :] = value

    height = w.shape[0]
    update(slice(0, height - PATCH), grad_ref[0 : height - PATCH, :])
    tail = slice(height - PATCH, height)

    @pl.when(step < last)
    def _():
        update(tail, grad_ref[tail, :])

    @pl.when(step == last)
    def _():
        update(tail, head_ref[...])


def adam_final(clip, grad, head, w, m, v):
    height, width = w.shape
    steps = 2
    block = pl.BlockSpec((height // steps, width), lambda c: (c, 0))
    padded = jnp.concatenate([grad, head], axis=0)
    return pl.pallas_call(
        adam_final_body,
        grid=(steps,),
        in_specs=[SMEM, block, whole_block(head.shape), block, block, block],
        out_specs=[block] * 3,
        out_shape=[shaped(w.shape, F32)] * 3,
        compiler_params=params(58),
        name="adam_final",
    )(clip, padded, head, w, m, v)


def adam_rest_body(rates, clip_ref, *refs):
    clip = clip_ref[0]
    count = len(rates)
    ins, outs = refs[: 4 * count], refs[4 * count :]
    for k, rate in enumerate(rates):
        w, g, m, v = [r[...] for r in ins[4 * k : 4 * k + 4]]
        for ref, value in zip(outs[3 * k : 3 * k + 3], adam(w, g, m, v, clip, rate)):
            ref[...] = value


def adam_rest(clip, groups):
    vmem = pl.BlockSpec(memory_space=pltpu.VMEM)
    arrays, results, rates = [], [], []
    for w, g, m, v, rate in groups:
        arrays += [w, g, m, v]
        results += [shaped(w.shape, F32)] * 3
        rates.append(rate)
    return pl.pallas_call(
        functools.partial(adam_rest_body, tuple(rates)),
        in_specs=[SMEM] + [vmem] * len(arrays),
        out_specs=[vmem] * len(results),
        out_shape=results,
        compiler_params=pltpu.CompilerParams(vmem_limit_bytes=48 * MIB),
        name="adam_rest",
    )(clip, *arrays)


def silu_slope(values):
    sigmoid_part = jax.nn.sigmoid(values)
    return sigmoid_part * (1.0 + values * (1.0 - sigmoid_part))


def squared(values):
    return jnp.sum(values * values)


def position_table(width):
    half = width // 2
    rate = np.exp(-math.log(10000.0) * (np.arange(width) % half) / half)
    angle = np.arange(LEN)[:, None] * rate[None, :]
    table = np.where(np.arange(width)[None, :] < half, np.sin(angle), np.cos(angle))
    return table.astype(np.float32)


def on_device(
    latents,
    noise,
    timesteps,
    labels,
    loss_mask,
    weights_in,
    weights_out,
    time_mlp,
    embed_table,
    final_layer,
    bias_table,
    final_bias,
    momentum_in,
    momentum_out,
    momentum_time,
    momentum_embed,
    momentum_final,
    momentum_bias,
    momentum_final_bias,
    variance_in,
    variance_out,
    variance_time,
    variance_embed,
    variance_final,
    variance_bias,
    variance_final_bias,
):
    layers, block, _, narrow = weights_in.shape
    place = Place(block)
    rows, cols = place.rows, place.cols
    width = final_layer.shape[0]
    row_samples = timesteps.shape[0]
    samples = row_samples // cols
    every_sample = row_samples * rows
    tokens = samples * LEN
    base = layers * 14
    hidden_blocks = weights_out.shape[1] - 1

    def my_cols(v, axis):
        return lax.dynamic_slice_in_dim(v, place.col * narrow, narrow, axis)

    in_view = [jnp.transpose(v, (0, 2, 1, 3)) for v in (weights_in, momentum_in, variance_in)]
    attn_low, mlp_low, mode_low = pack_weights(in_view[0], weights_out)
    pieces = []
    for layer in range(layers):
        attn = attn_low[layer]
        if place.direct:
            attn = attn.reshape(2, block // 2, attn.shape[1])
        pieces.append(attn)
        pieces.append(mlp_low[layer])

    embed_low = embed_table.astype(BF16)
    one_hot_row = (labels[:, None] == jnp.arange(CLASSES, dtype=jnp.int32)[None, :]).astype(BF16)
    class_rows = jnp.dot(
        one_hot_row, embed_low[:CLASSES], preferred_element_type=F32
    ).astype(BF16)
    whole_numbers = jnp.concatenate(
        [timesteps // 32, timesteps % 32, labels // 32, labels % 32]
    ).astype(BF16)
    time_rows = time_mlp.shape[0]
    flat = jnp.concatenate(
        [
            time_mlp.astype(BF16).T.reshape(-1),
            class_rows.reshape(-1),
            whole_numbers,
        ]
    )
    size = -(-flat.shape[0] // 2048) * 2048
    flat = jnp.concatenate([flat, jnp.zeros((size - flat.shape[0],), BF16)])
    gathered = gather_all(place, flat.reshape(-1, 128)).reshape(rows, cols, size)
    time_size = narrow * time_rows
    time_blocks = gathered[:, :, :time_size].reshape(rows, cols, narrow, time_rows)
    class_size = row_samples * narrow
    class_part = gathered[:, :, time_size : time_size + class_size]
    class_part = class_part.reshape(rows, cols, row_samples, narrow)
    class_part = jnp.swapaxes(class_part, 1, 2).reshape(every_sample, width).astype(F32)
    numbers = gathered[:, 0, time_size + class_size : time_size + class_size + 4 * row_samples]
    numbers = numbers.astype(jnp.int32).reshape(rows, 4, row_samples)
    all_steps = (numbers[:, 0] * 32 + numbers[:, 1]).reshape(-1)
    all_labels = (numbers[:, 2] * 32 + numbers[:, 3]).reshape(-1)
    time_full = jnp.transpose(time_blocks, (0, 3, 1, 2)).reshape(rows * time_rows, width)

    shared = gather_cols(
        place, jnp.concatenate([bias_table, embed_low[CLASSES:].astype(F32)], axis=0)
    )
    bias_full = jnp.swapaxes(shared, 0, 1).reshape(-1, width)

    half_freq = FREQ // 2
    freq_rate = jnp.asarray(
        np.exp(-math.log(10000.0) * np.arange(half_freq) / half_freq).astype(np.float32)
    )
    angle_grid = all_steps.astype(F32)[:, None] * freq_rate[None, :]
    freq_low = jnp.concatenate([jnp.cos(angle_grid), jnp.sin(angle_grid)], axis=1).astype(BF16)
    first_time = (
        jnp.dot(freq_low, time_full[:FREQ], preferred_element_type=F32) + bias_full[base]
    )
    first_act = jax.nn.silu(first_time).astype(BF16)
    condition = (
        jnp.dot(first_act, time_full[FREQ:], preferred_element_type=F32)
        + bias_full[base + 1]
        + class_part
    )
    cond_act = jax.nn.silu(condition).astype(BF16)

    cond_rows = lax.dynamic_slice_in_dim(cond_act, place.row * block, block, 1)
    partial = jnp.einsum("sd,lkde->slke", cond_rows, mode_low, preferred_element_type=F32)
    modes = scatter_modes(place, partial.reshape(every_sample, layers * 6, narrow))
    modes = modes.reshape(samples, layers, 6, width) + jnp.stack(
        [bias_full[14 * layer : 14 * layer + 6] for layer in range(layers)]
    )
    final_view = [v.T for v in (final_layer, momentum_final, variance_final)]
    final_low = final_view[0].astype(BF16)
    own_start = place.row * row_samples + place.col * samples
    cond_own = lax.dynamic_slice_in_dim(cond_act, own_start, samples, 0)
    final_mod = (
        jnp.einsum("sd,ed->se", cond_own, final_low[: 2 * width], preferred_element_type=F32)
        + final_bias[: 2 * width]
    ).reshape(samples, 2, width)

    own_tokens = place.col * tokens
    latents = lax.dynamic_slice_in_dim(latents, own_tokens, tokens, 0)
    noise = lax.dynamic_slice_in_dim(noise, own_tokens, tokens, 0)
    mask = lax.dynamic_slice_in_dim(loss_mask, own_tokens, tokens, 0).astype(F32)
    steps_own = lax.dynamic_slice_in_dim(timesteps, place.col * samples, samples, 0).astype(F32)
    alpha_bar = jnp.cos((steps_own / STEPS_T + 0.008) / 1.008 * (math.pi / 2)) ** 2
    keep_part = jnp.repeat(jnp.sqrt(alpha_bar), LEN)[:, None]
    noise_part = jnp.repeat(jnp.sqrt(1.0 - alpha_bar), LEN)[:, None]
    noisy = (keep_part * latents + noise_part * noise).astype(BF16)
    residual = embed_tokens(base, noisy, shared, jnp.asarray(position_table(width)))

    def attn_step(layer):
        def work(buffers, x, mods):
            return attention_forward(place, block, 14 * layer, buffers, x, mods, shared)

        return work

    def mlp_step(layer):
        def work(buffers, x, mods):
            return mlp_forward(place, block, 14 * layer, buffers, x, mods, shared)

        return work

    def attn_back(buffers, *operands):
        return attention_backward(place, block, buffers, *operands)

    def mlp_back(buffers, *operands):
        return mlp_backward(place, block, buffers, *operands)

    head_low = final_low[2 * width :]

    def last_step(x):
        return final_step(
            x, final_mod, head_low, final_bias[2 * width :][None], noise, mask[:, None]
        )

    mods_a = [modes[:, layer, 0:3] for layer in range(layers)]
    mods_b = [modes[:, layer, 3:6] for layer in range(layers)]
    buffers = [None] * (2 * layers)
    fore_a, fore_b = [None] * layers, [None] * layers
    entry = [None] * layers
    back_a, back_b = [None] * layers, [None] * layers
    summed = [None] * (2 * layers)
    if place.direct and layers == 2:
        stages = Stages()
        spread = [Spread(v) for v in pieces]
        a0, b0, a1, b1 = spread
        (t1, t3, t2), _ = stages.run(a0.turns((1, 3, 2)))
        a0.turned(t1, t2, t3)
        got, _ = stages.run(a0.first() + b0.turns((1, 3)))
        t1, t3 = got[2:]
        got, _ = stages.run(a0.second(*got[:2]) + b0.turns((2,)) + a0.cores())
        b0.turned(t1, got[2], t3)
        cores = got[3:]
        got, _ = stages.run(b0.first() + a1.turns((1, 3)) + a0.late_cores(*got[:2]))
        buffers[0] = a0.buffers(cores, got[4:])
        t1, t3 = got[2:4]
        got, _ = stages.run(b0.second(*got[:2]) + a1.turns((2,)) + b0.cores())
        a1.turned(t1, got[2], t3)
        cores = got[3:]
        got, (fore_a[0],) = stages.run(
            a1.first() + b1.turns((1, 3)) + b0.late_cores(*got[:2]),
            [(attn_step(0), buffers[0], residual, mods_a[0])],
        )
        buffers[1] = b0.buffers(cores, got[4:])
        t1, t3 = got[2:4]
        got, (fore_b[0],) = stages.run(
            a1.second(*got[:2]) + b1.turns((2,)) + a1.cores(),
            [(mlp_step(0), buffers[1], fore_a[0][0], mods_b[0])],
        )
        b1.turned(t1, got[2], t3)
        cores = got[3:]
        got, _ = stages.run(b1.first() + a1.late_cores(*got[:2]))
        buffers[2] = a1.buffers(cores, got[2:])
        got, (fore_a[1],) = stages.run(
            b1.second(*got[:2]) + b1.cores(),
            [(attn_step(1), buffers[2], fore_b[0][0], mods_a[1])],
        )
        cores = got[2:]
        got, _ = stages.run(b1.late_cores(*got[:2]))
        buffers[3] = b1.buffers(cores, got)
        _, (fore_b[1],) = stages.run([], [(mlp_step(1), buffers[3], fore_a[1][0], mods_b[1])])
        entry = [residual, fore_b[0][0]]
        last = last_step(fore_b[1][0])

        def back_b_work(layer, grad):
            out, h, u, m = fore_b[layer]
            return (mlp_back, buffers[2 * layer + 1], grad, fore_a[layer][0], mods_b[layer], m, h, u)

        def back_a_work(layer, grad):
            out, h, qkv, p, o, a = fore_a[layer]
            return (
                attn_back, buffers[2 * layer], grad, entry[layer], mods_a[layer], a, h, qkv, p, o,
            )

        _, ((back_b[1], grads),) = stages.run([], [back_b_work(1, last[0])])
        gb1 = Gathered(grads)
        core_b1, ((back_a[1], grads),) = stages.run(gb1.cores, [back_a_work(1, back_b[1][0])])
        ga1 = Gathered(grads)
        got, ((back_b[0], grads),) = stages.run(
            gb1.first(core_b1) + ga1.cores, [back_b_work(0, back_a[1][0])]
        )
        core_a1 = got[2:]
        gb0 = Gathered(grads)
        got, _ = stages.run(gb1.second(got[:2]) + gb0.cores)
        gb1.third(got[:2])
        core_b0 = got[2:]
        got, ((back_a[0], grads),) = stages.run(
            gb0.first(core_b0) + gb1.turns((1, 3)), [back_a_work(0, back_b[0][0])]
        )
        turned_b1 = got[2:]
        ga0 = Gathered(grads)
        got, _ = stages.run(gb0.second(got[:2]) + gb1.turns((2,)) + ga0.cores)
        summed[3] = gb1.total(turned_b1 + got[2:3])
        core_a0 = got[3:]
        gb0.third(got[:2])
        got, _ = stages.run(ga1.first(core_a1) + gb0.turns((1, 3)))
        turned_b0 = got[2:]
        got, _ = stages.run(ga1.second(got[:2]) + ga0.first(core_a0) + gb0.turns((2,)))
        summed[1] = gb0.total(turned_b0 + got[4:])
        ga1.third(got[:2])
        got, _ = stages.run(ga0.second(got[2:4]) + ga1.turns((1, 3, 2)))
        summed[2] = ga1.total(got[2:])
        ga0.third(got[:2])
        got, _ = stages.run(ga0.turns((1, 3, 2)))
        summed[0] = ga0.total(got)
    else:
        grad = residual
        for layer in range(layers):
            buffers[2 * layer] = plain_gather(place, "attn", pieces[2 * layer][None])
            buffers[2 * layer + 1] = plain_gather(place, "mlp", pieces[2 * layer + 1])
            entry[layer] = grad
            fore_a[layer] = attn_step(layer)(buffers[2 * layer], grad, mods_a[layer])
            grad = fore_a[layer][0]
            fore_b[layer] = mlp_step(layer)(buffers[2 * layer + 1], grad, mods_b[layer])
            grad = fore_b[layer][0]
        last = last_step(grad)
        grad = last[0]
        for layer in reversed(range(layers)):
            out, h, u, m = fore_b[layer]
            back_b[layer], grads = mlp_back(
                buffers[2 * layer + 1], grad, fore_a[layer][0], mods_b[layer], m, h, u
            )
            summed[2 * layer + 1] = plain_scatter(place, grads)
            grad = back_b[layer][0]
            out, h, qkv, p, o, a = fore_a[layer]
            back_a[layer], grads = attn_back(
                buffers[2 * layer], grad, entry[layer], mods_a[layer], a, h, qkv, p, o
            )
            summed[2 * layer] = plain_scatter(place, grads)
            grad = back_a[layer][0]

    _, loss_parts, grad_head, grad_head_bias, grad_final_mod = last
    found = place.found_at()
    sample = jnp.arange(every_sample, dtype=jnp.int32)
    at = jnp.stack([found[sample // samples] * 16, sample % samples], axis=1)
    feature = jnp.arange(width, dtype=jnp.int32)[:, None]
    picked = jnp.arange(narrow, dtype=jnp.int32)[None, :] + place.col * narrow
    pick = (feature == picked).astype(BF16)
    mode_blocks, partials = [None] * layers, []
    own_squares = jnp.zeros((), F32)
    for layer in reversed(range(layers)):
        parts = [back_a[layer][1].reshape(-1, width), back_b[layer][1].reshape(-1, width)]
        top = layer == layers - 1
        if top:
            parts.append(grad_final_mod.reshape(-1, width))
        parts = jnp.concatenate(parts, axis=0).astype(BF16)
        parts = jnp.concatenate([parts, jnp.zeros((16 - parts.shape[0], width), BF16)], axis=0)
        near = gather_near(place, parts)
        got = modes_backward(
            near, at, cond_rows, pick, mode_low[layer], *((cond_act, final_low) if top else ())
        )
        mode_blocks[layer] = got[0]
        partials.append(got[1])
        own_squares = own_squares + got[2][0, 0]
        if top:
            final_grad, cond_final, final_squares = got[3:]
    while len(partials) > 2:
        partials[-2:] = [partials[-2] + partials[-1]]
    small = []
    for layer in range(layers):
        _, dmod_a, dbias_a, dtail_a = back_a[layer]
        _, dmod_b, dbias_b, dtail_b = back_b[layer]
        small += [dmod_a, dmod_b, dbias_a, dbias_b, dtail_a, dtail_b]
    start = 16 * layers + 2 * PATCH
    height = -(-(start + 16 + every_sample) // 32) * 32
    small += [
        grad_head,
        grad_head_bias,
        loss_parts,
        mask[:, None],
        grad_final_mod,
        back_a[0][0],
        noisy,
    ] + partials
    small = collect(layers, small, place.row[None].astype(jnp.int32), height, width)
    small = sum_all(place, small)
    head_grad = small[start - 2 * PATCH : start - PATCH]
    patch_grad = small[start - PATCH : start]
    final_bias_grad = jnp.concatenate(
        [small[start + 1], small[start + 2], small[start + 3, :PATCH]]
    )
    loss_total = jnp.sum(small[start + 4, :PATCH])
    count_total = small[start + 5, 0]
    grad_cond = small[start + 16 : start + 16 + every_sample] + cond_final

    grad_condition = grad_cond * silu_slope(condition)
    one_hot = (all_labels[:, None] == jnp.arange(CLASSES, dtype=jnp.int32)[None, :]).astype(F32)
    grad_classes = jnp.einsum(
        "sd,sc->dc", my_cols(grad_condition, 1), one_hot, precision=HIGHEST
    )
    condition_low = grad_condition.astype(BF16)
    grad_first = jnp.einsum(
        "se,de->sd", condition_low, time_full[FREQ:], preferred_element_type=F32
    ) * silu_slope(first_time)
    first_low = grad_first.astype(BF16)
    time_inputs = lax.dynamic_slice_in_dim(
        jnp.concatenate([freq_low, first_act], axis=1), place.row * time_rows, time_rows, 1
    )
    time_outputs = my_cols(
        jnp.where((place.row + 1) * time_rows <= FREQ, first_low, condition_low), 1
    )
    time_grad = jnp.einsum("sd,se->ed", time_inputs, time_outputs, preferred_element_type=F32)

    own_rows, shared_squares = [], jnp.zeros((), F32)
    for layer in range(layers):
        rows_at = small[16 * layer : 16 * layer + 16]
        own = my_cols(rows_at, 1)
        mlp_rows = lax.dynamic_index_in_dim(rows_at[6:10], place.col, 0, False)
        attn_rows = lax.dynamic_index_in_dim(rows_at[10:14], place.col, 0, False)
        attn_rows = attn_rows[: 3 * narrow].reshape(3, narrow)
        own_rows += [own[:6], attn_rows[0:1], attn_rows[2:3]]
        own_rows += [mlp_rows[: hidden_blocks * narrow].reshape(hidden_blocks, narrow), own[14:16]]
        counted = rows_at[10:14, : 3 * narrow].reshape(4, 3, narrow)[:, 0::2]
        shared_squares = (
            shared_squares + squared(rows_at[:10]) + squared(counted) + squared(rows_at[14:])
        )
    time_bias = jnp.stack([jnp.sum(grad_first, axis=0), jnp.sum(grad_condition, axis=0)])
    patch_bias = small[start : start + 1]
    own_rows += [my_cols(time_bias, 1), my_cols(patch_bias, 1)]
    bias_grad = jnp.concatenate(own_rows, axis=0)
    shared_squares = (
        shared_squares
        + squared(time_bias)
        + squared(small[start - 2 * PATCH : start + 3])
        + squared(small[start + 3, :PATCH])
        + final_squares[0, 0]
    )
    own_squares = own_squares + squared(time_grad) + squared(grad_classes) / rows
    for value in summed:
        own_squares = own_squares + squared(value)
    grad_norm = jnp.sqrt(sum_scalar(place, own_squares) + shared_squares)
    clip_factor = jnp.minimum(1.0, CLIP_NORM / (grad_norm + 1e-06))
    clip = clip_factor[None]

    results = [loss_total, count_total, grad_norm]
    attn_sums = jnp.stack([summed[2 * k].reshape(block, 4 * narrow) for k in range(layers)])
    mlp_sums = jnp.stack([summed[2 * k + 1] for k in range(layers)])
    new_blocks = adam_blocks(
        clip,
        jnp.stack(mode_blocks),
        attn_sums,
        mlp_sums,
        in_view,
        [weights_out, momentum_out, variance_out],
    )
    results += [jnp.transpose(v, (0, 2, 1, 3)) for v in new_blocks[:3]] + list(new_blocks[3:])
    embed_grad = jnp.concatenate([grad_classes, my_cols(patch_grad, 1).T], axis=1)
    rest = adam_rest(
        clip,
        [
            (time_mlp.T, time_grad, momentum_time.T, variance_time.T, RATE),
            (embed_table.T, embed_grad, momentum_embed.T, variance_embed.T, RATE),
            (bias_table, bias_grad, momentum_bias, variance_bias, RATE_BIAS),
            (
                final_bias[None],
                final_bias_grad[None],
                momentum_final_bias[None],
                variance_final_bias[None],
                RATE_BIAS,
            ),
        ],
    )
    results += [v.T for v in rest[:6]]
    results += [v.T for v in adam_final(clip, final_grad, head_grad, *final_view)]
    results += list(rest[6:9]) + [v[0] for v in rest[9:]]
    return tuple(results)


def solution(mesh):
    tokens, latents = P("row", None), P("row")
    weights = (
        P(None, "row", None, "col"),
        P(None, None, "col", "row"),
        P("row", "col"),
        P(None, "col"),
        P(),
        P(None, "col"),
        P(),
    )
    updated = []
    for spec in weights:
        updated += [spec] * 3
    return jax.shard_map(
        on_device,
        mesh=mesh,
        in_specs=(tokens, tokens, latents, latents, latents) + weights * 3,
        out_specs=(P(), P(), P()) + tuple(updated),
        check_vma=False,
    )
```

time: 1920 us -> 686 us (0.36)
  waiting for transfers between devices: 983 us -> 180 us
  local copies, waits for them, and re-layouts: 333 us -> 77.9 us
  blocking collectives: 226 us -> 0 us
  Pallas kernels: 0 us -> 196 us
  matrix products: 169 us -> 9.29 us
  starting transfers between devices: 13 us -> 120 us
  other arithmetic: 160 us -> 76.5 us
    unnamed x29 -> x0, waiting for transfers between devices: 387 us -> none
    all_gather x11 -> x0, waiting for transfers between devices: 338 us -> none  [the longest x4 117 us: gather_grads(): return lax.all_gather(values, 'col', axis=1, tiled=True)]
    unnamed x422 -> x342, local copies, waits for them, and re-layouts: 253 us -> 35.9 us
    reduce_scatter x9 -> x0, waiting for transfers between devices: 199 us -> none  [the longest x4 118 us: input_grads(): lax.psum_scatter(partial_sum.astype(jnp.bfloat16), 'col', scatter_dimensi...]
    pallas_call x0 -> x17, Pallas kernels: none -> 196 us  [the longest x2 52.5 us: attention_backward(): pl.pallas_call(functools.partial(attention_backward_body, table, len(buff...]
    psum x12 -> x0, blocking collectives: 185 us -> none  [the longest x2 80.8 us: on_device(): lax.psum((widen_cols(grad_bias_rows), widen_cols(grad_embed_cols), wide_f...]
    ppermute x0 -> x128, waiting for transfers between devices: none -> 180 us  [the longest x42 80.4 us: turn_z(): lax.ppermute(v, 'row', [(r, (r // 2 + k) % 4 * 2 + r % 2) for r in range(...]
    dot_general x49 -> x8, matrix products: 141 us -> 9.29 us  [the longest x1 2.62 us: on_device(): jnp.dot(first_act, time_full[FREQ:], preferred_element_type=F32)]
  transfers between devices with their start and end apart: 25 -> 128, of which waited for: 24 -> 46; matrix products, arithmetic and copies ran while one was open for 18% -> 20% of each run, Pallas kernels for 0% -> 20%
where the time goes in v1:
time: 686 us; the launch traced here: 676 us
  Pallas kernels  196 us (29%)
  waiting for transfers between devices  180 us (26%)
  starting transfers between devices  120 us (17%)
  local copies, waits for them, and re-layouts  77.9 us (11%)
  other arithmetic  76.5 us (11%)
  between operations  17 us (2%)
  matrix products  9.29 us (1%)
    ppermute x42, waiting for transfers between devices, turn_z(): lax.ppermute(v, 'row', [(r, (r // 2 + k) % 4 * 2 + r % 2) for r in range(...  80.4 us
    ppermute x42, starting transfers between devices, turn_z(): lax.ppermute(v, 'row', [(r, (r // 2 + k) % 4 * 2 + r % 2) for r in range(...  61.2 us
    ppermute x23, waiting for transfers between devices, swap_x(): return lax.ppermute(v, 'col', [(c, c ^ 2) for c in range(4)])  60.2 us
    pallas_call x2, Pallas kernels, attention_backward(): pl.pallas_call(functools.partial(attention_backward_body, table, len(buff...  52.5 us
    pallas_call x2, Pallas kernels, mlp_backward(): pl.pallas_call(functools.partial(mlp_backward_body, tables, len(buffers))...  45 us
    unnamed x342, local copies, waits for them, and re-layouts  35.9 us
    ppermute x22, waiting for transfers between devices, swap_y(): return lax.ppermute(v, 'row', [(r, r ^ 1) for r in range(8)])  33.6 us
    convert_element_type x24, other arithmetic, add_low(): return (a.astype(F32) + b.astype(F32)).astype(BF16)  33 us
  transfers between devices with their start and end apart: 128, of which 46 were waited for; matrix products, arithmetic and copies ran while one was open for 20% of the time, Pallas kernels for 20%

profile of v1, /device:TPU:0, one launch (start us, length us, event | category | flops | bytes accessed | tf_op | source)
XLA Modules:
  0.0 676.3 jit_solution(5478557127736722612)
XLA Ops:
  2.6 5.1 collective-permute-start.23
  48.8 4.3 collective-permute-done.6
  58.8 10.6 %collective-permute-done.7 = bf16[2,96,768]{2,1,0:T(8,128)(2,1)S(1)} collective-permute-done((bf16[2,96,768]{2,1,0:T(8,128)(2,1)}, bf16[2,96,768]{2,1,0:T(8,128)(2,1)S(1)}, u32[]{:S(2)}, u32[]{:S(2)}) %collective-permute-start.7) | collective-permute-done | bytes 294944 | tf_op jit(solution)/shard_map/ppermute | solution.py:105
  74.3 10.4 %collective-permute-done.9.refs_3_ = bf16[8,48,768]{2,1,0:T(8,128)(2,1)} collective-permute-done((bf16[8,48,768]{2,1,0:T(8,128)(2,1)S(1)}, bf16[8,48,768]{2,1,0:T(8,128)(2,1)}, u32[]{:S(2)}, u32[]{:S(2)}) %collective-permute-start.9) | collective-permute-done | bytes 589856 | tf_op jit(solution)/shard_map/ppermute | solution.py:93
  111.2 5.5 collective-permute-done.18
  129.9 7.8 %collective-permute-done.33 = f32[2,2,12,192]{3,1,0,2:T(2,128)S(1)} collective-permute-done((f32[2,2,12,192]{3,1,0,2:T(2,128)S(1)}, f32[2,2,12,192]{3,1,0,2:T(2,128)S(1)}, u32[]{:S(2)}, u32[]{:S(2)}) %collective-permute-start.33) | collective-permute-done | bytes 36896 | tf_op jit(solution)/shard_map/ppermute | solution.py:93
  146.9 15.7 %attention_forward.2 = (f32[512,768]{1,0:T(8,128)}, bf16[512,768]{1,0:T(8,128)(2,1)}, bf16[4,512,576]{2,1,0:T(8,128)(2,1)}, bf16[4,3,2,256,256]{4,3,2,1,0:T(8,12...) custom-call(s32[12]{0:T(128)} %concatenate.115.offsets, f32[512,768]{1,0:T(8,128)} %copy-done.6, ...), custom_call_target="tpu_custom_call" | custom-call | flops 2818572288 | bytes 16515072 | tf_op jit(solution)/shard_map/attention_forward/pallas_call | solution.py:685
  165.0 5.9 collective-permute-done.42
  173.7 14.4 %mlp_forward.2 = (f32[512,768]{1,0:T(8,128)}, bf16[512,768]{1,0:T(8,128)(2,1)}, f32[4,512,768]{2,1,0:T(8,128)}, f32[512,768]{1,0:T(8,128)}) custom-call(s32[12]{0:T(128)} %concatenate.115.offsets, f32[512,768]{1,0:T(8,128)} %get-tuple-element.479.x_ref, f32[2,3,768]{2,1,0:T(4,128)} %get-tuple-element.480.mod_ref, f32[4,47,192]{2,1,0:T(8,128)} %bitcast.315, ...), custom_call_target="tpu_custom_call" | custom-call | flops 4831838208 | bytes 21233664 | tf_op jit(solution)/shard_map/mlp_forward/pallas_call | solution.py:719
  192.0 12.6 %collective-permute-done.49 = bf16[4,96,768]{2,1,0:T(8,128)(2,1)S(1)} collective-permute-done((bf16[4,96,768]{2,1,0:T(8,128)(2,1)S(1)}, bf16[4,96,768]{2,1,0:T(8,128)(2,1)S(1)}, u32[]{:S(2)}, u32[]{:S(2)}) %collective-permute-start.49) | collective-permute-done | bytes 589856 | tf_op jit(solution)/shard_map/ppermute | solution.py:101
  208.5 15.8 %attention_forward.3 = (f32[512,768]{1,0:T(8,128)}, bf16[512,768]{1,0:T(8,128)(2,1)}, bf16[4,512,576]{2,1,0:T(8,128)(2,1)}, bf16[4,3,2,256,256]{4,3,2,1,0:T(8,12...) custom-call(s32[12]{0:T(128)} %concatenate.115.offsets, f32[512,768]{1,0:T(8,128)} %get-tuple-element.449.x_ref, ...), custom_call_target="tpu_custom_call" | custom-call | flops 2818572288 | bytes 16515072 | tf_op jit(solution)/shard_map/attention_forward/pallas_call | solution.py:685
  224.3 7.6 %collective-permute-done.52.refs_1_ = bf16[8,96,768]{2,1,0:T(8,128)(2,1)} collective-permute-done((bf16[8,96,768]{2,1,0:T(8,128)(2,1)S(1)}, bf16[8,96,768]{2,1,0:T(8,128)(2,1)}, u32[]{:S(2)}, u32[]{:S(2)}) %collective-permute-start.52) | collective-permute-done | bytes 1179680 | tf_op jit(solution)/shard_map/ppermute | solution.py:101
  238.4 14.6 %mlp_forward.3 = (f32[512,768]{1,0:T(8,128)}, bf16[512,768]{1,0:T(8,128)(2,1)}, f32[4,512,768]{2,1,0:T(8,128)}, f32[512,768]{1,0:T(8,128)}) custom-call(s32[12]{0:T(128)} %concatenate.115.offsets, f32[512,768]{1,0:T(8,128)} %get-tuple-element.421.x_ref, f32[2,3,768]{2,1,0:T(4,128)} %get-tuple-element.422.mod_ref, f32[4,47,192]{2,1,0:T(8,128)} %bitcast.317, ...), custom_call_target="tpu_custom_call" | custom-call | flops 4831838208 | bytes 21233664 | tf_op jit(solution)/shard_map/mlp_forward/pallas_call | solution.py:719
  259.1 22.4 %mlp_backward.2 = (f32[512,768]{1,0:T(8,128)}, f32[2,3,768]{2,1,0:T(4,128)}, f32[4,1,768]{2,1,0:T(1,128)}, f32[1,768]{1,0:T(1,128)}, bf16[8,96,768]{2,1,0:T(8,12...) custom-call(s32[12]{0:T(128)} %concatenate.115.offsets, ...), custom_call_target="tpu_custom_call" | custom-call | flops 9663676416 | bytes 34603008 | tf_op jit(solution)/shard_map/mlp_backward/pallas_call | solution.py:754
  288.3 26.1 %attention_backward.2 = (f32[512,768]{1,0:T(8,128)}, f32[2,3,768]{2,1,0:T(4,128)}, f32[4,1,576]{2,1,0:T(1,128)}, f32[1,768]{1,0:T(1,128)}, bf16[8,48,768]{2,1,0:...) custom-call(s32[12]{0:T(128)} %concatenate.115.offsets, ...), custom_call_target="tpu_custom_call" | custom-call | flops 5838471168 | bytes 25165824 | tf_op jit(solution)/shard_map/attention_backward/pallas_call | solution.py:798
  332.1 22.6 %mlp_backward.3 = (f32[512,768]{1,0:T(8,128)}, f32[2,3,768]{2,1,0:T(4,128)}, f32[4,1,768]{2,1,0:T(1,128)}, f32[1,768]{1,0:T(1,128)}, bf16[8,96,768]{2,1,0:T(8,12...) custom-call(s32[12]{0:T(128)} %concatenate.115.offsets, ...), custom_call_target="tpu_custom_call" | custom-call | flops 9663676416 | bytes 34603008 | tf_op jit(solution)/shard_map/mlp_backward/pallas_call | solution.py:754
  369.6 9.5 %collective-permute-done.70 = bf16[4,96,768]{2,1,0:T(8,128)(2,1)} collective-permute-done((bf16[4,96,768]{2,1,0:T(8,128)(2,1)}, bf16[4,96,768]{2,1,0:T(8,128)(2,1)}, u32[]{:S(2)}, u32[]{:S(2)}) %collective-permute-start.70) | collective-permute-done | bytes 589856 | tf_op jit(solution)/shard_map/ppermute | solution.py:93
  388.1 26.4 %attention_backward.3 = (f32[512,768]{1,0:T(8,128)}, f32[2,3,768]{2,1,0:T(4,128)}, f32[4,1,576]{2,1,0:T(1,128)}, f32[1,768]{1,0:T(1,128)}, bf16[8,48,768]{2,1,0:...) custom-call(s32[12]{0:T(128)} %concatenate.115.offsets, ...), custom_call_target="tpu_custom_call" | custom-call | flops 5838471168 | bytes 25165824 | tf_op jit(solution)/shard_map/attention_backward/pallas_call | solution.py:798
  439.2 7.6 %modes_backward.2 = (f32[6,96,192]{2,1,0:T(8,128)S(1)}, f32[64,96]{1,0:T(8,128)S(1)}, f32[1,1]{1,0:T(1,128)}, f32[1536,768]{1,0:T(8,128)}, f32[64,768]{1,0:T(8,128)S(1)}, /*index=5*/f32[1,1]{1,0:T(1,128)}) custom-call(bf16[512,768]{1,0:T(8,128)(2,1)} %bitcast.75.refs_0_, s32[64,2]{1,0:T(8,128)S(1)} %copy.121.refs_1_, ...), custom_call_target="tpu_custom_call" | custom-call | tf_op jit(solution)/shard_map/modes_backward/pallas_call | solution.py:958
  461.9 4.3 collective-permute-done.87
  496.2 12.5 %collective-permute-done.93 = f32[40,768]{1,0:T(8,128)S(1)} collective-permute-done((f32[40,768]{1,0:T(8,128)S(1)}, f32[40,768]{1,0:T(8,128)S(1)}, u32[]{:S(2)}, u32[]{:S(2)}) %collective-permute-start.93) | collective-permute-done | bytes 122912 | tf_op jit(solution)/shard_map/ppermute | solution.py:105
  508.8 6.8 %collective-permute-done.94 = f32[40,768]{1,0:T(8,128)S(1)} collective-permute-done((f32[40,768]{1,0:T(8,128)S(1)}, f32[40,768]{1,0:T(8,128)S(1)}, u32[]{:S(2)}, u32[]{:S(2)}) %collective-permute-start.94) | collective-permute-done | bytes 122912 | tf_op jit(solution)/shard_map/ppermute | solution.py:105
  527.6 4.9 pad_maximum_fusion.grad_ref
  546.9 6.3 collective-permute-done.107
  562.3 4.2 collective-permute-done.112
  569.7 8.1 %collective-permute-done.111 = bf16[8,48,768]{2,1,0:T(8,128)(2,1)S(1)} collective-permute-done((bf16[8,48,768]{2,1,0:T(8,128)(2,1)}, bf16[8,48,768]{2,1,0:T(8,128)(2,1)S(1)}, u32[]{:S(2)}, u32[]{:S(2)}) %collective-permute-start.111) | collective-permute-done | bytes 589856 | tf_op jit(solution)/shard_map/ppermute | solution.py:93
  587.2 5.6 collective-permute-done.116
  593.2 3.7 collective-permute-done.119
  604.4 4.0 collective-permute-done.121
  608.3 3.8 collective-permute-done.122
  653.2 12.9 %adam_final.1 = (f32[1552,768]{1,0:T(8,128)}, f32[1552,768]{1,0:T(8,128)}, f32[1552,768]{1,0:T(8,128)}) custom-call(f32[1]{0:T(128)} %bitcast.101.clip_ref, f32[1552,768]{1,0:T(8,128)} %pad_maximum_fusion.grad_ref, f32[16,768]{1,0:T(8,128)} %copy-done.95, f32[1552,768]{1,0:T(8,128)} %bitcast.326, f32[1552,768]{1,0:T(8,128)} %bitcast.328, f32[1552,768]{1,0:T(8,128)} %bitcast.329), custom_call_target="tpu_custom_call" | custom-call | tf_op jit(solution)/shard_map/adam_final/pallas_call | solution.py:1098
  666.0 8.9 %adam_blocks.1 = (f32[2,13,96,192]{3,2,1,0:T(8,128)}, f32[2,13,96,192]{3,2,1,0:T(8,128)}, f32[2,13,96,192]{3,2,1,0:T(8,128)}, f32[2,5,192,96]{3,2,1,0:T(8,128)},...) custom-call(f32[1]{0:T(128)} %bitcast.101.clip_ref, f32[2,6,96,192]{3,2,1,0:T(8,128)} %pad_maximum_fusion.1.mode_ref, ...), custom_call_target="tpu_custom_call" | custom-call | tf_op jit(solution)/shard_map/adam_blocks/pallas_call | solution.py:1059
  (834 shorter events, 328.3 us)
Async XLA Ops:
  53.7 20.6 %collective-permute-start.11 = (bf16[8,48,768]{2,1,0:T(8,128)(2,1)S(1)}, bf16[8,48,768]{2,1,0:T(8,128)(2,1)S(1)}, u32[]{:S(2)}, u32[]{:S(2)}) collective-permute-start(bf16[8,48,768]{2,1,0:T(8,128)(2,1)S(1)} %constant_dynamic-update-slice_fusion.5.refs_2_), channel_id=1, source_target_pairs={{0,1},{1,0},{2,3},{3,2},{4,5},{5,4},{6,7},{7,6},{8,9},{9,8},{10,11... | collective-permute-start | bytes 1769480 | tf_op jit(solution)/shard_map/ppermute | solution.py:97
  56.9 30.4 %collective-permute-start.28 = (bf16[2,2,4,208,128]{4,3,0,2,1:T(8,128)(2,1)S(1)}, bf16[2,2,4,208,128]{4,3,0,2,1:T(8,128)(2,1)S(1)}, u32[]{:S(2)}, u32[]{:S(2)}) collective-permute-start(bf16[2,2,4,208,128]{4,3,0,2,1:T(8,128)(2,1)S(1)} %pad_maximum_fusion.3), channel_id=1, source_target_pairs={{0,1},{1,0},{2,3},{3,2},{4,5},{5,4},{6,7},{7,6},{8,9},{9,8},{10,11... | collective-permute-start | bytes 2555912 | tf_op jit(solution)/shard_map/ppermute | solution.py:97
  86.8 20.6 %collective-permute-start.16 = (bf16[8,48,768]{2,1,0:T(8,128)(2,1)}, bf16[8,48,768]{2,1,0:T(8,128)(2,1)}, u32[]{:S(2)}, u32[]{:S(2)}) collective-permute-start(bf16[8,48,768]{2,1,0:T(8,128)(2,1)} %collective-permute-done.8.refs_1_), channel_id=1, source_target_pairs={{0,1},{1,0},{2,3},{3,2},{4,5},{5,4},{6,7},{7,6},{8,9},{9,8},{10,11... | collective-permute-start | bytes 1769480 | tf_op jit(solution)/shard_map/ppermute | solution.py:97
  86.8 20.6 %collective-permute-start.17 = (bf16[8,48,768]{2,1,0:T(8,128)(2,1)}, bf16[8,48,768]{2,1,0:T(8,128)(2,1)}, u32[]{:S(2)}, u32[]{:S(2)}) collective-permute-start(bf16[8,48,768]{2,1,0:T(8,128)(2,1)} %collective-permute-done.9.refs_3_), channel_id=1, source_target_pairs={{0,1},{1,0},{2,3},{3,2},{4,5},{5,4},{6,7},{7,6},{8,9},{9,8},{10,11... | collective-permute-start | bytes 1769480 | tf_op jit(solution)/shard_map/ppermute | solution.py:97
  108.2 32.6 %collective-permute-start.19 = (bf16[8,96,768]{2,1,0:T(8,128)(2,1)}, bf16[8,96,768]{2,1,0:T(8,128)(2,1)}, u32[]{:S(2)}, u32[]{:S(2)}) collective-permute-start(bf16[8,96,768]{2,1,0:T(8,128)(2,1)} %constant_dynamic-update-slice_fusion.10.refs_0_), channel_id=1, source_target_pairs={{0,4},{4,0},{8,12},{12,8},{16,20},{20,16},{24,28},{28,24},{1,5},{5... | collective-permute-start | bytes 3538952 | tf_op jit(solution)/shard_map/ppermute | solution.py:101
  109.7 31.1 %collective-permute-start.20 = (bf16[8,96,768]{2,1,0:T(8,128)(2,1)}, bf16[8,96,768]{2,1,0:T(8,128)(2,1)}, u32[]{:S(2)}, u32[]{:S(2)}) collective-permute-start(bf16[8,96,768]{2,1,0:T(8,128)(2,1)} %constant_dynamic-update-slice_fusion.15.refs_2_), channel_id=1, source_target_pairs={{0,2},{1,3},{2,0},{3,1},{4,6},{5,7},{6,4},{7,5},{8,10},{9,11},{10,... | collective-permute-start | bytes 3538952 | tf_op jit(solution)/shard_map/ppermute | solution.py:93
  140.8 30.1 %collective-permute-start.40 = (bf16[8,96,768]{2,1,0:T(8,128)(2,1)}, bf16[8,96,768]{2,1,0:T(8,128)(2,1)}, u32[]{:S(2)}, u32[]{:S(2)}) collective-permute-start(bf16[8,96,768]{2,1,0:T(8,128)(2,1)} %collective-permute-done.19.refs_1_), channel_id=1, source_target_pairs={{0,1},{1,0},{2,3},{3,2},{4,5},{5,4},{6,7},{7,6},{8,9},{9,8},{10,11... | collective-permute-start | bytes 3538952 | tf_op jit(solution)/shard_map/ppermute | solution.py:97
  140.9 30.1 %collective-permute-start.41 = (bf16[8,96,768]{2,1,0:T(8,128)(2,1)}, bf16[8,96,768]{2,1,0:T(8,128)(2,1)}, u32[]{:S(2)}, u32[]{:S(2)}) collective-permute-start(bf16[8,96,768]{2,1,0:T(8,128)(2,1)} %collective-permute-done.20.refs_3_), channel_id=1, source_target_pairs={{0,1},{1,0},{2,3},{3,2},{4,5},{5,4},{6,7},{7,6},{8,9},{9,8},{10,11... | collective-permute-start | bytes 3538952 | tf_op jit(solution)/shard_map/ppermute | solution.py:97
  141.4 21.3 %collective-permute-start.39 = (bf16[4,48,768]{2,1,0:T(8,128)(2,1)S(1)}, bf16[4,48,768]{2,1,0:T(8,128)(2,1)S(1)}, u32[]{:S(2)}, u32[]{:S(2)}) collective-permute-start(bf16[4,48,768]{2,1,0:T(8,128)(2,1)S(1)} %pad_maximum_fusion.14), channel_id=1, source_target_pairs={{0,4},{4,0},{8,12},{12,8},{16,20},{20,16},{24,28},{28,24},{1,5},{5... | collective-permute-start | bytes 884744 | tf_op jit(solution)/shard_map/ppermute | solution.py:101
  142.6 21.5 %collective-permute-start.38 = (bf16[4,48,768]{2,1,0:T(8,128)(2,1)S(1)}, bf16[4,48,768]{2,1,0:T(8,128)(2,1)S(1)}, u32[]{:S(2)}, u32[]{:S(2)}) collective-permute-start(bf16[4,48,768]{2,1,0:T(8,128)(2,1)S(1)} %pad_maximum_fusion.13), channel_id=1, source_target_pairs={{0,2},{1,3},{2,0},{3,1},{4,6},{5,7},{6,4},{7,5},{8,10},{9,11},{10,... | collective-permute-start | bytes 884744 | tf_op jit(solution)/shard_map/ppermute | solution.py:93
  205.1 26.9 %collective-permute-start.52 = (bf16[8,96,768]{2,1,0:T(8,128)(2,1)S(1)}, bf16[8,96,768]{2,1,0:T(8,128)(2,1)}, u32[]{:S(2)}, u32[]{:S(2)}) collective-permute-start(bf16[8,96,768]{2,1,0:T(8,128)(2,1)S(1)} %constant_dynamic-update-slice_fusion.37.refs_0_), channel_id=1, source_target_pairs={{0,4},{4,0},{8,12},{12,8},{16,20},{20,16},{24,28},{28,24},{1,5},{5... | collective-permute-start | bytes 3538952 | tf_op jit(solution)/shard_map/ppermute | solution.py:101
  206.5 26.5 %collective-permute-start.53 = (bf16[8,96,768]{2,1,0:T(8,128)(2,1)S(1)}, bf16[8,96,768]{2,1,0:T(8,128)(2,1)}, u32[]{:S(2)}, u32[]{:S(2)}) collective-permute-start(bf16[8,96,768]{2,1,0:T(8,128)(2,1)S(1)} %constant_dynamic-update-slice_fusion.42.refs_2_), channel_id=1, source_target_pairs={{0,2},{1,3},{2,0},{3,1},{4,6},{5,7},{6,4},{7,5},{8,10},{9,11},{10,... | collective-permute-start | bytes 3538952 | tf_op jit(solution)/shard_map/ppermute | solution.py:93
  208.0 25.0 %collective-permute-start.54 = (bf16[8,96,768]{2,1,0:T(8,128)(2,1)S(1)}, bf16[8,96,768]{2,1,0:T(8,128)(2,1)S(1)}, u32[]{:S(2)}, u32[]{:S(2)}) collective-permute-start(bf16[8,96,768]{2,1,0:T(8,128)(2,1)S(1)} %constant_dynamic-update-slice_fusion.37.refs_0_), channel_id=1, source_target_pairs={{0,1},{1,0},{2,3},{3,2},{4,5},{5,4},{6,7},{7,6},{8,9},{9,8},{10,11... | collective-permute-start | bytes 3538952 | tf_op jit(solution)/shard_map/ppermute | solution.py:97
  208.0 25.1 %collective-permute-start.55 = (bf16[8,96,768]{2,1,0:T(8,128)(2,1)S(1)}, bf16[8,96,768]{2,1,0:T(8,128)(2,1)}, u32[]{:S(2)}, u32[]{:S(2)}) collective-permute-start(bf16[8,96,768]{2,1,0:T(8,128)(2,1)S(1)} %constant_dynamic-update-slice_fusion.42.refs_2_), channel_id=1, source_target_pairs={{0,1},{1,0},{2,3},{3,2},{4,5},{5,4},{6,7},{7,6},{8,9},{9,8},{10,11... | collective-permute-start | bytes 3538952 | tf_op jit(solution)/shard_map/ppermute | solution.py:97
  281.5 33.7 %collective-permute-start.59 = (bf16[8,96,768]{2,1,0:T(8,128)(2,1)}, bf16[8,96,768]{2,1,0:T(8,128)(2,1)}, u32[]{:S(2)}, u32[]{:S(2)}) collective-permute-start(bf16[8,96,768]{2,1,0:T(8,128)(2,1)} %get-tuple-element.447), channel_id=1, source_target_pairs={{0,1},{1,0},{2,3},{3,2},{4,5},{5,4},{6,7},{7,6},{8,9},{9,8},{10,11... | collective-permute-start | bytes 3538952 | tf_op jit(solution)/shard_map/ppermute | solution.py:97
  283.6 34.7 %collective-permute-start.58 = (bf16[8,96,768]{2,1,0:T(8,128)(2,1)}, bf16[8,96,768]{2,1,0:T(8,128)(2,1)}, u32[]{:S(2)}, u32[]{:S(2)}) collective-permute-start(bf16[8,96,768]{2,1,0:T(8,128)(2,1)} %get-tuple-element.446), channel_id=1, source_target_pairs={{0,1},{1,0},{2,3},{3,2},{4,5},{5,4},{6,7},{7,6},{8,9},{9,8},{10,11... | collective-permute-start | bytes 3538952 | tf_op jit(solution)/shard_map/ppermute | solution.py:97
  283.7 37.3 %collective-permute-start.60 = (bf16[8,96,768]{2,1,0:T(8,128)(2,1)}, bf16[8,96,768]{2,1,0:T(8,128)(2,1)}, u32[]{:S(2)}, u32[]{:S(2)}) collective-permute-start(bf16[8,96,768]{2,1,0:T(8,128)(2,1)} %get-tuple-element.469), channel_id=1, source_target_pairs={{0,1},{1,0},{2,3},{3,2},{4,5},{5,4},{6,7},{7,6},{8,9},{9,8},{10,11... | collective-permute-start | bytes 3538952 | tf_op jit(solution)/shard_map/ppermute | solution.py:97
  284.1 36.8 %collective-permute-start.61 = (bf16[8,96,768]{2,1,0:T(8,128)(2,1)}, bf16[8,96,768]{2,1,0:T(8,128)(2,1)}, u32[]{:S(2)}, u32[]{:S(2)}) collective-permute-start(bf16[8,96,768]{2,1,0:T(8,128)(2,1)} %get-tuple-element.470), channel_id=1, source_target_pairs={{0,1},{1,0},{2,3},{3,2},{4,5},{5,4},{6,7},{7,6},{8,9},{9,8},{10,11... | collective-permute-start | bytes 3538952 | tf_op jit(solution)/shard_map/ppermute | solution.py:97
  320.9 33.7 %collective-permute-start.63 = (bf16[8,96,768]{2,1,0:T(8,128)(2,1)}, bf16[8,96,768]{2,1,0:T(8,128)(2,1)}, u32[]{:S(2)}, u32[]{:S(2)}) collective-permute-start(bf16[8,96,768]{2,1,0:T(8,128)(2,1)} %add_convert_fusion.10), channel_id=1, source_target_pairs={{0,2},{1,3},{2,0},{3,1},{4,6},{5,7},{6,4},{7,5},{8,10},{9,11},{10,... | collective-permute-start | bytes 3538952 | tf_op jit(solution)/shard_map/ppermute | solution.py:93
  330.8 27.4 %collective-permute-start.62 = (bf16[8,96,768]{2,1,0:T(8,128)(2,1)}, bf16[8,96,768]{2,1,0:T(8,128)(2,1)S(1)}, u32[]{:S(2)}, u32[]{:S(2)}) collective-permute-start(bf16[8,96,768]{2,1,0:T(8,128)(2,1)} %add_convert_fusion.11), channel_id=1, source_target_pairs={{0,4},{4,0},{8,12},{12,8},{16,20},{20,16},{24,28},{28,24},{1,5},{5... | collective-permute-start | bytes 3538952 | tf_op jit(solution)/shard_map/ppermute | solution.py:101
  331.5 31.0 %collective-permute-start.64 = (bf16[8,48,768]{2,1,0:T(8,128)(2,1)}, bf16[8,48,768]{2,1,0:T(8,128)(2,1)}, u32[]{:S(2)}, u32[]{:S(2)}) collective-permute-start(bf16[8,48,768]{2,1,0:T(8,128)(2,1)} %get-tuple-element.499), channel_id=1, source_target_pairs={{0,1},{1,0},{2,3},{3,2},{4,5},{5,4},{6,7},{7,6},{8,9},{9,8},{10,11... | collective-permute-start | bytes 1769480 | tf_op jit(solution)/shard_map/ppermute | solution.py:97
  331.6 31.0 %collective-permute-start.65 = (bf16[8,48,768]{2,1,0:T(8,128)(2,1)}, bf16[8,48,768]{2,1,0:T(8,128)(2,1)}, u32[]{:S(2)}, u32[]{:S(2)}) collective-permute-start(bf16[8,48,768]{2,1,0:T(8,128)(2,1)} %get-tuple-element.500), channel_id=1, source_target_pairs={{0,1},{1,0},{2,3},{3,2},{4,5},{5,4},{6,7},{7,6},{8,9},{9,8},{10,11... | collective-permute-start | bytes 1769480 | tf_op jit(solution)/shard_map/ppermute | solution.py:97
  332.1 30.4 %collective-permute-start.66 = (bf16[8,48,768]{2,1,0:T(8,128)(2,1)}, bf16[8,48,768]{2,1,0:T(8,128)(2,1)}, u32[]{:S(2)}, u32[]{:S(2)}) collective-permute-start(bf16[8,48,768]{2,1,0:T(8,128)(2,1)} %get-tuple-element.501), channel_id=1, source_target_pairs={{0,1},{1,0},{2,3},{3,2},{4,5},{5,4},{6,7},{7,6},{8,9},{9,8},{10,11... | collective-permute-start | bytes 1769480 | tf_op jit(solution)/shard_map/ppermute | solution.py:97
  367.5 61.5 %collective-permute-start.78 = (bf16[8,16,768]{2,1,0:T(8,128)(2,1)}, bf16[8,16,768]{2,1,0:T(8,128)(2,1)}, u32[]{:S(2)}, u32[]{:S(2)}) collective-permute-start(bf16[8,16,768]{2,1,0:T(8,128)(2,1)} %get-tuple-element.770), channel_id=1, source_target_pairs={{0,2},{1,3},{2,0},{3,1},{4,6},{5,7},{6,4},{7,5},{8,10},{9,11},{10,... | collective-permute-start | bytes 589832 | tf_op jit(solution)/shard_map/ppermute | solution.py:93
  446.9 32.9 %collective-permute-start.96 = (bf16[8,96,768]{2,1,0:T(8,128)(2,1)S(1)}, bf16[8,96,768]{2,1,0:T(8,128)(2,1)S(1)}, u32[]{:S(2)}, u32[]{:S(2)}) collective-permute-start(bf16[8,96,768]{2,1,0:T(8,128)(2,1)S(1)} %copy-done.62), channel_id=1, source_target_pairs={{0,2},{1,3},{2,0},{3,1},{4,6},{5,7},{6,4},{7,5},{8,10},{9,11},{10,... | collective-permute-start | bytes 3538952 | tf_op jit(solution)/shard_map/ppermute | solution.py:93
  447.5 39.6 %collective-permute-start.95 = (bf16[8,96,768]{2,1,0:T(8,128)(2,1)S(1)}, bf16[8,96,768]{2,1,0:T(8,128)(2,1)S(1)}, u32[]{:S(2)}, u32[]{:S(2)}) collective-permute-start(bf16[8,96,768]{2,1,0:T(8,128)(2,1)S(1)} %copy-done.61), channel_id=1, source_target_pairs={{0,4},{4,0},{8,12},{12,8},{16,20},{20,16},{24,28},{28,24},{1,5},{5... | collective-permute-start | bytes 3538952 | tf_op jit(solution)/shard_map/ppermute | solution.py:101
  469.1 21.5 %collective-permute-start.97 = (bf16[2,96,768]{2,1,0:T(8,128)(2,1)S(1)}, bf16[2,96,768]{2,1,0:T(8,128)(2,1)S(1)}, u32[]{:S(2)}, u32[]{:S(2)}) collective-permute-start(bf16[2,96,768]{2,1,0:T(8,128)(2,1)S(1)} %copy-done.99), channel_id=1, source_target_pairs={{0,24},{4,28},{8,0},{12,4},{16,8},{20,12},{24,16},{28,20},{1,25},{... | collective-permute-start | bytes 884744 | tf_op jit(solution)/shard_map/ppermute | solution.py:105
  490.6 46.6 %collective-permute-start.102 = (bf16[2,96,768]{2,1,0:T(8,128)(2,1)}, bf16[2,96,768]{2,1,0:T(8,128)(2,1)}, u32[]{:S(2)}, u32[]{:S(2)}) collective-permute-start(bf16[2,96,768]{2,1,0:T(8,128)(2,1)} %pad_maximum_fusion.17), channel_id=1, source_target_pairs={{0,16},{4,20},{8,24},{12,28},{16,0},{20,4},{24,8},{28,12},{1,17},{... | collective-permute-start | bytes 884744 | tf_op jit(solution)/shard_map/ppermute | solution.py:105
  490.7 41.9 %collective-permute-start.100 = (bf16[4,96,768]{2,1,0:T(8,128)(2,1)}, bf16[4,96,768]{2,1,0:T(8,128)(2,1)}, u32[]{:S(2)}, u32[]{:S(2)}) collective-permute-start(bf16[4,96,768]{2,1,0:T(8,128)(2,1)} %slice.690), channel_id=1, source_target_pairs={{0,2},{1,3},{2,0},{3,1},{4,6},{5,7},{6,4},{7,5},{8,10},{9,11},{10,... | collective-permute-start | bytes 1769480 | tf_op jit(solution)/shard_map/ppermute | solution.py:93
  492.3 42.1 %collective-permute-start.101 = (bf16[4,96,768]{2,1,0:T(8,128)(2,1)}, bf16[4,96,768]{2,1,0:T(8,128)(2,1)}, u32[]{:S(2)}, u32[]{:S(2)}) collective-permute-start(bf16[4,96,768]{2,1,0:T(8,128)(2,1)} %slice.691), channel_id=1, source_target_pairs={{0,4},{4,0},{8,12},{12,8},{16,20},{20,16},{24,28},{28,24},{1,5},{5... | collective-permute-start | bytes 1769480 | tf_op jit(solution)/shard_map/ppermute | solution.py:101
  493.3 43.9 %collective-permute-start.105 = (bf16[8,48,768]{2,1,0:T(8,128)(2,1)}, bf16[8,48,768]{2,1,0:T(8,128)(2,1)}, u32[]{:S(2)}, u32[]{:S(2)}) collective-permute-start(bf16[8,48,768]{2,1,0:T(8,128)(2,1)} %get-tuple-element.563), channel_id=1, source_target_pairs={{0,1},{1,0},{2,3},{3,2},{4,5},{5,4},{6,7},{7,6},{8,9},{9,8},{10,11... | collective-permute-start | bytes 1769480 | tf_op jit(solution)/shard_map/ppermute | solution.py:97
  515.7 21.6 %collective-permute-start.103 = (bf16[8,48,768]{2,1,0:T(8,128)(2,1)}, bf16[8,48,768]{2,1,0:T(8,128)(2,1)}, u32[]{:S(2)}, u32[]{:S(2)}) collective-permute-start(bf16[8,48,768]{2,1,0:T(8,128)(2,1)} %get-tuple-element.561), channel_id=1, source_target_pairs={{0,1},{1,0},{2,3},{3,2},{4,5},{5,4},{6,7},{7,6},{8,9},{9,8},{10,11... | collective-permute-start | bytes 1769480 | tf_op jit(solution)/shard_map/ppermute | solution.py:97
  (247 other events, 2392.7 us)

commit v2 on v1

v2 whole, which is shorter than its diff:
```python
import functools
import math

import jax
import jax.numpy as jnp
import numpy as np
from jax import lax
from jax.experimental import pallas as pl
from jax.experimental.pallas import tpu as pltpu
from jax.sharding import PartitionSpec as P

HEAD_DIM = 64
CLASSES = 1000
FREQ = 256
PATCH = 16
LEN = 256
STEPS_T = 1000
STEP = 10

HIGHEST = lax.Precision.HIGHEST
EPS_NORM = 1e-06
CLIP_NORM = 1.0
RATE = 0.05
RATE_BIAS = 0.25
BETA_ONE = 0.9
BETA_TWO = 0.999
DECAY = 0.01
ADAM_EPS = 1e-08

F32 = jnp.float32
BF16 = jnp.bfloat16
MIB = 1024 * 1024
ANY = pl.BlockSpec(memory_space=pl.ANY)
SMEM = pl.BlockSpec(memory_space=pltpu.SMEM)
NT = (((1,), (1,)), ((), ()))
TN = (((0,), (0,)), ((), ()))


def dot_nt(a, b):
    return lax.dot_general(a, b, NT, preferred_element_type=F32)


def dot_tn(a, b):
    return lax.dot_general(a, b, TN, preferred_element_type=F32)


def dot_nn(a, b):
    return jnp.dot(a, b, preferred_element_type=F32)


class Place:
    def __init__(self, row_block):
        self.rows = lax.axis_size("row")
        self.cols = lax.axis_size("col")
        self.row = lax.axis_index("row")
        self.col = lax.axis_index("col")
        self.direct = self.rows == 8 and self.cols == 4 and row_block % 32 == 0
        self.z = self.row // 2
        self.y = self.row % 2
        self.x = self.col // 2
        self.core = self.col % 2
        self.half = row_block // 2
        self.table = self.route_table() if self.direct else jnp.zeros((8,), jnp.int32)

    def route_table(self):
        z, y, x, core = self.z, self.y, self.x, self.core
        e = jnp.arange(64, dtype=jnp.int32)
        owner = core ^ (e // 32)
        later, first, kc, kz = e // 16 % 2, e // 8 % 2, e // 4 % 2, e % 4
        kx = jnp.where(owner == 0, first, later)
        ky = jnp.where(owner == 0, later, first)
        cols = (x ^ kx) * 2 + (owner ^ kc)
        rows = ((z + 4 - kz) % 4 * 2 + (y ^ ky)) * 2 * self.half + owner * self.half
        e = jnp.arange(16, dtype=jnp.int32)
        col, owner, ky = e // 4, core ^ (e // 2 % 2), e % 2
        kx = (col // 2) ^ x
        later = jnp.where(owner == 0, ky, kx)
        first = jnp.where(owner == 0, kx, ky)
        slots = jnp.stack([later, first, (col % 2) ^ owner], axis=1).reshape(-1)
        owner, ky, kz = core ^ (e // 8), e // 4 % 2, e % 4
        outs = ((z + 4 - kz) % 4 * 2 + (y ^ ky)) * 2 * self.half + owner * self.half
        return jnp.concatenate([cols, rows, slots, outs]).astype(jnp.int32)

    def found_at(self):
        device = jnp.arange(self.rows * self.cols, dtype=jnp.int32)
        if not self.direct:
            return device
        row, col = device // 4, device % 4
        kz = (self.z + 4 - row // 2) % 4
        ky = (row % 2) ^ self.y
        kx = (col // 2) ^ self.x
        kc = (col % 2) ^ self.core
        return ((kc * 2 + kx) * 2 + ky) * 4 + kz


def swap_x(v):
    return lax.ppermute(v, "col", [(c, c ^ 2) for c in range(4)])


def swap_core(v):
    return lax.ppermute(v, "col", [(c, c ^ 1) for c in range(4)])


def swap_y(v):
    return lax.ppermute(v, "row", [(r, r ^ 1) for r in range(8)])


def swap_first(v):
    pairs = [(d, d ^ 2 if d % 2 == 0 else d ^ 4) for d in range(32)]
    return lax.ppermute(v, ("row", "col"), pairs)


def swap_second(v):
    pairs = [(d, d ^ 4 if d % 2 == 0 else d ^ 2) for d in range(32)]
    return lax.ppermute(v, ("row", "col"), pairs)


def turn_z(v, k):
    return lax.ppermute(v, "row", [(r, (r // 2 + k) % 4 * 2 + r % 2) for r in range(8)])


def pair(index, own, other):
    first = index == 0
    return jnp.stack([jnp.where(first, own, other), jnp.where(first, other, own)])


def gather_z(place, own):
    got = [own] + [turn_z(own, k) for k in (1, 2, 3)]
    ring = jnp.stack([got[3], got[2], got[1], got[0], got[3], got[2], got[1]])
    return lax.dynamic_slice_in_dim(ring, 3 - place.z, 4, 0)


def gather_cols(place, own):
    if not place.direct:
        return lax.all_gather(own, "col")
    both = pair(place.core, own, swap_core(own))
    return pair(place.x, both, swap_x(both)).reshape((4,) + own.shape)


def near_z(own):
    return jnp.stack([own] + [turn_z(own, k) for k in (1, 2, 3)])


def near_y(every):
    return jnp.concatenate([every, swap_y(every)])


def near_rows(own):
    return near_y(near_z(own))


def near_x(every):
    return jnp.concatenate([every, swap_x(every)])


def near_core(every):
    return jnp.concatenate([every, swap_core(every)])


def near_cols(every):
    return near_core(near_x(every))


def gather_near(place, own):
    if not place.direct:
        return lax.all_gather(own, ("row", "col"))
    return near_cols(near_rows(own))


def sum_along_z(place, own):
    parts = own.reshape((4, own.shape[0] // 4) + own.shape[1:])
    total = lax.dynamic_index_in_dim(parts, place.z, 0, False)
    for k in (1, 2, 3):
        total = total + turn_z(
            lax.dynamic_index_in_dim(parts, (place.z + k) % 4, 0, False), k
        )
    return total


def sum_with(swap):
    return lambda total: total + swap(total)


def sum_spread(place, total):
    every = gather_z(place, total)
    return every.reshape((-1,) + total.shape[1:])


def sum_scalar(place, value):
    if not place.direct:
        return lax.psum(value, ("row", "col"))
    total = jnp.broadcast_to(value, (8, 128))
    total = total + swap_core(total)
    total = total + swap_x(total)
    total = total + swap_y(total)
    total = total + lax.ppermute(total, "row", [(r, r ^ 2) for r in range(8)])
    total = total + lax.ppermute(total, "row", [(r, r ^ 4) for r in range(8)])
    return total[0, 0]


def scatter_plain(place, partial, mine):
    _, count, narrow = partial.shape
    summed = lax.psum_scatter(partial, "row", scatter_dimension=0, tiled=True)
    spread = lax.all_gather(summed, "col")
    spread = lax.dynamic_slice_in_dim(spread, place.col * mine, mine, 1)
    return jnp.transpose(spread, (1, 2, 0, 3)).reshape(mine, count, place.cols * narrow)


def scatter_y(place, partial):
    samples, count, narrow = partial.shape
    by_y = partial.reshape(4, 2, samples // 8, count, narrow)
    own = lax.dynamic_index_in_dim(by_y, place.y, 1, False)
    return own + swap_y(lax.dynamic_index_in_dim(by_y, 1 - place.y, 1, False))


def scatter_z(place, own):
    total = lax.dynamic_index_in_dim(own, place.z, 0, False)
    for k in (1, 2, 3):
        total = total + turn_z(lax.dynamic_index_in_dim(own, (place.z + k) % 4, 0, False), k)
    return total


def scatter_x(place, total, mine):
    _, count, narrow = total.shape
    by_x = total.reshape(2, 2, mine, count, narrow)
    own = lax.dynamic_index_in_dim(by_x, place.x, 0, False)
    got = swap_x(lax.dynamic_index_in_dim(by_x, 1 - place.x, 0, False))
    return pair(place.x, own, got)


def scatter_core(place, both):
    _, _, mine, count, narrow = both.shape
    own = lax.dynamic_index_in_dim(both, place.core, 1, False)
    got = swap_core(lax.dynamic_index_in_dim(both, 1 - place.core, 1, False))
    every = pair(place.core, own, got)
    return jnp.transpose(every, (2, 3, 1, 0, 4)).reshape(mine, count, 4 * narrow)


class Route:
    def __init__(self, place, buffers):
        self.direct = place.direct
        self.half = place.half
        self.cols = place.cols
        self.count = len(buffers)
        if self.direct:
            matrices = buffers[0].shape[2]
            self.outs = [(2, 8, 2, matrices) + buffers[0].shape[3:]] * 2
        else:
            self.outs = [buffers[0].shape]

    def load(self, table, buffers, matrix, target, sems):
        if not self.direct:
            for c in range(self.cols):
                pltpu.make_async_copy(buffers[0].at[matrix, c], target.at[c], sems.at[c]).start()
            return
        for e in range(64):
            first, kc, kz = e // 8 % 2, e // 4 % 2, e % 4
            row = pl.multiple_of(table[64 + e], 16)
            pltpu.make_async_copy(
                buffers[e // 16].at[first * 4 + kz, kc, matrix],
                target.at[table[e], pl.ds(row, self.half), :],
                sems.at[table[e]],
            ).start()

    def store(self, table, c, matrix, source, grads, sem):
        if not self.direct:
            pltpu.make_async_copy(source, grads[0].at[matrix, c], sem).start()
            return
        for owner in range(2):
            for ky in range(2):
                at = 128 + ((c * 2 + owner) * 2 + ky) * 3
                for kz in range(4):
                    row = pl.multiple_of(table[176 + (owner * 2 + ky) * 4 + kz], 16)
                    pltpu.make_async_copy(
                        source.at[pl.ds(row, self.half), :],
                        grads[owner].at[
                            table[at], table[at + 1] * 4 + kz, table[at + 2], matrix
                        ],
                        sem,
                    ).start()


class Stages:
    def __init__(self):
        self.last = None

    def run(self, moves, works=()):
        operands = ([v for _, v in moves], [w[1:] for w in works])
        if self.last is not None:
            operands, _ = lax.optimization_barrier((operands, self.last))
        moved = [move(v) for (move, _), v in zip(moves, operands[0])]
        done = [w[0](*v) for w, v in zip(works, operands[1])]
        self.last = (moved, done)
        return moved, done


def turn(k):
    return lambda v: turn_z(v, k)


class Spread:
    def __init__(self, kept, got):
        self.own = jnp.stack([kept, got])

    def turns(self, ks):
        return [(turn(k), self.own) for k in ks]

    def turned(self, one, two, three):
        self.z = jnp.stack([self.own, one, two, three])

    def first(self):
        return [(swap_first, self.z)]

    def second(self, got):
        self.p = jnp.concatenate([self.z, got])
        return [(swap_second, self.p)]

    def core(self):
        return [(swap_core, self.p)]

    def late_core(self, q):
        self.q = q
        return [(swap_core, q)]

    def buffers(self, core, late_core):
        return [self.p, self.q, core, late_core]


def add_up(*parts):
    total = parts[0].astype(F32)
    for part in parts[1:]:
        total = total + part.astype(F32)
    return total


class Gathered:
    def __init__(self, buffers):
        self.own = buffers[0]
        self.core = [(swap_core, buffers[1])]

    def first(self, got):
        self.got = got
        return [(swap_second, add_up(self.own[1], got[1]).astype(BF16))]

    def second(self, got):
        self.parts = (self.own[0], self.got[0], got)
        return [(swap_first, add_up(*[v[4:] for v in self.parts]).astype(BF16))]

    def third(self, got):
        self.z = [add_up(*[v[k] for v in self.parts], got[k]).astype(BF16) for k in range(4)]

    def turns(self, ks=(1, 3, 2)):
        return [(turn(4 - k), self.z[k]) for k in ks]

    def total(self, got):
        return add_up(self.z[0], *got)


def plain_gather(parts):
    every = lax.all_gather(lax.all_gather(parts, "row", axis=1, tiled=True), "col")
    return jnp.swapaxes(every, 0, 1)


def plain_scatter(grads):
    summed = lax.psum_scatter(grads.astype(F32), "row", scatter_dimension=2, tiled=True)
    return lax.psum_scatter(summed, "col", scatter_dimension=1, tiled=False)


def normal(v):
    center = jnp.mean(v, axis=-1, keepdims=True)
    moved = v - center
    inverse = lax.rsqrt(jnp.mean(moved * moved, axis=-1, keepdims=True) + EPS_NORM)
    return moved * inverse, inverse


def wait_all(ref, sem):
    pltpu.make_async_copy(ref, ref, sem).wait()


def row_of(shared_ref, at):
    return jnp.concatenate(
        [shared_ref[c, at : at + 1, :] for c in range(shared_ref.shape[0])], axis=1
    )


def attention_forward_body(route, base, table, x_ref, mod_ref, shared_ref, *refs):
    n_buf = route.count
    buffers = refs[:n_buf]
    out_ref, h_ref, qkv_ref, p_ref, o_ref, a_ref, w_ref, sems = refs[n_buf:]
    c = pl.program_id(0)
    samples = mod_ref.shape[0]

    @pl.when(c == 0)
    def _():
        route.load(table, buffers, 0, w_ref, sems)
        for s in range(samples):
            rows = pl.ds(s * LEN, LEN)
            n, _ = normal(x_ref[rows, :])
            h_ref[rows, :] = (n * (1.0 + mod_ref[s, 1:2]) + mod_ref[s, 0:1]).astype(BF16)
        a_ref[...] = jnp.zeros_like(a_ref)

    wait_all(w_ref.at[c], sems.at[c])
    width = shared_ref.shape[-1]
    query_bias = shared_ref[c, base + 6 : base + 7, :]
    value_bias = shared_ref[c, base + 7 : base + 8, :]
    bias = jnp.concatenate([query_bias, jnp.zeros_like(query_bias), value_bias], axis=1)
    triple = dot_nn(h_ref[...], w_ref[c, :, : 3 * width]) + bias
    qkv_ref[0] = triple.astype(BF16)
    for s in range(samples):
        rows = pl.ds(s * LEN, LEN)
        pieces = []
        for j in range(width // HEAD_DIM):
            q = qkv_ref[0, rows, j * HEAD_DIM : (j + 1) * HEAD_DIM]
            k = qkv_ref[0, rows, width + j * HEAD_DIM : width + (j + 1) * HEAD_DIM]
            v = qkv_ref[0, rows, 2 * width + j * HEAD_DIM : 2 * width + (j + 1) * HEAD_DIM]
            scores = dot_nt(q, k) * HEAD_DIM ** (-0.5)
            powers = jnp.exp(scores - jnp.max(scores, axis=-1, keepdims=True))
            probs = (powers / jnp.sum(powers, axis=-1, keepdims=True)).astype(BF16)
            p_ref[0, j, s] = probs
            pieces.append(dot_nn(probs, v).astype(BF16))
        o_ref[0, rows, :] = jnp.concatenate(pieces, axis=1)
    a_ref[...] += dot_nt(o_ref[0], w_ref[c, :, 3 * width :])

    @pl.when(c == pl.num_programs(0) - 1)
    def _():
        a_ref[...] += row_of(shared_ref, base + 12)
        for s in range(samples):
            rows = pl.ds(s * LEN, LEN)
            out_ref[rows, :] = x_ref[rows, :] + mod_ref[s, 2:3] * a_ref[rows, :]


def mlp_forward_body(route, base, table, x_ref, mod_ref, shared_ref, *refs):
    n_buf = route.count
    buffers = refs[:n_buf]
    out_ref, h_ref, u_ref, m_ref, wi_ref, wo_ref, sems_i, sems_o = refs[n_buf:]
    c = pl.program_id(0)
    samples = mod_ref.shape[0]

    @pl.when(c == 0)
    def _():
        route.load(table, buffers, 0, wi_ref, sems_i)
        route.load(table, buffers, 1, wo_ref, sems_o)
        for s in range(samples):
            rows = pl.ds(s * LEN, LEN)
            n, _ = normal(x_ref[rows, :])
            h_ref[rows, :] = (n * (1.0 + mod_ref[s, 1:2]) + mod_ref[s, 0:1]).astype(BF16)
        m_ref[...] = jnp.zeros_like(m_ref)

    wait_all(wi_ref.at[c], sems_i.at[c])
    blocks = wi_ref.shape[-1] // shared_ref.shape[-1]
    bias = jnp.concatenate(
        [shared_ref[c, base + 8 + k : base + 9 + k, :] for k in range(blocks)], axis=1
    )
    hidden = dot_nn(h_ref[...], wi_ref[c]) + bias
    u_ref[0] = hidden
    active = jax.nn.gelu(hidden, approximate=True).astype(BF16)
    wait_all(wo_ref.at[c], sems_o.at[c])
    m_ref[...] += dot_nt(active, wo_ref[c])

    @pl.when(c == pl.num_programs(0) - 1)
    def _():
        m_ref[...] += row_of(shared_ref, base + 13)
        for s in range(samples):
            rows = pl.ds(s * LEN, LEN)
            out_ref[rows, :] = x_ref[rows, :] + mod_ref[s, 2:3] * m_ref[rows, :]


def norm_backward(s, x_ref, mod_ref, dx_ref, dh_ref, out_ref, dmod_ref):
    rows = pl.ds(s * LEN, LEN)
    n, inverse = normal(x_ref[rows, :])
    dh = dh_ref[rows, :]
    dmod_ref[s, 0:1] = jnp.sum(dh, axis=0, keepdims=True)
    dmod_ref[s, 1:2] = jnp.sum(dh * n, axis=0, keepdims=True)
    dn = dh * (1.0 + mod_ref[s, 1:2])
    back = inverse * (
        dn
        - jnp.mean(dn, axis=-1, keepdims=True)
        - n * jnp.mean(dn * n, axis=-1, keepdims=True)
    )
    if dx_ref is None:
        out_ref[rows, :] = back
    else:
        out_ref[rows, :] = dx_ref[rows, :] + back


def branch_gradient(dx_ref, mod_ref, branch_ref, dmod_ref, sum_ref, low_ref):
    total = None
    for s in range(mod_ref.shape[0]):
        rows = pl.ds(s * LEN, LEN)
        dx = dx_ref[rows, :]
        dmod_ref[s, 2:3] = jnp.sum(dx * branch_ref[rows, :], axis=0, keepdims=True)
        db = mod_ref[s, 2:3] * dx
        low_ref[rows, :] = db.astype(BF16)
        part = jnp.sum(db, axis=0, keepdims=True)
        total = part if total is None else total + part
    sum_ref[...] = total


def gelu_slope(u):
    k = math.sqrt(2.0 / math.pi)
    square = u * u
    t = jnp.tanh(k * (u + 0.044715 * square * u))
    half = 0.5 * (1.0 + t)
    slope = half + 0.5 * u * (1.0 - t * t) * (k * (1.0 + 3 * 0.044715 * square))
    return u * half, slope


def mlp_backward_body(
    route, table, dx_ref, x_ref, mod_ref, m_ref, h_ref, u_ref, *refs
):
    n_buf, n_out = route.count, len(route.outs)
    buffers = refs[:n_buf]
    out_ref, dmod_ref, dbias_ref, dtail_ref = refs[n_buf : n_buf + 4]
    grads = refs[n_buf + 4 : n_buf + n_out + 4]
    wi_ref, wo_ref, low_ref, dh_ref, gi_ref, go_ref, sems_i, sems_o, sems_gi, sems_go = refs[
        n_buf + n_out + 4 :
    ]
    c = pl.program_id(0)
    count = route.cols
    samples = mod_ref.shape[0]

    @pl.when(c == 0)
    def _():
        route.load(table, buffers, 1, wo_ref, sems_o)
        route.load(table, buffers, 0, wi_ref, sems_i)
        branch_gradient(dx_ref, mod_ref, m_ref, dmod_ref, dtail_ref, low_ref)
        dh_ref[...] = jnp.zeros_like(dh_ref)

    slot = lax.rem(c, 2)

    @pl.when(c >= 2)
    def _():
        wait_all(gi_ref.at[slot], sems_gi.at[slot])
        wait_all(go_ref.at[slot], sems_go.at[slot])

    wait_all(wo_ref.at[c], sems_o.at[c])
    active, slope = gelu_slope(u_ref[0])
    low = low_ref[...]
    go_ref[slot] = dot_tn(low, active.astype(BF16)).astype(BF16)
    route.store(table, c, 1, go_ref.at[slot], grads, sems_go.at[slot])
    du = dot_nn(low, wo_ref[c]) * slope
    dbias_ref[c] = jnp.sum(du, axis=0, keepdims=True)
    du = du.astype(BF16)
    gi_ref[slot] = dot_tn(h_ref[...], du).astype(BF16)
    route.store(table, c, 0, gi_ref.at[slot], grads, sems_gi.at[slot])
    wait_all(wi_ref.at[c], sems_i.at[c])
    dh_ref[...] += dot_nt(du, wi_ref[c])

    @pl.when(c == count - 1)
    def _():
        for s in range(samples):
            norm_backward(s, x_ref, mod_ref, dx_ref, dh_ref, out_ref, dmod_ref)
        for k in range(2):
            wait_all(gi_ref.at[k], sems_gi.at[k])
            wait_all(go_ref.at[k], sems_go.at[k])


def attention_backward_body(
    route, table, dx_ref, x_ref, mod_ref, a_ref, h_ref, qkv_ref, p_ref, o_ref, *refs
):
    n_buf, n_out = route.count, len(route.outs)
    buffers = refs[:n_buf]
    out_ref, dmod_ref, dbias_ref, dtail_ref = refs[n_buf : n_buf + 4]
    grads = refs[n_buf + 4 : n_buf + n_out + 4]
    w_ref, low_ref, dh_ref, d_ref, g_ref, sems, sems_g = refs[n_buf + n_out + 4 :]
    c = pl.program_id(0)
    count = route.cols
    samples = mod_ref.shape[0]
    width = qkv_ref.shape[-1] // 3
    factor = HEAD_DIM ** (-0.5)

    @pl.when(c == 0)
    def _():
        route.load(table, buffers, 0, w_ref, sems)
        branch_gradient(dx_ref, mod_ref, a_ref, dmod_ref, dtail_ref, low_ref)
        dh_ref[...] = jnp.zeros_like(dh_ref)

    slot = lax.rem(c, 2)

    @pl.when(c >= 2)
    def _():
        wait_all(g_ref.at[slot], sems_g.at[slot])

    wait_all(w_ref.at[c], sems.at[c])
    do_all = dot_nn(low_ref[...], w_ref[c, :, 3 * width :]).astype(BF16)
    sums = [None] * (width // HEAD_DIM)
    for s in range(samples):
        rows = pl.ds(s * LEN, LEN)
        dqs, dks, dvs = [], [], []
        for j in range(width // HEAD_DIM):
            q = qkv_ref[0, rows, j * HEAD_DIM : (j + 1) * HEAD_DIM]
            k = qkv_ref[0, rows, width + j * HEAD_DIM : width + (j + 1) * HEAD_DIM]
            v = qkv_ref[0, rows, 2 * width + j * HEAD_DIM : 2 * width + (j + 1) * HEAD_DIM]
            o = o_ref[0, rows, j * HEAD_DIM : (j + 1) * HEAD_DIM]
            do = do_all[s * LEN : (s + 1) * LEN, j * HEAD_DIM : (j + 1) * HEAD_DIM]
            probs = p_ref[0, j, s]
            dp = dot_nt(do, v)
            delta = jnp.sum(do.astype(F32) * o.astype(F32), axis=-1, keepdims=True)
            ds = (probs.astype(F32) * (dp - delta)).astype(BF16)
            dqs.append(dot_nn(ds, k) * factor)
            dks.append(dot_tn(ds, q) * factor)
            dvs.append(dot_tn(probs, do))
        joined = jnp.concatenate(dqs + dks + dvs, axis=1)
        part = jnp.sum(joined, axis=0, keepdims=True)
        sums = part if s == 0 else sums + part
        d_ref[rows, :] = joined.astype(BF16)
    dbias_ref[c] = sums
    grad_in = dot_tn(h_ref[...], d_ref[...])
    grad_out = dot_tn(low_ref[...], o_ref[0])
    g_ref[slot] = jnp.concatenate([grad_in, grad_out], axis=1).astype(BF16)
    route.store(table, c, 0, g_ref.at[slot], grads, sems_g.at[slot])
    dh_ref[...] += dot_nt(d_ref[...], w_ref[c, :, : 3 * width])

    @pl.when(c == count - 1)
    def _():
        for s in range(samples):
            norm_backward(s, x_ref, mod_ref, dx_ref, dh_ref, out_ref, dmod_ref)
        for k in range(2):
            wait_all(g_ref.at[k], sems_g.at[k])


def final_body(
    x_ref, mod_ref, head_ref, bias_ref, noise_ref, mask_ref,
    dx_ref, loss_ref, dhead_ref, dbias_ref, dmod_ref, h_ref, dh_ref,
):
    samples = mod_ref.shape[0]
    for s in range(samples):
        rows = pl.ds(s * LEN, LEN)
        n, _ = normal(x_ref[rows, :])
        h_ref[rows, :] = (n * (1.0 + mod_ref[s, 1:2]) + mod_ref[s, 0:1]).astype(BF16)
    predicted = dot_nt(h_ref[...], head_ref[...]) + bias_ref[...]
    error = predicted - noise_ref[...]
    masked = mask_ref[...] * error
    loss_ref[...] = jnp.sum(masked * error, axis=0, keepdims=True)
    dpred = 2.0 * masked
    dbias_ref[...] = jnp.sum(dpred, axis=0, keepdims=True)
    low = dpred.astype(BF16)
    dhead_ref[...] = dot_tn(low, h_ref[...])
    dh_ref[...] = dot_nn(low, head_ref[...])
    for s in range(samples):
        norm_backward(s, x_ref, mod_ref, None, dh_ref, dx_ref, dmod_ref)


def whole_block(shape):
    rank = len(shape)
    return pl.BlockSpec(shape, lambda c: (0,) * rank, pipeline_mode=pl.Buffered(1))


def whole_out(shape):
    rank = len(shape)
    return pl.BlockSpec(shape, lambda c: (0,) * rank)


def block_of(shape):
    rank = len(shape)
    return pl.BlockSpec((1,) + tuple(shape[1:]), lambda c: (c,) + (0,) * (rank - 1))


def params(mib):
    return pltpu.CompilerParams(
        dimension_semantics=("arbitrary",), vmem_limit_bytes=mib * MIB
    )


def cost(flops, nbytes, exps=0):
    return pl.CostEstimate(flops=int(flops), bytes_accessed=int(nbytes), transcendentals=int(exps))


def shaped(shape, dtype):
    return jax.ShapeDtypeStruct(tuple(shape), dtype)


def attention_forward(place, base, buffers, x, mods, shared):
    route = Route(place, buffers)
    count = place.cols
    tokens, width = x.shape
    samples = mods.shape[0]
    narrow = shared.shape[-1]
    heads = narrow // HEAD_DIM
    outs = [
        shaped((tokens, width), F32),
        shaped((tokens, width), BF16),
        shaped((count, tokens, 3 * narrow), BF16),
        shaped((count, heads, samples, LEN, LEN), BF16),
        shaped((count, tokens, narrow), BF16),
        shaped((tokens, width), F32),
    ]
    return pl.pallas_call(
        functools.partial(attention_forward_body, route, base),
        grid=(count,),
        in_specs=[SMEM, whole_block(x.shape), whole_block(mods.shape), whole_block(shared.shape)]
        + [ANY] * len(buffers),
        out_specs=[whole_out(outs[0].shape), whole_out(outs[1].shape)]
        + [block_of(o.shape) for o in outs[2:5]]
        + [whole_out(outs[5].shape)],
        out_shape=outs,
        scratch_shapes=[
            pltpu.VMEM((count, width, 4 * narrow), BF16),
            pltpu.SemaphoreType.DMA((count,)),
        ],
        compiler_params=params(58),
        cost_estimate=cost(
            2 * tokens * width * width * 4 + 4 * tokens * LEN * width,
            8 * width * width + 30 * tokens * width,
            tokens * LEN * width // HEAD_DIM,
        ),
        name="attention_forward",
    )(place.table, x, mods, shared, *buffers)


def mlp_forward(place, base, buffers, x, mods, shared):
    route = Route(place, buffers)
    count = place.cols
    tokens, width = x.shape
    wide = buffers[0].shape[-1]
    outs = [
        shaped((tokens, width), F32),
        shaped((tokens, width), BF16),
        shaped((count, tokens, wide), F32),
        shaped((tokens, width), F32),
    ]
    return pl.pallas_call(
        functools.partial(mlp_forward_body, route, base),
        grid=(count,),
        in_specs=[SMEM, whole_block(x.shape), whole_block(mods.shape), whole_block(shared.shape)]
        + [ANY] * len(buffers),
        out_specs=[whole_out(outs[0].shape), whole_out(outs[1].shape), block_of(outs[2].shape)]
        + [whole_out(outs[3].shape)],
        out_shape=outs,
        scratch_shapes=[
            pltpu.VMEM((count, width, wide), BF16),
            pltpu.VMEM((count, width, wide), BF16),
            pltpu.SemaphoreType.DMA((count,)),
            pltpu.SemaphoreType.DMA((count,)),
        ],
        compiler_params=params(58),
        cost_estimate=cost(
            2 * tokens * width * wide * count * 2,
            4 * width * wide * count + 30 * tokens * width,
            tokens * wide * count,
        ),
        name="mlp_forward",
    )(place.table, x, mods, shared, *buffers)


def mlp_backward(place, buffers, dx, x, mods, m, h, u):
    route = Route(place, buffers)
    count = place.cols
    tokens, width = x.shape
    wide = u.shape[-1]
    outs = [
        shaped((tokens, width), F32),
        shaped(mods.shape, F32),
        shaped((count, 1, wide), F32),
        shaped((1, width), F32),
    ] + [shaped(v, BF16) for v in route.outs]
    out = pl.pallas_call(
        functools.partial(mlp_backward_body, route),
        grid=(count,),
        in_specs=[SMEM, whole_block(x.shape), whole_block(x.shape), whole_block(mods.shape)]
        + [whole_block(m.shape), whole_block(h.shape), block_of(u.shape)]
        + [ANY] * len(buffers),
        out_specs=[whole_out(x.shape), whole_out(mods.shape), whole_out(outs[2].shape)]
        + [whole_out((1, width))]
        + [ANY] * len(route.outs),
        out_shape=outs,
        scratch_shapes=[
            pltpu.VMEM((count, width, wide), BF16),
            pltpu.VMEM((count, width, wide), BF16),
            pltpu.VMEM((tokens, width), BF16),
            pltpu.VMEM((tokens, width), F32),
            pltpu.VMEM((2, width, wide), BF16),
            pltpu.VMEM((2, width, wide), BF16),
            pltpu.SemaphoreType.DMA((count,)),
            pltpu.SemaphoreType.DMA((count,)),
            pltpu.SemaphoreType.DMA((2,)),
            pltpu.SemaphoreType.DMA((2,)),
        ],
        compiler_params=params(58),
        cost_estimate=cost(
            4 * 2 * tokens * width * wide * count,
            8 * width * wide * count + 40 * tokens * width,
            tokens * wide * count,
        ),
        name="mlp_backward",
    )(place.table, dx, x, mods, m, h, u, *buffers)
    return out[:4], out[4:]


def attention_backward(place, buffers, dx, x, mods, a, h, qkv, p, o):
    route = Route(place, buffers)
    count = place.cols
    tokens, width = x.shape
    narrow = o.shape[-1]
    outs = [
        shaped((tokens, width), F32),
        shaped(mods.shape, F32),
        shaped((count, 1, 3 * narrow), F32),
        shaped((1, width), F32),
    ] + [shaped(v, BF16) for v in route.outs]
    out = pl.pallas_call(
        functools.partial(attention_backward_body, route),
        grid=(count,),
        in_specs=[SMEM, whole_block(x.shape), whole_block(x.shape), whole_block(mods.shape)]
        + [whole_block(a.shape), whole_block(h.shape)]
        + [block_of(qkv.shape), block_of(p.shape), block_of(o.shape)]
        + [ANY] * len(buffers),
        out_specs=[whole_out(x.shape), whole_out(mods.shape), whole_out(outs[2].shape)]
        + [whole_out((1, width))]
        + [ANY] * len(route.outs),
        out_shape=outs,
        scratch_shapes=[
            pltpu.VMEM((count, width, 4 * narrow), BF16),
            pltpu.VMEM((tokens, width), BF16),
            pltpu.VMEM((tokens, width), F32),
            pltpu.VMEM((tokens, 3 * narrow), BF16),
            pltpu.VMEM((2, width, 4 * narrow), BF16),
            pltpu.SemaphoreType.DMA((count,)),
            pltpu.SemaphoreType.DMA((2,)),
        ],
        compiler_params=params(58),
        cost_estimate=cost(
            4 * tokens * width * width * 4 + 10 * tokens * LEN * width,
            16 * width * width + 40 * tokens * width,
        ),
        name="attention_backward",
    )(place.table, dx, x, mods, a, h, qkv, p, o, *buffers)
    return out[:4], out[4:]


def final_step(x, mods, head, bias, noise, mask):
    tokens, width = x.shape
    vmem = pl.BlockSpec(memory_space=pltpu.VMEM)
    return pl.pallas_call(
        final_body,
        in_specs=[vmem] * 6,
        out_specs=[vmem] * 5,
        out_shape=[
            shaped((tokens, width), F32),
            shaped((1, PATCH), F32),
            shaped((PATCH, width), F32),
            shaped((1, PATCH), F32),
            shaped(mods.shape, F32),
        ],
        scratch_shapes=[pltpu.VMEM((tokens, width), BF16), pltpu.VMEM((tokens, width), F32)],
        compiler_params=pltpu.CompilerParams(vmem_limit_bytes=32 * MIB),
        cost_estimate=cost(6 * tokens * width * PATCH, 12 * tokens * width),
        name="final_step",
    )(x, mods, head, bias, noise, mask)


def pack_body(in_ref, out_ref, block_ref, mode_ref):
    blocks = out_ref.shape[1] - 1
    for k in range(6):
        mode_ref[0, k] = in_ref[0, k].astype(BF16)
    attn = [in_ref[0, 6 + k] for k in range(3)] + [out_ref[0, 0].T]
    block_ref[0] = jnp.concatenate(attn, axis=1).astype(BF16)
    first = [in_ref[0, 9 + k] for k in range(blocks)]
    block_ref[1] = jnp.concatenate(first, axis=1).astype(BF16)
    second = [out_ref[0, 1 + k].T for k in range(blocks)]
    block_ref[2] = jnp.concatenate(second, axis=1).astype(BF16)


def pack_weights(weights_in, weights_out):
    layers, kinds, block, narrow = weights_in.shape
    outs = [
        shaped((3 * layers, block, 4 * narrow), BF16),
        shaped((layers, 6, block, narrow), BF16),
    ]
    return pl.pallas_call(
        pack_body,
        grid=(layers,),
        in_specs=[block_of(weights_in.shape), block_of(weights_out.shape)],
        out_specs=[
            pl.BlockSpec((3, block, 4 * narrow), lambda c: (c, 0, 0)),
            block_of(outs[1].shape),
        ],
        out_shape=outs,
        compiler_params=params(32),
        name="pack_weights",
    )(weights_in, weights_out)


def embed_body(base, noisy_ref, shared_ref, table_ref, out_ref):
    patch = jnp.concatenate(
        [
            shared_ref[c, base + 3 : base + 3 + PATCH, :]
            for c in range(shared_ref.shape[0])
        ],
        axis=1,
    ).astype(BF16)
    constant = row_of(shared_ref, base + 2) + table_ref[...]
    for s in range(noisy_ref.shape[0] // LEN):
        rows = pl.ds(s * LEN, LEN)
        out_ref[rows, :] = dot_nn(noisy_ref[rows, :], patch) + constant


def embed_tokens(base, noisy, shared, table):
    vmem = pl.BlockSpec(memory_space=pltpu.VMEM)
    return pl.pallas_call(
        functools.partial(embed_body, base),
        in_specs=[vmem] * 3,
        out_specs=vmem,
        out_shape=shaped((noisy.shape[0], table.shape[1]), F32),
        compiler_params=pltpu.CompilerParams(vmem_limit_bytes=32 * MIB),
        name="embed_tokens",
    )(noisy, shared, table)


def silu_slope(values):
    sigmoid_part = jax.nn.sigmoid(values)
    return sigmoid_part * (1.0 + values * (1.0 - sigmoid_part))


TIME_BLOCK = 128
CLASS_AT, FREQ_AT, LABEL_AT = 192, 208, 224


def condition_body(base, found, near_ref, shared_ref, *refs):
    cond_ref, act_ref, first_ref, first_act_ref, freq_ref, label_ref, class_ref, wave_ref = refs
    cols, _, narrow = shared_ref.shape
    rows = near_ref.shape[0] // cols
    steps = FREQ // TIME_BLOCK
    for r in range(rows):
        at = slice(r * 8, r * 8 + 8)
        for c in range(cols):
            block = near_ref[found[r * cols + c], CLASS_AT:, :].astype(F32)
            joined = jnp.concatenate([block[:8], block[8:16, : narrow - 128]], axis=1)
            class_ref[at, c * narrow : (c + 1) * narrow] = joined
            if c == 0:
                wave_ref[at, :TIME_BLOCK] = block[16:24]
                wave_ref[at, TIME_BLOCK:] = block[24:32]
                label_ref[at, :] = block[32:40] * 32.0 + block[40:48]
    freq = wave_ref[...].astype(BF16)
    freq_ref[...] = freq

    def product(left, first_row, count):
        parts = []
        for c in range(cols):
            total = None
            for k in range(count):
                block = near_ref[found[(first_row + k) * cols + c], :CLASS_AT, :]
                part = dot_nt(left[:, k * TIME_BLOCK : (k + 1) * TIME_BLOCK], block)
                total = part if total is None else total + part
            parts.append(total)
        return jnp.concatenate(parts, axis=1)

    first = product(freq, 0, steps) + row_of(shared_ref, base)
    first_ref[...] = first
    first_act = (first * jax.nn.sigmoid(first)).astype(BF16)
    first_act_ref[...] = first_act
    cond = product(first_act, steps, rows - steps) + row_of(shared_ref, base + 1)
    cond = cond + class_ref[...]
    cond_ref[...] = cond
    act_ref[...] = (cond * jax.nn.sigmoid(cond)).astype(BF16)


def condition_step(base, found, near, shared, samples, width):
    vmem = pl.BlockSpec(memory_space=pltpu.VMEM)
    outs = [
        shaped((samples, width), F32),
        shaped((samples, width), BF16),
        shaped((samples, width), F32),
        shaped((samples, width), BF16),
        shaped((samples, FREQ), BF16),
        shaped((samples, 128), F32),
    ]
    return pl.pallas_call(
        functools.partial(condition_body, base),
        in_specs=[SMEM, vmem, vmem],
        out_specs=[vmem] * len(outs),
        out_shape=outs,
        scratch_shapes=[pltpu.VMEM((samples, width), F32), pltpu.VMEM((samples, FREQ), F32)],
        compiler_params=pltpu.CompilerParams(vmem_limit_bytes=32 * MIB),
        name="condition_step",
    )(found, near, shared)


def condition_back_body(
    layers, blocks, found, spot, small_ref, part_ref, final_ref, square_ref, cond_ref, first_ref,
    input_ref, label_ref, pick_ref, near_ref, time_ref, embed_ref, bias_ref, own_ref, shared_ref,
    grad_ref,
):
    row, col = spot[0], spot[1]
    samples, width = cond_ref.shape
    narrow = pick_ref.shape[1]
    cols = width // narrow
    rows = near_ref.shape[0] // cols
    steps = FREQ // TIME_BLOCK
    start = 16 * layers + 2 * PATCH
    pick = pick_ref[...]
    pick_wide = pick.astype(F32)

    def own_cols(v):
        return jnp.dot(v, pick_wide, precision=HIGHEST, preferred_element_type=F32)

    def squares(v):
        return jnp.sum(v * v, keepdims=True)

    block_rows = part_ref.shape[2]
    for r in range(rows):
        part = part_ref[found[r * cols + col]]
        grad_ref[:, r * block_rows : (r + 1) * block_rows] = part
    grad_cond = (grad_ref[...] + final_ref[...]) * silu_slope(cond_ref[...])
    low = grad_cond.astype(BF16)
    parts = []
    for r in range(steps, rows):
        total = None
        for c in range(cols):
            block = near_ref[found[r * cols + c], :CLASS_AT, :]
            part = dot_nn(low[:, c * narrow : (c + 1) * narrow], block)
            total = part if total is None else total + part
        parts.append(total)
    grad_first = jnp.concatenate(parts, axis=1) * silu_slope(first_ref[...])
    is_first = (row < steps).astype(F32)
    outputs = grad_first.astype(BF16).astype(F32) * is_first + low.astype(F32) * (1.0 - is_first)
    outputs = dot_nn(outputs.astype(BF16), pick).astype(BF16)
    time_grad = dot_tn(outputs, input_ref[...])
    time_ref[...] = time_grad
    hot = lax.broadcasted_iota(jnp.int32, (samples, CLASSES), 1).astype(F32)
    hot = (hot == label_ref[:, 0:1]).astype(F32)
    class_grad = lax.dot_general(
        own_cols(grad_cond), hot, TN, precision=HIGHEST, preferred_element_type=F32
    )
    patch = own_cols(small_ref[start - PATCH : start, :])
    embed_ref[...] = jnp.concatenate([class_grad, patch.T], axis=1)
    own_ref[...] = squares(time_grad) + squares(class_grad) * (1.0 / rows)
    time_bias = jnp.concatenate(
        [jnp.sum(grad_first, axis=0, keepdims=True), jnp.sum(grad_cond, axis=0, keepdims=True)],
        axis=0,
    )
    total = square_ref[...] + squares(time_bias) + squares(small_ref[start - 2 * PATCH : start + 3, :])
    total = total + squares(small_ref[start + 3 : start + 4, :PATCH])
    own = own_cols(small_ref[: start + 16, :])
    lines = []
    for layer in range(layers):
        at = 16 * layer
        total = total + squares(small_ref[at : at + 6 + cols, :])
        total = total + squares(small_ref[at + 10 : at + 10 + cols, :narrow])
        total = total + squares(small_ref[at + 10 : at + 10 + cols, 2 * narrow : 3 * narrow])
        total = total + squares(small_ref[at + 14 : at + 16, :])
        attn = small_ref[pl.ds(at + 10 + col, 1), :]
        mlp = small_ref[pl.ds(at + 6 + col, 1), :]
        lines += [own[at : at + 6], attn[:, :narrow], attn[:, 2 * narrow : 3 * narrow]]
        lines += [mlp[:, k * narrow : (k + 1) * narrow] for k in range(blocks)]
        lines += [own[at + 14 : at + 16]]
    lines += [own_cols(time_bias), own[start : start + 1]]
    bias_ref[...] = jnp.concatenate(lines, axis=0)
    shared_ref[...] = total


def condition_back(
    layers, blocks, found, spot, small, part, final, squares, cond, first, inputs, labels, pick, near
):
    vmem = pl.BlockSpec(memory_space=pltpu.VMEM)
    narrow = pick.shape[1]
    outs = [
        shaped((narrow, TIME_BLOCK), F32),
        shaped((narrow, CLASSES + PATCH), F32),
        shaped((14 * layers + 3, narrow), F32),
        shaped((1, 1), F32),
        shaped((1, 1), F32),
    ]
    operands = [small, part, final, squares, cond, first, inputs, labels, pick, near]
    return pl.pallas_call(
        functools.partial(condition_back_body, layers, blocks),
        in_specs=[SMEM, SMEM] + [vmem] * len(operands),
        out_specs=[vmem] * len(outs),
        out_shape=outs,
        scratch_shapes=[pltpu.VMEM(cond.shape, F32)],
        compiler_params=pltpu.CompilerParams(vmem_limit_bytes=48 * MIB),
        name="condition_back",
    )(found, spot, *operands)


def modes_backward_body(
    layers, near_ref, at_ref, rows_ref, pick_ref, mode_ref, act_ref, final_ref,
    block_ref, part_ref, square_ref, grad_ref, cond_ref, shared_ref,
):
    near = near_ref[...]
    at = at_ref[...]
    samples = at.shape[0]
    where = lax.broadcasted_iota(jnp.int32, (samples, near.shape[0]), 1)
    cols, narrow = mode_ref.shape[0], mode_ref.shape[4]
    spreads = []
    for layer in range(layers):
        for k in range(6):
            offset = 12 * layer + 6 * (k // 3) + k % 3
            spreads.append((where == at[:, 0:1] + at[:, 1:2] * 3 + offset).astype(BF16))
    for k in range(2):
        spreads.append((where == at[:, 0:1] + at[:, 1:2] * 2 + 12 * layers + k).astype(BF16))
    rows = dot_nn(jnp.concatenate(spreads, axis=0), near).astype(BF16)
    mine = dot_nn(rows[: 6 * layers * samples], pick_ref[...]).astype(BF16)

    total = None
    squares = jnp.zeros((1, 1), F32)
    for layer in range(layers):
        for k in range(6):
            at_row = (6 * layer + k) * samples
            low = rows[at_row : at_row + samples]
            grad = dot_tn(rows_ref[...], mine[at_row : at_row + samples])
            block_ref[layer, k] = grad
            squares = squares + jnp.sum(grad * grad, keepdims=True)
            full = jnp.concatenate([mode_ref[c, layer, k] for c in range(cols)], axis=1)
            part = dot_nt(low, full)
            total = part if total is None else total + part
    part_ref[...] = total
    square_ref[...] = squares
    width = act_ref.shape[1]
    at_row = 6 * layers * samples
    shift, scale = rows[at_row : at_row + samples], rows[at_row + samples :]
    squares = jnp.zeros((1, 1), F32)
    for k, low in enumerate((shift, scale)):
        grad = dot_tn(low, act_ref[...])
        grad_ref[k * width : (k + 1) * width, :] = grad
        squares = squares + jnp.sum(grad * grad, keepdims=True)
    cond_ref[...] = dot_nn(shift, final_ref[:width, :]) + dot_nn(
        scale, final_ref[width : 2 * width, :]
    )
    shared_ref[...] = squares


def modes_backward(near, at, cond_rows, pick, mode_full, act, final):
    vmem = pl.BlockSpec(memory_space=pltpu.VMEM)
    samples, block = cond_rows.shape
    width = near.shape[2]
    layers, narrow = mode_full.shape[1], mode_full.shape[4]
    outs = [
        shaped((layers, 6, block, narrow), F32),
        shaped((samples, block), F32),
        shaped((1, 1), F32),
        shaped((2 * width, width), F32),
        shaped((samples, width), F32),
        shaped((1, 1), F32),
    ]
    operands = [near.reshape(-1, width), at, cond_rows, pick, mode_full, act, final]
    return pl.pallas_call(
        functools.partial(modes_backward_body, layers),
        in_specs=[vmem] * len(operands),
        out_specs=[vmem] * len(outs),
        out_shape=outs,
        compiler_params=pltpu.CompilerParams(vmem_limit_bytes=56 * MIB),
        name="modes_backward",
    )(*operands)


def modes_backward_plain(near, cond_rows, mode_full, act, final, col):
    layers, narrow, width = mode_full.shape[1], mode_full.shape[4], near.shape[2]
    devices = near.shape[0]
    samples = act.shape[0] // devices
    low = near[:, : 12 * layers].reshape(devices, layers, 2, samples, 3, width)
    low = jnp.transpose(low, (1, 2, 4, 0, 3, 5)).reshape(layers, 6, devices * samples, width)
    mine = lax.dynamic_slice_in_dim(low, col * narrow, narrow, 3)
    block = jnp.einsum("sd,lkse->lkde", cond_rows, mine, preferred_element_type=F32)
    full = jnp.transpose(mode_full, (1, 2, 3, 0, 4)).reshape(layers, 6, -1, width)
    part = jnp.einsum("lkse,lkde->sd", low, full, preferred_element_type=F32)
    ends = near[:, 12 * layers : 12 * layers + 2 * samples].reshape(-1, 2, width)
    grad = jnp.einsum("ske,sd->ked", ends, act, preferred_element_type=F32)
    cond = jnp.einsum(
        "ske,ked->sd", ends, final[: 2 * width].reshape(2, width, width), preferred_element_type=F32
    )
    grad = grad.reshape(2 * width, width)
    return block, part, squared(block)[None, None], grad, cond, squared(grad)[None, None]


def collect_body(layers, *refs):
    out_ref = refs[-1]
    at = 0
    out_ref[...] = jnp.zeros_like(out_ref)
    take = list(refs[:-1])
    for _ in range(layers):
        dmod_a, dmod_b, dbias_a, dbias_b, dtail_a, dtail_b = [take.pop(0) for _ in range(6)]
        for k, source in enumerate((dmod_a, dmod_b)):
            total = source[0]
            for s in range(1, source.shape[0]):
                total = total + source[s]
            out_ref[at + 3 * k : at + 3 * k + 3, :] = total
        for c in range(dbias_b.shape[0]):
            out_ref[at + 6 + c : at + 7 + c, : dbias_b.shape[2]] = dbias_b[c]
            out_ref[at + 10 + c : at + 11 + c, : dbias_a.shape[2]] = dbias_a[c]
        out_ref[at + 14 : at + 15, :] = dtail_a[...]
        out_ref[at + 15 : at + 16, :] = dtail_b[...]
        at += 16
    head, head_bias, loss, mask, dfinal, dx, noisy = take
    out_ref[at : at + PATCH, :] = head[...]
    out_ref[at + PATCH : at + 2 * PATCH, :] = dot_tn(noisy[...], dx[...].astype(BF16))
    at += 2 * PATCH
    out_ref[at : at + 1, :] = jnp.sum(dx[...], axis=0, keepdims=True)
    total = dfinal[0]
    for s in range(1, dfinal.shape[0]):
        total = total + dfinal[s]
    out_ref[at + 1 : at + 3, :] = total
    out_ref[at + 3 : at + 4, 0:PATCH] = head_bias[...]
    out_ref[at + 4 : at + 5, 0:PATCH] = loss[...]
    out_ref[at + 5 : at + 6, 0:1] = jnp.sum(mask[...], keepdims=True)


def collect(layers, parts, height, width):
    vmem = pl.BlockSpec(memory_space=pltpu.VMEM)
    return pl.pallas_call(
        functools.partial(collect_body, layers),
        in_specs=[vmem] * len(parts),
        out_specs=vmem,
        out_shape=shaped((height, width), F32),
        compiler_params=pltpu.CompilerParams(vmem_limit_bytes=48 * MIB),
        name="collect_small",
    )(*parts)


def adam(weight, gradient, moment, second, clip, rate):
    gradient = gradient * clip
    moment = BETA_ONE * moment + (1.0 - BETA_ONE) * gradient
    second = BETA_TWO * second + (1.0 - BETA_TWO) * gradient * gradient
    update = (
        moment / (1.0 - BETA_ONE**STEP) / (jnp.sqrt(second / (1.0 - BETA_TWO**STEP)) + ADAM_EPS)
    )
    return weight - rate * (update + DECAY * weight), moment, second


def adam_blocks_body(layers, halves, clip_ref, spot, *refs):
    clip = clip_ref[0]
    per = 5 if halves else 3
    sums = [refs[per * layer : per * layer + per] for layer in range(layers)]
    refs = refs[per * layers :]
    wi, mi, vi, wo, mo, vo = refs[:6]
    out_i, out_o = refs[6:9], refs[9:12]
    total_ref = refs[12]
    narrow = wi.shape[3]

    def fill(layer):
        group = sums[layer]
        for k in range(3):
            if not halves:
                total_ref[k] = group[1][0] if k == 0 else group[2][k - 1]
                continue
            half = total_ref.shape[1] // 2
            mine, other = group[1:3] if k == 0 else group[3:5]
            at = 0 if k == 0 else k - 1
            core = spot[1] % 2
            total_ref[k, pl.ds(pl.multiple_of(core * half, 8), half), :] = mine[0, at]
            total_ref[k, pl.ds(pl.multiple_of((1 - core) * half, 8), half), :] = other[at]

    def update(layer, mode_ref):
        for k in range(wi.shape[1]):
            if k < 6:
                grad = mode_ref[layer, k]
            elif k < 9:
                grad = total_ref[0, :, (k - 6) * narrow : (k - 5) * narrow]
            else:
                grad = total_ref[1, :, (k - 9) * narrow : (k - 8) * narrow]
            new = adam(wi[0, k], grad, mi[0, k], vi[0, k], clip, RATE)
            for ref, value in zip(out_i, new):
                ref[0, k] = value
        for k in range(wo.shape[1]):
            if k == 0:
                grad = total_ref[0, :, 3 * narrow :]
            else:
                grad = total_ref[2, :, (k - 1) * narrow : k * narrow]
            new = adam(wo[0, k], grad.T, mo[0, k], vo[0, k], clip, RATE)
            for ref, value in zip(out_o, new):
                ref[0, k] = value

    for layer in range(layers):

        @pl.when(pl.program_id(0) == layer)
        def _(layer=layer):
            fill(layer)
            update(layer, sums[layer][0])


def adam_blocks(clip, spot, sums, ins, outs):
    arrays = list(ins) + list(outs)
    grads = [v for group in sums for v in group]
    halves = len(sums[0]) == 5
    results = [shaped(v.shape, F32) for v in arrays]
    block, narrow = ins[0].shape[2:]
    return pl.pallas_call(
        functools.partial(adam_blocks_body, len(sums), halves),
        grid=(ins[0].shape[0],),
        in_specs=[SMEM, SMEM]
        + [whole_block(v.shape) for v in grads]
        + [block_of(v.shape) for v in arrays],
        out_specs=[block_of(v.shape) for v in results],
        out_shape=results,
        scratch_shapes=[pltpu.VMEM((3, block, 4 * narrow), F32)],
        compiler_params=params(58),
        name="adam_blocks",
    )(clip, spot, *grads, *arrays)


def adam_final_body(clip_ref, grad_ref, head_ref, w, m, v, *outs):
    clip = clip_ref[0]
    step = pl.program_id(0)
    last = pl.num_programs(0) - 1

    @pl.when(step < last)
    def _():
        new = adam(w[...], grad_ref[...], m[...], v[...], clip, RATE)
        for ref, value in zip(outs, new):
            ref[...] = value

    @pl.when(step == last)
    def _():
        rows = slice(0, PATCH)
        new = adam(w[rows, :], head_ref[...], m[rows, :], v[rows, :], clip, RATE)
        for ref, value in zip(outs, new):
            ref[rows, :] = value


def adam_final(clip, grad, head, w, m, v):
    width = w.shape[1]
    height = 256
    steps = grad.shape[0] // height
    part = pl.BlockSpec((height, width), lambda c: (c, 0))
    grad_part = pl.BlockSpec((height, width), lambda c: (jnp.minimum(c, steps - 1), 0))
    return pl.pallas_call(
        adam_final_body,
        grid=(steps + 1,),
        in_specs=[SMEM, grad_part, whole_block(head.shape)] + [part] * 3,
        out_specs=[part] * 3,
        out_shape=[shaped(w.shape, F32)] * 3,
        compiler_params=params(58),
        name="adam_final",
    )(clip, grad, head, w, m, v)


def adam_rest_body(rates, clip_ref, *refs):
    clip = clip_ref[0]
    count = len(rates)
    ins, outs = refs[: 4 * count], refs[4 * count :]
    for k, rate in enumerate(rates):
        w, g, m, v = [r[...] for r in ins[4 * k : 4 * k + 4]]
        for ref, value in zip(outs[3 * k : 3 * k + 3], adam(w, g, m, v, clip, rate)):
            ref[...] = value


def adam_rest(clip, groups):
    vmem = pl.BlockSpec(memory_space=pltpu.VMEM)
    arrays, results, rates = [], [], []
    for w, g, m, v, rate in groups:
        arrays += [w, g, m, v]
        results += [shaped(w.shape, F32)] * 3
        rates.append(rate)
    return pl.pallas_call(
        functools.partial(adam_rest_body, tuple(rates)),
        in_specs=[SMEM] + [vmem] * len(arrays),
        out_specs=[vmem] * len(results),
        out_shape=results,
        compiler_params=pltpu.CompilerParams(vmem_limit_bytes=58 * MIB),
        name="adam_rest",
    )(clip, *arrays)


def squared(values):
    return jnp.sum(values * values)


def position_table(width):
    half = width // 2
    rate = np.exp(-math.log(10000.0) * (np.arange(width) % half) / half)
    angle = np.arange(LEN)[:, None] * rate[None, :]
    table = np.where(np.arange(width)[None, :] < half, np.sin(angle), np.cos(angle))
    return table.astype(np.float32)


def on_device(
    latents,
    noise,
    timesteps,
    labels,
    loss_mask,
    weights_in,
    weights_out,
    time_mlp,
    embed_table,
    final_layer,
    bias_table,
    final_bias,
    momentum_in,
    momentum_out,
    momentum_time,
    momentum_embed,
    momentum_final,
    momentum_bias,
    momentum_final_bias,
    variance_in,
    variance_out,
    variance_time,
    variance_embed,
    variance_final,
    variance_bias,
    variance_final_bias,
):
    layers, block, _, narrow = weights_in.shape
    place = Place(block)
    rows, cols = place.rows, place.cols
    width = final_layer.shape[0]
    row_samples = timesteps.shape[0]
    samples = row_samples // cols
    every_sample = row_samples * rows
    tokens = samples * LEN
    base = layers * 14
    hidden_blocks = weights_out.shape[1] - 1

    def my_cols(v, axis):
        return lax.dynamic_slice_in_dim(v, place.col * narrow, narrow, axis)

    in_view = [jnp.transpose(v, (0, 2, 1, 3)) for v in (weights_in, momentum_in, variance_in)]
    packed, mode_low = pack_weights(in_view[0], weights_out)

    embed_low = embed_table.astype(BF16)
    one_hot_row = (labels[:, None] == jnp.arange(CLASSES, dtype=jnp.int32)[None, :]).astype(BF16)
    class_rows = jnp.dot(
        one_hot_row, embed_low[:CLASSES], preferred_element_type=F32
    ).astype(BF16)
    half_freq = FREQ // 2
    freq_rate = jnp.asarray(
        np.exp(-math.log(10000.0) * np.arange(half_freq) / half_freq).astype(np.float32)
    )
    angle_grid = timesteps.astype(F32)[:, None] * freq_rate[None, :]
    freq_row = jnp.concatenate([jnp.cos(angle_grid), jnp.sin(angle_grid)], axis=1).astype(BF16)
    time_rows = time_mlp.shape[0]
    mine = jnp.concatenate([bias_table, embed_low[CLASSES:].astype(F32)], axis=0)
    final_view = [v.T for v in (final_layer, momentum_final, variance_final)]
    final_low = final_view[0].astype(BF16)
    found = place.found_at()
    sample = jnp.arange(every_sample, dtype=jnp.int32)
    mode_height = -(-(12 * layers + 4) // 16) * 16
    at = jnp.stack([found[sample // samples] * mode_height, sample % samples], axis=1)
    feature = jnp.arange(width, dtype=jnp.int32)[:, None]
    picked = jnp.arange(narrow, dtype=jnp.int32)[None, :] + place.col * narrow
    pick = (feature == picked).astype(BF16)
    spot = jnp.stack([place.row, place.col]).astype(jnp.int32)

    def partial_modes(cond_act):
        cond_rows = lax.dynamic_slice_in_dim(cond_act, place.row * block, block, 1)
        partial = jnp.einsum("sd,lkde->slke", cond_rows, mode_low, preferred_element_type=F32)
        return cond_rows, partial.reshape(every_sample, layers * 6, narrow)

    def own_modes(total, shared, cond_act):
        bias_full = jnp.swapaxes(shared, 0, 1).reshape(-1, width)
        modes = total.reshape(samples, layers, 6, width) + jnp.stack(
            [bias_full[14 * layer : 14 * layer + 6] for layer in range(layers)]
        )
        own_start = place.row * row_samples + place.col * samples
        cond_own = lax.dynamic_slice_in_dim(cond_act, own_start, samples, 0)
        final_mod = (
            jnp.einsum("sd,ed->se", cond_own, final_low[: 2 * width], preferred_element_type=F32)
            + final_bias[: 2 * width]
        ).reshape(samples, 2, width)
        mods_a = [modes[:, layer, 0:3] for layer in range(layers)]
        mods_b = [modes[:, layer, 3:6] for layer in range(layers)]
        return mods_a, mods_b, final_mod

    own_tokens = place.col * tokens
    latents = lax.dynamic_slice_in_dim(latents, own_tokens, tokens, 0)
    noise = lax.dynamic_slice_in_dim(noise, own_tokens, tokens, 0)
    mask = lax.dynamic_slice_in_dim(loss_mask, own_tokens, tokens, 0).astype(F32)
    steps_own = lax.dynamic_slice_in_dim(timesteps, place.col * samples, samples, 0).astype(F32)
    alpha_bar = jnp.cos((steps_own / STEPS_T + 0.008) / 1.008 * (math.pi / 2)) ** 2
    keep_part = jnp.repeat(jnp.sqrt(alpha_bar), LEN)[:, None]
    noise_part = jnp.repeat(jnp.sqrt(1.0 - alpha_bar), LEN)[:, None]
    noisy = (keep_part * latents + noise_part * noise).astype(BF16)
    position = jnp.asarray(position_table(width))

    def attn_step(layer):
        def work(buffers, x, mods, shared):
            return attention_forward(place, 14 * layer, buffers, x, mods, shared)

        return work

    def mlp_step(layer):
        def work(buffers, x, mods, shared):
            return mlp_forward(place, 14 * layer, buffers, x, mods, shared)

        return work

    def attn_back(buffers, *operands):
        return attention_backward(place, buffers, *operands)

    def mlp_back(buffers, *operands):
        return mlp_backward(place, buffers, *operands)

    head_low = final_low[2 * width :]

    def last_step(x, final_mod):
        return final_step(
            x, final_mod, head_low, final_bias[2 * width :][None], noise, mask[:, None]
        )

    def mode_parts(back_a, back_b, grad_final_mod):
        parts = []
        for layer in range(layers):
            parts += [back_a[layer][1], back_b[layer][1]]
        parts = [v.reshape(-1, width) for v in parts + [grad_final_mod]]
        spare = mode_height - sum(v.shape[0] for v in parts)
        return jnp.concatenate(parts + [jnp.zeros((spare, width), F32)], axis=0).astype(BF16)

    start = 16 * layers + 2 * PATCH
    height = -(-(start + 16) // 32) * 32

    def collected(back_a, back_b, last):
        small = []
        for layer in range(layers):
            _, dmod_a, dbias_a, dtail_a = back_a[layer]
            _, dmod_b, dbias_b, dtail_b = back_b[layer]
            small += [dmod_a, dmod_b, dbias_a, dbias_b, dtail_a, dtail_b]
        _, loss_parts, grad_head, grad_head_bias, grad_final_mod = last
        small += [grad_head, grad_head_bias, loss_parts, mask[:, None], grad_final_mod]
        small += [back_a[0][0], noisy]
        return collect(layers, small, height, width)

    buffers = [None] * (2 * layers)
    fore_a, fore_b = [None] * layers, [None] * layers
    entry = [None] * layers
    back_a, back_b = [None] * layers, [None] * layers
    summed = [None] * (2 * layers)
    if place.direct and layers == 2:
        stages = Stages()
        halves = packed.reshape(3 * layers, 2, place.half, packed.shape[2])
        kept = lax.dynamic_index_in_dim(halves, place.core, 1, False)
        sent = lax.dynamic_index_in_dim(halves, 1 - place.core, 1, False)
        (got,), _ = stages.run([(swap_core, sent)])
        a0, b0, a1, b1 = [
            Spread(kept[k : k + n], got[k : k + n]) for k, n in ((0, 1), (1, 2), (3, 1), (4, 2))
        ]
        wide = jnp.broadcast_to
        own_block = jnp.concatenate(
            [
                time_mlp.astype(BF16).T,
                class_rows[:, :128],
                jnp.pad(class_rows[:, 128:], ((0, 0), (0, 256 - narrow))),
                freq_row[:, :128],
                freq_row[:, 128:],
                wide((labels // 32).astype(BF16)[:, None], (row_samples, 128)),
                wide((labels % 32).astype(BF16)[:, None], (row_samples, 128)),
            ],
            axis=0,
        )
        (t1, t3, t2), (near, shared) = stages.run(
            a0.turns((1, 3, 2)),
            [(near_rows, own_block), (functools.partial(gather_cols, place), mine)],
        )
        a0.turned(t1, t2, t3)

        got, (near, residual) = stages.run(
            a0.first() + b0.turns((1, 3)),
            [
                (near_x, near),
                (functools.partial(embed_tokens, base), noisy, shared, position),
            ],
        )
        t1, t3 = got[1:]

        def condition_work(near, shared, found):
            near = near_core(near)
            got = condition_step(base, found, near, shared, every_sample, width)
            return near, got, partial_modes(got[1])

        got, ((near, conditions, (cond_rows, partial)),) = stages.run(
            a0.second(got[0]) + b0.turns((2,)) + a0.core(),
            [(condition_work, near, shared, found)],
        )
        condition, cond_act, first_time, first_act, freq_low, all_labels = conditions
        b0.turned(t1, got[1], t3)
        core = got[2]
        got, (total,) = stages.run(
            b0.first() + a1.turns((1, 3)) + a0.late_core(got[0]),
            [(functools.partial(scatter_y, place), partial)],
        )
        buffers[0] = a0.buffers(core, got[3])
        t1, t3 = got[1:3]

        def scatter_work(total):
            return scatter_x(place, scatter_z(place, total), samples)

        got, (total,) = stages.run(
            b0.second(got[0]) + a1.turns((2,)) + b0.core(), [(scatter_work, total)]
        )
        a1.turned(t1, got[1], t3)
        core = got[2]

        def modes_work(total, shared, cond_act):
            return own_modes(scatter_core(place, total), shared, cond_act)

        got, ((mods_a, mods_b, final_mod),) = stages.run(
            a1.first() + b1.turns((1, 3)) + b0.late_core(got[0]),
            [(modes_work, total, shared, cond_act)],
        )
        buffers[1] = b0.buffers(core, got[3])
        t1, t3 = got[1:3]
        got, (fore_a[0],) = stages.run(
            a1.second(got[0]) + b1.turns((2,)) + a1.core(),
            [(attn_step(0), buffers[0], residual, mods_a[0], shared)],
        )
        b1.turned(t1, got[1], t3)
        core = got[2]
        got, (fore_b[0],) = stages.run(
            b1.first() + a1.late_core(got[0]),
            [(mlp_step(0), buffers[1], fore_a[0][0], mods_b[0], shared)],
        )
        buffers[2] = a1.buffers(core, got[1])
        got, (fore_a[1],) = stages.run(
            b1.second(got[0]) + b1.core(),
            [(attn_step(1), buffers[2], fore_b[0][0], mods_a[1], shared)],
        )
        core = got[1]
        got, _ = stages.run(b1.late_core(got[0]))
        buffers[3] = b1.buffers(core, got[0])
        got, (fore_b[1],) = stages.run(
            [(swap_x, mode_low)], [(mlp_step(1), buffers[3], fore_a[1][0], mods_b[1], shared)]
        )
        mode_half = pair(place.x, mode_low, got[0])
        entry = [residual, fore_b[0][0]]
        last = last_step(fore_b[1][0], final_mod)

        def back_b_work(layer, grad):
            out, h, u, m = fore_b[layer]
            return (mlp_back, buffers[2 * layer + 1], grad, fore_a[layer][0], mods_b[layer], m, h, u)

        def back_a_work(layer, grad):
            out, h, qkv, p, o, a = fore_a[layer]
            return (
                attn_back, buffers[2 * layer], grad, entry[layer], mods_a[layer], a, h, qkv, p, o,
            )

        got, ((back_b[1], grads),) = stages.run(
            [(swap_core, mode_half)], [back_b_work(1, last[0])]
        )
        mode_full = jnp.swapaxes(pair(place.core, mode_half, got[0]), 0, 1)
        mode_full = mode_full.reshape((4,) + mode_low.shape)
        gb1 = Gathered(grads)
        got, ((back_a[1], grads),) = stages.run(gb1.core, [back_a_work(1, back_b[1][0])])
        ga1 = Gathered(grads)
        got, ((back_b[0], grads),) = stages.run(
            gb1.first(got[0]) + ga1.core, [back_b_work(0, back_a[1][0])]
        )
        core_a1 = got[1]
        gb0 = Gathered(grads)
        got, ((back_a[0], grads),) = stages.run(
            gb1.second(got[0]) + ga1.first(core_a1) + gb0.core, [back_a_work(0, back_b[0][0])]
        )
        gb1.third(got[0])
        ga0 = Gathered(grads)

        def sum_work(back_a, back_b, last):
            return sum_along_z(place, collected(back_a, back_b, last))

        moded = mode_parts(back_a, back_b, last[4])
        t2_a1 = ga1.second(got[1])
        got, (near_modes, small) = stages.run(
            gb0.first(got[2]) + gb1.turns((1, 3)) + ga0.core,
            [(near_z, moded), (sum_work, back_a, back_b, last)],
        )
        turned_b1 = got[1:3]
        t2_b0 = gb0.second(got[0])
        got, (near_modes, small) = stages.run(
            ga0.first(got[3]) + t2_a1 + gb1.turns((2,)),
            [(near_y, near_modes), (sum_with(swap_core), small)],
        )
        total_b1 = gb1.total(turned_b1 + got[2:])
        ga1.third(got[1])
        t2_a0 = ga0.second(got[0])
        got, (near_modes, small) = stages.run(
            t2_b0 + ga1.turns((1, 3)), [(near_x, near_modes), (sum_with(swap_x), small)]
        )
        turned_a1 = got[1:]
        gb0.third(got[0])
        got, (near_modes, small) = stages.run(
            t2_a0 + ga1.turns((2,)) + gb0.turns((1, 3)),
            [(near_core, near_modes), (sum_with(swap_y), small)],
        )
        total_a1 = ga1.total(turned_a1 + got[1:2])
        turned_b0 = got[2:]
        ga0.third(got[0])

        def modes_back_work(near):
            return modes_backward(near, at, cond_rows, pick, mode_full, cond_act, final_low)

        got, (moded, small) = stages.run(
            gb0.turns((2,)),
            [(modes_back_work, near_modes), (functools.partial(sum_spread, place), small)],
        )
        total_b0 = gb0.total(turned_b0 + got)
        time_inputs = lax.dynamic_slice_in_dim(
            jnp.concatenate([freq_low, first_act], axis=1), place.row * time_rows, time_rows, 1
        )
        turned_a0, (part,) = stages.run(ga0.turns((1, 3)), [(near_z, moded[1])])
        got, (part,) = stages.run(ga0.turns((2,)), [(near_y, part)])
        total_a0 = ga0.total(turned_a0 + got)
        ends = condition_back(
            layers, hidden_blocks, found, spot, small, part, moded[4], moded[5], condition,
            first_time, time_inputs, all_labels, pick, near,
        )
        late = swap_core(
            jnp.concatenate([total_b1[1], total_b0[1], total_a1[1], total_a0[1]])
        )
        summed = [total_a0, total_b0, total_a1, total_b1]
        sums = [
            (moded[0], total_a0, late[5:6], total_b0, late[2:4]),
            (moded[0], total_a1, late[4:5], total_b1, late[0:2]),
        ]
        time_grad, embed_grad, bias_grad, own_part, shared_part = ends
        own_squares = own_part[0, 0] + moded[2][0, 0]
        shared_squares = shared_part[0, 0]
        final_grad = moded[3]
    else:
        shared = gather_cols(place, mine)
        time_full = lax.all_gather(time_mlp.astype(BF16), "row", axis=0, tiled=True)
        time_full = lax.all_gather(time_full, "col", axis=1, tiled=True)
        class_full = lax.all_gather(class_rows, "col", axis=1, tiled=True)
        class_full = lax.all_gather(class_full, "row", axis=0, tiled=True).astype(F32)
        freq_low = lax.all_gather(freq_row, "row", axis=0, tiled=True)
        all_labels = lax.all_gather(labels, "row", axis=0, tiled=True)
        bias_full = jnp.swapaxes(shared, 0, 1).reshape(-1, width)
        first_time = (
            jnp.dot(freq_low, time_full[:FREQ], preferred_element_type=F32) + bias_full[base]
        )
        first_act = jax.nn.silu(first_time).astype(BF16)
        condition = (
            jnp.dot(first_act, time_full[FREQ:], preferred_element_type=F32)
            + bias_full[base + 1]
            + class_full
        )
        cond_act = jax.nn.silu(condition).astype(BF16)
        cond_rows, partial = partial_modes(cond_act)
        mods_a, mods_b, final_mod = own_modes(
            scatter_plain(place, partial, samples), shared, cond_act
        )
        grad = embed_tokens(base, noisy, shared, position)
        for layer in range(layers):
            buffers[2 * layer] = [plain_gather(packed[3 * layer : 3 * layer + 1])]
            buffers[2 * layer + 1] = [plain_gather(packed[3 * layer + 1 : 3 * layer + 3])]
            entry[layer] = grad
            fore_a[layer] = attn_step(layer)(buffers[2 * layer], grad, mods_a[layer], shared)
            grad = fore_a[layer][0]
            fore_b[layer] = mlp_step(layer)(buffers[2 * layer + 1], grad, mods_b[layer], shared)
            grad = fore_b[layer][0]
        last = last_step(grad, final_mod)
        grad = last[0]
        for layer in reversed(range(layers)):
            out, h, u, m = fore_b[layer]
            back_b[layer], grads = mlp_back(
                buffers[2 * layer + 1], grad, fore_a[layer][0], mods_b[layer], m, h, u
            )
            summed[2 * layer + 1] = plain_scatter(grads[0])
            grad = back_b[layer][0]
            out, h, qkv, p, o, a = fore_a[layer]
            back_a[layer], grads = attn_back(
                buffers[2 * layer], grad, entry[layer], mods_a[layer], a, h, qkv, p, o
            )
            summed[2 * layer] = plain_scatter(grads[0])
            grad = back_a[layer][0]
        mode_full = lax.all_gather(mode_low, "col")
        near = gather_near(place, mode_parts(back_a, back_b, last[4]))
        moded = modes_backward_plain(
            near, cond_rows, mode_full, cond_act, final_low, place.col
        )
        mode_blocks, part, square, final_grad, cond_final, final_squares = moded
        own_squares = square[0, 0]
        small = lax.psum(collected(back_a, back_b, last), ("row", "col"))
        grad_cond = lax.all_gather(part, "row", axis=1, tiled=True) + cond_final
        grad_condition = grad_cond * silu_slope(condition)
        one_hot = (all_labels[:, None] == jnp.arange(CLASSES, dtype=jnp.int32)[None, :]).astype(F32)
        grad_classes = jnp.einsum(
            "sd,sc->dc", my_cols(grad_condition, 1), one_hot, precision=HIGHEST
        )
        condition_low = grad_condition.astype(BF16)
        grad_first = jnp.einsum(
            "se,de->sd", condition_low, time_full[FREQ:], preferred_element_type=F32
        ) * silu_slope(first_time)
        time_inputs = lax.dynamic_slice_in_dim(
            jnp.concatenate([freq_low, first_act], axis=1), place.row * time_rows, time_rows, 1
        )
        time_outputs = jnp.where(
            (place.row + 1) * time_rows <= FREQ, grad_first.astype(BF16), condition_low
        )
        time_grad = jnp.einsum(
            "sd,se->ed", time_inputs, my_cols(time_outputs, 1), preferred_element_type=F32
        )
        own_rows, shared_squares = [], jnp.zeros((), F32)
        for layer in range(layers):
            rows_at = small[16 * layer : 16 * layer + 16]
            own = my_cols(rows_at, 1)
            mlp_rows = lax.dynamic_index_in_dim(rows_at[6:10], place.col, 0, False)
            attn_rows = lax.dynamic_index_in_dim(rows_at[10:14], place.col, 0, False)
            attn_rows = attn_rows[: 3 * narrow].reshape(3, narrow)
            own_rows += [own[:6], attn_rows[0:1], attn_rows[2:3]]
            own_rows += [mlp_rows.reshape(hidden_blocks, narrow), own[14:16]]
            counted = rows_at[10:14, : 3 * narrow].reshape(4, 3, narrow)[:, 0::2]
            shared_squares = (
                shared_squares + squared(rows_at[:10]) + squared(counted) + squared(rows_at[14:])
            )
        time_bias = jnp.stack([jnp.sum(grad_first, axis=0), jnp.sum(grad_condition, axis=0)])
        own_rows += [my_cols(time_bias, 1), my_cols(small[start : start + 1], 1)]
        bias_grad = jnp.concatenate(own_rows, axis=0)
        shared_squares = (
            shared_squares
            + squared(time_bias)
            + squared(small[start - 2 * PATCH : start + 3])
            + squared(small[start + 3, :PATCH])
            + final_squares[0, 0]
        )
        own_squares = own_squares + squared(time_grad) + squared(grad_classes) / rows
        sums = [(mode_blocks, summed[2 * k], summed[2 * k + 1]) for k in range(layers)]
        patch_grad = my_cols(small[start - PATCH : start], 1)
        embed_grad = jnp.concatenate([grad_classes, patch_grad.T], axis=1)

    head_grad = small[start - 2 * PATCH : start - PATCH]
    final_bias_grad = jnp.concatenate(
        [small[start + 1], small[start + 2], small[start + 3, :PATCH]]
    )
    loss_total = jnp.sum(small[start + 4, :PATCH])
    count_total = small[start + 5, 0]
    for value in summed:
        own_squares = own_squares + squared(value)
    grad_norm = jnp.sqrt(sum_scalar(place, own_squares) + shared_squares)
    clip_factor = jnp.minimum(1.0, CLIP_NORM / (grad_norm + 1e-06))
    clip = clip_factor[None]

    results = [loss_total, count_total, grad_norm]
    new_blocks = adam_blocks(clip, spot, sums, in_view, [weights_out, momentum_out, variance_out])
    results += [jnp.transpose(v, (0, 2, 1, 3)) for v in new_blocks[:3]] + list(new_blocks[3:])
    rest = adam_rest(
        clip,
        [
            (time_mlp.T, time_grad, momentum_time.T, variance_time.T, RATE),
            (embed_table.T, embed_grad, momentum_embed.T, variance_embed.T, RATE),
            (bias_table, bias_grad, momentum_bias, variance_bias, RATE_BIAS),
        ],
    )
    results += [v.T for v in rest[:6]]
    results += [v.T for v in adam_final(clip, final_grad, head_grad, *final_view)]
    results += list(rest[6:9])
    results += adam(
        final_bias, final_bias_grad, momentum_final_bias, variance_final_bias, clip_factor,
        RATE_BIAS,
    )
    return tuple(results)


def solution(mesh):
    tokens, latents = P("row", None), P("row")
    weights = (
        P(None, "row", None, "col"),
        P(None, None, "col", "row"),
        P("row", "col"),
        P(None, "col"),
        P(),
        P(None, "col"),
        P(),
    )
    updated = []
    for spec in weights:
        updated += [spec] * 3
    return jax.shard_map(
        on_device,
        mesh=mesh,
        in_specs=(tokens, tokens, latents, latents, latents) + weights * 3,
        out_specs=(P(), P(), P()) + tuple(updated),
        check_vma=False,
    )
```

time: 686 us -> 612 us (0.89)
  waiting for transfers between devices: 180 us -> 145 us
  local copies, waits for them, and re-layouts: 77.9 us -> 50.2 us
  Pallas kernels: 196 us -> 208 us
  between operations: 17 us -> 9.24 us
    ppermute x23 -> x7, waiting for transfers between devices: 60.2 us -> 20.2 us  [swap_x(): return lax.ppermute(v, 'col', [(c, c ^ 2) for c in range(4)])]
    ppermute x0 -> x16, waiting for transfers between devices: none -> 25 us  [the longest x8 15.2 us: swap_second(): return lax.ppermute(v, ('row', 'col'), pairs)]
    ppermute x23 -> x7, starting transfers between devices: 25.8 us -> 6.99 us  [swap_x(): return lax.ppermute(v, 'col', [(c, c ^ 2) for c in range(4)])]
    ppermute x42, waiting for transfers between devices: 80.4 us -> 62.9 us  [turn_z(): lax.ppermute(v, 'row', [(r, (r // 2 + k) % 4 * 2 + r % 2) for r in range(...]
    ppermute x0 -> x16, starting transfers between devices: none -> 17.4 us  [the longest x8 9.97 us: swap_first(): return lax.ppermute(v, ('row', 'col'), pairs)]
    ppermute x22 -> x6, starting transfers between devices: 23.5 us -> 9.88 us  [swap_y(): return lax.ppermute(v, 'row', [(r, r ^ 1) for r in range(8)])]
    unnamed x342 -> x216, local copies, waits for them, and re-layouts: 35.9 us -> 22.4 us
    pallas_call x12 -> x13, Pallas kernels: 191 us -> 201 us  [the longest x2 49.1 us: attention_backward(): pl.pallas_call(functools.partial(attention_backward_body, route), grid=(c...]
  transfers between devices with their start and end apart: 128 -> 94, of which waited for: 46 -> 39; matrix products, arithmetic and copies ran while one was open for 20% -> 17% of each run, Pallas kernels for 20% -> 33%
where the time goes in v2:
time: 612 us; the launch traced here: 604 us
  Pallas kernels  208 us (34%)
  waiting for transfers between devices  145 us (24%)
  starting transfers between devices  116 us (19%)
  other arithmetic  72.1 us (12%)
  local copies, waits for them, and re-layouts  50.2 us (8%)
  between operations  9.24 us (2%)
    ppermute x42, starting transfers between devices, turn_z(): lax.ppermute(v, 'row', [(r, (r // 2 + k) % 4 * 2 + r % 2) for r in range(...  67.3 us
    ppermute x42, waiting for transfers between devices, turn_z(): lax.ppermute(v, 'row', [(r, (r // 2 + k) % 4 * 2 + r % 2) for r in range(...  62.9 us
    pallas_call x2, Pallas kernels, attention_backward(): pl.pallas_call(functools.partial(attention_backward_body, route), grid=(c...  49.1 us
    pallas_call x2, Pallas kernels, mlp_backward(): pl.pallas_call(functools.partial(mlp_backward_body, route), grid=(count,)...  46.8 us
    pallas_call x2, Pallas kernels, attention_forward(): pl.pallas_call(functools.partial(attention_forward_body, route, base), gr...  32.8 us
    pallas_call x2, Pallas kernels, mlp_forward(): pl.pallas_call(functools.partial(mlp_forward_body, route, base), grid=(co...  31.9 us
    ppermute x6, waiting for transfers between devices, swap_y(): return lax.ppermute(v, 'row', [(r, r ^ 1) for r in range(8)])  30.5 us
    unnamed x216, local copies, waits for them, and re-layouts  22.4 us
  transfers between devices with their start and end apart: 94, of which 39 were waited for; matrix products, arithmetic and copies ran while one was open for 17% of the time, Pallas kernels for 33%

profile of v2, /device:TPU:0, one launch (start us, length us, event | category | flops | bytes accessed | tf_op | source)
XLA Modules:
  0.0 604.2 jit_solution(15517939704293437287)
XLA Ops:
  41.6 3.8 collective-permute-done.12
  46.4 5.3 collective-permute-done.11
  60.0 11.3 %collective-permute-done.14 = bf16[2,2,48,768]{3,2,1,0:T(8,128)(2,1)} collective-permute-done((bf16[2,2,48,768]{3,2,1,0:T(8,128)(2,1)}, bf16[2,2,48,768]{3,2,1,0:T(8,128)(2,1)}, u32[]{:S(2)}, u32[]{:S(2)}) %collective-permute-start.14) | collective-permute-done | bytes 294944 | tf_op jit(solution)/shard_map/ppermute | solution.py:119
  86.3 5.3 collective-permute-done.20
  96.9 8.0 %collective-permute-start.29 = (bf16[8,2,2,48,768]{4,3,2,1,0:T(8,128)(2,1)}, bf16[8,2,2,48,768]{4,3,2,1,0:T(8,128)(2,1)}, u32[]{:S(2)}, u32[]{:S(2)}) collective-permute-start(bf16[8,2,2,48,768]{4,3,2,1,0:T(8,128)(2,1)} %constant_dynamic-update-slice_fusion.19.refs_0_), channel_id=1, source_target_pairs={{0,1},{1,0},{2,3},{3,2},{4,5},{5,4},{6,7},{7,6},{8,9},{9,8},{10,11... | collective-permute-start | bytes 7077896 | tf_op jit(solution)/shard_map/ppermute | solution.py:101
  104.9 4.1 bitcast_convert_fusion.final_ref
  117.4 3.6 collective-permute-done.26
  129.7 5.6 collective-permute-done.23
  145.4 4.0 collective-permute-start.33
  153.6 3.9 collective-permute-done.30
  164.7 16.4 %attention_forward.2 = (f32[512,768]{1,0:T(8,128)}, bf16[512,768]{1,0:T(8,128)(2,1)}, bf16[4,512,576]{2,1,0:T(8,128)(2,1)}, bf16[4,3,2,256,256]{4,3,2,1,0:T(8,12...) custom-call(s32[192]{0:T(256)} %pad_add_fusion.1.table, f32[512,768]{1,0:T(8,128)} %copy-done.6, ...), custom_call_target="tpu_custom_call" | custom-call | flops 2818572288 | bytes 16515072 | tf_op jit(solution)/shard_map/attention_forward/pallas_call | solution.py:688
  189.2 15.8 %mlp_forward.2 = (f32[512,768]{1,0:T(8,128)}, bf16[512,768]{1,0:T(8,128)(2,1)}, f32[4,512,768]{2,1,0:T(8,128)}, f32[512,768]{1,0:T(8,128)}) custom-call(s32[192]{0:T(256)} %pad_add_fusion.1.table, f32[512,768]{1,0:T(8,128)} %get-tuple-element.415.x_ref, f32[2,3,768]{2,1,0:T(4,128)} %get-tuple-element.416.mod_ref, f32[4,47,192]{2,1,0:T(8,128)} %bitcast.537, ...), custom_call_target="tpu_custom_call" | custom-call | flops 4831838208 | bytes 21233664 | tf_op jit(solution)/shard_map/mlp_forward/pallas_call | solution.py:722
  208.3 16.4 %attention_forward.3 = (f32[512,768]{1,0:T(8,128)}, bf16[512,768]{1,0:T(8,128)(2,1)}, bf16[4,512,576]{2,1,0:T(8,128)(2,1)}, bf16[4,3,2,256,256]{4,3,2,1,0:T(8,12...) custom-call(s32[192]{0:T(256)} %pad_add_fusion.1.table, f32[512,768]{1,0:T(8,128)} %get-tuple-element.397.x_ref, ...), custom_call_target="tpu_custom_call" | custom-call | flops 2818572288 | bytes 16515072 | tf_op jit(solution)/shard_map/attention_forward/pallas_call | solution.py:688
  224.7 11.9 %collective-permute-done.40.refs_1_ = bf16[8,2,2,48,768]{4,3,2,1,0:T(8,128)(2,1)} collective-permute-done((bf16[8,2,2,48,768]{4,3,2,1,0:T(8,128)(2,1)}, bf16[8,2,2,48,768]{4,3,2,1,0:T(8,128)(2,1)}, u32[]{:S(2)}, u32[]{:S(2)}) %collective-permute-start.40) | collective-permute-done | bytes 2359328 | tf_op jit(solution)/shard_map/ppermute | solution.py:115
  242.5 16.0 %mlp_forward.3 = (f32[512,768]{1,0:T(8,128)}, bf16[512,768]{1,0:T(8,128)(2,1)}, f32[4,512,768]{2,1,0:T(8,128)}, f32[512,768]{1,0:T(8,128)}) custom-call(s32[192]{0:T(256)} %pad_add_fusion.1.table, f32[512,768]{1,0:T(8,128)} %get-tuple-element.379.x_ref, f32[2,3,768]{2,1,0:T(4,128)} %get-tuple-element.380.mod_ref, f32[4,47,192]{2,1,0:T(8,128)} %bitcast.539, ...), custom_call_target="tpu_custom_call" | custom-call | flops 4831838208 | bytes 21233664 | tf_op jit(solution)/shard_map/mlp_forward/pallas_call | solution.py:722
  263.2 23.4 %mlp_backward.2 = (f32[512,768]{1,0:T(8,128)}, f32[2,3,768]{2,1,0:T(4,128)}, f32[4,1,768]{2,1,0:T(1,128)}, f32[1,768]{1,0:T(1,128)}, bf16[2,8,2,2,48,768]{5,4,3,...) custom-call(s32[192]{0:T(256)} %pad_add_fusion.1.table, f32[512,768]{1,0:T(8,128)} %copy-done.34, ...), custom_call_target="tpu_custom_call" | custom-call | flops 9663676416 | bytes 34603008 | tf_op jit(solution)/shard_map/mlp_backward/pallas_call | solution.py:757
  287.3 24.6 %attention_backward.2 = (f32[512,768]{1,0:T(8,128)}, f32[2,3,768]{2,1,0:T(4,128)}, f32[4,1,576]{2,1,0:T(1,128)}, f32[1,768]{1,0:T(1,128)}, bf16[2,8,2,1,48,768]{...) custom-call(s32[192]{0:T(256)} %pad_add_fusion.1.table, f32[512,768]{1,0:T(8,128)} %get-tuple-element.396.dx_ref, ...), custom_call_target="tpu_custom_call" | custom-call | flops 5838471168 | bytes 25165824 | tf_op jit(solution)/shard_map/attention_backward/pallas_call | solution.py:801
  317.3 23.5 %mlp_backward.3 = (f32[512,768]{1,0:T(8,128)}, f32[2,3,768]{2,1,0:T(4,128)}, f32[4,1,768]{2,1,0:T(1,128)}, f32[1,768]{1,0:T(1,128)}, bf16[2,8,2,2,48,768]{5,4,3,...) custom-call(s32[192]{0:T(256)} %pad_add_fusion.1.table, f32[512,768]{1,0:T(8,128)} %get-tuple-element.414.dx_ref, ...), custom_call_target="tpu_custom_call" | custom-call | flops 9663676416 | bytes 34603008 | tf_op jit(solution)/shard_map/mlp_backward/pallas_call | solution.py:757
  353.3 24.5 %attention_backward.3 = (f32[512,768]{1,0:T(8,128)}, f32[2,3,768]{2,1,0:T(4,128)}, f32[4,1,576]{2,1,0:T(1,128)}, f32[1,768]{1,0:T(1,128)}, bf16[2,8,2,1,48,768]{...) custom-call(s32[192]{0:T(256)} %pad_add_fusion.1.table, f32[512,768]{1,0:T(8,128)} %get-tuple-element.434.dx_ref, ...), custom_call_target="tpu_custom_call" | custom-call | flops 5838471168 | bytes 25165824 | tf_op jit(solution)/shard_map/attention_backward/pallas_call | solution.py:801
  382.3 4.5 fusion.1
  407.6 5.7 collective-permute-start.60
  416.0 5.4 collective-permute-done.60
  428.6 19.3 %collective-permute-done.62 = bf16[4,32,768]{2,1,0:T(8,128)(2,1)S(1)} collective-permute-done((bf16[4,32,768]{2,1,0:T(8,128)(2,1)}, bf16[4,32,768]{2,1,0:T(8,128)(2,1)S(1)}, u32[]{:S(2)}, u32[]{:S(2)}) %collective-permute-start.62) | collective-permute-done | bytes 196640 | tf_op jit(solution)/shard_map/ppermute | solution.py:105
  462.6 10.9 %collective-permute-done.68 = f32[24,768]{1,0:T(8,128)S(1)} collective-permute-done((f32[24,768]{1,0:T(8,128)S(1)}, f32[24,768]{1,0:T(8,128)S(1)}, u32[]{:S(2)}, u32[]{:S(2)}) %collective-permute-start.68) | collective-permute-done | bytes 73760 | tf_op jit(solution)/shard_map/ppermute | solution.py:97
  481.0 3.7 collective-permute-start.75
  493.5 4.3 collective-permute-done.76
  503.8 9.2 %modes_backward.1 = (f32[2,6,96,192]{3,2,1,0:T(8,128)}, f32[64,96]{1,0:T(8,128)}, f32[1,1]{1,0:T(1,128)}, f32[1536,768]{1,0:T(8,128)}, f32[64,768]{1,0:T(8,128)}, /*index=5*/f32[1,1]{1,0:T(1,128)}) custom-call(bf16[1024,768]{1,0:T(8,128)(2,1)} %bitcast.552, s32[64,2]{1,0:T(8,128)} %copy.250.at_ref, bf16[64,96]{1,0:T(8,128)(2,1)} %copy-done.76, ...), custom_call_target="tpu_custom_call" | custom-call | tf_op jit(solution)/shard_map/modes_backward/pallas_call | solution.py:1137
  515.3 5.0 collective-permute-done.80
  539.8 5.0 condition_back.1
  571.5 13.4 %adam_final.1 = (f32[1552,768]{1,0:T(8,128)}, f32[1552,768]{1,0:T(8,128)}, f32[1552,768]{1,0:T(8,128)}) custom-call(f32[1]{0:T(128)} %bitcast.187.clip_ref, f32[1536,768]{1,0:T(8,128)} %get-tuple-element.501.grad_ref, f32[16,768]{1,0:T(8,128)} %slice.686.head_ref, f32[1552,768]{1,0:T(8,128)} %bitcast.550, f32[1552,768]{1,0:T(8,128)} %bitcast.553, ...), custom_call_target="tpu_custom_call" | custom-call | tf_op jit(solution)/shard_map/adam_final/pallas_call | solution.py:1316
  584.9 4.1 adam_rest.1
  591.3 11.3 %adam_blocks.1 = (f32[2,13,96,192]{3,2,1,0:T(8,128)}, f32[2,13,96,192]{3,2,1,0:T(8,128)}, f32[2,13,96,192]{3,2,1,0:T(8,128)}, f32[2,5,192,96]{3,2,1,0:T(8,128)},...) custom-call(f32[1]{0:T(128)} %bitcast.187.clip_ref, s32[2]{0:T(128)} %copy-done.33, ...), custom_call_target="tpu_custom_call" | custom-call | tf_op jit(solution)/shard_map/adam_blocks/pallas_call | solution.py:1277
  (552 shorter events, 265.8 us)
Async XLA Ops:
  53.7 18.9 %collective-permute-start.16 = (bf16[16,240,128]{2,1,0:T(8,128)(2,1)}, bf16[16,240,128]{2,1,0:T(8,128)(2,1)}, u32[]{:S(2)}, u32[]{:S(2)}) collective-permute-start(bf16[16,240,128]{2,1,0:T(8,128)(2,1)} %pad_maximum_fusion.4), channel_id=1, source_target_pairs={{0,1},{1,0},{2,3},{3,2},{4,5},{5,4},{6,7},{7,6},{8,9},{9,8},{10,11... | collective-permute-start | bytes 2949128 | tf_op jit(solution)/shard_map/ppermute | solution.py:101
  53.8 22.5 %collective-permute-start.15 = (bf16[8,2,1,48,768]{4,3,2,1,0:T(8,128)(2,1)}, bf16[8,2,1,48,768]{4,3,2,1,0:T(8,128)(2,1)}, u32[]{:S(2)}, u32[]{:S(2)}) collective-permute-start(bf16[8,2,1,48,768]{4,3,2,1,0:T(8,128)(2,1)} %constant_dynamic-update-slice_fusion.12.refs_0_), channel_id=1, source_target_pairs={{0,4},{1,3},{2,6},{3,1},{4,0},{5,7},{6,2},{7,5},{8,12},{9,11},{10,... | collective-permute-start | bytes 3538952 | tf_op jit(solution)/shard_map/ppermute | solution.py:115
  54.3 22.0 %collective-permute-start.17 = (bf16[8,2,1,48,768]{4,3,2,1,0:T(8,128)(2,1)}, bf16[8,2,1,48,768]{4,3,2,1,0:T(8,128)(2,1)}, u32[]{:S(2)}, u32[]{:S(2)}) collective-permute-start(bf16[8,2,1,48,768]{4,3,2,1,0:T(8,128)(2,1)} %constant_dynamic-update-slice_fusion.12.refs_0_), channel_id=1, source_target_pairs={{0,1},{1,0},{2,3},{3,2},{4,5},{5,4},{6,7},{7,6},{8,9},{9,8},{10,11... | collective-permute-start | bytes 3538952 | tf_op jit(solution)/shard_map/ppermute | solution.py:101
  95.4 41.8 %collective-permute-start.24 = (bf16[8,2,2,48,768]{4,3,2,1,0:T(8,128)(2,1)}, bf16[8,2,2,48,768]{4,3,2,1,0:T(8,128)(2,1)}, u32[]{:S(2)}, u32[]{:S(2)}) collective-permute-start(bf16[8,2,2,48,768]{4,3,2,1,0:T(8,128)(2,1)} %constant_dynamic-update-slice_fusion.19.refs_0_), channel_id=1, source_target_pairs={{0,4},{1,3},{2,6},{3,1},{4,0},{5,7},{6,2},{7,5},{8,12},{9,11},{10,... | collective-permute-start | bytes 7077896 | tf_op jit(solution)/shard_map/ppermute | solution.py:115
  96.9 40.3 %collective-permute-start.29 = (bf16[8,2,2,48,768]{4,3,2,1,0:T(8,128)(2,1)}, bf16[8,2,2,48,768]{4,3,2,1,0:T(8,128)(2,1)}, u32[]{:S(2)}, u32[]{:S(2)}) collective-permute-start(bf16[8,2,2,48,768]{4,3,2,1,0:T(8,128)(2,1)} %constant_dynamic-update-slice_fusion.19.refs_0_), channel_id=1, source_target_pairs={{0,1},{1,0},{2,3},{3,2},{4,5},{5,4},{6,7},{7,6},{8,9},{9,8},{10,11... | collective-permute-start | bytes 7077896 | tf_op jit(solution)/shard_map/ppermute | solution.py:101
  137.2 23.4 %collective-permute-start.34 = (bf16[8,2,2,48,768]{4,3,2,1,0:T(8,128)(2,1)}, bf16[8,2,2,48,768]{4,3,2,1,0:T(8,128)(2,1)}, u32[]{:S(2)}, u32[]{:S(2)}) collective-permute-start(bf16[8,2,2,48,768]{4,3,2,1,0:T(8,128)(2,1)} %collective-permute-done.24.refs_1_), channel_id=1, source_target_pairs={{0,1},{1,0},{2,3},{3,2},{4,5},{5,4},{6,7},{7,6},{8,9},{9,8},{10,11... | collective-permute-start | bytes 7077896 | tf_op jit(solution)/shard_map/ppermute | solution.py:101
  160.6 21.8 %collective-permute-start.36 = (bf16[8,2,1,48,768]{4,3,1,2,0:T(8,128)(2,1)}, bf16[8,2,1,48,768]{4,3,1,2,0:T(8,128)(2,1)}, u32[]{:S(2)}, u32[]{:S(2)}) collective-permute-start(bf16[8,2,1,48,768]{4,3,1,2,0:T(8,128)(2,1)} %constant_dynamic-update-slice_fusion.24), channel_id=1, source_target_pairs={{0,4},{1,3},{2,6},{3,1},{4,0},{5,7},{6,2},{7,5},{8,12},{9,11},{10,... | collective-permute-start | bytes 3538952 | tf_op jit(solution)/shard_map/ppermute | solution.py:115
  161.5 20.9 %collective-permute-start.37 = (bf16[8,2,1,48,768]{4,3,1,2,0:T(8,128)(2,1)}, bf16[8,2,1,48,768]{4,3,1,2,0:T(8,128)(2,1)}, u32[]{:S(2)}, u32[]{:S(2)}) collective-permute-start(bf16[8,2,1,48,768]{4,3,1,2,0:T(8,128)(2,1)} %constant_dynamic-update-slice_fusion.24), channel_id=1, source_target_pairs={{0,1},{1,0},{2,3},{3,2},{4,5},{5,4},{6,7},{7,6},{8,9},{9,8},{10,11... | collective-permute-start | bytes 3538952 | tf_op jit(solution)/shard_map/ppermute | solution.py:101
  161.8 19.3 %collective-permute-start.35 = (bf16[2,2,48,768]{3,2,1,0:T(8,128)(2,1)}, bf16[2,2,48,768]{3,2,1,0:T(8,128)(2,1)S(1)}, u32[]{:S(2)}, u32[]{:S(2)}) collective-permute-start(bf16[2,2,48,768]{3,2,1,0:T(8,128)(2,1)} %get-tuple-element.320), channel_id=1, source_target_pairs={{0,16},{4,20},{8,24},{12,28},{16,0},{20,4},{24,8},{28,12},{1,17},{... | collective-permute-start | bytes 884744 | tf_op jit(solution)/shard_map/ppermute | solution.py:119
  182.4 22.7 %collective-permute-start.38 = (bf16[4,2,2,48,768]{4,3,2,1,0:T(8,128)(2,1)S(1)}, bf16[4,2,2,48,768]{4,3,2,1,0:T(8,128)(2,1)}, u32[]{:S(2)}, u32[]{:S(2)}) collective-permute-start(bf16[4,2,2,48,768]{4,3,2,1,0:T(8,128)(2,1)S(1)} %pad_maximum_fusion.2), channel_id=1, source_target_pairs={{0,2},{1,5},{2,0},{3,7},{4,6},{5,1},{6,4},{7,3},{8,10},{9,13},{10,... | collective-permute-start | bytes 3538952 | tf_op jit(solution)/shard_map/ppermute | solution.py:110
  185.1 22.3 %collective-permute-start.39 = (bf16[8,2,1,48,768]{4,3,1,2,0:T(8,128)(2,1)}, bf16[8,2,1,48,768]{4,3,1,2,0:T(8,128)(2,1)}, u32[]{:S(2)}, u32[]{:S(2)}) collective-permute-start(bf16[8,2,1,48,768]{4,3,1,2,0:T(8,128)(2,1)} %collective-permute-done.36), channel_id=1, source_target_pairs={{0,1},{1,0},{2,3},{3,2},{4,5},{5,4},{6,7},{7,6},{8,9},{9,8},{10,11... | collective-permute-start | bytes 3538952 | tf_op jit(solution)/shard_map/ppermute | solution.py:101
  207.4 29.2 %collective-permute-start.40 = (bf16[8,2,2,48,768]{4,3,2,1,0:T(8,128)(2,1)}, bf16[8,2,2,48,768]{4,3,2,1,0:T(8,128)(2,1)}, u32[]{:S(2)}, u32[]{:S(2)}) collective-permute-start(bf16[8,2,2,48,768]{4,3,2,1,0:T(8,128)(2,1)} %constant_dynamic-update-slice_fusion.29.refs_0_), channel_id=1, source_target_pairs={{0,4},{1,3},{2,6},{3,1},{4,0},{5,7},{6,2},{7,5},{8,12},{9,11},{10,... | collective-permute-start | bytes 7077896 | tf_op jit(solution)/shard_map/ppermute | solution.py:115
  207.9 28.7 %collective-permute-start.41 = (bf16[8,2,2,48,768]{4,3,2,1,0:T(8,128)(2,1)}, bf16[8,2,2,48,768]{4,3,2,1,0:T(8,128)(2,1)S(1)}, u32[]{:S(2)}, u32[]{:S(2)}) collective-permute-start(bf16[8,2,2,48,768]{4,3,2,1,0:T(8,128)(2,1)} %constant_dynamic-update-slice_fusion.29.refs_0_), channel_id=1, source_target_pairs={{0,1},{1,0},{2,3},{3,2},{4,5},{5,4},{6,7},{7,6},{8,9},{9,8},{10,11... | collective-permute-start | bytes 7077896 | tf_op jit(solution)/shard_map/ppermute | solution.py:101
  241.5 20.2 %collective-permute-start.43 = (bf16[2,6,96,192]{3,2,1,0:T(8,128)(2,1)S(1)}, bf16[2,6,96,192]{3,2,1,0:T(8,128)(2,1)S(1)}, u32[]{:S(2)}, u32[]{:S(2)}) collective-permute-start(bf16[2,6,96,192]{3,2,1,0:T(8,128)(2,1)S(1)} %get-tuple-element.365), channel_id=1, source_target_pairs={{0,2},{1,3},{2,0},{3,1},{4,6},{5,7},{6,4},{7,5},{8,10},{9,11},{10,... | collective-permute-start | bytes 1327112 | tf_op jit(solution)/shard_map/ppermute | solution.py:97
  263.2 23.4 %collective-permute-start.44 = (bf16[2,2,6,96,192]{4,3,2,1,0:T(8,128)(2,1)S(1)}, bf16[2,2,6,96,192]{4,3,2,1,0:T(8,128)(2,1)S(1)}, u32[]{:S(2)}, u32[]{:S(2)}) collective-permute-start(bf16[2,2,6,96,192]{4,3,2,1,0:T(8,128)(2,1)S(1)} %pad_maximum_fusion.3), channel_id=1, source_target_pairs={{0,1},{1,0},{2,3},{3,2},{4,5},{5,4},{6,7},{7,6},{8,9},{9,8},{10,11... | collective-permute-start | bytes 2654216 | tf_op jit(solution)/shard_map/ppermute | solution.py:101
  286.6 25.4 %collective-permute-start.45 = (bf16[2,8,2,2,48,768]{5,4,3,2,1,0:T(8,128)(2,1)}, bf16[2,8,2,2,48,768]{5,4,3,2,1,0:T(8,128)(2,1)}, u32[]{:S(2)}, u32[]{:S(2)}) collective-permute-start(bf16[2,8,2,2,48,768]{5,4,3,2,1,0:T(8,128)(2,1)} %get-tuple-element.395), channel_id=1, source_target_pairs={{0,1},{1,0},{2,3},{3,2},{4,5},{5,4},{6,7},{7,6},{8,9},{9,8},{10,11... | collective-permute-start | bytes 14155784 | tf_op jit(solution)/shard_map/ppermute | solution.py:101
  315.1 29.0 %collective-permute-start.46 = (bf16[8,2,2,48,768]{4,3,2,1,0:T(8,128)(2,1)S(1)}, bf16[8,2,2,48,768]{4,3,2,1,0:T(8,128)(2,1)}, u32[]{:S(2)}, u32[]{:S(2)}) collective-permute-start(bf16[8,2,2,48,768]{4,3,2,1,0:T(8,128)(2,1)S(1)} %fusion), channel_id=1, source_target_pairs={{0,4},{1,3},{2,6},{3,1},{4,0},{5,7},{6,2},{7,5},{8,12},{9,11},{10,... | collective-permute-start | bytes 7077896 | tf_op jit(solution)/shard_map/ppermute | solution.py:115
  316.7 30.9 %collective-permute-start.47 = (bf16[2,8,2,1,48,768]{5,4,2,3,1,0:T(8,128)(2,1)}, bf16[2,8,2,1,48,768]{5,4,2,3,1,0:T(8,128)(2,1)}, u32[]{:S(2)}, u32[]{:S(2)}) collective-permute-start(bf16[2,8,2,1,48,768]{5,4,2,3,1,0:T(8,128)(2,1)} %bitcast.80), channel_id=1, source_target_pairs={{0,1},{1,0},{2,3},{3,2},{4,5},{5,4},{6,7},{7,6},{8,9},{9,8},{10,11... | collective-permute-start | bytes 7077896 | tf_op jit(solution)/shard_map/ppermute | solution.py:101
  350.2 32.1 %collective-permute-start.48 = (bf16[2,8,2,2,48,768]{5,4,3,2,1,0:T(8,128)(2,1)}, bf16[2,8,2,2,48,768]{5,4,3,2,1,0:T(8,128)(2,1)}, u32[]{:S(2)}, u32[]{:S(2)}) collective-permute-start(bf16[2,8,2,2,48,768]{5,4,3,2,1,0:T(8,128)(2,1)} %get-tuple-element.432), channel_id=1, source_target_pairs={{0,1},{1,0},{2,3},{3,2},{4,5},{5,4},{6,7},{7,6},{8,9},{9,8},{10,11... | collective-permute-start | bytes 14155784 | tf_op jit(solution)/shard_map/ppermute | solution.py:101
  350.2 29.1 %collective-permute-start.49 = (bf16[4,2,2,48,768]{4,3,2,1,0:T(8,128)(2,1)}, bf16[4,2,2,48,768]{4,3,2,1,0:T(8,128)(2,1)}, u32[]{:S(2)}, u32[]{:S(2)}) collective-permute-start(bf16[4,2,2,48,768]{4,3,2,1,0:T(8,128)(2,1)} %fusion.5), channel_id=1, source_target_pairs={{0,2},{1,5},{2,0},{3,7},{4,6},{5,1},{6,4},{7,3},{8,10},{9,13},{10,... | collective-permute-start | bytes 3538952 | tf_op jit(solution)/shard_map/ppermute | solution.py:110
  352.7 34.2 %collective-permute-start.50 = (bf16[8,2,1,48,768]{4,3,1,2,0:T(8,128)(2,1)}, bf16[8,2,1,48,768]{4,3,1,2,0:T(8,128)(2,1)}, u32[]{:S(2)}, u32[]{:S(2)}) collective-permute-start(bf16[8,2,1,48,768]{4,3,1,2,0:T(8,128)(2,1)} %bitcast.572), channel_id=1, source_target_pairs={{0,4},{1,3},{2,6},{3,1},{4,0},{5,7},{6,2},{7,5},{8,12},{9,11},{10,... | collective-permute-start | bytes 3538952 | tf_op jit(solution)/shard_map/ppermute | solution.py:115
  386.9 26.5 %collective-permute-start.52 = (bf16[2,8,2,1,48,768]{5,4,2,3,1,0:T(8,128)(2,1)}, bf16[2,8,2,1,48,768]{5,4,2,3,1,0:T(8,128)(2,1)}, u32[]{:S(2)}, u32[]{:S(2)}) collective-permute-start(bf16[2,8,2,1,48,768]{5,4,2,3,1,0:T(8,128)(2,1)} %bitcast.97), channel_id=1, source_target_pairs={{0,1},{1,0},{2,3},{3,2},{4,5},{5,4},{6,7},{7,6},{8,9},{9,8},{10,11... | collective-permute-start | bytes 7077896 | tf_op jit(solution)/shard_map/ppermute | solution.py:101
  387.0 34.5 %collective-permute-start.51 = (bf16[8,2,2,48,768]{4,3,2,1,0:T(8,128)(2,1)}, bf16[8,2,2,48,768]{4,3,2,1,0:T(8,128)(2,1)}, u32[]{:S(2)}, u32[]{:S(2)}) collective-permute-start(bf16[8,2,2,48,768]{4,3,2,1,0:T(8,128)(2,1)} %fusion.1), channel_id=1, source_target_pairs={{0,4},{1,3},{2,6},{3,1},{4,0},{5,7},{6,2},{7,5},{8,12},{9,11},{10,... | collective-permute-start | bytes 7077896 | tf_op jit(solution)/shard_map/ppermute | solution.py:115
  421.5 28.9 %collective-permute-start.64 = (bf16[8,2,1,48,768]{4,3,1,2,0:T(8,128)(2,1)}, bf16[8,2,1,48,768]{4,3,1,2,0:T(8,128)(2,1)}, u32[]{:S(2)}, u32[]{:S(2)}) collective-permute-start(bf16[8,2,1,48,768]{4,3,1,2,0:T(8,128)(2,1)} %bitcast.120), channel_id=1, source_target_pairs={{0,4},{1,3},{2,6},{3,1},{4,0},{5,7},{6,2},{7,5},{8,12},{9,11},{10,... | collective-permute-start | bytes 3538952 | tf_op jit(solution)/shard_map/ppermute | solution.py:115
  423.0 25.9 %collective-permute-start.61 = (bf16[4,2,1,48,768]{4,3,1,2,0:T(8,128)(2,1)}, bf16[4,2,1,48,768]{4,3,1,2,0:T(8,128)(2,1)}, u32[]{:S(2)}, u32[]{:S(2)}) collective-permute-start(bf16[4,2,1,48,768]{4,3,1,2,0:T(8,128)(2,1)} %bitcast.114), channel_id=1, source_target_pairs={{0,2},{1,5},{2,0},{3,7},{4,6},{5,1},{6,4},{7,3},{8,10},{9,13},{10,... | collective-permute-start | bytes 1769480 | tf_op jit(solution)/shard_map/ppermute | solution.py:110
  423.8 26.6 %collective-permute-start.65 = (bf16[2,2,48,768]{3,2,1,0:T(8,128)(2,1)}, bf16[2,2,48,768]{3,2,1,0:T(8,128)(2,1)S(1)}, u32[]{:S(2)}, u32[]{:S(2)}) collective-permute-start(bf16[2,2,48,768]{3,2,1,0:T(8,128)(2,1)} %get-tuple-element.483), channel_id=1, source_target_pairs={{0,16},{4,20},{8,24},{12,28},{16,0},{20,4},{24,8},{28,12},{1,17},{... | collective-permute-start | bytes 884744 | tf_op jit(solution)/shard_map/ppermute | solution.py:119
  424.4 23.5 %collective-permute-start.62 = (bf16[4,32,768]{2,1,0:T(8,128)(2,1)}, bf16[4,32,768]{2,1,0:T(8,128)(2,1)S(1)}, u32[]{:S(2)}, u32[]{:S(2)}) collective-permute-start(bf16[4,32,768]{2,1,0:T(8,128)(2,1)} %pad_maximum_fusion.15), channel_id=1, source_target_pairs={{0,4},{4,0},{8,12},{12,8},{16,20},{20,16},{24,28},{28,24},{1,5},{5... | collective-permute-start | bytes 589832 | tf_op jit(solution)/shard_map/ppermute | solution.py:105
  450.4 23.3 %collective-permute-start.66 = (bf16[4,2,2,48,768]{4,3,2,1,0:T(8,128)(2,1)S(1)}, bf16[4,2,2,48,768]{4,3,2,1,0:T(8,128)(2,1)S(1)}, u32[]{:S(2)}, u32[]{:S(2)}) collective-permute-start(bf16[4,2,2,48,768]{4,3,2,1,0:T(8,128)(2,1)S(1)} %fusion.4), channel_id=1, source_target_pairs={{0,2},{1,5},{2,0},{3,7},{4,6},{5,1},{6,4},{7,3},{8,10},{9,13},{10,... | collective-permute-start | bytes 3538952 | tf_op jit(solution)/shard_map/ppermute | solution.py:110
  455.7 17.9 %collective-permute-start.67 = (bf16[8,32,768]{2,1,0:T(8,128)(2,1)S(1)}, bf16[8,32,768]{2,1,0:T(8,128)(2,1)S(1)}, u32[]{:S(2)}, u32[]{:S(2)}) collective-permute-start(bf16[8,32,768]{2,1,0:T(8,128)(2,1)S(1)} %pad_maximum_fusion.9), channel_id=1, source_target_pairs={{0,2},{1,3},{2,0},{3,1},{4,6},{5,7},{6,4},{7,5},{8,10},{9,11},{10,... | collective-permute-start | bytes 1179656 | tf_op jit(solution)/shard_map/ppermute | solution.py:97
  459.0 18.0 %collective-permute-start.69 = (bf16[2,1,48,768]{3,2,0,1:T(8,128)(2,1)S(1)}, bf16[2,1,48,768]{3,2,0,1:T(8,128)(2,1)S(1)}, u32[]{:S(2)}, u32[]{:S(2)}) collective-permute-start(bf16[2,1,48,768]{3,2,0,1:T(8,128)(2,1)S(1)} %get-tuple-element.487), channel_id=1, source_target_pairs={{0,24},{4,28},{8,0},{12,4},{16,8},{20,12},{24,16},{28,20},{1,25},{... | collective-permute-start | bytes 442376 | tf_op jit(solution)/shard_map/ppermute | solution.py:119
  502.1 18.1 %collective-permute-start.80 = (bf16[2,2,48,768]{3,2,1,0:T(8,128)(2,1)}, bf16[2,2,48,768]{3,2,1,0:T(8,128)(2,1)S(1)}, u32[]{:S(2)}, u32[]{:S(2)}) collective-permute-start(bf16[2,2,48,768]{3,2,1,0:T(8,128)(2,1)} %get-tuple-element.498), channel_id=1, source_target_pairs={{0,16},{4,20},{8,24},{12,28},{16,0},{20,4},{24,8},{28,12},{1,17},{... | collective-permute-start | bytes 884744 | tf_op jit(solution)/shard_map/ppermute | solution.py:119
  553.7 36.0 %collective-permute-start.93 = (f32[6,48,768]{2,1,0:T(8,128)S(1)}, f32[6,48,768]{2,1,0:T(8,128)S(1)}, u32[]{:S(2)}, u32[]{:S(2)}) collective-permute-start(f32[6,48,768]{2,1,0:T(8,128)S(1)} %pad_maximum_fusion.5), channel_id=1, source_target_pairs={{0,1},{1,0},{2,3},{3,2},{4,5},{5,4},{6,7},{7,6},{8,9},{9,8},{10,11... | collective-permute-start | bytes 2654216 | tf_op jit(solution)/shard_map/ppermute | solution.py:101
  (153 other events, 1817.6 us)

commit v3 on v2

--- a/solution.py
+++ b/solution.py
@@ -46,6 +46,10 @@
 
 def dot_nn(a, b):
     return jnp.dot(a, b, preferred_element_type=F32)
+
+
+def along(k):
+    return k % 2 * 2 + k // 2
 
 
 class Place:
@@ -70,7 +74,7 @@
         kx = jnp.where(owner == 0, first, later)
         ky = jnp.where(owner == 0, later, first)
         cols = (x ^ kx) * 2 + (owner ^ kc)
-        rows = ((z + 4 - kz) % 4 * 2 + (y ^ ky)) * 2 * self.half + owner * self.half
+        rows = ((z ^ along(kz)) * 2 + (y ^ ky)) * 2 * self.half + owner * self.half
         e = jnp.arange(16, dtype=jnp.int32)
         col, owner, ky = e // 4, core ^ (e // 2 % 2), e % 2
         kx = (col // 2) ^ x
@@ -78,15 +82,17 @@
         first = jnp.where(owner == 0, kx, ky)
         slots = jnp.stack([later, first, (col % 2) ^ owner], axis=1).reshape(-1)
         owner, ky, kz = core ^ (e // 8), e // 4 % 2, e % 4
-        outs = ((z + 4 - kz) % 4 * 2 + (y ^ ky)) * 2 * self.half + owner * self.half
-        return jnp.concatenate([cols, rows, slots, outs]).astype(jnp.int32)
+        outs = ((z ^ along(kz)) * 2 + (y ^ ky)) * 2 * self.half + owner * self.half
+        step = jnp.arange(4, dtype=jnp.int32)
+        order = (x ^ (step % 2)) * 2 + (core ^ (step // 2))
+        return jnp.concatenate([cols, rows, slots, outs, order, core[None]]).astype(jnp.int32)
 
     def found_at(self):
         device = jnp.arange(self.rows * self.cols, dtype=jnp.int32)
         if not self.direct:
             return device
         row, col = device // 4, device % 4
-        kz = (self.z + 4 - row // 2) % 4
+        kz = along(row // 2 ^ self.z)
         ky = (row % 2) ^ self.y
         kx = (col // 2) ^ self.x
         kc = (col % 2) ^ self.core
@@ -115,19 +121,21 @@
     return lax.ppermute(v, ("row", "col"), pairs)
 
 
-def turn_z(v, k):
-    return lax.ppermute(v, "row", [(r, (r // 2 + k) % 4 * 2 + r % 2) for r in range(8)])
+def swap_far(v):
+    return lax.ppermute(v, "row", [(r, r ^ 4) for r in range(8)])
+
+
+def swap_near(v):
+    return lax.ppermute(v, "row", [(r, r ^ 2) for r in range(8)])
+
+
+def swap_beyond(v):
+    return lax.ppermute(v, "row", [(r, r ^ 6) for r in range(8)])
 
 
 def pair(index, own, other):
     first = index == 0
     return jnp.stack([jnp.where(first, own, other), jnp.where(first, other, own)])
-
-
-def gather_z(place, own):
-    got = [own] + [turn_z(own, k) for k in (1, 2, 3)]
-    ring = jnp.stack([got[3], got[2], got[1], got[0], got[3], got[2], got[1]])
-    return lax.dynamic_slice_in_dim(ring, 3 - place.z, 4, 0)
 
 
 def gather_cols(place, own):
@@ -138,7 +146,12 @@
 
 
 def near_z(own):
-    return jnp.stack([own] + [turn_z(own, k) for k in (1, 2, 3)])
+    both = jnp.stack([own, swap_far(own)])
+    return jnp.concatenate([both, swap_near(both)])
+
+
+def near_z_at_once(own):
+    return jnp.stack([own, swap_far(own), swap_near(own), swap_beyond(own)])
 
 
 def near_y(every):
@@ -167,14 +180,18 @@
     return near_cols(near_rows(own))
 
 
+def sum_parts(place, parts):
+    z = place.z
+
+    def two(at):
+        return jnp.stack([lax.dynamic_index_in_dim(parts, k, 0, False) for k in (at, at ^ 2)])
+
+    total = two(z) + swap_near(two(z ^ 1))
+    return total[0] + swap_far(total[1])
+
+
 def sum_along_z(place, own):
-    parts = own.reshape((4, own.shape[0] // 4) + own.shape[1:])
-    total = lax.dynamic_index_in_dim(parts, place.z, 0, False)
-    for k in (1, 2, 3):
-        total = total + turn_z(
-            lax.dynamic_index_in_dim(parts, (place.z + k) % 4, 0, False), k
-        )
-    return total
+    return sum_parts(place, own.reshape((4, own.shape[0] // 4) + own.shape[1:]))
 
 
 def sum_with(swap):
@@ -182,19 +199,17 @@
 
 
 def sum_spread(place, total):
-    every = gather_z(place, total)
-    return every.reshape((-1,) + total.shape[1:])
+    far = pair(place.z // 2, total, swap_far(total))
+    every = pair(place.z % 2, far, swap_near(far))
+    return jnp.swapaxes(every, 0, 1).reshape((-1,) + total.shape[1:])
 
 
 def sum_scalar(place, value):
     if not place.direct:
         return lax.psum(value, ("row", "col"))
     total = jnp.broadcast_to(value, (8, 128))
-    total = total + swap_core(total)
-    total = total + swap_x(total)
-    total = total + swap_y(total)
-    total = total + lax.ppermute(total, "row", [(r, r ^ 2) for r in range(8)])
-    total = total + lax.ppermute(total, "row", [(r, r ^ 4) for r in range(8)])
+    for swap in (swap_far, swap_near, swap_y, swap_x, swap_core):
+        total = total + swap(total)
     return total[0, 0]
 
 
@@ -214,10 +229,7 @@
 
 
 def scatter_z(place, own):
-    total = lax.dynamic_index_in_dim(own, place.z, 0, False)
-    for k in (1, 2, 3):
-        total = total + turn_z(lax.dynamic_index_in_dim(own, (place.z + k) % 4, 0, False), k)
-    return total
+    return sum_parts(place, own)
 
 
 def scatter_x(place, total, mine):
@@ -248,19 +260,37 @@
         else:
             self.outs = [buffers[0].shape]
 
-    def load(self, table, buffers, matrix, target, sems):
+    def column(self, table, step):
+        return table[192 + step] if self.direct else step
+
+    def load(self, table, buffers, moves):
         if not self.direct:
             for c in range(self.cols):
-                pltpu.make_async_copy(buffers[0].at[matrix, c], target.at[c], sems.at[c]).start()
+                for matrix, target, sems in moves:
+                    pltpu.make_async_copy(
+                        buffers[0].at[matrix, c], target.at[c], sems.at[c]
+                    ).start()
             return
-        for e in range(64):
-            first, kc, kz = e // 8 % 2, e // 4 % 2, e % 4
-            row = pl.multiple_of(table[64 + e], 16)
-            pltpu.make_async_copy(
-                buffers[e // 16].at[first * 4 + kz, kc, matrix],
-                target.at[table[e], pl.ds(row, self.half), :],
-                sems.at[table[e]],
-            ).start()
+        for core in range(2):
+
+            @pl.when(table[196] == core)
+            def _(core=core):
+                entries = []
+                for e in range(64):
+                    owner, later, first, kc = core ^ (e // 32), e // 16 % 2, e // 8 % 2, e // 4 % 2
+                    kx = first if owner == 0 else later
+                    entries.append(((owner ^ kc ^ core) * 2 + kx, e))
+                for step in range(4):
+                    for matrix, target, sems in moves:
+                        for at, e in entries:
+                            if at != step:
+                                continue
+                            row = pl.multiple_of(table[64 + e], 16)
+                            pltpu.make_async_copy(
+                                buffers[e // 16].at[e // 8 % 2 * 4 + e % 4, e // 4 % 2, matrix],
+                                target.at[step, pl.ds(row, self.half), :],
+                                sems.at[step],
+                            ).start()
 
     def store(self, table, c, matrix, source, grads, sem):
         if not self.direct:
@@ -284,29 +314,38 @@
     def __init__(self):
         self.last = None
 
-    def run(self, moves, works=()):
-        operands = ([v for _, v in moves], [w[1:] for w in works])
+    def run(self, moves, works=(), late=()):
+        operands = ([v for _, v in moves], [w[1:] for w in works], [v for _, v in late])
         if self.last is not None:
             operands, _ = lax.optimization_barrier((operands, self.last))
         moved = [move(v) for (move, _), v in zip(moves, operands[0])]
         done = [w[0](*v) for w, v in zip(works, operands[1])]
+        if late:
+            held, _ = lax.optimization_barrier((operands[2], done))
+            moved += [move(v) for (move, _), v in zip(late, held)]
         self.last = (moved, done)
         return moved, done
-
-
-def turn(k):
-    return lambda v: turn_z(v, k)
 
 
 class Spread:
     def __init__(self, kept, got):
         self.own = jnp.stack([kept, got])
 
-    def turns(self, ks):
-        return [(turn(k), self.own) for k in ks]
-
-    def turned(self, one, two, three):
-        self.z = jnp.stack([self.own, one, two, three])
+    def far(self):
+        return [(swap_far, self.own)]
+
+    def near(self, got):
+        self.two = jnp.stack([self.own, got])
+        return [(swap_near, self.two)]
+
+    def at_once(self):
+        return [(swap_far, self.own), (swap_near, self.own), (swap_beyond, self.own)]
+
+    def along_at_once(self, got):
+        self.z = jnp.stack([self.own] + list(got))
+
+    def along(self, got):
+        self.z = jnp.concatenate([self.two, got])
 
     def first(self):
         return [(swap_first, self.z)]
@@ -346,14 +385,16 @@
         self.parts = (self.own[0], self.got[0], got)
         return [(swap_first, add_up(*[v[4:] for v in self.parts]).astype(BF16))]
 
-    def third(self, got):
-        self.z = [add_up(*[v[k] for v in self.parts], got[k]).astype(BF16) for k in range(4)]
-
-    def turns(self, ks=(1, 3, 2)):
-        return [(turn(4 - k), self.z[k]) for k in ks]
+    def near(self, got):
+        self.parts = self.parts + (got,)
+        return [(swap_near, add_up(*[v[2:4] for v in self.parts]).astype(BF16))]
+
+    def far(self, got):
+        self.last = got
+        return [(swap_far, add_up(*[v[1] for v in self.parts], got[1]).astype(BF16))]
 
     def total(self, got):
-        return add_up(self.z[0], *got)
+        return add_up(*[v[0] for v in self.parts], self.last[0], got)
 
 
 def plain_gather(parts):
@@ -392,7 +433,7 @@
 
     @pl.when(c == 0)
     def _():
-        route.load(table, buffers, 0, w_ref, sems)
+        route.load(table, buffers, [(0, w_ref, sems)])
         for s in range(samples):
             rows = pl.ds(s * LEN, LEN)
             n, _ = normal(x_ref[rows, :])
@@ -401,24 +442,32 @@
 
     wait_all(w_ref.at[c], sems.at[c])
     width = shared_ref.shape[-1]
-    query_bias = shared_ref[c, base + 6 : base + 7, :]
-    value_bias = shared_ref[c, base + 7 : base + 8, :]
+    col = route.column(table, c)
+    query_bias = shared_ref[col, base + 6 : base + 7, :]
+    value_bias = shared_ref[col, base + 7 : base + 8, :]
     bias = jnp.concatenate([query_bias, jnp.zeros_like(query_bias), value_bias], axis=1)
     triple = dot_nn(h_ref[...], w_ref[c, :, : 3 * width]) + bias
     qkv_ref[0] = triple.astype(BF16)
+    triple = triple.astype(BF16)
+    heads = width // HEAD_DIM
+
+    def part(s, k, j):
+        at = k * width + j * HEAD_DIM
+        return triple[s * LEN : (s + 1) * LEN, at : at + HEAD_DIM]
+
+    each = [(s, j) for s in range(samples) for j in range(heads)]
+    scores = [dot_nt(part(s, 1, j), part(s, 0, j)) * HEAD_DIM ** (-0.5) for s, j in each]
+    probs = []
+    for score in scores:
+        powers = jnp.exp(score - jnp.max(score, axis=0, keepdims=True))
+        probs.append((powers * (1.0 / jnp.sum(powers, axis=0, keepdims=True))).astype(BF16))
+    for (s, j), prob in zip(each, probs):
+        p_ref[0, j, s] = prob
+    outs = [dot_tn(prob, part(s, 2, j)).astype(BF16) for (s, j), prob in zip(each, probs)]
     for s in range(samples):
-        rows = pl.ds(s * LEN, LEN)
-        pieces = []
-        for j in range(width // HEAD_DIM):
-            q = qkv_ref[0, rows, j * HEAD_DIM : (j + 1) * HEAD_DIM]
-            k = qkv_ref[0, rows, width + j * HEAD_DIM : width + (j + 1) * HEAD_DIM]
-            v = qkv_ref[0, rows, 2 * width + j * HEAD_DIM : 2 * width + (j + 1) * HEAD_DIM]
-            scores = dot_nt(q, k) * HEAD_DIM ** (-0.5)
-            powers = jnp.exp(scores - jnp.max(scores, axis=-1, keepdims=True))
-            probs = (powers / jnp.sum(powers, axis=-1, keepdims=True)).astype(BF16)
-            p_ref[0, j, s] = probs
-            pieces.append(dot_nn(probs, v).astype(BF16))
-        o_ref[0, rows, :] = jnp.concatenate(pieces, axis=1)
+        o_ref[0, pl.ds(s * LEN, LEN), :] = jnp.concatenate(
+            outs[s * heads : (s + 1) * heads], axis=1
+        )
     a_ref[...] += dot_nt(o_ref[0], w_ref[c, :, 3 * width :])
 
     @pl.when(c == pl.num_programs(0) - 1)
@@ -438,8 +487,7 @@
 
     @pl.when(c == 0)
     def _():
-        route.load(table, buffers, 0, wi_ref, sems_i)
-        route.load(table, buffers, 1, wo_ref, sems_o)
+        route.load(table, buffers, [(0, wi_ref, sems_i), (1, wo_ref, sems_o)])
         for s in range(samples):
             rows = pl.ds(s * LEN, LEN)
             n, _ = normal(x_ref[rows, :])
@@ -447,9 +495,10 @@
         m_ref[...] = jnp.zeros_like(m_ref)
 
     wait_all(wi_ref.at[c], sems_i.at[c])
+    col = route.column(table, c)
     blocks = wi_ref.shape[-1] // shared_ref.shape[-1]
     bias = jnp.concatenate(
-        [shared_ref[c, base + 8 + k : base + 9 + k, :] for k in range(blocks)], axis=1
+        [shared_ref[col, base + 8 + k : base + 9 + k, :] for k in range(blocks)], axis=1
     )
     hidden = dot_nn(h_ref[...], wi_ref[c]) + bias
     u_ref[0] = hidden
@@ -521,8 +570,7 @@
 
     @pl.when(c == 0)
     def _():
-        route.load(table, buffers, 1, wo_ref, sems_o)
-        route.load(table, buffers, 0, wi_ref, sems_i)
+        route.load(table, buffers, [(1, wo_ref, sems_o), (0, wi_ref, sems_i)])
         branch_gradient(dx_ref, mod_ref, m_ref, dmod_ref, dtail_ref, low_ref)
         dh_ref[...] = jnp.zeros_like(dh_ref)
 
@@ -537,12 +585,12 @@
     active, slope = gelu_slope(u_ref[0])
     low = low_ref[...]
     go_ref[slot] = dot_tn(low, active.astype(BF16)).astype(BF16)
-    route.store(table, c, 1, go_ref.at[slot], grads, sems_go.at[slot])
+    route.store(table, route.column(table, c), 1, go_ref.at[slot], grads, sems_go.at[slot])
     du = dot_nn(low, wo_ref[c]) * slope
-    dbias_ref[c] = jnp.sum(du, axis=0, keepdims=True)
+    dbias_ref[route.column(table, c)] = jnp.sum(du, axis=0, keepdims=True)
     du = du.astype(BF16)
     gi_ref[slot] = dot_tn(h_ref[...], du).astype(BF16)
-    route.store(table, c, 0, gi_ref.at[slot], grads, sems_gi.at[slot])
+    route.store(table, route.column(table, c), 0, gi_ref.at[slot], grads, sems_gi.at[slot])
     wait_all(wi_ref.at[c], sems_i.at[c])
     dh_ref[...] += dot_nt(du, wi_ref[c])
 
@@ -571,7 +619,7 @@
 
     @pl.when(c == 0)
     def _():
-        route.load(table, buffers, 0, w_ref, sems)
+        route.load(table, buffers, [(0, w_ref, sems)])
         branch_gradient(dx_ref, mod_ref, a_ref, dmod_ref, dtail_ref, low_ref)
         dh_ref[...] = jnp.zeros_like(dh_ref)
 
@@ -583,32 +631,37 @@
 
     wait_all(w_ref.at[c], sems.at[c])
     do_all = dot_nn(low_ref[...], w_ref[c, :, 3 * width :]).astype(BF16)
-    sums = [None] * (width // HEAD_DIM)
+    heads = width // HEAD_DIM
+    each = [(s, j) for s in range(samples) for j in range(heads)]
+
+    def part(s, k, j):
+        at = k * width + j * HEAD_DIM
+        return qkv_ref[0, pl.ds(s * LEN, LEN), at : at + HEAD_DIM]
+
+    def given(s, j):
+        return do_all[s * LEN : (s + 1) * LEN, j * HEAD_DIM : (j + 1) * HEAD_DIM]
+
+    dps = [dot_nt(part(s, 2, j), given(s, j)) for s, j in each]
+    dss = []
+    for (s, j), dp in zip(each, dps):
+        probs = p_ref[0, j, s].astype(F32)
+        delta = jnp.sum(probs * dp, axis=0, keepdims=True)
+        dss.append((probs * (dp - delta)).astype(BF16))
+    dqs = [dot_tn(ds, part(s, 1, j)) * factor for (s, j), ds in zip(each, dss)]
+    dks = [dot_nn(ds, part(s, 0, j)) * factor for (s, j), ds in zip(each, dss)]
+    dvs = [dot_nn(p_ref[0, j, s], given(s, j)) for s, j in each]
+    sums = None
     for s in range(samples):
-        rows = pl.ds(s * LEN, LEN)
-        dqs, dks, dvs = [], [], []
-        for j in range(width // HEAD_DIM):
-            q = qkv_ref[0, rows, j * HEAD_DIM : (j + 1) * HEAD_DIM]
-            k = qkv_ref[0, rows, width + j * HEAD_DIM : width + (j + 1) * HEAD_DIM]
-            v = qkv_ref[0, rows, 2 * width + j * HEAD_DIM : 2 * width + (j + 1) * HEAD_DIM]
-            o = o_ref[0, rows, j * HEAD_DIM : (j + 1) * HEAD_DIM]
-            do = do_all[s * LEN : (s + 1) * LEN, j * HEAD_DIM : (j + 1) * HEAD_DIM]
-            probs = p_ref[0, j, s]
-            dp = dot_nt(do, v)
-            delta = jnp.sum(do.astype(F32) * o.astype(F32), axis=-1, keepdims=True)
-            ds = (probs.astype(F32) * (dp - delta)).astype(BF16)
-            dqs.append(dot_nn(ds, k) * factor)
-            dks.append(dot_tn(ds, q) * factor)
-            dvs.append(dot_tn(probs, do))
-        joined = jnp.concatenate(dqs + dks + dvs, axis=1)
-        part = jnp.sum(joined, axis=0, keepdims=True)
-        sums = part if s == 0 else sums + part
-        d_ref[rows, :] = joined.astype(BF16)
-    dbias_ref[c] = sums
+        at = slice(s * heads, (s + 1) * heads)
+        joined = jnp.concatenate(dqs[at] + dks[at] + dvs[at], axis=1)
+        total = jnp.sum(joined, axis=0, keepdims=True)
+        sums = total if s == 0 else sums + total
+        d_ref[pl.ds(s * LEN, LEN), :] = joined.astype(BF16)
+    dbias_ref[route.column(table, c)] = sums
     grad_in = dot_tn(h_ref[...], d_ref[...])
     grad_out = dot_tn(low_ref[...], o_ref[0])
     g_ref[slot] = jnp.concatenate([grad_in, grad_out], axis=1).astype(BF16)
-    route.store(table, c, 0, g_ref.at[slot], grads, sems_g.at[slot])
+    route.store(table, route.column(table, c), 0, g_ref.at[slot], grads, sems_g.at[slot])
     dh_ref[...] += dot_nt(d_ref[...], w_ref[c, :, : 3 * width])
 
     @pl.when(c == count - 1)
@@ -1422,7 +1475,6 @@
     time_rows = time_mlp.shape[0]
     mine = jnp.concatenate([bias_table, embed_low[CLASSES:].astype(F32)], axis=0)
     final_view = [v.T for v in (final_layer, momentum_final, variance_final)]
-    final_low = final_view[0].astype(BF16)
     found = place.found_at()
     sample = jnp.arange(every_sample, dtype=jnp.int32)
     mode_height = -(-(12 * layers + 4) // 16) * 16
@@ -1437,7 +1489,7 @@
         partial = jnp.einsum("sd,lkde->slke", cond_rows, mode_low, preferred_element_type=F32)
         return cond_rows, partial.reshape(every_sample, layers * 6, narrow)
 
-    def own_modes(total, shared, cond_act):
+    def own_modes(total, shared, cond_act, final_low):
         bias_full = jnp.swapaxes(shared, 0, 1).reshape(-1, width)
         modes = total.reshape(samples, layers, 6, width) + jnp.stack(
             [bias_full[14 * layer : 14 * layer + 6] for layer in range(layers)]
@@ -1481,11 +1533,9 @@
     def mlp_back(buffers, *operands):
         return mlp_backward(place, buffers, *operands)
 
-    head_low = final_low[2 * width :]
-
-    def last_step(x, final_mod):
+    def last_step(x, final_mod, final_low):
         return final_step(
-            x, final_mod, head_low, final_bias[2 * width :][None], noise, mask[:, None]
+            x, final_mod, final_low[2 * width :], final_bias[2 * width :][None], noise, mask[:, None]
         )
 
     def mode_parts(back_a, back_b, grad_final_mod):
@@ -1537,20 +1587,22 @@
             ],
             axis=0,
         )
-        (t1, t3, t2), (near, shared) = stages.run(
-            a0.turns((1, 3, 2)),
-            [(near_rows, own_block), (functools.partial(gather_cols, place), mine)],
-        )
-        a0.turned(t1, t2, t3)
-
+        got, (near, shared, final_low) = stages.run(
+            a0.at_once(),
+            [
+                (near_rows, own_block),
+                (functools.partial(gather_cols, place), mine),
+                (lambda v: v.astype(BF16), final_view[0]),
+            ],
+        )
+        a0.along_at_once(got)
         got, (near, residual) = stages.run(
-            a0.first() + b0.turns((1, 3)),
+            a0.first() + b0.far(),
             [
                 (near_x, near),
                 (functools.partial(embed_tokens, base), noisy, shared, position),
             ],
         )
-        t1, t3 = got[1:]
 
         def condition_work(near, shared, found):
             near = near_core(near)
@@ -1558,42 +1610,47 @@
             return near, got, partial_modes(got[1])
 
         got, ((near, conditions, (cond_rows, partial)),) = stages.run(
-            a0.second(got[0]) + b0.turns((2,)) + a0.core(),
+            a0.second(got[0]) + b0.near(got[1]),
             [(condition_work, near, shared, found)],
-        )
+            a0.core(),
+        )
+        b0.along(got[1])
         condition, cond_act, first_time, first_act, freq_low, all_labels = conditions
-        b0.turned(t1, got[1], t3)
         core = got[2]
         got, (total,) = stages.run(
-            b0.first() + a1.turns((1, 3)) + a0.late_core(got[0]),
+            b0.first() + a1.far() + a0.late_core(got[0]),
             [(functools.partial(scatter_y, place), partial)],
         )
-        buffers[0] = a0.buffers(core, got[3])
-        t1, t3 = got[1:3]
-
-        def scatter_work(total):
-            return scatter_x(place, scatter_z(place, total), samples)
-
-        got, (total,) = stages.run(
-            b0.second(got[0]) + a1.turns((2,)) + b0.core(), [(scatter_work, total)]
-        )
-        a1.turned(t1, got[1], t3)
-        core = got[2]
+        buffers[0] = a0.buffers(core, got[2])
+
+        two = a1.near(got[1])[0][1]
+
+        def scatter_work(total, two):
+            blocks = swap_near(two)
+            total, blocks = lax.optimization_barrier((scatter_z(place, total), blocks))
+            return blocks, scatter_x(place, total, samples)
+
+        got, ((blocks, total),) = stages.run(
+            b0.second(got[0]) + b0.core(), [(scatter_work, total, two)]
+        )
+        a1.along(blocks)
+        core = got[1]
 
         def modes_work(total, shared, cond_act):
-            return own_modes(scatter_core(place, total), shared, cond_act)
+            return own_modes(scatter_core(place, total), shared, cond_act, final_low)
 
         got, ((mods_a, mods_b, final_mod),) = stages.run(
-            a1.first() + b1.turns((1, 3)) + b0.late_core(got[0]),
+            b1.far() + b0.late_core(got[0]),
             [(modes_work, total, shared, cond_act)],
-        )
-        buffers[1] = b0.buffers(core, got[3])
-        t1, t3 = got[1:3]
+            a1.first(),
+        )
+        buffers[1] = b0.buffers(core, got[1])
+        got = [got[2], got[0]]
         got, (fore_a[0],) = stages.run(
-            a1.second(got[0]) + b1.turns((2,)) + a1.core(),
+            a1.second(got[0]) + b1.near(got[1]) + a1.core(),
             [(attn_step(0), buffers[0], residual, mods_a[0], shared)],
         )
-        b1.turned(t1, got[1], t3)
+        b1.along(got[1])
         core = got[2]
         got, (fore_b[0],) = stages.run(
             b1.first() + a1.late_core(got[0]),
@@ -1612,7 +1669,7 @@
         )
         mode_half = pair(place.x, mode_low, got[0])
         entry = [residual, fore_b[0][0]]
-        last = last_step(fore_b[1][0], final_mod)
+        last = last_step(fore_b[1][0], final_mod, final_low)
 
         def back_b_work(layer, grad):
             out, h, u, m = fore_b[layer]
@@ -1640,7 +1697,7 @@
         got, ((back_a[0], grads),) = stages.run(
             gb1.second(got[0]) + ga1.first(core_a1) + gb0.core, [back_a_work(0, back_b[0][0])]
         )
-        gb1.third(got[0])
+        zn_b1 = gb1.near(got[0])
         ga0 = Gathered(grads)
 
         def sum_work(back_a, back_b, last):
@@ -1649,45 +1706,43 @@
         moded = mode_parts(back_a, back_b, last[4])
         t2_a1 = ga1.second(got[1])
         got, (near_modes, small) = stages.run(
-            gb0.first(got[2]) + gb1.turns((1, 3)) + ga0.core,
+            gb0.first(got[2]) + ga0.core,
             [(near_z, moded), (sum_work, back_a, back_b, last)],
-        )
-        turned_b1 = got[1:3]
+            zn_b1,
+        )
+        got = [got[0], got[2], got[1]]
         t2_b0 = gb0.second(got[0])
         got, (near_modes, small) = stages.run(
-            ga0.first(got[3]) + t2_a1 + gb1.turns((2,)),
+            ga0.first(got[2]) + t2_a1 + gb1.far(got[1]),
             [(near_y, near_modes), (sum_with(swap_core), small)],
         )
-        total_b1 = gb1.total(turned_b1 + got[2:])
-        ga1.third(got[1])
+        total_b1 = gb1.total(got[2])
         t2_a0 = ga0.second(got[0])
         got, (near_modes, small) = stages.run(
-            t2_b0 + ga1.turns((1, 3)), [(near_x, near_modes), (sum_with(swap_x), small)]
-        )
-        turned_a1 = got[1:]
-        gb0.third(got[0])
+            t2_b0 + ga1.near(got[1]), [(near_x, near_modes), (sum_with(swap_x), small)]
+        )
         got, (near_modes, small) = stages.run(
-            t2_a0 + ga1.turns((2,)) + gb0.turns((1, 3)),
+            gb0.near(got[0]) + ga1.far(got[1]),
             [(near_core, near_modes), (sum_with(swap_y), small)],
-        )
-        total_a1 = ga1.total(turned_a1 + got[1:2])
-        turned_b0 = got[2:]
-        ga0.third(got[0])
+            t2_a0,
+        )
+        got = [got[2], got[1], got[0]]
+        total_a1 = ga1.total(got[1])
 
         def modes_back_work(near):
             return modes_backward(near, at, cond_rows, pick, mode_full, cond_act, final_low)
 
         got, (moded, small) = stages.run(
-            gb0.turns((2,)),
+            gb0.far(got[2]) + ga0.near(got[0]),
             [(modes_back_work, near_modes), (functools.partial(sum_spread, place), small)],
         )
-        total_b0 = gb0.total(turned_b0 + got)
+        total_b0 = gb0.total(got[0])
         time_inputs = lax.dynamic_slice_in_dim(
             jnp.concatenate([freq_low, first_act], axis=1), place.row * time_rows, time_rows, 1
         )
-        turned_a0, (part,) = stages.run(ga0.turns((1, 3)), [(near_z, moded[1])])
-        got, (part,) = stages.run(ga0.turns((2,)), [(near_y, part)])
-        total_a0 = ga0.total(turned_a0 + got)
+        got, (part,) = stages.run(ga0.far(got[1]), [(near_z_at_once, moded[1])])
+        total_a0 = ga0.total(got[0])
+        part = near_y(part)
         ends = condition_back(
             layers, hidden_blocks, found, spot, small, part, moded[4], moded[5], condition,
             first_time, time_inputs, all_labels, pick, near,
@@ -1705,6 +1760,7 @@
         shared_squares = shared_part[0, 0]
         final_grad = moded[3]
     else:
+        final_low = final_view[0].astype(BF16)
         shared = gather_cols(place, mine)
         time_full = lax.all_gather(time_mlp.astype(BF16), "row", axis=0, tiled=True)
         time_full = lax.all_gather(time_full, "col", axis=1, tiled=True)
@@ -1725,7 +1781,7 @@
         cond_act = jax.nn.silu(condition).astype(BF16)
         cond_rows, partial = partial_modes(cond_act)
         mods_a, mods_b, final_mod = own_modes(
-            scatter_plain(place, partial, samples), shared, cond_act
+            scatter_plain(place, partial, samples), shared, cond_act, final_low
         )
         grad = embed_tokens(base, noisy, shared, position)
         for layer in range(layers):
@@ -1736,7 +1792,7 @@
             grad = fore_a[layer][0]
             fore_b[layer] = mlp_step(layer)(buffers[2 * layer + 1], grad, mods_b[layer], shared)
             grad = fore_b[layer][0]
-        last = last_step(grad, final_mod)
+        last = last_step(grad, final_mod, final_low)
         grad = last[0]
         for layer in reversed(range(layers)):
             out, h, u, m = fore_b[layer]

time: 612 us -> 603 us (0.985)
  waiting for transfers between devices: 145 us -> 177 us
  Pallas kernels: 208 us -> 190 us
  starting transfers between devices: 116 us -> 98 us
  local copies, waits for them, and re-layouts: 50.2 us -> 36.8 us
  other arithmetic: 72.1 us -> 79.2 us
    ppermute x44 -> x32, waiting for transfers between devices: 66.3 us -> 95 us  [the longest x15 51.7 us: swap_near(): return lax.ppermute(v, 'row', [(r, r ^ 2) for r in range(8)])]
    ppermute x44 -> x32, starting transfers between devices: 70.3 us -> 54 us  [the longest x15 33.9 us: swap_far(): return lax.ppermute(v, 'row', [(r, r ^ 4) for r in range(8)])]
    concatenate x2 -> x8, other arithmetic: 1.94 us -> 11 us  [the longest x3 6.7 us: second(): self.p = jnp.concatenate([self.z, got])]
    unnamed x216 -> x202, local copies, waits for them, and re-layouts: 22.4 us -> 13.8 us
    pallas_call x2, Pallas kernels: 49.1 us -> 41.5 us  [attention_backward(): pl.pallas_call(functools.partial(attention_backward_body, route), grid=(c...]
    concatenate x4 -> x1, local copies, waits for them, and re-layouts: 6.25 us -> 0.04 us  [second(): self.p = jnp.concatenate([self.z, got])]
    convert_element_type x7 -> x9, other arithmetic: 16.2 us -> 19.3 us  [the longest x4 8.15 us: near(): return [(swap_near, add_up(*[v[2:4] for v in self.parts]).astype(BF16))]]
  transfers between devices with their start and end apart: 94 -> 82, of which waited for: 39 -> 36; matrix products, arithmetic and copies ran while one was open for 17% -> 16% of each run, Pallas kernels for 33% -> 30%
where the time goes in v3:
time: 603 us; the launch traced here: 593 us
  Pallas kernels  190 us (32%)
  waiting for transfers between devices  177 us (29%)
  starting transfers between devices  98 us (16%)
  other arithmetic  79.2 us (13%)
  local copies, waits for them, and re-layouts  36.8 us (6%)
  between operations  9.1 us (2%)
    ppermute x15, waiting for transfers between devices, swap_near(): return lax.ppermute(v, 'row', [(r, r ^ 2) for r in range(8)])  51.7 us
    pallas_call x2, Pallas kernels, mlp_backward(): pl.pallas_call(functools.partial(mlp_backward_body, route), grid=(count,)...  44.2 us
    ppermute x15, waiting for transfers between devices, swap_far(): return lax.ppermute(v, 'row', [(r, r ^ 4) for r in range(8)])  42.1 us
    pallas_call x2, Pallas kernels, attention_backward(): pl.pallas_call(functools.partial(attention_backward_body, route), grid=(c...  41.5 us
    ppermute x15, starting transfers between devices, swap_far(): return lax.ppermute(v, 'row', [(r, r ^ 4) for r in range(8)])  33.9 us
    ppermute x6, waiting for transfers between devices, swap_y(): return lax.ppermute(v, 'row', [(r, r ^ 1) for r in range(8)])  33.2 us
    pallas_call x2, Pallas kernels, mlp_forward(): pl.pallas_call(functools.partial(mlp_forward_body, route, base), grid=(co...  29.3 us
    pallas_call x2, Pallas kernels, attention_forward(): pl.pallas_call(functools.partial(attention_forward_body, route, base), gr...  26.8 us
  transfers between devices with their start and end apart: 82, of which 36 were waited for; matrix products, arithmetic and copies ran while one was open for 16% of the time, Pallas kernels for 30%

profile of v3, /device:TPU:0, one launch (start us, length us, event | category | flops | bytes accessed | tf_op | source)
XLA Modules:
  0.0 593.5 jit_solution(11231927117048384036)
XLA Ops:
  10.5 4.0 collective-permute-start.4
  20.7 4.1 convert_element_type.750.final_ref
  33.1 4.6 collective-permute-done.6
  42.7 11.5 %collective-permute-done.9 = bf16[2,2,48,768]{3,2,1,0:T(8,128)(2,1)S(1)} collective-permute-done((bf16[2,2,48,768]{3,2,1,0:T(8,128)(2,1)S(1)}, bf16[2,2,48,768]{3,2,1,0:T(8,128)(2,1)S(1)}, u32[]{:S(2)}, u32[]{:S(2)}) %collective-permute-start.9) | collective-permute-done | bytes 294944 | tf_op jit(solution)/shard_map/ppermute | solution.py:125
  66.2 14.2 %collective-permute-done.12 = bf16[2,2,2,48,768]{4,3,2,1,0:T(8,128)(2,1)S(1)} collective-permute-done((bf16[2,2,2,48,768]{4,3,2,1,0:T(8,128)(2,1)S(1)}, bf16[2,2,2,48,768]{4,3,2,1,0:T(8,128)(2,1)S(1)}, u32[]{:S(2)}, u32[]{:S(2)}) %collective-permute-start.12) | collective-permute-done | bytes 589856 | tf_op jit(solution)/shard_map/ppermute | solution.py:129
  90.6 7.4 %collective-permute-done.18 = bf16[2,1,48,768]{3,2,1,0:T(8,128)(2,1)S(1)} collective-permute-done((bf16[2,1,48,768]{3,2,1,0:T(8,128)(2,1)S(1)}, bf16[2,1,48,768]{3,2,1,0:T(8,128)(2,1)S(1)}, u32[]{:S(2)}, u32[]{:S(2)}) %collective-permute-start.18) | collective-permute-done | bytes 147488 | tf_op jit(solution)/shard_map/ppermute | solution.py:125
  103.6 7.9 %collective-permute-start.25 = (bf16[8,2,2,48,768]{4,3,2,1,0:T(8,128)(2,1)}, bf16[8,2,2,48,768]{4,3,2,1,0:T(8,128)(2,1)}, u32[]{:S(2)}, u32[]{:S(2)}) collective-permute-start(bf16[8,2,2,48,768]{4,3,2,1,0:T(8,128)(2,1)} %pad_maximum_fusion.refs_0_), channel_id=1, source_target_pairs={{0,1},{1,0},{2,3},{3,2},{4,5},{5,4},{6,7},{7,6},{8,9},{9,8},{10,11... | collective-permute-start | bytes 7077896 | tf_op jit(solution)/shard_map/ppermute | solution.py:107
  115.9 6.1 %collective-permute-done.21 = f32[2,8,12,192]{3,1,2,0:T(8,128)} collective-permute-done((f32[2,8,12,192]{3,1,2,0:T(8,128)}, f32[2,8,12,192]{3,1,2,0:T(8,128)}, u32[]{:S(2)}, u32[]{:S(2)}) %collective-permute-start.21) | collective-permute-done | bytes 147488 | tf_op jit(solution)/shard_map/ppermute | solution.py:129
  150.8 13.8 %collective-permute-done.26 = bf16[2,2,48,768]{3,2,1,0:T(8,128)(2,1)S(1)} collective-permute-done((bf16[2,2,48,768]{3,2,1,0:T(8,128)(2,1)}, bf16[2,2,48,768]{3,2,1,0:T(8,128)(2,1)S(1)}, u32[]{:S(2)}, u32[]{:S(2)}) %collective-permute-start.26) | collective-permute-done | bytes 294944 | tf_op jit(solution)/shard_map/ppermute | solution.py:125
  171.3 13.5 %attention_forward.2 = (f32[512,768]{1,0:T(8,128)}, bf16[512,768]{1,0:T(8,128)(2,1)}, bf16[4,512,576]{2,1,0:T(8,128)(2,1)}, bf16[4,3,2,256,256]{4,3,2,1,0:T(8,12...) custom-call(s32[197]{0:T(256)} %concatenate.83.table, f32[512,768]{1,0:T(8,128)} %copy-done.6, ...), custom_call_target="tpu_custom_call" | custom-call | flops 2818572288 | bytes 16515072 | tf_op jit(solution)/shard_map/attention_forward/pallas_call | solution.py:741
  188.3 14.5 %mlp_forward.2 = (f32[512,768]{1,0:T(8,128)}, bf16[512,768]{1,0:T(8,128)(2,1)}, f32[4,512,768]{2,1,0:T(8,128)}, f32[512,768]{1,0:T(8,128)}) custom-call(s32[197]{0:T(256)} %concatenate.83.table, f32[512,768]{1,0:T(8,128)} %get-tuple-element.416.x_ref, f32[2,3,768]{2,1,0:T(4,128)} %get-tuple-element.417.mod_ref, f32[4,47,192]{2,1,0:T(8,128)} %bitcast.470, ...), custom_call_target="tpu_custom_call" | custom-call | flops 4831838208 | bytes 21233664 | tf_op jit(solution)/shard_map/mlp_forward/pallas_call | solution.py:775
  206.3 13.3 %attention_forward.3 = (f32[512,768]{1,0:T(8,128)}, bf16[512,768]{1,0:T(8,128)(2,1)}, bf16[4,512,576]{2,1,0:T(8,128)(2,1)}, bf16[4,3,2,256,256]{4,3,2,1,0:T(8,12...) custom-call(s32[197]{0:T(256)} %concatenate.83.table, f32[512,768]{1,0:T(8,128)} %get-tuple-element.398.x_ref, ...), custom_call_target="tpu_custom_call" | custom-call | flops 2818572288 | bytes 16515072 | tf_op jit(solution)/shard_map/attention_forward/pallas_call | solution.py:741
  219.7 14.1 %collective-permute-done.35.refs_1_ = bf16[8,2,2,48,768]{4,3,2,1,0:T(8,128)(2,1)} collective-permute-done((bf16[8,2,2,48,768]{4,3,2,1,0:T(8,128)(2,1)S(1)}, bf16[8,2,2,48,768]{4,3,2,1,0:T(8,128)(2,1)}, u32[]{:S(2)}, u32[]{:S(2)}) %collective-permute-start.35) | collective-permute-done | bytes 2359328 | tf_op jit(solution)/shard_map/ppermute | solution.py:121
  240.2 14.8 %mlp_forward.3 = (f32[512,768]{1,0:T(8,128)}, bf16[512,768]{1,0:T(8,128)(2,1)}, f32[4,512,768]{2,1,0:T(8,128)}, f32[512,768]{1,0:T(8,128)}) custom-call(s32[197]{0:T(256)} %concatenate.83.table, f32[512,768]{1,0:T(8,128)} %get-tuple-element.380.x_ref, f32[2,3,768]{2,1,0:T(4,128)} %get-tuple-element.381.mod_ref, f32[4,47,192]{2,1,0:T(8,128)} %bitcast.472, ...), custom_call_target="tpu_custom_call" | custom-call | flops 4831838208 | bytes 21233664 | tf_op jit(solution)/shard_map/mlp_forward/pallas_call | solution.py:775
  259.7 21.9 %mlp_backward.2 = (f32[512,768]{1,0:T(8,128)}, f32[2,3,768]{2,1,0:T(4,128)}, f32[4,1,768]{2,1,0:T(1,128)}, f32[1,768]{1,0:T(1,128)}, bf16[2,8,2,2,48,768]{5,4,3,...) custom-call(s32[197]{0:T(256)} %concatenate.83.table, f32[512,768]{1,0:T(8,128)} %copy-done.34, ...), custom_call_target="tpu_custom_call" | custom-call | flops 9663676416 | bytes 34603008 | tf_op jit(solution)/shard_map/mlp_backward/pallas_call | solution.py:810
  282.2 20.8 %attention_backward.2 = (f32[512,768]{1,0:T(8,128)}, f32[2,3,768]{2,1,0:T(4,128)}, f32[4,1,576]{2,1,0:T(1,128)}, f32[1,768]{1,0:T(1,128)}, bf16[2,8,2,1,48,768]{...) custom-call(s32[197]{0:T(256)} %concatenate.83.table, f32[512,768]{1,0:T(8,128)} %get-tuple-element.397.dx_ref, ...), custom_call_target="tpu_custom_call" | custom-call | flops 5838471168 | bytes 25165824 | tf_op jit(solution)/shard_map/attention_backward/pallas_call | solution.py:854
  306.9 22.3 %mlp_backward.3 = (f32[512,768]{1,0:T(8,128)}, f32[2,3,768]{2,1,0:T(4,128)}, f32[4,1,768]{2,1,0:T(1,128)}, f32[1,768]{1,0:T(1,128)}, bf16[2,8,2,2,48,768]{5,4,3,...) custom-call(s32[197]{0:T(256)} %concatenate.83.table, f32[512,768]{1,0:T(8,128)} %get-tuple-element.415.dx_ref, ...), custom_call_target="tpu_custom_call" | custom-call | flops 9663676416 | bytes 34603008 | tf_op jit(solution)/shard_map/mlp_backward/pallas_call | solution.py:810
  329.2 5.9 collective-permute-done.41
  343.5 20.7 %attention_backward.3 = (f32[512,768]{1,0:T(8,128)}, f32[2,3,768]{2,1,0:T(4,128)}, f32[4,1,576]{2,1,0:T(1,128)}, f32[1,768]{1,0:T(1,128)}, bf16[2,8,2,1,48,768]{...) custom-call(s32[197]{0:T(256)} %concatenate.83.table, f32[512,768]{1,0:T(8,128)} %get-tuple-element.434.dx_ref, ...), custom_call_target="tpu_custom_call" | custom-call | flops 5838471168 | bytes 25165824 | tf_op jit(solution)/shard_map/attention_backward/pallas_call | solution.py:854
  365.2 5.0 collective-permute-done.44
  386.8 4.3 collective-permute-done.51
  395.1 8.9 %collective-permute-done.52 = bf16[2,2,2,48,768]{4,3,2,1,0:T(8,128)(2,1)S(1)} collective-permute-done((bf16[2,2,2,48,768]{4,3,2,1,0:T(8,128)(2,1)S(1)}, bf16[2,2,2,48,768]{4,3,2,1,0:T(8,128)(2,1)S(1)}, u32[]{:S(2)}, u32[]{:S(2)}) %collective-permute-start.52) | collective-permute-done | bytes 589856 | tf_op jit(solution)/shard_map/ppermute | solution.py:129
  419.4 17.7 %collective-permute-done.54 = bf16[4,32,768]{2,1,0:T(8,128)(2,1)S(1)} collective-permute-done((bf16[4,32,768]{2,1,0:T(8,128)(2,1)S(1)}, bf16[4,32,768]{2,1,0:T(8,128)(2,1)S(1)}, u32[]{:S(2)}, u32[]{:S(2)}) %collective-permute-start.54) | collective-permute-done | bytes 196640 | tf_op jit(solution)/shard_map/ppermute | solution.py:111
  447.1 9.5 %collective-permute-done.61 = f32[24,768]{1,0:T(8,128)S(1)} collective-permute-done((f32[24,768]{1,0:T(8,128)S(1)}, f32[24,768]{1,0:T(8,128)S(1)}, u32[]{:S(2)}, u32[]{:S(2)}) %collective-permute-start.61) | collective-permute-done | bytes 73760 | tf_op jit(solution)/shard_map/ppermute | solution.py:103
  477.1 8.6 %collective-permute-done.62 = bf16[2,2,2,48,768]{4,3,2,1,0:T(8,128)(2,1)S(1)} collective-permute-done((bf16[2,2,2,48,768]{4,3,2,1,0:T(8,128)(2,1)S(1)}, bf16[2,2,2,48,768]{4,3,2,1,0:T(8,128)(2,1)S(1)}, u32[]{:S(2)}, u32[]{:S(2)}) %collective-permute-start.62) | collective-permute-done | bytes 589856 | tf_op jit(solution)/shard_map/ppermute | solution.py:129
  500.7 9.2 %modes_backward.1 = (f32[2,6,96,192]{3,2,1,0:T(8,128)}, f32[64,96]{1,0:T(8,128)}, f32[1,1]{1,0:T(1,128)}, f32[1536,768]{1,0:T(8,128)}, f32[64,768]{1,0:T(8,128)}, /*index=5*/f32[1,1]{1,0:T(1,128)}) custom-call(bf16[1024,768]{1,0:T(8,128)(2,1)} %bitcast.487, s32[64,2]{1,0:T(8,128)} %copy.331.at_ref, bf16[64,96]{1,0:T(8,128)(2,1)} %copy-done.76, ...), custom_call_target="tpu_custom_call" | custom-call | tf_op jit(solution)/shard_map/modes_backward/pallas_call | solution.py:1190
  510.0 4.6 collective-permute-done.69
  524.7 4.9 collective-permute-done.74
  529.7 5.1 condition_back.1
  561.1 13.4 %adam_final.1 = (f32[1552,768]{1,0:T(8,128)}, f32[1552,768]{1,0:T(8,128)}, f32[1552,768]{1,0:T(8,128)}) custom-call(f32[1]{0:T(128)} %bitcast.171.clip_ref, f32[1536,768]{1,0:T(8,128)} %get-tuple-element.502.grad_ref, f32[16,768]{1,0:T(8,128)} %slice.652.head_ref, f32[1552,768]{1,0:T(8,128)} %bitcast.483, f32[1552,768]{1,0:T(8,128)} %bitcast.485, ...), custom_call_target="tpu_custom_call" | custom-call | tf_op jit(solution)/shard_map/adam_final/pallas_call | solution.py:1369
  574.5 4.1 adam_rest.1
  580.9 11.3 %adam_blocks.1 = (f32[2,13,96,192]{3,2,1,0:T(8,128)}, f32[2,13,96,192]{3,2,1,0:T(8,128)}, f32[2,13,96,192]{3,2,1,0:T(8,128)}, f32[2,5,192,96]{3,2,1,0:T(8,128)},...) custom-call(f32[1]{0:T(128)} %bitcast.171.clip_ref, s32[2]{0:T(128)} %copy-done.33, ...), custom_call_target="tpu_custom_call" | custom-call | tf_op jit(solution)/shard_map/adam_blocks/pallas_call | solution.py:1330
  (526 shorter events, 242.5 us)
Async XLA Ops:
  14.6 18.4 %collective-permute-start.1 = (bf16[2,1,48,768]{3,2,0,1:T(8,128)(2,1)S(1)}, bf16[2,1,48,768]{3,2,0,1:T(8,128)(2,1)S(1)}, u32[]{:S(2)}, u32[]{:S(2)}) collective-permute-start(bf16[2,1,48,768]{3,2,0,1:T(8,128)(2,1)S(1)} %get-tuple-element.281), channel_id=1, source_target_pairs={{0,16},{4,20},{8,24},{12,28},{16,0},{20,4},{24,8},{28,12},{1,17},{... | collective-permute-start | bytes 442376 | tf_op jit(solution)/shard_map/ppermute | solution.py:125
  14.6 18.4 %collective-permute-start.2 = (bf16[2,1,48,768]{3,2,0,1:T(8,128)(2,1)S(1)}, bf16[2,1,48,768]{3,2,0,1:T(8,128)(2,1)S(1)}, u32[]{:S(2)}, u32[]{:S(2)}) collective-permute-start(bf16[2,1,48,768]{3,2,0,1:T(8,128)(2,1)S(1)} %get-tuple-element.281), channel_id=1, source_target_pairs={{0,8},{4,12},{8,0},{12,4},{16,24},{20,28},{24,16},{28,20},{1,9},{5... | collective-permute-start | bytes 442376 | tf_op jit(solution)/shard_map/ppermute | solution.py:129
  57.2 24.3 %collective-permute-start.13 = (bf16[8,2,1,48,768]{4,3,2,1,0:T(8,128)(2,1)}, bf16[8,2,1,48,768]{4,3,2,1,0:T(8,128)(2,1)}, u32[]{:S(2)}, u32[]{:S(2)}) collective-permute-start(bf16[8,2,1,48,768]{4,3,2,1,0:T(8,128)(2,1)} %copy-done.82), channel_id=1, source_target_pairs={{0,4},{1,3},{2,6},{3,1},{4,0},{5,7},{6,2},{7,5},{8,12},{9,11},{10,... | collective-permute-start | bytes 3538952 | tf_op jit(solution)/shard_map/ppermute | solution.py:121
  84.2 18.3 %collective-permute-start.19 = (bf16[8,2,1,48,768]{4,3,2,1,0:T(8,128)(2,1)}, bf16[8,2,1,48,768]{4,3,2,1,0:T(8,128)(2,1)}, u32[]{:S(2)}, u32[]{:S(2)}) collective-permute-start(bf16[8,2,1,48,768]{4,3,2,1,0:T(8,128)(2,1)} %collective-permute-done.13.refs_1_), channel_id=1, source_target_pairs={{0,1},{1,0},{2,3},{3,2},{4,5},{5,4},{6,7},{7,6},{8,9},{9,8},{10,11... | collective-permute-start | bytes 3538952 | tf_op jit(solution)/shard_map/ppermute | solution.py:107
  102.5 33.6 %collective-permute-start.20 = (bf16[8,2,2,48,768]{4,3,2,1,0:T(8,128)(2,1)}, bf16[8,2,2,48,768]{4,3,2,1,0:T(8,128)(2,1)}, u32[]{:S(2)}, u32[]{:S(2)}) collective-permute-start(bf16[8,2,2,48,768]{4,3,2,1,0:T(8,128)(2,1)} %pad_maximum_fusion.refs_0_), channel_id=1, source_target_pairs={{0,4},{1,3},{2,6},{3,1},{4,0},{5,7},{6,2},{7,5},{8,12},{9,11},{10,... | collective-permute-start | bytes 7077896 | tf_op jit(solution)/shard_map/ppermute | solution.py:121
  103.6 32.5 %collective-permute-start.25 = (bf16[8,2,2,48,768]{4,3,2,1,0:T(8,128)(2,1)}, bf16[8,2,2,48,768]{4,3,2,1,0:T(8,128)(2,1)}, u32[]{:S(2)}, u32[]{:S(2)}) collective-permute-start(bf16[8,2,2,48,768]{4,3,2,1,0:T(8,128)(2,1)} %pad_maximum_fusion.refs_0_), channel_id=1, source_target_pairs={{0,1},{1,0},{2,3},{3,2},{4,5},{5,4},{6,7},{7,6},{8,9},{9,8},{10,11... | collective-permute-start | bytes 7077896 | tf_op jit(solution)/shard_map/ppermute | solution.py:107
  136.1 32.5 %collective-permute-start.29 = (bf16[8,2,2,48,768]{4,3,2,1,0:T(8,128)(2,1)}, bf16[8,2,2,48,768]{4,3,2,1,0:T(8,128)(2,1)}, u32[]{:S(2)}, u32[]{:S(2)}) collective-permute-start(bf16[8,2,2,48,768]{4,3,2,1,0:T(8,128)(2,1)} %collective-permute-done.20.refs_1_), channel_id=1, source_target_pairs={{0,1},{1,0},{2,3},{3,2},{4,5},{5,4},{6,7},{7,6},{8,9},{9,8},{10,11... | collective-permute-start | bytes 7077896 | tf_op jit(solution)/shard_map/ppermute | solution.py:107
  145.2 21.3 %collective-permute-start.28 = (bf16[4,2,1,48,768]{4,3,1,2,0:T(8,128)(2,1)}, bf16[4,2,1,48,768]{4,3,1,2,0:T(8,128)(2,1)S(1)}, u32[]{:S(2)}, u32[]{:S(2)}) collective-permute-start(bf16[4,2,1,48,768]{4,3,1,2,0:T(8,128)(2,1)} %pad_maximum_fusion.11), channel_id=1, source_target_pairs={{0,2},{1,5},{2,0},{3,7},{4,6},{5,1},{6,4},{7,3},{8,10},{9,13},{10,... | collective-permute-start | bytes 1769480 | tf_op jit(solution)/shard_map/ppermute | solution.py:116
  146.9 17.7 %collective-permute-start.26 = (bf16[2,2,48,768]{3,2,1,0:T(8,128)(2,1)}, bf16[2,2,48,768]{3,2,1,0:T(8,128)(2,1)S(1)}, u32[]{:S(2)}, u32[]{:S(2)}) collective-permute-start(bf16[2,2,48,768]{3,2,1,0:T(8,128)(2,1)} %get-tuple-element.314), channel_id=1, source_target_pairs={{0,16},{4,20},{8,24},{12,28},{16,0},{20,4},{24,8},{28,12},{1,17},{... | collective-permute-start | bytes 884744 | tf_op jit(solution)/shard_map/ppermute | solution.py:125
  168.6 18.1 %collective-permute-start.31 = (bf16[8,2,1,48,768]{4,3,1,2,0:T(8,128)(2,1)}, bf16[8,2,1,48,768]{4,3,1,2,0:T(8,128)(2,1)}, u32[]{:S(2)}, u32[]{:S(2)}) collective-permute-start(bf16[8,2,1,48,768]{4,3,1,2,0:T(8,128)(2,1)} %pad_maximum_fusion.3), channel_id=1, source_target_pairs={{0,4},{1,3},{2,6},{3,1},{4,0},{5,7},{6,2},{7,5},{8,12},{9,11},{10,... | collective-permute-start | bytes 3538952 | tf_op jit(solution)/shard_map/ppermute | solution.py:121
  204.7 29.0 %collective-permute-start.35 = (bf16[8,2,2,48,768]{4,3,2,1,0:T(8,128)(2,1)S(1)}, bf16[8,2,2,48,768]{4,3,2,1,0:T(8,128)(2,1)}, u32[]{:S(2)}, u32[]{:S(2)}) collective-permute-start(bf16[8,2,2,48,768]{4,3,2,1,0:T(8,128)(2,1)S(1)} %pad_maximum_fusion.1.refs_0_), channel_id=1, source_target_pairs={{0,4},{1,3},{2,6},{3,1},{4,0},{5,7},{6,2},{7,5},{8,12},{9,11},{10,... | collective-permute-start | bytes 7077896 | tf_op jit(solution)/shard_map/ppermute | solution.py:121
  206.3 27.4 %collective-permute-start.36 = (bf16[8,2,2,48,768]{4,3,2,1,0:T(8,128)(2,1)S(1)}, bf16[8,2,2,48,768]{4,3,2,1,0:T(8,128)(2,1)}, u32[]{:S(2)}, u32[]{:S(2)}) collective-permute-start(bf16[8,2,2,48,768]{4,3,2,1,0:T(8,128)(2,1)S(1)} %pad_maximum_fusion.1.refs_0_), channel_id=1, source_target_pairs={{0,1},{1,0},{2,3},{3,2},{4,5},{5,4},{6,7},{7,6},{8,9},{9,8},{10,11... | collective-permute-start | bytes 7077896 | tf_op jit(solution)/shard_map/ppermute | solution.py:107
  238.6 19.6 %collective-permute-start.38 = (bf16[2,6,96,192]{3,2,1,0:T(8,128)(2,1)S(1)}, bf16[2,6,96,192]{3,2,1,0:T(8,128)(2,1)S(1)}, u32[]{:S(2)}, u32[]{:S(2)}) collective-permute-start(bf16[2,6,96,192]{3,2,1,0:T(8,128)(2,1)S(1)} %get-tuple-element.366), channel_id=1, source_target_pairs={{0,2},{1,3},{2,0},{3,1},{4,6},{5,7},{6,4},{7,5},{8,10},{9,11},{10,... | collective-permute-start | bytes 1327112 | tf_op jit(solution)/shard_map/ppermute | solution.py:103
  259.7 21.9 %collective-permute-start.39 = (bf16[2,2,6,96,192]{4,3,2,1,0:T(8,128)(2,1)S(1)}, bf16[2,2,6,96,192]{4,3,2,1,0:T(8,128)(2,1)S(1)}, u32[]{:S(2)}, u32[]{:S(2)}) collective-permute-start(bf16[2,2,6,96,192]{4,3,2,1,0:T(8,128)(2,1)S(1)} %pad_maximum_fusion.5), channel_id=1, source_target_pairs={{0,1},{1,0},{2,3},{3,2},{4,5},{5,4},{6,7},{7,6},{8,9},{9,8},{10,11... | collective-permute-start | bytes 2654216 | tf_op jit(solution)/shard_map/ppermute | solution.py:107
  281.6 21.4 %collective-permute-start.40 = (bf16[2,8,2,2,48,768]{5,4,3,2,1,0:T(8,128)(2,1)}, bf16[2,8,2,2,48,768]{5,4,3,2,1,0:T(8,128)(2,1)}, u32[]{:S(2)}, u32[]{:S(2)}) collective-permute-start(bf16[2,8,2,2,48,768]{5,4,3,2,1,0:T(8,128)(2,1)} %get-tuple-element.396), channel_id=1, source_target_pairs={{0,1},{1,0},{2,3},{3,2},{4,5},{5,4},{6,7},{7,6},{8,9},{9,8},{10,11... | collective-permute-start | bytes 14155784 | tf_op jit(solution)/shard_map/ppermute | solution.py:107
  306.1 29.0 %collective-permute-start.41 = (bf16[8,2,2,48,768]{4,3,2,1,0:T(8,128)(2,1)S(1)}, bf16[8,2,2,48,768]{4,3,2,1,0:T(8,128)(2,1)}, u32[]{:S(2)}, u32[]{:S(2)}) collective-permute-start(bf16[8,2,2,48,768]{4,3,2,1,0:T(8,128)(2,1)S(1)} %fusion), channel_id=1, source_target_pairs={{0,4},{1,3},{2,6},{3,1},{4,0},{5,7},{6,2},{7,5},{8,12},{9,11},{10,... | collective-permute-start | bytes 7077896 | tf_op jit(solution)/shard_map/ppermute | solution.py:121
  306.9 31.7 %collective-permute-start.42 = (bf16[2,8,2,1,48,768]{5,4,2,3,1,0:T(8,128)(2,1)}, bf16[2,8,2,1,48,768]{5,4,2,3,1,0:T(8,128)(2,1)}, u32[]{:S(2)}, u32[]{:S(2)}) collective-permute-start(bf16[2,8,2,1,48,768]{5,4,2,3,1,0:T(8,128)(2,1)} %bitcast.73), channel_id=1, source_target_pairs={{0,1},{1,0},{2,3},{3,2},{4,5},{5,4},{6,7},{7,6},{8,9},{9,8},{10,11... | collective-permute-start | bytes 7077896 | tf_op jit(solution)/shard_map/ppermute | solution.py:107
  341.3 31.0 %collective-permute-start.43 = (bf16[2,8,2,2,48,768]{5,4,3,2,1,0:T(8,128)(2,1)}, bf16[2,8,2,2,48,768]{5,4,3,2,1,0:T(8,128)(2,1)}, u32[]{:S(2)}, u32[]{:S(2)}) collective-permute-start(bf16[2,8,2,2,48,768]{5,4,3,2,1,0:T(8,128)(2,1)} %get-tuple-element.433), channel_id=1, source_target_pairs={{0,1},{1,0},{2,3},{3,2},{4,5},{5,4},{6,7},{7,6},{8,9},{9,8},{10,11... | collective-permute-start | bytes 14155784 | tf_op jit(solution)/shard_map/ppermute | solution.py:107
  341.3 28.9 %collective-permute-start.44 = (bf16[4,2,2,48,768]{4,3,2,1,0:T(8,128)(2,1)}, bf16[4,2,2,48,768]{4,3,2,1,0:T(8,128)(2,1)}, u32[]{:S(2)}, u32[]{:S(2)}) collective-permute-start(bf16[4,2,2,48,768]{4,3,2,1,0:T(8,128)(2,1)} %fusion.5), channel_id=1, source_target_pairs={{0,2},{1,5},{2,0},{3,7},{4,6},{5,1},{6,4},{7,3},{8,10},{9,13},{10,... | collective-permute-start | bytes 3538952 | tf_op jit(solution)/shard_map/ppermute | solution.py:116
  341.9 33.6 %collective-permute-start.45 = (bf16[8,2,1,48,768]{4,3,1,2,0:T(8,128)(2,1)}, bf16[8,2,1,48,768]{4,3,1,2,0:T(8,128)(2,1)}, u32[]{:S(2)}, u32[]{:S(2)}) collective-permute-start(bf16[8,2,1,48,768]{4,3,1,2,0:T(8,128)(2,1)} %bitcast.511), channel_id=1, source_target_pairs={{0,4},{1,3},{2,6},{3,1},{4,0},{5,7},{6,2},{7,5},{8,12},{9,11},{10,... | collective-permute-start | bytes 3538952 | tf_op jit(solution)/shard_map/ppermute | solution.py:121
  375.5 30.8 %collective-permute-start.47 = (bf16[2,8,2,1,48,768]{5,4,2,3,1,0:T(8,128)(2,1)S(1)}, bf16[2,8,2,1,48,768]{5,4,2,3,1,0:T(8,128)(2,1)S(1)}, u32[]{:S(2)}, u32[]{:S(2)}) collective-permute-start(bf16[2,8,2,1,48,768]{5,4,2,3,1,0:T(8,128)(2,1)S(1)} %bitcast.549), channel_id=1, source_target_pairs={{0,1},{1,0},{2,3},{3,2},{4,5},{5,4},{6,7},{7,6},{8,9},{9,8},{10,11... | collective-permute-start | bytes 7077896 | tf_op jit(solution)/shard_map/ppermute | solution.py:107
  377.7 30.3 %collective-permute-start.46 = (bf16[8,2,2,48,768]{4,3,2,1,0:T(8,128)(2,1)S(1)}, bf16[8,2,2,48,768]{4,3,2,1,0:T(8,128)(2,1)S(1)}, u32[]{:S(2)}, u32[]{:S(2)}) collective-permute-start(bf16[8,2,2,48,768]{4,3,2,1,0:T(8,128)(2,1)S(1)} %fusion.1), channel_id=1, source_target_pairs={{0,4},{1,3},{2,6},{3,1},{4,0},{5,7},{6,2},{7,5},{8,12},{9,11},{10,... | collective-permute-start | bytes 7077896 | tf_op jit(solution)/shard_map/ppermute | solution.py:121
  409.7 29.8 %collective-permute-start.56 = (bf16[8,2,1,48,768]{4,3,1,2,0:T(8,128)(2,1)}, bf16[8,2,1,48,768]{4,3,1,2,0:T(8,128)(2,1)}, u32[]{:S(2)}, u32[]{:S(2)}) collective-permute-start(bf16[8,2,1,48,768]{4,3,1,2,0:T(8,128)(2,1)} %bitcast.101), channel_id=1, source_target_pairs={{0,4},{1,3},{2,6},{3,1},{4,0},{5,7},{6,2},{7,5},{8,12},{9,11},{10,... | collective-permute-start | bytes 3538952 | tf_op jit(solution)/shard_map/ppermute | solution.py:121
  411.0 26.2 %collective-permute-start.53 = (bf16[4,2,1,48,768]{4,3,1,2,0:T(8,128)(2,1)}, bf16[4,2,1,48,768]{4,3,1,2,0:T(8,128)(2,1)S(1)}, u32[]{:S(2)}, u32[]{:S(2)}) collective-permute-start(bf16[4,2,1,48,768]{4,3,1,2,0:T(8,128)(2,1)} %bitcast.99), channel_id=1, source_target_pairs={{0,2},{1,5},{2,0},{3,7},{4,6},{5,1},{6,4},{7,3},{8,10},{9,13},{10,... | collective-permute-start | bytes 1769480 | tf_op jit(solution)/shard_map/ppermute | solution.py:116
  413.7 25.8 %collective-permute-start.57 = (bf16[2,2,48,768]{3,2,1,0:T(8,128)(2,1)}, bf16[2,2,48,768]{3,2,1,0:T(8,128)(2,1)}, u32[]{:S(2)}, u32[]{:S(2)}) collective-permute-start(bf16[2,2,48,768]{3,2,1,0:T(8,128)(2,1)} %fusion.21), channel_id=1, source_target_pairs={{0,16},{4,20},{8,24},{12,28},{16,0},{20,4},{24,8},{28,12},{1,17},{... | collective-permute-start | bytes 884744 | tf_op jit(solution)/shard_map/ppermute | solution.py:125
  415.9 21.2 %collective-permute-start.54 = (bf16[4,32,768]{2,1,0:T(8,128)(2,1)S(1)}, bf16[4,32,768]{2,1,0:T(8,128)(2,1)S(1)}, u32[]{:S(2)}, u32[]{:S(2)}) collective-permute-start(bf16[4,32,768]{2,1,0:T(8,128)(2,1)S(1)} %pad_maximum_fusion.22), channel_id=1, source_target_pairs={{0,4},{4,0},{8,12},{12,8},{16,20},{20,16},{24,28},{28,24},{1,5},{5... | collective-permute-start | bytes 589832 | tf_op jit(solution)/shard_map/ppermute | solution.py:111
  439.4 21.5 %collective-permute-start.58 = (bf16[4,2,2,48,768]{4,3,2,1,0:T(8,128)(2,1)}, bf16[4,2,2,48,768]{4,3,2,1,0:T(8,128)(2,1)}, u32[]{:S(2)}, u32[]{:S(2)}) collective-permute-start(bf16[4,2,2,48,768]{4,3,2,1,0:T(8,128)(2,1)} %fusion.4), channel_id=1, source_target_pairs={{0,2},{1,5},{2,0},{3,7},{4,6},{5,1},{6,4},{7,3},{8,10},{9,13},{10,... | collective-permute-start | bytes 3538952 | tf_op jit(solution)/shard_map/ppermute | solution.py:116
  467.1 18.6 %collective-permute-start.62 = (bf16[2,2,2,48,768]{4,3,2,1,0:T(8,128)(2,1)S(1)}, bf16[2,2,2,48,768]{4,3,2,1,0:T(8,128)(2,1)S(1)}, u32[]{:S(2)}, u32[]{:S(2)}) collective-permute-start(bf16[2,2,2,48,768]{4,3,2,1,0:T(8,128)(2,1)S(1)} %fusion.13), channel_id=1, source_target_pairs={{0,8},{4,12},{8,0},{12,4},{16,24},{20,28},{24,16},{28,20},{1,9},{5... | collective-permute-start | bytes 1769480 | tf_op jit(solution)/shard_map/ppermute | solution.py:129
  470.1 17.9 %collective-permute-start.65 = (bf16[4,2,1,48,768]{4,3,1,2,0:T(8,128)(2,1)S(1)}, bf16[4,2,1,48,768]{4,3,1,2,0:T(8,128)(2,1)S(1)}, u32[]{:S(2)}, u32[]{:S(2)}) collective-permute-start(bf16[4,2,1,48,768]{4,3,1,2,0:T(8,128)(2,1)S(1)} %bitcast.522), channel_id=1, source_target_pairs={{0,2},{1,5},{2,0},{3,7},{4,6},{5,1},{6,4},{7,3},{8,10},{9,13},{10,... | collective-permute-start | bytes 1769480 | tf_op jit(solution)/shard_map/ppermute | solution.py:116
  497.8 17.9 %collective-permute-start.70 = (bf16[2,2,48,768]{3,2,1,0:T(8,128)(2,1)}, bf16[2,2,48,768]{3,2,1,0:T(8,128)(2,1)S(1)}, u32[]{:S(2)}, u32[]{:S(2)}) collective-permute-start(bf16[2,2,48,768]{3,2,1,0:T(8,128)(2,1)} %fusion.20), channel_id=1, source_target_pairs={{0,16},{4,20},{8,24},{12,28},{16,0},{20,4},{24,8},{28,12},{1,17},{... | collective-permute-start | bytes 884744 | tf_op jit(solution)/shard_map/ppermute | solution.py:125
  520.3 17.9 %collective-permute-start.75 = (bf16[2,1,48,768]{3,2,1,0:T(8,128)(2,1)S(1)}, bf16[2,1,48,768]{3,2,1,0:T(8,128)(2,1)S(1)}, u32[]{:S(2)}, u32[]{:S(2)}) collective-permute-start(bf16[2,1,48,768]{3,2,1,0:T(8,128)(2,1)S(1)} %fusion.31), channel_id=1, source_target_pairs={{0,16},{4,20},{8,24},{12,28},{16,0},{20,4},{24,8},{28,12},{1,17},{... | collective-permute-start | bytes 442376 | tf_op jit(solution)/shard_map/ppermute | solution.py:125
  546.5 32.8 %collective-permute-start.81 = (f32[6,48,768]{2,1,0:T(8,128)S(1)}, f32[6,48,768]{2,1,0:T(8,128)S(1)}, u32[]{:S(2)}, u32[]{:S(2)}) collective-permute-start(f32[6,48,768]{2,1,0:T(8,128)S(1)} %pad_maximum_fusion.7), channel_id=1, source_target_pairs={{0,1},{1,0},{2,3},{3,2},{4,5},{5,4},{6,7},{7,6},{8,9},{9,8},{10,11... | collective-permute-start | bytes 2654216 | tf_op jit(solution)/shard_map/ppermute | solution.py:107
  (141 other events, 1590.3 us)

commit v4 on v3

--- a/solution.py
+++ b/solution.py
@@ -129,6 +129,10 @@
     return lax.ppermute(v, "row", [(r, r ^ 2) for r in range(8)])
 
 
+def swap_across(v):
+    return lax.ppermute(v, ("row", "col"), [(d, d ^ 6) for d in range(32)])
+
+
 def swap_beyond(v):
     return lax.ppermute(v, "row", [(r, r ^ 6) for r in range(8)])
 
@@ -208,8 +212,9 @@
     if not place.direct:
         return lax.psum(value, ("row", "col"))
     total = jnp.broadcast_to(value, (8, 128))
-    for swap in (swap_far, swap_near, swap_y, swap_x, swap_core):
-        total = total + swap(total)
+    total = total + swap_far(total) + (swap_near(total) + swap_beyond(total))
+    total = total + swap_x(total) + (swap_y(total) + swap_across(total))
+    total = total + swap_core(total)
     return total[0, 0]
 
 
@@ -1587,12 +1592,11 @@
             ],
             axis=0,
         )
-        got, (near, shared, final_low) = stages.run(
+        got, (near, shared) = stages.run(
             a0.at_once(),
             [
                 (near_rows, own_block),
                 (functools.partial(gather_cols, place), mine),
-                (lambda v: v.astype(BF16), final_view[0]),
             ],
         )
         a0.along_at_once(got)
@@ -1630,8 +1634,9 @@
             total, blocks = lax.optimization_barrier((scatter_z(place, total), blocks))
             return blocks, scatter_x(place, total, samples)
 
-        got, ((blocks, total),) = stages.run(
-            b0.second(got[0]) + b0.core(), [(scatter_work, total, two)]
+        got, ((blocks, total), final_low) = stages.run(
+            b0.second(got[0]) + b0.core(),
+            [(scatter_work, total, two), (lambda v: v.astype(BF16), final_view[0])],
         )
         a1.along(blocks)
         core = got[1]

time: 603 us -> 602 us (level)
  starting transfers between devices: 98 us -> 106 us
  waiting for transfers between devices: 177 us -> 169 us
    ppermute x6, waiting for transfers between devices: 33.2 us -> 27.1 us  [swap_y(): return lax.ppermute(v, 'row', [(r, r ^ 1) for r in range(8)])]
    unnamed x202 -> x198, local copies, waits for them, and re-layouts: 13.8 us -> 13.8 us
  transfers between devices with their start and end apart: 82 -> 84, of which waited for: 36 -> 35; matrix products, arithmetic and copies ran while one was open for 16% -> 16% of each run, Pallas kernels for 30% -> 30%
where the time goes in v4:
time: 602 us; the launch traced here: 592 us
  Pallas kernels  190 us (32%)
  waiting for transfers between devices  169 us (28%)
  starting transfers between devices  106 us (18%)
  other arithmetic  77.3 us (13%)
  local copies, waits for them, and re-layouts  36.4 us (6%)
  between operations  9.14 us (2%)
    ppermute x15, waiting for transfers between devices, swap_near(): return lax.ppermute(v, 'row', [(r, r ^ 2) for r in range(8)])  52.3 us
    pallas_call x2, Pallas kernels, mlp_backward(): pl.pallas_call(functools.partial(mlp_backward_body, route), grid=(count,)...  44.2 us
    pallas_call x2, Pallas kernels, attention_backward(): pl.pallas_call(functools.partial(attention_backward_body, route), grid=(c...  41.5 us
    ppermute x15, waiting for transfers between devices, swap_far(): return lax.ppermute(v, 'row', [(r, r ^ 4) for r in range(8)])  38.4 us
    ppermute x15, starting transfers between devices, swap_far(): return lax.ppermute(v, 'row', [(r, r ^ 4) for r in range(8)])  38 us
    pallas_call x2, Pallas kernels, mlp_forward(): pl.pallas_call(functools.partial(mlp_forward_body, route, base), grid=(co...  29.3 us
    ppermute x6, waiting for transfers between devices, swap_y(): return lax.ppermute(v, 'row', [(r, r ^ 1) for r in range(8)])  27.1 us
    pallas_call x2, Pallas kernels, attention_forward(): pl.pallas_call(functools.partial(attention_forward_body, route, base), gr...  26.8 us
  transfers between devices with their start and end apart: 84, of which 35 were waited for; matrix products, arithmetic and copies ran while one was open for 16% of the time, Pallas kernels for 30%

profile of v4, /device:TPU:0, one launch (start us, length us, event | category | flops | bytes accessed | tf_op | source)
XLA Modules:
  0.0 591.8 jit_solution(4354267644272570818)
XLA Ops:
  10.5 4.0 collective-permute-start.4
  25.5 4.8 collective-permute-done.5
  32.3 5.6 collective-permute-done.6
  42.7 11.5 %collective-permute-done.9 = bf16[2,2,48,768]{3,2,1,0:T(8,128)(2,1)S(1)} collective-permute-done((bf16[2,2,48,768]{3,2,1,0:T(8,128)(2,1)S(1)}, bf16[2,2,48,768]{3,2,1,0:T(8,128)(2,1)S(1)}, u32[]{:S(2)}, u32[]{:S(2)}) %collective-permute-start.9) | collective-permute-done | bytes 294944 | tf_op jit(solution)/shard_map/ppermute | solution.py:125
  66.2 14.3 %collective-permute-done.12 = bf16[2,2,2,48,768]{4,3,2,1,0:T(8,128)(2,1)S(1)} collective-permute-done((bf16[2,2,2,48,768]{4,3,2,1,0:T(8,128)(2,1)S(1)}, bf16[2,2,2,48,768]{4,3,2,1,0:T(8,128)(2,1)S(1)}, u32[]{:S(2)}, u32[]{:S(2)}) %collective-permute-start.12) | collective-permute-done | bytes 589856 | tf_op jit(solution)/shard_map/ppermute | solution.py:129
  90.6 7.4 %collective-permute-done.18 = bf16[2,1,48,768]{3,2,1,0:T(8,128)(2,1)S(1)} collective-permute-done((bf16[2,1,48,768]{3,2,1,0:T(8,128)(2,1)S(1)}, bf16[2,1,48,768]{3,2,1,0:T(8,128)(2,1)S(1)}, u32[]{:S(2)}, u32[]{:S(2)}) %collective-permute-start.18) | collective-permute-done | bytes 147488 | tf_op jit(solution)/shard_map/ppermute | solution.py:125
  103.8 7.6 %collective-permute-start.25 = (bf16[8,2,2,48,768]{4,3,2,1,0:T(8,128)(2,1)}, bf16[8,2,2,48,768]{4,3,2,1,0:T(8,128)(2,1)}, u32[]{:S(2)}, u32[]{:S(2)}) collective-permute-start(bf16[8,2,2,48,768]{4,3,2,1,0:T(8,128)(2,1)} %pad_maximum_fusion.refs_0_), channel_id=1, source_target_pairs={{0,1},{1,0},{2,3},{3,2},{4,5},{5,4},{6,7},{7,6},{8,9},{9,8},{10,11... | collective-permute-start | bytes 7077896 | tf_op jit(solution)/shard_map/ppermute | solution.py:107
  115.8 6.1 %collective-permute-done.21 = f32[2,8,12,192]{3,1,2,0:T(8,128)} collective-permute-done((f32[2,8,12,192]{3,1,2,0:T(8,128)}, f32[2,8,12,192]{3,1,2,0:T(8,128)}, u32[]{:S(2)}, u32[]{:S(2)}) %collective-permute-start.21) | collective-permute-done | bytes 147488 | tf_op jit(solution)/shard_map/ppermute | solution.py:129
  122.9 4.0 collective-permute-start.22
  128.8 4.0 convert_element_type.750.final_ref
  150.8 13.8 %collective-permute-done.26 = bf16[2,2,48,768]{3,2,1,0:T(8,128)(2,1)S(1)} collective-permute-done((bf16[2,2,48,768]{3,2,1,0:T(8,128)(2,1)}, bf16[2,2,48,768]{3,2,1,0:T(8,128)(2,1)S(1)}, u32[]{:S(2)}, u32[]{:S(2)}) %collective-permute-start.26) | collective-permute-done | bytes 294944 | tf_op jit(solution)/shard_map/ppermute | solution.py:125
  171.5 13.5 %attention_forward.2 = (f32[512,768]{1,0:T(8,128)}, bf16[512,768]{1,0:T(8,128)(2,1)}, bf16[4,512,576]{2,1,0:T(8,128)(2,1)}, bf16[4,3,2,256,256]{4,3,2,1,0:T(8,12...) custom-call(s32[197]{0:T(256)} %concatenate.83.table, f32[512,768]{1,0:T(8,128)} %copy-done.6, ...), custom_call_target="tpu_custom_call" | custom-call | flops 2818572288 | bytes 16515072 | tf_op jit(solution)/shard_map/attention_forward/pallas_call | solution.py:746
  188.3 14.5 %mlp_forward.2 = (f32[512,768]{1,0:T(8,128)}, bf16[512,768]{1,0:T(8,128)(2,1)}, f32[4,512,768]{2,1,0:T(8,128)}, f32[512,768]{1,0:T(8,128)}) custom-call(s32[197]{0:T(256)} %concatenate.83.table, f32[512,768]{1,0:T(8,128)} %get-tuple-element.416.x_ref, f32[2,3,768]{2,1,0:T(4,128)} %get-tuple-element.417.mod_ref, f32[4,47,192]{2,1,0:T(8,128)} %bitcast.470, ...), custom_call_target="tpu_custom_call" | custom-call | flops 4831838208 | bytes 21233664 | tf_op jit(solution)/shard_map/mlp_forward/pallas_call | solution.py:780
  206.4 13.3 %attention_forward.3 = (f32[512,768]{1,0:T(8,128)}, bf16[512,768]{1,0:T(8,128)(2,1)}, bf16[4,512,576]{2,1,0:T(8,128)(2,1)}, bf16[4,3,2,256,256]{4,3,2,1,0:T(8,12...) custom-call(s32[197]{0:T(256)} %concatenate.83.table, f32[512,768]{1,0:T(8,128)} %get-tuple-element.398.x_ref, ...), custom_call_target="tpu_custom_call" | custom-call | flops 2818572288 | bytes 16515072 | tf_op jit(solution)/shard_map/attention_forward/pallas_call | solution.py:746
  219.7 14.1 %collective-permute-done.35.refs_1_ = bf16[8,2,2,48,768]{4,3,2,1,0:T(8,128)(2,1)} collective-permute-done((bf16[8,2,2,48,768]{4,3,2,1,0:T(8,128)(2,1)S(1)}, bf16[8,2,2,48,768]{4,3,2,1,0:T(8,128)(2,1)}, u32[]{:S(2)}, u32[]{:S(2)}) %collective-permute-start.35) | collective-permute-done | bytes 2359328 | tf_op jit(solution)/shard_map/ppermute | solution.py:121
  240.2 14.8 %mlp_forward.3 = (f32[512,768]{1,0:T(8,128)}, bf16[512,768]{1,0:T(8,128)(2,1)}, f32[4,512,768]{2,1,0:T(8,128)}, f32[512,768]{1,0:T(8,128)}) custom-call(s32[197]{0:T(256)} %concatenate.83.table, f32[512,768]{1,0:T(8,128)} %get-tuple-element.380.x_ref, f32[2,3,768]{2,1,0:T(4,128)} %get-tuple-element.381.mod_ref, f32[4,47,192]{2,1,0:T(8,128)} %bitcast.472, ...), custom_call_target="tpu_custom_call" | custom-call | flops 4831838208 | bytes 21233664 | tf_op jit(solution)/shard_map/mlp_forward/pallas_call | solution.py:780
  259.7 21.9 %mlp_backward.2 = (f32[512,768]{1,0:T(8,128)}, f32[2,3,768]{2,1,0:T(4,128)}, f32[4,1,768]{2,1,0:T(1,128)}, f32[1,768]{1,0:T(1,128)}, bf16[2,8,2,2,48,768]{5,4,3,...) custom-call(s32[197]{0:T(256)} %concatenate.83.table, f32[512,768]{1,0:T(8,128)} %copy-done.34, ...), custom_call_target="tpu_custom_call" | custom-call | flops 9663676416 | bytes 34603008 | tf_op jit(solution)/shard_map/mlp_backward/pallas_call | solution.py:815
  282.2 20.8 %attention_backward.2 = (f32[512,768]{1,0:T(8,128)}, f32[2,3,768]{2,1,0:T(4,128)}, f32[4,1,576]{2,1,0:T(1,128)}, f32[1,768]{1,0:T(1,128)}, bf16[2,8,2,1,48,768]{...) custom-call(s32[197]{0:T(256)} %concatenate.83.table, f32[512,768]{1,0:T(8,128)} %get-tuple-element.397.dx_ref, ...), custom_call_target="tpu_custom_call" | custom-call | flops 5838471168 | bytes 25165824 | tf_op jit(solution)/shard_map/attention_backward/pallas_call | solution.py:859
  307.0 22.3 %mlp_backward.3 = (f32[512,768]{1,0:T(8,128)}, f32[2,3,768]{2,1,0:T(4,128)}, f32[4,1,768]{2,1,0:T(1,128)}, f32[1,768]{1,0:T(1,128)}, bf16[2,8,2,2,48,768]{5,4,3,...) custom-call(s32[197]{0:T(256)} %concatenate.83.table, f32[512,768]{1,0:T(8,128)} %get-tuple-element.415.dx_ref, ...), custom_call_target="tpu_custom_call" | custom-call | flops 9663676416 | bytes 34603008 | tf_op jit(solution)/shard_map/mlp_backward/pallas_call | solution.py:815
  329.3 5.8 collective-permute-done.41
  343.6 20.7 %attention_backward.3 = (f32[512,768]{1,0:T(8,128)}, f32[2,3,768]{2,1,0:T(4,128)}, f32[4,1,576]{2,1,0:T(1,128)}, f32[1,768]{1,0:T(1,128)}, bf16[2,8,2,1,48,768]{...) custom-call(s32[197]{0:T(256)} %concatenate.83.table, f32[512,768]{1,0:T(8,128)} %get-tuple-element.434.dx_ref, ...), custom_call_target="tpu_custom_call" | custom-call | flops 5838471168 | bytes 25165824 | tf_op jit(solution)/shard_map/attention_backward/pallas_call | solution.py:859
  365.3 4.9 collective-permute-done.44
  395.3 8.5 %collective-permute-done.52 = bf16[2,2,2,48,768]{4,3,2,1,0:T(8,128)(2,1)S(1)} collective-permute-done((bf16[2,2,2,48,768]{4,3,2,1,0:T(8,128)(2,1)S(1)}, bf16[2,2,2,48,768]{4,3,2,1,0:T(8,128)(2,1)S(1)}, u32[]{:S(2)}, u32[]{:S(2)}) %collective-permute-start.52) | collective-permute-done | bytes 589856 | tf_op jit(solution)/shard_map/ppermute | solution.py:129
  420.6 16.6 %collective-permute-done.54 = bf16[4,32,768]{2,1,0:T(8,128)(2,1)S(1)} collective-permute-done((bf16[4,32,768]{2,1,0:T(8,128)(2,1)S(1)}, bf16[4,32,768]{2,1,0:T(8,128)(2,1)S(1)}, u32[]{:S(2)}, u32[]{:S(2)}) %collective-permute-start.54) | collective-permute-done | bytes 196640 | tf_op jit(solution)/shard_map/ppermute | solution.py:111
  446.6 10.0 %collective-permute-done.61 = f32[24,768]{1,0:T(8,128)S(1)} collective-permute-done((f32[24,768]{1,0:T(8,128)S(1)}, f32[24,768]{1,0:T(8,128)S(1)}, u32[]{:S(2)}, u32[]{:S(2)}) %collective-permute-start.61) | collective-permute-done | bytes 73760 | tf_op jit(solution)/shard_map/ppermute | solution.py:103
  472.7 4.4 collective-permute-start.66
  477.1 8.9 %collective-permute-done.62 = bf16[2,2,2,48,768]{4,3,2,1,0:T(8,128)(2,1)S(1)} collective-permute-done((bf16[2,2,2,48,768]{4,3,2,1,0:T(8,128)(2,1)S(1)}, bf16[2,2,2,48,768]{4,3,2,1,0:T(8,128)(2,1)S(1)}, u32[]{:S(2)}, u32[]{:S(2)}) %collective-permute-start.62) | collective-permute-done | bytes 589856 | tf_op jit(solution)/shard_map/ppermute | solution.py:129
  500.7 9.1 %modes_backward.1 = (f32[2,6,96,192]{3,2,1,0:T(8,128)}, f32[64,96]{1,0:T(8,128)}, f32[1,1]{1,0:T(1,128)}, f32[1536,768]{1,0:T(8,128)}, f32[64,768]{1,0:T(8,128)}, /*index=5*/f32[1,1]{1,0:T(1,128)}) custom-call(bf16[1024,768]{1,0:T(8,128)(2,1)} %bitcast.487, s32[64,2]{1,0:T(8,128)} %copy.331.at_ref, bf16[64,96]{1,0:T(8,128)(2,1)} %copy-done.73, ...), custom_call_target="tpu_custom_call" | custom-call | tf_op jit(solution)/shard_map/modes_backward/pallas_call | solution.py:1195
  529.9 5.0 condition_back.1
  559.3 13.4 %adam_final.1 = (f32[1552,768]{1,0:T(8,128)}, f32[1552,768]{1,0:T(8,128)}, f32[1552,768]{1,0:T(8,128)}) custom-call(f32[1]{0:T(128)} %bitcast.171.clip_ref, f32[1536,768]{1,0:T(8,128)} %get-tuple-element.502.grad_ref, f32[16,768]{1,0:T(8,128)} %slice.652.head_ref, f32[1552,768]{1,0:T(8,128)} %bitcast.483, f32[1552,768]{1,0:T(8,128)} %bitcast.485, ...), custom_call_target="tpu_custom_call" | custom-call | tf_op jit(solution)/shard_map/adam_final/pallas_call | solution.py:1374
  572.7 4.1 adam_rest.1
  579.1 11.3 %adam_blocks.1 = (f32[2,13,96,192]{3,2,1,0:T(8,128)}, f32[2,13,96,192]{3,2,1,0:T(8,128)}, f32[2,13,96,192]{3,2,1,0:T(8,128)}, f32[2,5,192,96]{3,2,1,0:T(8,128)},...) custom-call(f32[1]{0:T(128)} %bitcast.171.clip_ref, s32[2]{0:T(128)} %copy-done.33, ...), custom_call_target="tpu_custom_call" | custom-call | tf_op jit(solution)/shard_map/adam_blocks/pallas_call | solution.py:1335
  (524 shorter events, 241.7 us)
Async XLA Ops:
  14.6 17.6 %collective-permute-start.1 = (bf16[2,1,48,768]{3,2,0,1:T(8,128)(2,1)S(1)}, bf16[2,1,48,768]{3,2,0,1:T(8,128)(2,1)S(1)}, u32[]{:S(2)}, u32[]{:S(2)}) collective-permute-start(bf16[2,1,48,768]{3,2,0,1:T(8,128)(2,1)S(1)} %get-tuple-element.281), channel_id=1, source_target_pairs={{0,16},{4,20},{8,24},{12,28},{16,0},{20,4},{24,8},{28,12},{1,17},{... | collective-permute-start | bytes 442376 | tf_op jit(solution)/shard_map/ppermute | solution.py:125
  57.3 24.4 %collective-permute-start.13 = (bf16[8,2,1,48,768]{4,3,2,1,0:T(8,128)(2,1)}, bf16[8,2,1,48,768]{4,3,2,1,0:T(8,128)(2,1)}, u32[]{:S(2)}, u32[]{:S(2)}) collective-permute-start(bf16[8,2,1,48,768]{4,3,2,1,0:T(8,128)(2,1)} %copy-done.79), channel_id=1, source_target_pairs={{0,4},{1,3},{2,6},{3,1},{4,0},{5,7},{6,2},{7,5},{8,12},{9,11},{10,... | collective-permute-start | bytes 3538952 | tf_op jit(solution)/shard_map/ppermute | solution.py:121
  84.2 18.3 %collective-permute-start.19 = (bf16[8,2,1,48,768]{4,3,2,1,0:T(8,128)(2,1)}, bf16[8,2,1,48,768]{4,3,2,1,0:T(8,128)(2,1)}, u32[]{:S(2)}, u32[]{:S(2)}) collective-permute-start(bf16[8,2,1,48,768]{4,3,2,1,0:T(8,128)(2,1)} %collective-permute-done.13.refs_1_), channel_id=1, source_target_pairs={{0,1},{1,0},{2,3},{3,2},{4,5},{5,4},{6,7},{7,6},{8,9},{9,8},{10,11... | collective-permute-start | bytes 3538952 | tf_op jit(solution)/shard_map/ppermute | solution.py:107
  102.5 36.7 %collective-permute-start.20 = (bf16[8,2,2,48,768]{4,3,2,1,0:T(8,128)(2,1)}, bf16[8,2,2,48,768]{4,3,2,1,0:T(8,128)(2,1)}, u32[]{:S(2)}, u32[]{:S(2)}) collective-permute-start(bf16[8,2,2,48,768]{4,3,2,1,0:T(8,128)(2,1)} %pad_maximum_fusion.refs_0_), channel_id=1, source_target_pairs={{0,4},{1,3},{2,6},{3,1},{4,0},{5,7},{6,2},{7,5},{8,12},{9,11},{10,... | collective-permute-start | bytes 7077896 | tf_op jit(solution)/shard_map/ppermute | solution.py:121
  103.8 35.4 %collective-permute-start.25 = (bf16[8,2,2,48,768]{4,3,2,1,0:T(8,128)(2,1)}, bf16[8,2,2,48,768]{4,3,2,1,0:T(8,128)(2,1)}, u32[]{:S(2)}, u32[]{:S(2)}) collective-permute-start(bf16[8,2,2,48,768]{4,3,2,1,0:T(8,128)(2,1)} %pad_maximum_fusion.refs_0_), channel_id=1, source_target_pairs={{0,1},{1,0},{2,3},{3,2},{4,5},{5,4},{6,7},{7,6},{8,9},{9,8},{10,11... | collective-permute-start | bytes 7077896 | tf_op jit(solution)/shard_map/ppermute | solution.py:107
  114.6 18.9 %collective-permute-start.23 = (bf16[2,2,1,48,768]{4,3,1,2,0:T(8,128)(2,1)}, bf16[2,2,1,48,768]{4,3,1,2,0:T(8,128)(2,1)}, u32[]{:S(2)}, u32[]{:S(2)}) collective-permute-start(bf16[2,2,1,48,768]{4,3,1,2,0:T(8,128)(2,1)} %pad_maximum_fusion.17), channel_id=1, source_target_pairs={{0,8},{4,12},{8,0},{12,4},{16,24},{20,28},{24,16},{28,20},{1,9},{5... | collective-permute-start | bytes 884744 | tf_op jit(solution)/shard_map/ppermute | solution.py:129
  139.2 29.5 %collective-permute-start.29 = (bf16[8,2,2,48,768]{4,3,2,1,0:T(8,128)(2,1)}, bf16[8,2,2,48,768]{4,3,2,1,0:T(8,128)(2,1)}, u32[]{:S(2)}, u32[]{:S(2)}) collective-permute-start(bf16[8,2,2,48,768]{4,3,2,1,0:T(8,128)(2,1)} %collective-permute-done.20.refs_1_), channel_id=1, source_target_pairs={{0,1},{1,0},{2,3},{3,2},{4,5},{5,4},{6,7},{7,6},{8,9},{9,8},{10,11... | collective-permute-start | bytes 7077896 | tf_op jit(solution)/shard_map/ppermute | solution.py:107
  145.7 20.8 %collective-permute-start.28 = (bf16[4,2,1,48,768]{4,3,1,2,0:T(8,128)(2,1)}, bf16[4,2,1,48,768]{4,3,1,2,0:T(8,128)(2,1)S(1)}, u32[]{:S(2)}, u32[]{:S(2)}) collective-permute-start(bf16[4,2,1,48,768]{4,3,1,2,0:T(8,128)(2,1)} %pad_maximum_fusion.11), channel_id=1, source_target_pairs={{0,2},{1,5},{2,0},{3,7},{4,6},{5,1},{6,4},{7,3},{8,10},{9,13},{10,... | collective-permute-start | bytes 1769480 | tf_op jit(solution)/shard_map/ppermute | solution.py:116
  146.9 17.8 %collective-permute-start.26 = (bf16[2,2,48,768]{3,2,1,0:T(8,128)(2,1)}, bf16[2,2,48,768]{3,2,1,0:T(8,128)(2,1)S(1)}, u32[]{:S(2)}, u32[]{:S(2)}) collective-permute-start(bf16[2,2,48,768]{3,2,1,0:T(8,128)(2,1)} %get-tuple-element.314), channel_id=1, source_target_pairs={{0,16},{4,20},{8,24},{12,28},{16,0},{20,4},{24,8},{28,12},{1,17},{... | collective-permute-start | bytes 884744 | tf_op jit(solution)/shard_map/ppermute | solution.py:125
  168.7 18.1 %collective-permute-start.31 = (bf16[8,2,1,48,768]{4,3,1,2,0:T(8,128)(2,1)}, bf16[8,2,1,48,768]{4,3,1,2,0:T(8,128)(2,1)}, u32[]{:S(2)}, u32[]{:S(2)}) collective-permute-start(bf16[8,2,1,48,768]{4,3,1,2,0:T(8,128)(2,1)} %pad_maximum_fusion.3), channel_id=1, source_target_pairs={{0,4},{1,3},{2,6},{3,1},{4,0},{5,7},{6,2},{7,5},{8,12},{9,11},{10,... | collective-permute-start | bytes 3538952 | tf_op jit(solution)/shard_map/ppermute | solution.py:121
  169.2 17.6 %collective-permute-start.32 = (bf16[8,2,1,48,768]{4,3,1,2,0:T(8,128)(2,1)}, bf16[8,2,1,48,768]{4,3,1,2,0:T(8,128)(2,1)}, u32[]{:S(2)}, u32[]{:S(2)}) collective-permute-start(bf16[8,2,1,48,768]{4,3,1,2,0:T(8,128)(2,1)} %pad_maximum_fusion.3), channel_id=1, source_target_pairs={{0,1},{1,0},{2,3},{3,2},{4,5},{5,4},{6,7},{7,6},{8,9},{9,8},{10,11... | collective-permute-start | bytes 3538952 | tf_op jit(solution)/shard_map/ppermute | solution.py:107
  204.8 29.0 %collective-permute-start.35 = (bf16[8,2,2,48,768]{4,3,2,1,0:T(8,128)(2,1)S(1)}, bf16[8,2,2,48,768]{4,3,2,1,0:T(8,128)(2,1)}, u32[]{:S(2)}, u32[]{:S(2)}) collective-permute-start(bf16[8,2,2,48,768]{4,3,2,1,0:T(8,128)(2,1)S(1)} %pad_maximum_fusion.1.refs_0_), channel_id=1, source_target_pairs={{0,4},{1,3},{2,6},{3,1},{4,0},{5,7},{6,2},{7,5},{8,12},{9,11},{10,... | collective-permute-start | bytes 7077896 | tf_op jit(solution)/shard_map/ppermute | solution.py:121
  206.4 27.4 %collective-permute-start.36 = (bf16[8,2,2,48,768]{4,3,2,1,0:T(8,128)(2,1)S(1)}, bf16[8,2,2,48,768]{4,3,2,1,0:T(8,128)(2,1)}, u32[]{:S(2)}, u32[]{:S(2)}) collective-permute-start(bf16[8,2,2,48,768]{4,3,2,1,0:T(8,128)(2,1)S(1)} %pad_maximum_fusion.1.refs_0_), channel_id=1, source_target_pairs={{0,1},{1,0},{2,3},{3,2},{4,5},{5,4},{6,7},{7,6},{8,9},{9,8},{10,11... | collective-permute-start | bytes 7077896 | tf_op jit(solution)/shard_map/ppermute | solution.py:107
  238.7 19.5 %collective-permute-start.38 = (bf16[2,6,96,192]{3,2,1,0:T(8,128)(2,1)S(1)}, bf16[2,6,96,192]{3,2,1,0:T(8,128)(2,1)S(1)}, u32[]{:S(2)}, u32[]{:S(2)}) collective-permute-start(bf16[2,6,96,192]{3,2,1,0:T(8,128)(2,1)S(1)} %get-tuple-element.366), channel_id=1, source_target_pairs={{0,2},{1,3},{2,0},{3,1},{4,6},{5,7},{6,4},{7,5},{8,10},{9,11},{10,... | collective-permute-start | bytes 1327112 | tf_op jit(solution)/shard_map/ppermute | solution.py:103
  259.7 21.9 %collective-permute-start.39 = (bf16[2,2,6,96,192]{4,3,2,1,0:T(8,128)(2,1)S(1)}, bf16[2,2,6,96,192]{4,3,2,1,0:T(8,128)(2,1)S(1)}, u32[]{:S(2)}, u32[]{:S(2)}) collective-permute-start(bf16[2,2,6,96,192]{4,3,2,1,0:T(8,128)(2,1)S(1)} %pad_maximum_fusion.5), channel_id=1, source_target_pairs={{0,1},{1,0},{2,3},{3,2},{4,5},{5,4},{6,7},{7,6},{8,9},{9,8},{10,11... | collective-permute-start | bytes 2654216 | tf_op jit(solution)/shard_map/ppermute | solution.py:107
  281.6 21.4 %collective-permute-start.40 = (bf16[2,8,2,2,48,768]{5,4,3,2,1,0:T(8,128)(2,1)}, bf16[2,8,2,2,48,768]{5,4,3,2,1,0:T(8,128)(2,1)}, u32[]{:S(2)}, u32[]{:S(2)}) collective-permute-start(bf16[2,8,2,2,48,768]{5,4,3,2,1,0:T(8,128)(2,1)} %get-tuple-element.396), channel_id=1, source_target_pairs={{0,1},{1,0},{2,3},{3,2},{4,5},{5,4},{6,7},{7,6},{8,9},{9,8},{10,11... | collective-permute-start | bytes 14155784 | tf_op jit(solution)/shard_map/ppermute | solution.py:107
  306.1 29.0 %collective-permute-start.41 = (bf16[8,2,2,48,768]{4,3,2,1,0:T(8,128)(2,1)S(1)}, bf16[8,2,2,48,768]{4,3,2,1,0:T(8,128)(2,1)}, u32[]{:S(2)}, u32[]{:S(2)}) collective-permute-start(bf16[8,2,2,48,768]{4,3,2,1,0:T(8,128)(2,1)S(1)} %fusion), channel_id=1, source_target_pairs={{0,4},{1,3},{2,6},{3,1},{4,0},{5,7},{6,2},{7,5},{8,12},{9,11},{10,... | collective-permute-start | bytes 7077896 | tf_op jit(solution)/shard_map/ppermute | solution.py:121
  307.0 31.5 %collective-permute-start.42 = (bf16[2,8,2,1,48,768]{5,4,2,3,1,0:T(8,128)(2,1)}, bf16[2,8,2,1,48,768]{5,4,2,3,1,0:T(8,128)(2,1)}, u32[]{:S(2)}, u32[]{:S(2)}) collective-permute-start(bf16[2,8,2,1,48,768]{5,4,2,3,1,0:T(8,128)(2,1)} %bitcast.73), channel_id=1, source_target_pairs={{0,1},{1,0},{2,3},{3,2},{4,5},{5,4},{6,7},{7,6},{8,9},{9,8},{10,11... | collective-permute-start | bytes 7077896 | tf_op jit(solution)/shard_map/ppermute | solution.py:107
  341.3 30.9 %collective-permute-start.43 = (bf16[2,8,2,2,48,768]{5,4,3,2,1,0:T(8,128)(2,1)}, bf16[2,8,2,2,48,768]{5,4,3,2,1,0:T(8,128)(2,1)}, u32[]{:S(2)}, u32[]{:S(2)}) collective-permute-start(bf16[2,8,2,2,48,768]{5,4,3,2,1,0:T(8,128)(2,1)} %get-tuple-element.433), channel_id=1, source_target_pairs={{0,1},{1,0},{2,3},{3,2},{4,5},{5,4},{6,7},{7,6},{8,9},{9,8},{10,11... | collective-permute-start | bytes 14155784 | tf_op jit(solution)/shard_map/ppermute | solution.py:107
  341.3 28.9 %collective-permute-start.44 = (bf16[4,2,2,48,768]{4,3,2,1,0:T(8,128)(2,1)}, bf16[4,2,2,48,768]{4,3,2,1,0:T(8,128)(2,1)}, u32[]{:S(2)}, u32[]{:S(2)}) collective-permute-start(bf16[4,2,2,48,768]{4,3,2,1,0:T(8,128)(2,1)} %fusion.5), channel_id=1, source_target_pairs={{0,2},{1,5},{2,0},{3,7},{4,6},{5,1},{6,4},{7,3},{8,10},{9,13},{10,... | collective-permute-start | bytes 3538952 | tf_op jit(solution)/shard_map/ppermute | solution.py:116
  342.0 33.5 %collective-permute-start.45 = (bf16[8,2,1,48,768]{4,3,1,2,0:T(8,128)(2,1)}, bf16[8,2,1,48,768]{4,3,1,2,0:T(8,128)(2,1)}, u32[]{:S(2)}, u32[]{:S(2)}) collective-permute-start(bf16[8,2,1,48,768]{4,3,1,2,0:T(8,128)(2,1)} %bitcast.511), channel_id=1, source_target_pairs={{0,4},{1,3},{2,6},{3,1},{4,0},{5,7},{6,2},{7,5},{8,12},{9,11},{10,... | collective-permute-start | bytes 3538952 | tf_op jit(solution)/shard_map/ppermute | solution.py:121
  375.5 30.5 %collective-permute-start.47 = (bf16[2,8,2,1,48,768]{5,4,2,3,1,0:T(8,128)(2,1)S(1)}, bf16[2,8,2,1,48,768]{5,4,2,3,1,0:T(8,128)(2,1)S(1)}, u32[]{:S(2)}, u32[]{:S(2)}) collective-permute-start(bf16[2,8,2,1,48,768]{5,4,2,3,1,0:T(8,128)(2,1)S(1)} %bitcast.549), channel_id=1, source_target_pairs={{0,1},{1,0},{2,3},{3,2},{4,5},{5,4},{6,7},{7,6},{8,9},{9,8},{10,11... | collective-permute-start | bytes 7077896 | tf_op jit(solution)/shard_map/ppermute | solution.py:107
  377.2 30.4 %collective-permute-start.46 = (bf16[8,2,2,48,768]{4,3,2,1,0:T(8,128)(2,1)S(1)}, bf16[8,2,2,48,768]{4,3,2,1,0:T(8,128)(2,1)S(1)}, u32[]{:S(2)}, u32[]{:S(2)}) collective-permute-start(bf16[8,2,2,48,768]{4,3,2,1,0:T(8,128)(2,1)S(1)} %fusion.1), channel_id=1, source_target_pairs={{0,4},{1,3},{2,6},{3,1},{4,0},{5,7},{6,2},{7,5},{8,12},{9,11},{10,... | collective-permute-start | bytes 7077896 | tf_op jit(solution)/shard_map/ppermute | solution.py:121
  409.3 30.1 %collective-permute-start.56 = (bf16[8,2,1,48,768]{4,3,1,2,0:T(8,128)(2,1)}, bf16[8,2,1,48,768]{4,3,1,2,0:T(8,128)(2,1)}, u32[]{:S(2)}, u32[]{:S(2)}) collective-permute-start(bf16[8,2,1,48,768]{4,3,1,2,0:T(8,128)(2,1)} %bitcast.101), channel_id=1, source_target_pairs={{0,4},{1,3},{2,6},{3,1},{4,0},{5,7},{6,2},{7,5},{8,12},{9,11},{10,... | collective-permute-start | bytes 3538952 | tf_op jit(solution)/shard_map/ppermute | solution.py:121
  411.3 26.0 %collective-permute-start.53 = (bf16[4,2,1,48,768]{4,3,1,2,0:T(8,128)(2,1)}, bf16[4,2,1,48,768]{4,3,1,2,0:T(8,128)(2,1)}, u32[]{:S(2)}, u32[]{:S(2)}) collective-permute-start(bf16[4,2,1,48,768]{4,3,1,2,0:T(8,128)(2,1)} %bitcast.99), channel_id=1, source_target_pairs={{0,2},{1,5},{2,0},{3,7},{4,6},{5,1},{6,4},{7,3},{8,10},{9,13},{10,... | collective-permute-start | bytes 1769480 | tf_op jit(solution)/shard_map/ppermute | solution.py:116
  414.3 25.0 %collective-permute-start.57 = (bf16[2,2,48,768]{3,2,1,0:T(8,128)(2,1)}, bf16[2,2,48,768]{3,2,1,0:T(8,128)(2,1)S(1)}, u32[]{:S(2)}, u32[]{:S(2)}) collective-permute-start(bf16[2,2,48,768]{3,2,1,0:T(8,128)(2,1)} %fusion.21), channel_id=1, source_target_pairs={{0,16},{4,20},{8,24},{12,28},{16,0},{20,4},{24,8},{28,12},{1,17},{... | collective-permute-start | bytes 884744 | tf_op jit(solution)/shard_map/ppermute | solution.py:125
  417.2 20.0 %collective-permute-start.54 = (bf16[4,32,768]{2,1,0:T(8,128)(2,1)S(1)}, bf16[4,32,768]{2,1,0:T(8,128)(2,1)S(1)}, u32[]{:S(2)}, u32[]{:S(2)}) collective-permute-start(bf16[4,32,768]{2,1,0:T(8,128)(2,1)S(1)} %pad_maximum_fusion.22), channel_id=1, source_target_pairs={{0,4},{4,0},{8,12},{12,8},{16,20},{20,16},{24,28},{28,24},{1,5},{5... | collective-permute-start | bytes 589832 | tf_op jit(solution)/shard_map/ppermute | solution.py:111
  439.4 21.6 %collective-permute-start.58 = (bf16[4,2,2,48,768]{4,3,2,1,0:T(8,128)(2,1)}, bf16[4,2,2,48,768]{4,3,2,1,0:T(8,128)(2,1)}, u32[]{:S(2)}, u32[]{:S(2)}) collective-permute-start(bf16[4,2,2,48,768]{4,3,2,1,0:T(8,128)(2,1)} %fusion.4), channel_id=1, source_target_pairs={{0,2},{1,5},{2,0},{3,7},{4,6},{5,1},{6,4},{7,3},{8,10},{9,13},{10,... | collective-permute-start | bytes 3538952 | tf_op jit(solution)/shard_map/ppermute | solution.py:116
  467.1 18.9 %collective-permute-start.62 = (bf16[2,2,2,48,768]{4,3,2,1,0:T(8,128)(2,1)S(1)}, bf16[2,2,2,48,768]{4,3,2,1,0:T(8,128)(2,1)S(1)}, u32[]{:S(2)}, u32[]{:S(2)}) collective-permute-start(bf16[2,2,2,48,768]{4,3,2,1,0:T(8,128)(2,1)S(1)} %fusion.13), channel_id=1, source_target_pairs={{0,8},{4,12},{8,0},{12,4},{16,24},{20,28},{24,16},{28,20},{1,9},{5... | collective-permute-start | bytes 1769480 | tf_op jit(solution)/shard_map/ppermute | solution.py:129
  470.1 17.9 %collective-permute-start.65 = (bf16[4,2,1,48,768]{4,3,1,2,0:T(8,128)(2,1)S(1)}, bf16[4,2,1,48,768]{4,3,1,2,0:T(8,128)(2,1)S(1)}, u32[]{:S(2)}, u32[]{:S(2)}) collective-permute-start(bf16[4,2,1,48,768]{4,3,1,2,0:T(8,128)(2,1)S(1)} %bitcast.521), channel_id=1, source_target_pairs={{0,2},{1,5},{2,0},{3,7},{4,6},{5,1},{6,4},{7,3},{8,10},{9,13},{10,... | collective-permute-start | bytes 1769480 | tf_op jit(solution)/shard_map/ppermute | solution.py:116
  519.5 18.8 %collective-permute-start.75 = (bf16[2,1,48,768]{3,2,1,0:T(8,128)(2,1)S(1)}, bf16[2,1,48,768]{3,2,1,0:T(8,128)(2,1)S(1)}, u32[]{:S(2)}, u32[]{:S(2)}) collective-permute-start(bf16[2,1,48,768]{3,2,1,0:T(8,128)(2,1)S(1)} %fusion.31), channel_id=1, source_target_pairs={{0,16},{4,20},{8,24},{12,28},{16,0},{20,4},{24,8},{28,12},{1,17},{... | collective-permute-start | bytes 442376 | tf_op jit(solution)/shard_map/ppermute | solution.py:125
  548.3 29.2 %collective-permute-start.83 = (f32[6,48,768]{2,1,0:T(8,128)S(1)}, f32[6,48,768]{2,1,0:T(8,128)S(1)}, u32[]{:S(2)}, u32[]{:S(2)}) collective-permute-start(f32[6,48,768]{2,1,0:T(8,128)S(1)} %pad_maximum_fusion.7), channel_id=1, source_target_pairs={{0,1},{1,0},{2,3},{3,2},{4,5},{5,4},{6,7},{7,6},{8,9},{9,8},{10,11... | collective-permute-start | bytes 2654216 | tf_op jit(solution)/shard_map/ppermute | solution.py:107
  (141 other events, 1575.9 us)

commit v5 on v4

--- a/solution.py
+++ b/solution.py
@@ -1197,7 +1197,7 @@
         in_specs=[vmem] * len(operands),
         out_specs=[vmem] * len(outs),
         out_shape=outs,
-        compiler_params=pltpu.CompilerParams(vmem_limit_bytes=56 * MIB),
+        compiler_params=pltpu.CompilerParams(vmem_limit_bytes=40 * MIB),
         name="modes_backward",
     )(*operands)
 

time: 602 us -> 608 us (level)
  starting transfers between devices: 106 us -> 114 us
    unnamed x198 -> x216, local copies, waits for them, and re-layouts: 13.8 us -> 17.2 us
  transfers between devices with their start and end apart: 84 -> 84, of which waited for: 35 -> 35; matrix products, arithmetic and copies ran while one was open for 16% -> 15% of each run, Pallas kernels for 30% -> 29%
where the time goes in v5:
time: 608 us; the launch traced here: 598 us
  Pallas kernels  186 us (31%)
  waiting for transfers between devices  170 us (28%)
  starting transfers between devices  114 us (19%)
  other arithmetic  73.4 us (12%)
  local copies, waits for them, and re-layouts  41.6 us (7%)
  between operations  9.13 us (2%)
    ppermute x15, waiting for transfers between devices, swap_near(): return lax.ppermute(v, 'row', [(r, r ^ 2) for r in range(8)])  53 us
    pallas_call x2, Pallas kernels, mlp_backward(): pl.pallas_call(functools.partial(mlp_backward_body, route), grid=(count,)...  44.1 us
    pallas_call x2, Pallas kernels, attention_backward(): pl.pallas_call(functools.partial(attention_backward_body, route), grid=(c...  41.4 us
    ppermute x15, starting transfers between devices, swap_far(): return lax.ppermute(v, 'row', [(r, r ^ 4) for r in range(8)])  40.9 us
    ppermute x15, waiting for transfers between devices, swap_far(): return lax.ppermute(v, 'row', [(r, r ^ 4) for r in range(8)])  38.6 us
    pallas_call x2, Pallas kernels, mlp_forward(): pl.pallas_call(functools.partial(mlp_forward_body, route, base), grid=(co...  29.3 us
    pallas_call x2, Pallas kernels, attention_forward(): pl.pallas_call(functools.partial(attention_forward_body, route, base), gr...  26.9 us
    ppermute x6, waiting for transfers between devices, swap_y(): return lax.ppermute(v, 'row', [(r, r ^ 1) for r in range(8)])  25.5 us
  transfers between devices with their start and end apart: 84, of which 35 were waited for; matrix products, arithmetic and copies ran while one was open for 15% of the time, Pallas kernels for 29%

profile of v5, /device:TPU:0, one launch (start us, length us, event | category | flops | bytes accessed | tf_op | source)
XLA Modules:
  0.0 597.6 jit_solution(4985193971310260293)
XLA Ops:
  11.2 4.0 collective-permute-start.4
  26.2 4.8 collective-permute-done.5
  32.9 5.6 collective-permute-done.6
  43.4 11.5 %collective-permute-done.9 = bf16[2,2,48,768]{3,2,1,0:T(8,128)(2,1)S(1)} collective-permute-done((bf16[2,2,48,768]{3,2,1,0:T(8,128)(2,1)S(1)}, bf16[2,2,48,768]{3,2,1,0:T(8,128)(2,1)S(1)}, u32[]{:S(2)}, u32[]{:S(2)}) %collective-permute-start.9) | collective-permute-done | bytes 294944 | tf_op jit(solution)/shard_map/ppermute | solution.py:125
  66.9 14.3 %collective-permute-done.12 = bf16[2,2,2,48,768]{4,3,2,1,0:T(8,128)(2,1)S(1)} collective-permute-done((bf16[2,2,2,48,768]{4,3,2,1,0:T(8,128)(2,1)S(1)}, bf16[2,2,2,48,768]{4,3,2,1,0:T(8,128)(2,1)S(1)}, u32[]{:S(2)}, u32[]{:S(2)}) %collective-permute-start.12) | collective-permute-done | bytes 589856 | tf_op jit(solution)/shard_map/ppermute | solution.py:129
  90.1 7.4 %collective-permute-done.18 = bf16[2,1,48,768]{3,2,1,0:T(8,128)(2,1)S(1)} collective-permute-done((bf16[2,1,48,768]{3,2,1,0:T(8,128)(2,1)S(1)}, bf16[2,1,48,768]{3,2,1,0:T(8,128)(2,1)S(1)}, u32[]{:S(2)}, u32[]{:S(2)}) %collective-permute-start.18) | collective-permute-done | bytes 147488 | tf_op jit(solution)/shard_map/ppermute | solution.py:125
  104.6 6.7 %collective-permute-start.25 = (bf16[8,2,2,48,768]{4,3,2,1,0:T(8,128)(2,1)}, bf16[8,2,2,48,768]{4,3,2,1,0:T(8,128)(2,1)}, u32[]{:S(2)}, u32[]{:S(2)}) collective-permute-start(bf16[8,2,2,48,768]{4,3,2,1,0:T(8,128)(2,1)} %pad_maximum_fusion.refs_0_), channel_id=1, source_target_pairs={{0,1},{1,0},{2,3},{3,2},{4,5},{5,4},{6,7},{7,6},{8,9},{9,8},{10,11... | collective-permute-start | bytes 7077896 | tf_op jit(solution)/shard_map/ppermute | solution.py:107
  113.5 5.7 collective-permute-done.21
  135.4 4.8 collective-permute-start.29
  156.6 13.9 %collective-permute-done.26 = bf16[2,2,48,768]{3,2,1,0:T(8,128)(2,1)S(1)} collective-permute-done((bf16[2,2,48,768]{3,2,1,0:T(8,128)(2,1)}, bf16[2,2,48,768]{3,2,1,0:T(8,128)(2,1)S(1)}, u32[]{:S(2)}, u32[]{:S(2)}) %collective-permute-start.26) | collective-permute-done | bytes 294944 | tf_op jit(solution)/shard_map/ppermute | solution.py:125
  178.0 13.5 %attention_forward.2 = (f32[512,768]{1,0:T(8,128)}, bf16[512,768]{1,0:T(8,128)(2,1)}, bf16[4,512,576]{2,1,0:T(8,128)(2,1)}, bf16[4,3,2,256,256]{4,3,2,1,0:T(8,12...) custom-call(s32[197]{0:T(256)} %concatenate.83.table, f32[512,768]{1,0:T(8,128)} %copy-done.9, ...), custom_call_target="tpu_custom_call" | custom-call | flops 2818572288 | bytes 16515072 | tf_op jit(solution)/shard_map/attention_forward/pallas_call | solution.py:746
  194.9 14.5 %mlp_forward.2 = (f32[512,768]{1,0:T(8,128)}, bf16[512,768]{1,0:T(8,128)(2,1)}, f32[4,512,768]{2,1,0:T(8,128)}, f32[512,768]{1,0:T(8,128)}) custom-call(s32[197]{0:T(256)} %concatenate.83.table, f32[512,768]{1,0:T(8,128)} %get-tuple-element.416.x_ref, f32[2,3,768]{2,1,0:T(4,128)} %get-tuple-element.417.mod_ref, f32[4,47,192]{2,1,0:T(8,128)} %bitcast.472, ...), custom_call_target="tpu_custom_call" | custom-call | flops 4831838208 | bytes 21233664 | tf_op jit(solution)/shard_map/mlp_forward/pallas_call | solution.py:780
  214.3 13.3 %attention_forward.3 = (f32[512,768]{1,0:T(8,128)}, bf16[512,768]{1,0:T(8,128)(2,1)}, bf16[4,512,576]{2,1,0:T(8,128)(2,1)}, bf16[4,3,2,256,256]{4,3,2,1,0:T(8,12...) custom-call(s32[197]{0:T(256)} %concatenate.83.table, f32[512,768]{1,0:T(8,128)} %get-tuple-element.398.x_ref, ...), custom_call_target="tpu_custom_call" | custom-call | flops 2818572288 | bytes 16515072 | tf_op jit(solution)/shard_map/attention_forward/pallas_call | solution.py:746
  227.6 14.3 %collective-permute-done.35.refs_1_ = bf16[8,2,2,48,768]{4,3,2,1,0:T(8,128)(2,1)} collective-permute-done((bf16[8,2,2,48,768]{4,3,2,1,0:T(8,128)(2,1)}, bf16[8,2,2,48,768]{4,3,2,1,0:T(8,128)(2,1)}, u32[]{:S(2)}, u32[]{:S(2)}) %collective-permute-start.35) | collective-permute-done | bytes 2359328 | tf_op jit(solution)/shard_map/ppermute | solution.py:121
  248.3 14.8 %mlp_forward.3 = (f32[512,768]{1,0:T(8,128)}, bf16[512,768]{1,0:T(8,128)(2,1)}, f32[4,512,768]{2,1,0:T(8,128)}, f32[512,768]{1,0:T(8,128)}) custom-call(s32[197]{0:T(256)} %concatenate.83.table, f32[512,768]{1,0:T(8,128)} %get-tuple-element.380.x_ref, f32[2,3,768]{2,1,0:T(4,128)} %get-tuple-element.381.mod_ref, f32[4,47,192]{2,1,0:T(8,128)} %bitcast.474, ...), custom_call_target="tpu_custom_call" | custom-call | flops 4831838208 | bytes 21233664 | tf_op jit(solution)/shard_map/mlp_forward/pallas_call | solution.py:780
  267.8 21.9 %mlp_backward.2 = (f32[512,768]{1,0:T(8,128)}, f32[2,3,768]{2,1,0:T(4,128)}, f32[4,1,768]{2,1,0:T(1,128)}, f32[1,768]{1,0:T(1,128)}, bf16[2,8,2,2,48,768]{5,4,3,...) custom-call(s32[197]{0:T(256)} %concatenate.83.table, f32[512,768]{1,0:T(8,128)} %copy-done.43, ...), custom_call_target="tpu_custom_call" | custom-call | flops 9663676416 | bytes 34603008 | tf_op jit(solution)/shard_map/mlp_backward/pallas_call | solution.py:815
  290.3 20.8 %attention_backward.2 = (f32[512,768]{1,0:T(8,128)}, f32[2,3,768]{2,1,0:T(4,128)}, f32[4,1,576]{2,1,0:T(1,128)}, f32[1,768]{1,0:T(1,128)}, bf16[2,8,2,1,48,768]{...) custom-call(s32[197]{0:T(256)} %concatenate.83.table, f32[512,768]{1,0:T(8,128)} %get-tuple-element.397.dx_ref, ...), custom_call_target="tpu_custom_call" | custom-call | flops 5838471168 | bytes 25165824 | tf_op jit(solution)/shard_map/attention_backward/pallas_call | solution.py:859
  314.7 22.3 %mlp_backward.3 = (f32[512,768]{1,0:T(8,128)}, f32[2,3,768]{2,1,0:T(4,128)}, f32[4,1,768]{2,1,0:T(1,128)}, f32[1,768]{1,0:T(1,128)}, bf16[2,8,2,2,48,768]{5,4,3,...) custom-call(s32[197]{0:T(256)} %concatenate.83.table, f32[512,768]{1,0:T(8,128)} %get-tuple-element.415.dx_ref, ...), custom_call_target="tpu_custom_call" | custom-call | flops 9663676416 | bytes 34603008 | tf_op jit(solution)/shard_map/mlp_backward/pallas_call | solution.py:815
  337.0 6.1 %collective-permute-done.41 = bf16[8,2,2,48,768]{4,3,2,1,0:T(8,128)(2,1)} collective-permute-done((bf16[8,2,2,48,768]{4,3,2,1,0:T(8,128)(2,1)S(1)}, bf16[8,2,2,48,768]{4,3,2,1,0:T(8,128)(2,1)}, u32[]{:S(2)}, u32[]{:S(2)}) %collective-permute-start.41) | collective-permute-done | bytes 2359328 | tf_op jit(solution)/shard_map/ppermute | solution.py:121
  351.6 20.7 %attention_backward.3 = (f32[512,768]{1,0:T(8,128)}, f32[2,3,768]{2,1,0:T(4,128)}, f32[4,1,576]{2,1,0:T(1,128)}, f32[1,768]{1,0:T(1,128)}, bf16[2,8,2,1,48,768]{...) custom-call(s32[197]{0:T(256)} %concatenate.83.table, f32[512,768]{1,0:T(8,128)} %get-tuple-element.434.dx_ref, ...), custom_call_target="tpu_custom_call" | custom-call | flops 5838471168 | bytes 25165824 | tf_op jit(solution)/shard_map/attention_backward/pallas_call | solution.py:859
  373.4 5.1 collective-permute-done.44
  403.5 8.7 %collective-permute-done.52 = bf16[2,2,2,48,768]{4,3,2,1,0:T(8,128)(2,1)S(1)} collective-permute-done((bf16[2,2,2,48,768]{4,3,2,1,0:T(8,128)(2,1)S(1)}, bf16[2,2,2,48,768]{4,3,2,1,0:T(8,128)(2,1)S(1)}, u32[]{:S(2)}, u32[]{:S(2)}) %collective-permute-start.52) | collective-permute-done | bytes 589856 | tf_op jit(solution)/shard_map/ppermute | solution.py:129
  428.0 15.5 %collective-permute-done.54 = bf16[4,32,768]{2,1,0:T(8,128)(2,1)S(1)} collective-permute-done((bf16[4,32,768]{2,1,0:T(8,128)(2,1)S(1)}, bf16[4,32,768]{2,1,0:T(8,128)(2,1)S(1)}, u32[]{:S(2)}, u32[]{:S(2)}) %collective-permute-start.54) | collective-permute-done | bytes 196640 | tf_op jit(solution)/shard_map/ppermute | solution.py:111
  453.0 9.9 %collective-permute-done.61 = f32[24,768]{1,0:T(8,128)S(1)} collective-permute-done((f32[24,768]{1,0:T(8,128)S(1)}, f32[24,768]{1,0:T(8,128)S(1)}, u32[]{:S(2)}, u32[]{:S(2)}) %collective-permute-start.61) | collective-permute-done | bytes 73760 | tf_op jit(solution)/shard_map/ppermute | solution.py:103
  479.5 4.6 collective-permute-start.66
  484.1 7.2 %collective-permute-done.62 = bf16[2,2,2,48,768]{4,3,2,1,0:T(8,128)(2,1)S(1)} collective-permute-done((bf16[2,2,2,48,768]{4,3,2,1,0:T(8,128)(2,1)S(1)}, bf16[2,2,2,48,768]{4,3,2,1,0:T(8,128)(2,1)S(1)}, u32[]{:S(2)}, u32[]{:S(2)}) %collective-permute-start.62) | collective-permute-done | bytes 589856 | tf_op jit(solution)/shard_map/ppermute | solution.py:129
  505.9 5.0 modes_backward.1
  513.2 5.8 collective-permute-done.69
  535.5 5.1 condition_back.1
  565.2 13.4 %adam_final.1 = (f32[1552,768]{1,0:T(8,128)}, f32[1552,768]{1,0:T(8,128)}, f32[1552,768]{1,0:T(8,128)}) custom-call(f32[1]{0:T(128)} %bitcast.171.clip_ref, f32[1536,768]{1,0:T(8,128)} %copy-done.3, f32[16,768]{1,0:T(8,128)} %slice.652.head_ref, f32[1552,768]{1,0:T(8,128)} %bitcast.486, f32[1552,768]{1,0:T(8,128)} %bitcast.487, f32[1552,768]{1,0:T(8,128)} %bitcast.488), custom_call_target="tpu_custom_call" | custom-call | tf_op jit(solution)/shard_map/adam_final/pallas_call | solution.py:1374
  578.6 4.1 adam_rest.1
  585.0 11.3 %adam_blocks.1 = (f32[2,13,96,192]{3,2,1,0:T(8,128)}, f32[2,13,96,192]{3,2,1,0:T(8,128)}, f32[2,13,96,192]{3,2,1,0:T(8,128)}, f32[2,5,192,96]{3,2,1,0:T(8,128)},...) custom-call(f32[1]{0:T(128)} %bitcast.171.clip_ref, s32[2]{0:T(128)} %copy-done.42, f32[2,6,96,192]{3,2,1,0:T(8,128)} %copy-done.4, ...), custom_call_target="tpu_custom_call" | custom-call | tf_op jit(solution)/shard_map/adam_blocks/pallas_call | solution.py:1335
  (542 shorter events, 251.7 us)
Async XLA Ops:
  15.2 17.6 %collective-permute-start.1 = (bf16[2,1,48,768]{3,2,0,1:T(8,128)(2,1)S(1)}, bf16[2,1,48,768]{3,2,0,1:T(8,128)(2,1)S(1)}, u32[]{:S(2)}, u32[]{:S(2)}) collective-permute-start(bf16[2,1,48,768]{3,2,0,1:T(8,128)(2,1)S(1)} %get-tuple-element.281), channel_id=1, source_target_pairs={{0,16},{4,20},{8,24},{12,28},{16,0},{20,4},{24,8},{28,12},{1,17},{... | collective-permute-start | bytes 442376 | tf_op jit(solution)/shard_map/ppermute | solution.py:125
  58.0 24.4 %collective-permute-start.13 = (bf16[8,2,1,48,768]{4,3,2,1,0:T(8,128)(2,1)}, bf16[8,2,1,48,768]{4,3,2,1,0:T(8,128)(2,1)}, u32[]{:S(2)}, u32[]{:S(2)}) collective-permute-start(bf16[8,2,1,48,768]{4,3,2,1,0:T(8,128)(2,1)} %copy-done.89), channel_id=1, source_target_pairs={{0,4},{1,3},{2,6},{3,1},{4,0},{5,7},{6,2},{7,5},{8,12},{9,11},{10,... | collective-permute-start | bytes 3538952 | tf_op jit(solution)/shard_map/ppermute | solution.py:121
  84.8 18.1 %collective-permute-start.19 = (bf16[8,2,1,48,768]{4,3,2,1,0:T(8,128)(2,1)}, bf16[8,2,1,48,768]{4,3,2,1,0:T(8,128)(2,1)}, u32[]{:S(2)}, u32[]{:S(2)}) collective-permute-start(bf16[8,2,1,48,768]{4,3,2,1,0:T(8,128)(2,1)} %collective-permute-done.13.refs_1_), channel_id=1, source_target_pairs={{0,1},{1,0},{2,3},{3,2},{4,5},{5,4},{6,7},{7,6},{8,9},{9,8},{10,11... | collective-permute-start | bytes 3538952 | tf_op jit(solution)/shard_map/ppermute | solution.py:107
  102.9 32.4 %collective-permute-start.20 = (bf16[8,2,2,48,768]{4,3,2,1,0:T(8,128)(2,1)}, bf16[8,2,2,48,768]{4,3,2,1,0:T(8,128)(2,1)}, u32[]{:S(2)}, u32[]{:S(2)}) collective-permute-start(bf16[8,2,2,48,768]{4,3,2,1,0:T(8,128)(2,1)} %pad_maximum_fusion.refs_0_), channel_id=1, source_target_pairs={{0,4},{1,3},{2,6},{3,1},{4,0},{5,7},{6,2},{7,5},{8,12},{9,11},{10,... | collective-permute-start | bytes 7077896 | tf_op jit(solution)/shard_map/ppermute | solution.py:121
  104.6 30.7 %collective-permute-start.25 = (bf16[8,2,2,48,768]{4,3,2,1,0:T(8,128)(2,1)}, bf16[8,2,2,48,768]{4,3,2,1,0:T(8,128)(2,1)}, u32[]{:S(2)}, u32[]{:S(2)}) collective-permute-start(bf16[8,2,2,48,768]{4,3,2,1,0:T(8,128)(2,1)} %pad_maximum_fusion.refs_0_), channel_id=1, source_target_pairs={{0,1},{1,0},{2,3},{3,2},{4,5},{5,4},{6,7},{7,6},{8,9},{9,8},{10,11... | collective-permute-start | bytes 7077896 | tf_op jit(solution)/shard_map/ppermute | solution.py:107
  135.4 39.9 %collective-permute-start.29 = (bf16[8,2,2,48,768]{4,3,2,1,0:T(8,128)(2,1)}, bf16[8,2,2,48,768]{4,3,2,1,0:T(8,128)(2,1)}, u32[]{:S(2)}, u32[]{:S(2)}) collective-permute-start(bf16[8,2,2,48,768]{4,3,2,1,0:T(8,128)(2,1)} %collective-permute-done.20.refs_1_), channel_id=1, source_target_pairs={{0,1},{1,0},{2,3},{3,2},{4,5},{5,4},{6,7},{7,6},{8,9},{9,8},{10,11... | collective-permute-start | bytes 7077896 | tf_op jit(solution)/shard_map/ppermute | solution.py:107
  151.5 21.6 %collective-permute-start.28 = (bf16[4,2,1,48,768]{4,3,1,2,0:T(8,128)(2,1)}, bf16[4,2,1,48,768]{4,3,1,2,0:T(8,128)(2,1)S(1)}, u32[]{:S(2)}, u32[]{:S(2)}) collective-permute-start(bf16[4,2,1,48,768]{4,3,1,2,0:T(8,128)(2,1)} %pad_maximum_fusion.11), channel_id=1, source_target_pairs={{0,2},{1,5},{2,0},{3,7},{4,6},{5,1},{6,4},{7,3},{8,10},{9,13},{10,... | collective-permute-start | bytes 1769480 | tf_op jit(solution)/shard_map/ppermute | solution.py:116
  152.7 17.9 %collective-permute-start.26 = (bf16[2,2,48,768]{3,2,1,0:T(8,128)(2,1)}, bf16[2,2,48,768]{3,2,1,0:T(8,128)(2,1)S(1)}, u32[]{:S(2)}, u32[]{:S(2)}) collective-permute-start(bf16[2,2,48,768]{3,2,1,0:T(8,128)(2,1)} %get-tuple-element.314), channel_id=1, source_target_pairs={{0,16},{4,20},{8,24},{12,28},{16,0},{20,4},{24,8},{28,12},{1,17},{... | collective-permute-start | bytes 884744 | tf_op jit(solution)/shard_map/ppermute | solution.py:125
  175.2 18.1 %collective-permute-start.31 = (bf16[8,2,1,48,768]{4,3,1,2,0:T(8,128)(2,1)}, bf16[8,2,1,48,768]{4,3,1,2,0:T(8,128)(2,1)}, u32[]{:S(2)}, u32[]{:S(2)}) collective-permute-start(bf16[8,2,1,48,768]{4,3,1,2,0:T(8,128)(2,1)} %pad_maximum_fusion.3), channel_id=1, source_target_pairs={{0,4},{1,3},{2,6},{3,1},{4,0},{5,7},{6,2},{7,5},{8,12},{9,11},{10,... | collective-permute-start | bytes 3538952 | tf_op jit(solution)/shard_map/ppermute | solution.py:121
  175.8 17.6 %collective-permute-start.32 = (bf16[8,2,1,48,768]{4,3,1,2,0:T(8,128)(2,1)}, bf16[8,2,1,48,768]{4,3,1,2,0:T(8,128)(2,1)}, u32[]{:S(2)}, u32[]{:S(2)}) collective-permute-start(bf16[8,2,1,48,768]{4,3,1,2,0:T(8,128)(2,1)} %pad_maximum_fusion.3), channel_id=1, source_target_pairs={{0,1},{1,0},{2,3},{3,2},{4,5},{5,4},{6,7},{7,6},{8,9},{9,8},{10,11... | collective-permute-start | bytes 3538952 | tf_op jit(solution)/shard_map/ppermute | solution.py:107
  194.9 17.9 %collective-permute-start.34 = (bf16[8,2,1,48,768]{4,3,1,2,0:T(8,128)(2,1)}, bf16[8,2,1,48,768]{4,3,1,2,0:T(8,128)(2,1)}, u32[]{:S(2)}, u32[]{:S(2)}) collective-permute-start(bf16[8,2,1,48,768]{4,3,1,2,0:T(8,128)(2,1)} %collective-permute-done.31), channel_id=1, source_target_pairs={{0,1},{1,0},{2,3},{3,2},{4,5},{5,4},{6,7},{7,6},{8,9},{9,8},{10,11... | collective-permute-start | bytes 3538952 | tf_op jit(solution)/shard_map/ppermute | solution.py:107
  212.8 29.2 %collective-permute-start.35 = (bf16[8,2,2,48,768]{4,3,2,1,0:T(8,128)(2,1)}, bf16[8,2,2,48,768]{4,3,2,1,0:T(8,128)(2,1)}, u32[]{:S(2)}, u32[]{:S(2)}) collective-permute-start(bf16[8,2,2,48,768]{4,3,2,1,0:T(8,128)(2,1)} %pad_maximum_fusion.1.refs_0_), channel_id=1, source_target_pairs={{0,4},{1,3},{2,6},{3,1},{4,0},{5,7},{6,2},{7,5},{8,12},{9,11},{10,... | collective-permute-start | bytes 7077896 | tf_op jit(solution)/shard_map/ppermute | solution.py:121
  214.3 27.6 %collective-permute-start.36 = (bf16[8,2,2,48,768]{4,3,2,1,0:T(8,128)(2,1)}, bf16[8,2,2,48,768]{4,3,2,1,0:T(8,128)(2,1)S(1)}, u32[]{:S(2)}, u32[]{:S(2)}) collective-permute-start(bf16[8,2,2,48,768]{4,3,2,1,0:T(8,128)(2,1)} %pad_maximum_fusion.1.refs_0_), channel_id=1, source_target_pairs={{0,1},{1,0},{2,3},{3,2},{4,5},{5,4},{6,7},{7,6},{8,9},{9,8},{10,11... | collective-permute-start | bytes 7077896 | tf_op jit(solution)/shard_map/ppermute | solution.py:107
  246.8 19.5 %collective-permute-start.38 = (bf16[2,6,96,192]{3,2,1,0:T(8,128)(2,1)S(1)}, bf16[2,6,96,192]{3,2,1,0:T(8,128)(2,1)S(1)}, u32[]{:S(2)}, u32[]{:S(2)}) collective-permute-start(bf16[2,6,96,192]{3,2,1,0:T(8,128)(2,1)S(1)} %get-tuple-element.366), channel_id=1, source_target_pairs={{0,2},{1,3},{2,0},{3,1},{4,6},{5,7},{6,4},{7,5},{8,10},{9,11},{10,... | collective-permute-start | bytes 1327112 | tf_op jit(solution)/shard_map/ppermute | solution.py:103
  267.8 21.9 %collective-permute-start.39 = (bf16[2,2,6,96,192]{4,3,2,1,0:T(8,128)(2,1)S(1)}, bf16[2,2,6,96,192]{4,3,2,1,0:T(8,128)(2,1)S(1)}, u32[]{:S(2)}, u32[]{:S(2)}) collective-permute-start(bf16[2,2,6,96,192]{4,3,2,1,0:T(8,128)(2,1)S(1)} %pad_maximum_fusion.5), channel_id=1, source_target_pairs={{0,1},{1,0},{2,3},{3,2},{4,5},{5,4},{6,7},{7,6},{8,9},{9,8},{10,11... | collective-permute-start | bytes 2654216 | tf_op jit(solution)/shard_map/ppermute | solution.py:107
  289.7 21.3 %collective-permute-start.40 = (bf16[2,8,2,2,48,768]{5,4,3,2,1,0:T(8,128)(2,1)}, bf16[2,8,2,2,48,768]{5,4,3,2,1,0:T(8,128)(2,1)}, u32[]{:S(2)}, u32[]{:S(2)}) collective-permute-start(bf16[2,8,2,2,48,768]{5,4,3,2,1,0:T(8,128)(2,1)} %get-tuple-element.396), channel_id=1, source_target_pairs={{0,1},{1,0},{2,3},{3,2},{4,5},{5,4},{6,7},{7,6},{8,9},{9,8},{10,11... | collective-permute-start | bytes 14155784 | tf_op jit(solution)/shard_map/ppermute | solution.py:107
  314.1 29.0 %collective-permute-start.41 = (bf16[8,2,2,48,768]{4,3,2,1,0:T(8,128)(2,1)S(1)}, bf16[8,2,2,48,768]{4,3,2,1,0:T(8,128)(2,1)}, u32[]{:S(2)}, u32[]{:S(2)}) collective-permute-start(bf16[8,2,2,48,768]{4,3,2,1,0:T(8,128)(2,1)S(1)} %fusion), channel_id=1, source_target_pairs={{0,4},{1,3},{2,6},{3,1},{4,0},{5,7},{6,2},{7,5},{8,12},{9,11},{10,... | collective-permute-start | bytes 7077896 | tf_op jit(solution)/shard_map/ppermute | solution.py:121
  314.7 31.9 %collective-permute-start.42 = (bf16[2,8,2,1,48,768]{5,4,2,3,1,0:T(8,128)(2,1)}, bf16[2,8,2,1,48,768]{5,4,2,3,1,0:T(8,128)(2,1)}, u32[]{:S(2)}, u32[]{:S(2)}) collective-permute-start(bf16[2,8,2,1,48,768]{5,4,2,3,1,0:T(8,128)(2,1)} %bitcast.73), channel_id=1, source_target_pairs={{0,1},{1,0},{2,3},{3,2},{4,5},{5,4},{6,7},{7,6},{8,9},{9,8},{10,11... | collective-permute-start | bytes 7077896 | tf_op jit(solution)/shard_map/ppermute | solution.py:107
  349.4 31.2 %collective-permute-start.43 = (bf16[2,8,2,2,48,768]{5,4,3,2,1,0:T(8,128)(2,1)}, bf16[2,8,2,2,48,768]{5,4,3,2,1,0:T(8,128)(2,1)}, u32[]{:S(2)}, u32[]{:S(2)}) collective-permute-start(bf16[2,8,2,2,48,768]{5,4,3,2,1,0:T(8,128)(2,1)} %get-tuple-element.433), channel_id=1, source_target_pairs={{0,1},{1,0},{2,3},{3,2},{4,5},{5,4},{6,7},{7,6},{8,9},{9,8},{10,11... | collective-permute-start | bytes 14155784 | tf_op jit(solution)/shard_map/ppermute | solution.py:107
  349.4 29.2 %collective-permute-start.44 = (bf16[4,2,2,48,768]{4,3,2,1,0:T(8,128)(2,1)}, bf16[4,2,2,48,768]{4,3,2,1,0:T(8,128)(2,1)}, u32[]{:S(2)}, u32[]{:S(2)}) collective-permute-start(bf16[4,2,2,48,768]{4,3,2,1,0:T(8,128)(2,1)} %fusion.5), channel_id=1, source_target_pairs={{0,2},{1,5},{2,0},{3,7},{4,6},{5,1},{6,4},{7,3},{8,10},{9,13},{10,... | collective-permute-start | bytes 3538952 | tf_op jit(solution)/shard_map/ppermute | solution.py:116
  350.0 33.7 %collective-permute-start.45 = (bf16[8,2,1,48,768]{4,3,1,2,0:T(8,128)(2,1)}, bf16[8,2,1,48,768]{4,3,1,2,0:T(8,128)(2,1)}, u32[]{:S(2)}, u32[]{:S(2)}) collective-permute-start(bf16[8,2,1,48,768]{4,3,1,2,0:T(8,128)(2,1)} %bitcast.512), channel_id=1, source_target_pairs={{0,4},{1,3},{2,6},{3,1},{4,0},{5,7},{6,2},{7,5},{8,12},{9,11},{10,... | collective-permute-start | bytes 3538952 | tf_op jit(solution)/shard_map/ppermute | solution.py:121
  383.8 30.8 %collective-permute-start.47 = (bf16[2,8,2,1,48,768]{5,4,2,3,1,0:T(8,128)(2,1)}, bf16[2,8,2,1,48,768]{5,4,2,3,1,0:T(8,128)(2,1)S(1)}, u32[]{:S(2)}, u32[]{:S(2)}) collective-permute-start(bf16[2,8,2,1,48,768]{5,4,2,3,1,0:T(8,128)(2,1)} %bitcast.85), channel_id=1, source_target_pairs={{0,1},{1,0},{2,3},{3,2},{4,5},{5,4},{6,7},{7,6},{8,9},{9,8},{10,11... | collective-permute-start | bytes 7077896 | tf_op jit(solution)/shard_map/ppermute | solution.py:107
  385.5 30.7 %collective-permute-start.46 = (bf16[8,2,2,48,768]{4,3,2,1,0:T(8,128)(2,1)S(1)}, bf16[8,2,2,48,768]{4,3,2,1,0:T(8,128)(2,1)S(1)}, u32[]{:S(2)}, u32[]{:S(2)}) collective-permute-start(bf16[8,2,2,48,768]{4,3,2,1,0:T(8,128)(2,1)S(1)} %fusion.1), channel_id=1, source_target_pairs={{0,4},{1,3},{2,6},{3,1},{4,0},{5,7},{6,2},{7,5},{8,12},{9,11},{10,... | collective-permute-start | bytes 7077896 | tf_op jit(solution)/shard_map/ppermute | solution.py:121
  417.8 27.9 %collective-permute-start.56 = (bf16[8,2,1,48,768]{4,3,1,2,0:T(8,128)(2,1)}, bf16[8,2,1,48,768]{4,3,1,2,0:T(8,128)(2,1)}, u32[]{:S(2)}, u32[]{:S(2)}) collective-permute-start(bf16[8,2,1,48,768]{4,3,1,2,0:T(8,128)(2,1)} %bitcast.101), channel_id=1, source_target_pairs={{0,4},{1,3},{2,6},{3,1},{4,0},{5,7},{6,2},{7,5},{8,12},{9,11},{10,... | collective-permute-start | bytes 3538952 | tf_op jit(solution)/shard_map/ppermute | solution.py:121
  419.1 24.4 %collective-permute-start.53 = (bf16[4,2,1,48,768]{4,3,1,2,0:T(8,128)(2,1)}, bf16[4,2,1,48,768]{4,3,1,2,0:T(8,128)(2,1)}, u32[]{:S(2)}, u32[]{:S(2)}) collective-permute-start(bf16[4,2,1,48,768]{4,3,1,2,0:T(8,128)(2,1)} %bitcast.99), channel_id=1, source_target_pairs={{0,2},{1,5},{2,0},{3,7},{4,6},{5,1},{6,4},{7,3},{8,10},{9,13},{10,... | collective-permute-start | bytes 1769480 | tf_op jit(solution)/shard_map/ppermute | solution.py:116
  421.1 24.6 %collective-permute-start.57 = (bf16[2,2,48,768]{3,2,1,0:T(8,128)(2,1)}, bf16[2,2,48,768]{3,2,1,0:T(8,128)(2,1)S(1)}, u32[]{:S(2)}, u32[]{:S(2)}) collective-permute-start(bf16[2,2,48,768]{3,2,1,0:T(8,128)(2,1)} %fusion.21), channel_id=1, source_target_pairs={{0,16},{4,20},{8,24},{12,28},{16,0},{20,4},{24,8},{28,12},{1,17},{... | collective-permute-start | bytes 884744 | tf_op jit(solution)/shard_map/ppermute | solution.py:125
  424.5 19.0 %collective-permute-start.54 = (bf16[4,32,768]{2,1,0:T(8,128)(2,1)S(1)}, bf16[4,32,768]{2,1,0:T(8,128)(2,1)S(1)}, u32[]{:S(2)}, u32[]{:S(2)}) collective-permute-start(bf16[4,32,768]{2,1,0:T(8,128)(2,1)S(1)} %pad_maximum_fusion.22), channel_id=1, source_target_pairs={{0,4},{4,0},{8,12},{12,8},{16,20},{20,16},{24,28},{28,24},{1,5},{5... | collective-permute-start | bytes 589832 | tf_op jit(solution)/shard_map/ppermute | solution.py:111
  445.7 21.6 %collective-permute-start.58 = (bf16[4,2,2,48,768]{4,3,2,1,0:T(8,128)(2,1)}, bf16[4,2,2,48,768]{4,3,2,1,0:T(8,128)(2,1)}, u32[]{:S(2)}, u32[]{:S(2)}) collective-permute-start(bf16[4,2,2,48,768]{4,3,2,1,0:T(8,128)(2,1)} %fusion.4), channel_id=1, source_target_pairs={{0,2},{1,5},{2,0},{3,7},{4,6},{5,1},{6,4},{7,3},{8,10},{9,13},{10,... | collective-permute-start | bytes 3538952 | tf_op jit(solution)/shard_map/ppermute | solution.py:116
  472.0 19.4 %collective-permute-start.62 = (bf16[2,2,2,48,768]{4,3,2,1,0:T(8,128)(2,1)S(1)}, bf16[2,2,2,48,768]{4,3,2,1,0:T(8,128)(2,1)S(1)}, u32[]{:S(2)}, u32[]{:S(2)}) collective-permute-start(bf16[2,2,2,48,768]{4,3,2,1,0:T(8,128)(2,1)S(1)} %fusion.13), channel_id=1, source_target_pairs={{0,8},{4,12},{8,0},{12,4},{16,24},{20,28},{24,16},{28,20},{1,9},{5... | collective-permute-start | bytes 1769480 | tf_op jit(solution)/shard_map/ppermute | solution.py:129
  475.1 17.6 %collective-permute-start.65 = (bf16[4,2,1,48,768]{4,3,1,2,0:T(8,128)(2,1)S(1)}, bf16[4,2,1,48,768]{4,3,1,2,0:T(8,128)(2,1)S(1)}, u32[]{:S(2)}, u32[]{:S(2)}) collective-permute-start(bf16[4,2,1,48,768]{4,3,1,2,0:T(8,128)(2,1)S(1)} %bitcast.522), channel_id=1, source_target_pairs={{0,2},{1,5},{2,0},{3,7},{4,6},{5,1},{6,4},{7,3},{8,10},{9,13},{10,... | collective-permute-start | bytes 1769480 | tf_op jit(solution)/shard_map/ppermute | solution.py:116
  524.7 19.3 %collective-permute-start.75 = (bf16[2,1,48,768]{3,2,1,0:T(8,128)(2,1)S(1)}, bf16[2,1,48,768]{3,2,1,0:T(8,128)(2,1)S(1)}, u32[]{:S(2)}, u32[]{:S(2)}) collective-permute-start(bf16[2,1,48,768]{3,2,1,0:T(8,128)(2,1)S(1)} %fusion.31), channel_id=1, source_target_pairs={{0,16},{4,20},{8,24},{12,28},{16,0},{20,4},{24,8},{28,12},{1,17},{... | collective-permute-start | bytes 442376 | tf_op jit(solution)/shard_map/ppermute | solution.py:125
  553.2 30.2 %collective-permute-start.83 = (f32[6,48,768]{2,1,0:T(8,128)S(1)}, f32[6,48,768]{2,1,0:T(8,128)S(1)}, u32[]{:S(2)}, u32[]{:S(2)}) collective-permute-start(f32[6,48,768]{2,1,0:T(8,128)S(1)} %pad_maximum_fusion.7), channel_id=1, source_target_pairs={{0,1},{1,0},{2,3},{3,2},{4,5},{5,4},{6,7},{7,6},{8,9},{9,8},{10,11... | collective-permute-start | bytes 2654216 | tf_op jit(solution)/shard_map/ppermute | solution.py:107
  (150 other events, 1590.9 us)
